TPU v7x, 32 devices: a whole 2x2x4 slice. The times are simulated.
32 devices in a mesh: pair: 16 (over z, x, core), virt: 2 (over y).
Axes of the slice: x: 2, y: 2, z: 4, core: 2. Of those that a mesh axis runs over, the one named last changes fastest.
Arguments:
- amplitudes: bfloat16 [64, 1024, 1024], P('pair', None, 'virt'), may hold values from -0.1796875 to 0.1796875
- cholesky: bfloat16 [8, 1024, 1792], P(None, 'virt', 'pair'), may hold values from -0.1640625 to 0.1640625
- energy_first: float32 [8], replicated, may hold values from -3 to -0.3
- energy_second: float32 [8], replicated, may hold values from -3 to -0.3
- energy_virtual: float32 [1024], replicated, may hold values from 0.2 to 4
Outputs:
- residual: bfloat16 [64, 1024, 1024], P('pair', None, 'virt')
All inputs are finite; a program needn't handle non-finite values.
Results may differ from a plain program's by a relative error of at most 0.0095.
Values may be sent and summed in bfloat16 or wider, within the bound.
No kernel may reach another device: no remote copies, remote signals or barrier semaphores. Data moves between devices by JAX's collectives and lax.ppermute only.
A program may use at most 128 MiB of HBM per device.

v0:
```python
import jax
import jax.numpy as jnp
from jax import lax
from jax.sharding import PartitionSpec as P

OCC = 8


def from_partner(x, axis, bit):
    return lax.ppermute(x, axis, [(i, i ^ 1 << bit) for i in range(lax.axis_size(axis))])


def on_device(amplitudes, cholesky, energy_first, energy_second, energy_virtual):
    pair_count, virtual_count, local_virtual = amplitudes.shape
    tiles_count = lax.axis_size("virt")
    first_count = max(pair_count // OCC, 1)
    second_count = pair_count // first_count
    offset = lax.axis_index("pair") * pair_count
    first_start = offset // OCC
    second_start = offset % OCC
    column_start = lax.axis_index("virt") * local_virtual
    blocks = amplitudes.reshape(pair_count, tiles_count, local_virtual, local_virtual)
    arrived = lax.all_to_all(blocks, "virt", split_axis=1, concat_axis=1, tiled=True)
    mirrored = jnp.swapaxes(arrived, 2, 3).reshape(pair_count, virtual_count, local_virtual)
    combined = (2.0 * amplitudes.astype(jnp.float32) - mirrored.astype(jnp.float32)).astype(
        jnp.bfloat16
    )
    combined = combined.reshape(first_count, second_count, virtual_count, local_virtual)
    vectors = lax.all_gather(cholesky, "pair", axis=2, tiled=True)
    chosen = lax.dynamic_slice_in_dim(vectors, second_start, second_count, 0)
    half_width = chosen.shape[2] // 2
    pieces = []
    for part_index in range(2):
        picked = chosen[:, :, part_index * half_width : (part_index + 1) * half_width]
        partial_value = jnp.einsum(
            "ilad,ldq->iaq", combined, picked, preferred_element_type=jnp.float32
        )
        tile_sum = lax.psum(partial_value.astype(jnp.bfloat16), "virt")
        collected = tile_sum[None]
        collected = jnp.concatenate([collected, from_partner(collected, "pair", 0)], axis=0)
        pieces.append(jnp.sum(collected.astype(jnp.float32), axis=0).astype(jnp.bfloat16))
    reduced = jnp.concatenate(pieces, axis=2)
    cycle_term = jnp.einsum("iaq,lbq->ilab", reduced, chosen, preferred_element_type=jnp.float32)
    first_energy = lax.dynamic_slice_in_dim(energy_first, first_start, first_count, 0)
    second_energy = lax.dynamic_slice_in_dim(energy_second, second_start, second_count, 0)
    column_energy = lax.dynamic_slice_in_dim(energy_virtual, column_start, local_virtual, 0)
    virtual_pairs = energy_virtual[:, None] + column_energy[None, :]
    diagonal = (
        virtual_pairs[None, None, :, :]
        - first_energy[:, None, None, None]
        - second_energy[None, :, None, None]
    )
    values = amplitudes.reshape(first_count, second_count, virtual_count, local_virtual).astype(
        jnp.float32
    )
    result = diagonal * values + cycle_term
    return result.reshape(pair_count, virtual_count, local_virtual).astype(jnp.bfloat16)


def solution(mesh):
    return jax.shard_map(
        on_device,
        mesh=mesh,
        in_specs=(P("pair", None, "virt"), P(None, "virt", "pair"), P(), P(), P()),
        out_specs=P("pair", None, "virt"),
        check_vma=False,
    )
```

profile of v0, /device:TPU:0, one launch (start us, length us, event | category | flops | bytes accessed | tf_op | source)
XLA Modules:
  0.0 297.6 jit_solution(3874330547631116518)
XLA Ops:
  6.5 2.6 copy.20
  9.2 4.5 %copy.22 = bf16[4,2,512,512]{3,2,0,1:T(8,128)(2,1)} copy(bf16[4,2,512,512]{3,2,1,0:T(8,128)(2,1)} %bitcast.47) | data formatting | bytes 8388608 | tf_op jit(solution)/shard_map/reshape | solution.py:22
  13.7 5.6 %all-to-all-start = ((bf16[4,2,512,512]{3,2,0,1:T(8,128)(2,1)}), bf16[4,2,512,512]{3,2,0,1:T(8,128)(2,1)}, u32[]{:S(2)}, u32[]{:S(2)}) async-start(bf16[4,2,512,512]{3,2,0,1:T(8,128)(2,1)} %copy.22), calls=%async_computation | async-start | bytes 8388608 | tf_op jit(solution)/shard_map/all_to_all | solution.py:23
  19.3 0.0 all-reduce.3.cloned.1.call-start
  19.3 6.4 %copy.19 = bf16[4,1024,512]{1,2,0:T(8,128)(2,1)} copy(bf16[4,1024,512]{2,1,0:T(8,128)(2,1)} %param.5) | data formatting | bytes 8388608 | tf_op args[0]
  25.7 42.5 %all-to-all-done = bf16[4,2,512,512]{3,2,0,1:T(8,128)(2,1)} async-done(((bf16[4,2,512,512]{3,2,0,1:T(8,128)(2,1)}), bf16[4,2,512,512]{3,2,0,1:T(8,128)(2,1)}, u32[]{:S(2)}, u32[]{:S(2)}) %all-to-all-start) | async-done | bytes 4194336 | tf_op jit(solution)/shard_map/all_to_all | solution.py:23
  68.2 3.4 %convert_bitcast_fusion = f32[2,4,64,8,512]{4,3,2,1,0:T(8,128)S(1)} fusion(bf16[4,2,512,512]{3,2,0,1:T(8,128)(2,1)} %all-to-all-done), kind=kLoop, calls=%fused_computation.7 | loop fusion | flops 2097152 | bytes 12582912
  71.6 4.3 %copy.30 = f32[2,4,64,8,512]{4,3,0,2,1:T(8,128)} copy(f32[2,4,64,8,512]{4,3,2,1,0:T(8,128)S(1)} %convert_bitcast_fusion) | data formatting | bytes 16777216 | tf_op jit(solution)/shard_map/convert_element_type | solution.py:25
  75.9 50.3 %all-gather.2.cloned.1.call-done = bf16[8,512,1792]{1,0,2:T(8,128)(2,1)} async-done(((bf16[8,512,112]{1,0,2:T(8,128)(2,1)}), bf16[8,512,1792]{1,0,2:T(8,128)(2,1)}) %all-gather.2.cloned.1.call-update) | async-done | bytes 14680080 | tf_op jit(solution)/shard_map/all_gather | solution.py:29
  126.2 9.9 %constant_dynamic-slice_fusion = bf16[4,512,1792]{1,0,2:T(4,128)(2,1)} fusion(bf16[8,512,1792]{1,0,2:T(8,128)(2,1)} %all-gather.2.cloned.1.call-done, s32[]{:T(128)S(6)} %select_n.25), kind=kLoop, calls=%fused_computation.24 | loop fusion | bytes 14680068 | tf_op jit(solution)/shard_map/dynamic_slice | solution.py:30
  136.1 12.2 %copy.29 = bf16[4,512,1792]{2,1,0:T(8,128)(2,1)} copy(bf16[4,512,1792]{1,0,2:T(4,128)(2,1)} %constant_dynamic-slice_fusion) | data formatting | bytes 14680064
  148.4 11.7 %fusion.17 = bf16[1,1024,896]{2,1,0:T(8,128)(2,1)} fusion(bf16[4,512,1792]{2,1,0:T(8,128)(2,1)} %copy.29, f32[4,1024,512]{1,2,0:T(8,128)} %bitcast.48, bf16[4,1024,512]{1,2,0:T(8,128)(2,1)} %copy.19), kind=kOutput, calls=%fused_computation.22 | convolution fusion | flops 3767402496 | bytes 18087936 | tf_op jit(solution)/shard_map/ilad,ldq->iaq/dot_general | solution.py:35
  160.1 9.2 %fusion.20 = bf16[1,1024,896]{2,1,0:T(8,128)(2,1)} fusion(bf16[4,512,1792]{2,1,0:T(8,128)(2,1)S(1)} %copy-done, f32[4,1024,512]{1,2,0:T(8,128)} %bitcast.49, bf16[4,1024,512]{1,2,0:T(8,128)(2,1)S(1)} %copy-done.1), kind=kOutput, calls=%fused_computation.23 | convolution fusion | flops 3767402496 | bytes 18087936 | tf_op jit(solution)/shard_map/ilad,ldq->iaq/dot_general | solution.py:35
  169.4 95.7 %all-reduce.3.cloned.1.call-done = (bf16[1,1024,896]{2,1,0:T(8,128)(2,1)}, bf16[1,1024,896]{2,1,0:T(8,128)(2,1)}) async-done(((bf16[1,1024,896]{2,1,0:T(8,128)(2,1)}, bf16[1,1024,896]{2,1,0:T(8,128)(2,1)}), (bf16[1,1024,896]{2,1,0:T(8,128)(2,1)}, bf16[1,1024,896]{2,1,0:T(8,128)(2,1)})) %all-reduce.3.cloned.1.call-update) | async-done | bytes 3670032 | tf_op jit(solution)/shard_map/psum | solution.py:38
  265.1 0.5 collective-permute-start.1
  265.6 0.1 dynamic_slice.14
  265.7 0.7 dynamic_slice.13
  266.4 0.1 dynamic_slice.12
  266.4 1.0 add_subtract_fusion
  267.5 1.7 collective-permute-done
  269.2 3.0 bitcast_add_fusion.1
  272.2 1.7 bitcast_add_fusion
  274.0 10.6 %fusion.5 = bf16[4,1024,512]{1,2,0:T(8,128)(2,1)} fusion(bf16[4,1024,512]{1,2,0:T(8,128)(2,1)S(1)} %copy-done.2, f32[4]{0:T(128)S(1)} %dynamic_slice.14, f32[1024,512]{0,1:T(8,128)S(1)} %add_subtract_fusion, bf16[4,512,1792]{2,1,0:T(8,128)(2,1)S(1)} %bitcast.51, bf16[1,1024,896]{2,1,0:T(8,128)(2,1)S(1)} %bitcast_add_fusion, ...), kind=kOutput, calls=%fused_computation.8 | convolution fusion | flops 7534018560 | bytes 21495824 | tf_op jit(solution)/shard_map/iaq,lbq->ilab/dot_general | solution.py:43
  284.6 6.2 %copy.26 = bf16[4,1024,512]{2,1,0:T(8,128)(2,1)} copy(bf16[4,1024,512]{1,2,0:T(8,128)(2,1)} %fusion.5) | data formatting | bytes 8388608 | tf_op jit(solution)/shard_map/convert_element_type | solution.py:57
  (24 shorter events, 0.1 us)
Async XLA Ops:
  6.5 119.7 %all-gather.2.cloned.1.call-start = ((), (), s32[]{:S(2)}) async-start(), calls=%async_computation.1 | async-start | bytes 15597568 | tf_op jit(solution)/shard_map/all_gather | solution.py:29
  13.7 54.5 %all-to-all-start = ((bf16[4,2,512,512]{3,2,0,1:T(8,128)(2,1)}), bf16[4,2,512,512]{3,2,0,1:T(8,128)(2,1)}, u32[]{:S(2)}, u32[]{:S(2)}) async-start(bf16[4,2,512,512]{3,2,0,1:T(8,128)(2,1)} %copy.22), calls=%async_computation | async-start | bytes 8388608 | tf_op jit(solution)/shard_map/all_to_all | solution.py:23
  19.3 245.8 %all-reduce.3.cloned.1.call-start = ((), (), s32[]{:S(2)}) async-start(), calls=%async_computation.2 | async-start | bytes 7340032 | tf_op jit(solution)/shard_map/psum | solution.py:38
  148.4 11.8 %copy-start = (bf16[4,512,1792]{2,1,0:T(8,128)(2,1)S(1)}, bf16[4,512,1792]{2,1,0:T(8,128)(2,1)}, u32[]{:S(2)}) copy-start(bf16[4,512,1792]{2,1,0:T(8,128)(2,1)} %copy.29) | copy-start | bytes 22020100
  148.4 11.8 %copy-start.1 = (bf16[4,1024,512]{1,2,0:T(8,128)(2,1)S(1)}, bf16[4,1024,512]{1,2,0:T(8,128)(2,1)}, u32[]{:S(2)}) copy-start(bf16[4,1024,512]{1,2,0:T(8,128)(2,1)} %copy.19) | copy-start | bytes 12582916
  160.1 105.5 %copy-start.5 = (f32[8]{0:T(128)S(1)}, f32[8]{0:T(128)}, u32[]{:S(2)}) copy-start(f32[8]{0:T(128)} %param.8) | copy-start | bytes 100
  160.1 105.6 %copy-start.6 = (f32[8]{0:T(128)S(1)}, f32[8]{0:T(128)}, u32[]{:S(2)}) copy-start(f32[8]{0:T(128)} %param.7) | copy-start | bytes 100
  160.1 106.2 %copy-start.4 = (f32[1024]{0:T(1024)S(1)}, f32[1024]{0:T(1024)}, u32[]{:S(2)}) copy-start(f32[1024]{0:T(1024)} %param.9) | copy-start | bytes 12292
  169.4 104.6 %slice-start = ((s8[7340032]{0:T(1024)(128)(4,1)}), s8[3145728]{0:T(1024)(128)(4,1)S(1)}, s32[]{:S(2)}) async-start(s8[7340032]{0:T(1024)(128)(4,1)} %bitcast.50), calls=%async_computation.3 | async-start | bytes 6291456
  265.1 4.1 %collective-permute-start = (bf16[1,1,1024,896]{3,2,1,0:T(8,128)(2,1)}, bf16[1,1,1024,896]{3,2,1,0:T(8,128)(2,1)}, u32[]{:S(2)}, u32[]{:S(2)}) collective-permute-start(bf16[1,1,1024,896]{3,2,1,0:T(8,128)(2,1)} %bitcast.53), channel_id=1, source_target_pairs={{0,2},{2,0},{4,6},{6,4},{8,10},{10,8},{12,14},{14,12},{16,18},{18,... | collective-permute-start | bytes 5505032 | tf_op jit(solution)/shard_map/ppermute | solution.py:10
  265.1 7.1 %collective-permute-start.1 = (bf16[1,1,1024,896]{3,2,1,0:T(8,128)(2,1)}, bf16[1,1,1024,896]{3,2,1,0:T(8,128)(2,1)}, u32[]{:S(2)}, u32[]{:S(2)}) collective-permute-start(bf16[1,1,1024,896]{3,2,1,0:T(8,128)(2,1)} %bitcast.52), channel_id=1, source_target_pairs={{0,2},{2,0},{4,6},{6,4},{8,10},{10,8},{12,14},{14,12},{16,18},{18,... | collective-permute-start | bytes 5505032 | tf_op jit(solution)/shard_map/ppermute | solution.py:10
  266.4 5.9 %copy-start.3 = (bf16[1,1024,896]{2,1,0:T(8,128)(2,1)S(1)}, bf16[1,1024,896]{2,1,0:T(8,128)(2,1)}, u32[]{:S(2)}) copy-start(bf16[1,1024,896]{2,1,0:T(8,128)(2,1)} %get-tuple-element.5) | copy-start | bytes 5505028
  267.5 6.5 %slice-start.1 = ((s8[7340032]{0:T(1024)(128)(4,1)}), s8[4194304]{0:T(1024)(128)(4,1)S(1)}, s32[]{:S(2)}) async-start(s8[7340032]{0:T(1024)(128)(4,1)} %bitcast.50), calls=%async_computation.4 | async-start | bytes 8388608
  267.5 6.5 %copy-start.2 = (bf16[4,1024,512]{1,2,0:T(8,128)(2,1)S(1)}, bf16[4,1024,512]{1,2,0:T(8,128)(2,1)}, u32[]{:S(2)}) copy-start(bf16[4,1024,512]{1,2,0:T(8,128)(2,1)} %copy.19) | copy-start | bytes 12582916
Sparse Core Ops, SparseCore 0:
  9.6 116.5 all-gather.1
  169.5 95.5 all-reduce.2
where the time goes:
time: 298 us
  waiting for transfers between devices  190 us (64%)
  local copies, waits for them, and re-layouts  47 us (16%)
  matrix products  31.5 us (11%)
  between operations  13.5 us (5%)
  other arithmetic  9.11 us (3%)
  starting transfers between devices  6.12 us (2%)
    psum x1, waiting for transfers between devices, on_device(): tile_sum = lax.psum(partial_value.astype(jnp.bfloat16), 'virt')  95.7 us
    all_gather x1, waiting for transfers between devices, on_device(): vectors = lax.all_gather(cholesky, 'pair', axis=2, tiled=True)  50.3 us
    all_to_all x1, waiting for transfers between devices, on_device(): lax.all_to_all(blocks, 'virt', split_axis=1, concat_axis=1, tiled=True)  42.5 us
    unnamed x21, local copies, waits for them, and re-layouts  21.3 us
    dot_general x2, matrix products, on_device(): jnp.einsum('ilad,ldq->iaq', combined, picked, preferred_element_type=jnp....  21 us
    dot_general x1, matrix products, on_device(): jnp.einsum('iaq,lbq->ilab', reduced, chosen, preferred_element_type=jnp.f...  10.6 us
    dynamic_slice x1, local copies, waits for them, and re-layouts, on_device(): chosen = lax.dynamic_slice_in_dim(vectors, second_start, second_count, 0)  9.91 us
    convert_element_type x1, local copies, waits for them, and re-layouts, on_device(): result.reshape(pair_count, virtual_count, local_virtual)  6.19 us
  transfers between devices with their start and end apart: 5, of which 4 were waited for; matrix products, arithmetic and copies ran while one was open for 8% of the time, Pallas kernels for 0%

commit v1 on v0

v1 whole, which is shorter than its diff:
```python
import functools

import jax
import jax.numpy as jnp
from jax import lax
from jax.experimental import pallas as pl
from jax.experimental.pallas import tpu as pltpu
from jax.sharding import PartitionSpec as P

OCC = 8
BF16, F32 = jnp.bfloat16, jnp.float32
VMEM_LIMIT = 48 * 2**20


def params(steps=1):
    return pltpu.CompilerParams(
        dimension_semantics=("arbitrary",) * steps, vmem_limit_bytes=VMEM_LIMIT
    )


def anywhere(count):
    return [pl.BlockSpec(memory_space=pl.ANY)] * count


def swap(x, axis, bit):
    return lax.ppermute(x, axis, [(i, i ^ 1 << bit) for i in range(lax.axis_size(axis))])


def ring_of(count, groups):
    places = count // groups
    return list(range(0, places, 2)) + list(range(places - 1, 0, -2))


def along_ring(x, step, groups):
    order = ring_of(lax.axis_size("pair"), groups)
    pairs = [
        (a * groups + g, order[(n + step) % len(order)] * groups + g)
        for n, a in enumerate(order)
        for g in range(groups)
    ]
    return lax.ppermute(x, "pair", pairs)


def turn_kernel(tile, own, other, near, far):
    x = own[0].astype(F32)
    near[0] = (2.0 * x.T - x).astype(BF16)
    far[0] = other[0].T


def turn(tile, amplitudes):
    count, rows, width = amplitudes.shape
    block = (1, width, width)
    return pl.pallas_call(
        turn_kernel,
        grid_spec=pltpu.PrefetchScalarGridSpec(
            num_scalar_prefetch=1,
            grid=(count,),
            in_specs=[
                pl.BlockSpec(block, lambda j, t: (j, t[0], 0)),
                pl.BlockSpec(block, lambda j, t: (j, 1 - t[0], 0)),
            ],
            out_specs=[pl.BlockSpec(block, lambda j, t: (j, 0, 0))] * 2,
        ),
        out_shape=[jax.ShapeDtypeStruct((count, width, width), BF16)] * 2,
        compiler_params=params(),
        name="turn",
    )(tile, amplitudes, amplitudes)


def mix_kernel(far, arrived, out):
    out[...] = (2.0 * far[...].astype(F32) - arrived[...].astype(F32)).astype(BF16)


def mix(far, arrived):
    count, width, _ = far.shape
    spec = pl.BlockSpec((1, width, width), lambda j: (j, 0, 0))
    return pl.pallas_call(
        mix_kernel,
        grid=(count,),
        in_specs=[spec, spec],
        out_specs=spec,
        out_shape=jax.ShapeDtypeStruct(far.shape, BF16),
        compiler_params=params(),
        name="mix",
    )(far, arrived)


def partial_kernel(shards, halves, *refs):
    same, cross = refs[:shards], refs[shards : 2 * shards]
    mine, theirs = refs[2 * shards : 2 * shards + halves], refs[2 * shards + halves : 2 * shards + 2 * halves]
    outs, total = refs[-1 - halves : -1], refs[-1]
    j = pl.program_id(0)
    left = jnp.concatenate([r[0] for r in same], axis=0)
    right = jnp.concatenate([r[0] for r in cross], axis=0)
    for h in range(halves):
        value = jnp.dot(left, mine[h][0], preferred_element_type=F32)
        value += jnp.dot(right, theirs[h][0], preferred_element_type=F32)

        @pl.when(j == 0)
        def _():
            total[h] = value

        @pl.when(j > 0)
        def _():
            total[h] += value

        @pl.when(j == pl.num_programs(0) - 1)
        def _():
            outs[h][...] = total[h].astype(BF16)


def partial(same, cross, mine, theirs, after=()):
    shards, halves = len(same), len(mine)
    count, width, columns = mine[0].shape
    depth = same[0].shape[1]
    rows = shards * depth

    def body(*refs):
        keep = 2 * shards + 2 * halves
        partial_kernel(shards, halves, *refs[:keep], *refs[keep + len(after) :])

    return pl.pallas_call(
        body,
        grid=(count,),
        in_specs=[pl.BlockSpec((1, depth, width), lambda j: (j, 0, 0))] * (2 * shards)
        + [pl.BlockSpec((1, width, columns), lambda j: (j, 0, 0))] * (2 * halves)
        + anywhere(len(after)),
        out_specs=[pl.BlockSpec((rows, columns), lambda j: (0, 0))] * halves,
        out_shape=[jax.ShapeDtypeStruct((rows, columns), BF16)] * halves,
        scratch_shapes=[pltpu.VMEM((halves, rows, columns), F32)],
        compiler_params=params(),
        name="partial",
    )(*same, *cross, *mine, *theirs, *after)


def gate_kernel(count, *refs):
    pass


def gate(values, after):
    count = len(values)
    return pl.pallas_call(
        functools.partial(gate_kernel, count),
        in_specs=anywhere(count + len(after)),
        out_specs=anywhere(count),
        out_shape=[jax.ShapeDtypeStruct(v.shape, v.dtype) for v in values],
        input_output_aliases={n: n for n in range(count)},
        name="gate",
    )(*values, *after)


def join_kernel(near, far, near_sent, far_sent, out):
    out[0] = (near[...].astype(F32) + far_sent[...].astype(F32)).astype(BF16)
    out[1] = (far[...].astype(F32) + near_sent[...].astype(F32)).astype(BF16)


def join(near, far, near_sent, far_sent):
    rows, columns = near.shape
    return pl.pallas_call(
        join_kernel,
        in_specs=[pl.BlockSpec(memory_space=pltpu.VMEM)] * 4,
        out_specs=pl.BlockSpec(memory_space=pltpu.VMEM),
        out_shape=jax.ShapeDtypeStruct((2, rows, columns), BF16),
        compiler_params=pltpu.CompilerParams(vmem_limit_bytes=VMEM_LIMIT),
        name="join",
    )(near, far, near_sent, far_sent)


def residual_kernel(chunks, shards, first, last, after, tile, *refs):
    middles = refs[:chunks]
    vectors = refs[chunks : chunks + shards]
    rest = refs[chunks + shards :]
    if first:
        values, row_energy, column_energy, small = rest[:4]
        rest = rest[4:]
    else:
        before = rest[0]
        rest = rest[1:]
    out, turned, stacked = rest[after:]
    j, h = pl.program_id(0), pl.program_id(1)

    @pl.when(j == 0)
    def _():
        turned[h] = jnp.concatenate([m[h] for m in middles], axis=0).T

    @pl.when(h == 0)
    def _():
        stacked[...] = jnp.concatenate([v[0] for v in vectors], axis=0)

    total = jnp.dot(turned[h], stacked[...], preferred_element_type=F32)
    if first:
        diagonal = row_energy[...] + column_energy[...] - small[0] - small[1 + j]
        total += diagonal * values[0].astype(F32)
    else:
        total += before[0]
    out[0] = total.astype(out.dtype)


def residual(tile, middles, vectors, first=None, before=None, last=True, after=()):
    count, depth, width = vectors[0].shape
    columns = middles[0].shape[2]
    total_rows = sum(m.shape[1] for m in middles)
    assert total_rows == depth * len(vectors)
    by_row = pl.BlockSpec((1, columns, width), lambda j, h, t: (j, (t[0] + h) % 2, 0))
    in_specs = [pl.BlockSpec(m.shape, lambda j, h, t: (0, 0, 0)) for m in middles]
    in_specs += [pl.BlockSpec((1, depth, width), lambda j, h, t: (j, 0, 0))] * len(vectors)
    args = [*middles, *vectors]
    if first is not None:
        in_specs += [
            by_row,
            pl.BlockSpec((columns, 1), lambda j, h, t: ((t[0] + h) % 2, 0)),
            pl.BlockSpec((1, width), lambda j, h, t: (0, 0)),
            pl.BlockSpec(memory_space=pltpu.SMEM),
        ]
        args += first
    else:
        in_specs += [by_row]
        args += [before]
    return pl.pallas_call(
        functools.partial(
            residual_kernel, len(middles), len(vectors), first is not None, last, len(after)
        ),
        grid_spec=pltpu.PrefetchScalarGridSpec(
            num_scalar_prefetch=1,
            grid=(count, 2),
            in_specs=in_specs + anywhere(len(after)),
            out_specs=by_row,
            scratch_shapes=[
                pltpu.VMEM((2, columns, total_rows), BF16),
                pltpu.VMEM((total_rows, width), BF16),
            ],
        ),
        out_shape=jax.ShapeDtypeStruct((count, 2 * columns, width), BF16 if last else F32),
        compiler_params=params(2),
        name="residual",
    )(tile, *args, *after)


def two_tiles(amplitudes, cholesky, energy_first, energy_second, energy_virtual):
    count, virtual, width = amplitudes.shape
    groups = OCC // count
    places = lax.axis_size("pair") // groups
    place, group = lax.axis_index("pair") // groups, lax.axis_index("pair") % groups
    y = lax.axis_index("virt")
    tile = y.astype(jnp.int32).reshape(1)

    vectors = jnp.swapaxes(cholesky, 1, 2)
    same = [lax.dynamic_slice_in_dim(vectors, group * count, count, 0)]
    cross = [lax.dynamic_slice_in_dim(vectors, (1 - group) * count, count, 0)]

    ring = functools.partial(along_ring, groups=groups)
    half = places // 2
    forth_same, back_same = same[0], same[0]
    forth_cross, back_cross = cross[0], cross[0]
    for step in range(1, half):
        forth_same, back_same = ring(forth_same, 1), ring(back_same, -1)
        forth_cross, back_cross = ring(forth_cross, 1), ring(back_cross, -1)
        same += [forth_same, back_same]
        cross += [forth_cross, back_cross]
    same += [ring(forth_same, 1)]
    cross += [ring(back_cross, -1)]

    sent = lax.dynamic_slice_in_dim(amplitudes, (1 - y) * width, width, 1)
    arrived = swap(sent, "virt", 0)

    near, far_turned = turn(tile, amplitudes)
    near_theirs = swap(near, "pair", 0)

    (n1,) = partial(same[:3], cross[:3], [near], [near_theirs])
    (n2,) = partial(same[3:5], cross[3:5], [near], [near_theirs])
    far = mix(far_turned, arrived)
    far_theirs = swap(far, "pair", 0)
    n1, n2 = gate([n1, n2], [arrived])
    n1_sent, n2_sent = swap(n1, "virt", 0), swap(n2, "virt", 0)
    (f1,) = partial(same[:3], cross[:3], [far], [far_theirs])
    (f2,) = partial(same[3:5], cross[3:5], [far], [far_theirs])
    f1_sent, f2_sent = swap(f1, "virt", 0), swap(f2, "virt", 0)
    n3, f3 = partial(same[5:7], cross[5:7], [near, far], [near_theirs, far_theirs])
    n3_sent, f3_sent = swap(n3, "virt", 0), swap(f3, "virt", 0)
    n4, f4 = partial(same[7:], cross[7:], [near, far], [near_theirs, far_theirs])
    n4_sent, f4_sent = swap(n4, "virt", 0), swap(f4, "virt", 0)

    handed = [swap(v, "pair", 0) for v in cross]
    m1 = join(n1, f1, n1_sent, f1_sent)
    m2 = join(n2, f2, n2_sent, f2_sent)
    h1, h2 = swap(m1, "pair", 0), swap(m2, "pair", 0)
    m3 = join(n3, f3, n3_sent, f3_sent)
    h3 = swap(m3, "pair", 0)
    m4 = join(n4, f4, n4_sent, f4_sent)
    h4 = swap(m4, "pair", 0)

    small = jnp.concatenate(
        [
            lax.dynamic_slice_in_dim(energy_first, place, 1, 0),
            lax.dynamic_slice_in_dim(energy_second, group * count, count, 0),
        ]
    )
    column_energy = lax.dynamic_slice_in_dim(energy_virtual, y * width, width, 0)
    diagonal = [amplitudes, energy_virtual[:, None], column_energy[None, :], small]
    started = residual(
        tile, [m1, m2, h1, h2], same[:5] + handed[:5], first=diagonal, last=False
    )
    return residual(tile, [m3, m4, h3, h4], same[5:] + handed[5:], before=started)


def from_partner(x, axis, bit):
    return lax.ppermute(x, axis, [(i, i ^ 1 << bit) for i in range(lax.axis_size(axis))])


def any_tiles(amplitudes, cholesky, energy_first, energy_second, energy_virtual):
    pair_count, virtual_count, local_virtual = amplitudes.shape
    tiles_count = lax.axis_size("virt")
    first_count = max(pair_count // OCC, 1)
    second_count = pair_count // first_count
    offset = lax.axis_index("pair") * pair_count
    first_start = offset // OCC
    second_start = offset % OCC
    column_start = lax.axis_index("virt") * local_virtual
    blocks = amplitudes.reshape(pair_count, tiles_count, local_virtual, local_virtual)
    arrived = lax.all_to_all(blocks, "virt", split_axis=1, concat_axis=1, tiled=True)
    mirrored = jnp.swapaxes(arrived, 2, 3).reshape(pair_count, virtual_count, local_virtual)
    combined = (2.0 * amplitudes.astype(F32) - mirrored.astype(F32)).astype(BF16)
    combined = combined.reshape(first_count, second_count, virtual_count, local_virtual)
    vectors = lax.all_gather(cholesky, "pair", axis=2, tiled=True)
    chosen = lax.dynamic_slice_in_dim(vectors, second_start, second_count, 0)
    partial_value = jnp.einsum("ilad,ldq->iaq", combined, chosen, preferred_element_type=F32)
    collected = lax.psum(partial_value.astype(BF16), "virt").astype(F32)
    for bit in range((OCC // second_count).bit_length() - 1):
        collected = collected + from_partner(collected.astype(BF16), "pair", bit).astype(F32)
    reduced = collected.astype(BF16)
    cycle_term = jnp.einsum("iaq,lbq->ilab", reduced, chosen, preferred_element_type=F32)
    first_energy = lax.dynamic_slice_in_dim(energy_first, first_start, first_count, 0)
    second_energy = lax.dynamic_slice_in_dim(energy_second, second_start, second_count, 0)
    column_energy = lax.dynamic_slice_in_dim(energy_virtual, column_start, local_virtual, 0)
    virtual_pairs = energy_virtual[:, None] + column_energy[None, :]
    diagonal = (
        virtual_pairs[None, None, :, :]
        - first_energy[:, None, None, None]
        - second_energy[None, :, None, None]
    )
    values = amplitudes.reshape(first_count, second_count, virtual_count, local_virtual)
    result = diagonal * values.astype(F32) + cycle_term
    return result.reshape(pair_count, virtual_count, local_virtual).astype(BF16)


def on_device(amplitudes, *others):
    ring = lax.axis_size("pair") * amplitudes.shape[0] // OCC
    fits = lax.axis_size("virt") == 2 and amplitudes.shape[0] * 2 == OCC and ring == 8
    return (two_tiles if fits else any_tiles)(amplitudes, *others)


def solution(mesh):
    return jax.shard_map(
        on_device,
        mesh=mesh,
        in_specs=(P("pair", None, "virt"), P(None, "virt", "pair"), P(), P(), P()),
        out_specs=P("pair", None, "virt"),
        check_vma=False,
    )
```

time: 298 us -> 204 us (0.68)
  waiting for transfers between devices: 190 us -> 87.9 us
  Pallas kernels: 0 us -> 58.7 us
  matrix products: 31.5 us -> 0 us
  starting transfers between devices: 6.12 us -> 32.1 us
  local copies, waits for them, and re-layouts: 47 us -> 22.8 us
  between operations: 13.5 us -> 0.39 us
  other arithmetic: 9.11 us -> 0.76 us
    psum x1 -> x0, waiting for transfers between devices: 95.7 us -> none  [on_device(): tile_sum = lax.psum(partial_value.astype(jnp.bfloat16), 'virt')]
    ppermute x2 -> x37, waiting for transfers between devices: 1.72 us -> 87.9 us  [the longest x23 52.1 us: swap(): lax.ppermute(x, axis, [(i, i ^ 1 << bit) for i in range(lax.axis_size(axi...]
    pallas_call x0 -> x15, Pallas kernels: none -> 58.7 us  [the longest x6 27.7 us: partial(): pl.pallas_call(body, grid=(count,), in_specs=[pl.BlockSpec((1, depth, wid...]
    all_gather x1 -> x0, waiting for transfers between devices: 50.3 us -> none  [on_device(): vectors = lax.all_gather(cholesky, 'pair', axis=2, tiled=True)]
    all_to_all x1 -> x0, waiting for transfers between devices: 42.5 us -> none  [on_device(): lax.all_to_all(blocks, 'virt', split_axis=1, concat_axis=1, tiled=True)]
    ppermute x2 -> x37, starting transfers between devices: 0.51 us -> 32.1 us  [the longest x14 17.5 us: along_ring(): return lax.ppermute(x, 'pair', pairs)]
    dot_general x3 -> x0, matrix products: 31.5 us -> none  [the longest x2 21 us: on_device(): jnp.einsum('ilad,ldq->iaq', combined, picked, preferred_element_type=jnp....]
    convert_element_type x2 -> x0, local copies, waits for them, and re-layouts: 10.5 us -> none  [the longest x1 6.19 us: on_device(): result.reshape(pair_count, virtual_count, local_virtual)]
  transfers between devices with their start and end apart: 5 -> 37, of which waited for: 4 -> 15; matrix products, arithmetic and copies ran while one was open for 8% -> 1% of each run, Pallas kernels for 0% -> 24%
where the time goes in v1:
time: 204 us; the launch traced here: 203 us
  waiting for transfers between devices  87.9 us (43%)
  Pallas kernels  58.7 us (29%)
  starting transfers between devices  32.1 us (16%)
  local copies, waits for them, and re-layouts  22.8 us (11%)
    ppermute x23, waiting for transfers between devices, swap(): lax.ppermute(x, axis, [(i, i ^ 1 << bit) for i in range(lax.axis_size(axi...  52.1 us
    ppermute x14, waiting for transfers between devices, along_ring(): return lax.ppermute(x, 'pair', pairs)  35.8 us
    pallas_call x6, Pallas kernels, partial(): pl.pallas_call(body, grid=(count,), in_specs=[pl.BlockSpec((1, depth, wid...  27.7 us
    pallas_call x2, Pallas kernels, residual(): pl.pallas_call(functools.partial(residual_kernel, len(middles), len(vecto...  23.4 us
    unnamed x64, local copies, waits for them, and re-layouts  17.5 us
    ppermute x14, starting transfers between devices, along_ring(): return lax.ppermute(x, 'pair', pairs)  17.5 us
    ppermute x23, starting transfers between devices, swap(): lax.ppermute(x, axis, [(i, i ^ 1 << bit) for i in range(lax.axis_size(axi...  14.6 us
    pallas_call x1, Pallas kernels, turn(): pl.pallas_call(turn_kernel, grid_spec=pltpu.PrefetchScalarGridSpec(num_sc...  4.53 us
  transfers between devices with their start and end apart: 37, of which 15 were waited for; matrix products, arithmetic and copies ran while one was open for 1% of the time, Pallas kernels for 24%

profile of v1, /device:TPU:0, one launch (start us, length us, event | category | flops | bytes accessed | tf_op | source)
XLA Modules:
  0.0 202.7 jit_solution(1124598345460376934)
XLA Ops:
  0.0 3.1 %constant_dynamic-slice_fusion = bf16[4,512,512]{2,1,0:T(8,128)(2,1)} fusion(bf16[4,1024,512]{2,1,0:T(8,128)(2,1)} %refs_14_.1, s32[]{:T(128)S(6)} %select_n.30), kind=kLoop, calls=%fused_computation.2 | loop fusion | bytes 4194308 | tf_op jit(solution)/shard_map/dynamic_slice | solution.py:263
  3.1 3.0 %collective-permute-start.12 = (bf16[4,512,512]{2,1,0:T(8,128)(2,1)}, bf16[4,512,512]{2,1,0:T(8,128)(2,1)S(1)}, u32[]{:S(2)}, u32[]{:S(2)}) collective-permute-start(bf16[4,512,512]{2,1,0:T(8,128)(2,1)} %constant_dynamic-slice_fusion), channel_id=1, source_target_pairs={{0,1},{1,0},{2,3},{3,2},{4,5},{5,4},{6,7},{7,6},{8,9},{9,8},{10,11... | collective-permute-start | bytes 6291464 | tf_op jit(solution)/shard_map/ppermute | solution.py:26
  6.0 4.5 %turn.1 = (bf16[4,512,512]{2,1,0:T(8,128)(2,1)}, bf16[4,512,512]{2,1,0:T(8,128)(2,1)S(1)}) custom-call(s32[1]{0:T(128)} %bitcast.tile, bf16[4,1024,512]{2,1,0:T(8,128)(2,1)} %refs_14_.1, bf16[4,1024,512]{2,1,0:T(8,128)(2,1)} %refs_14_.1), custom_call_target="tpu_custom_call" | custom-call | tf_op jit(solution)/shard_map/turn/pallas_call | solution.py:53
  14.8 37.1 %collective-permute-done.12.arrived.refs_2_ = bf16[4,512,512]{2,1,0:T(8,128)(2,1)S(1)} collective-permute-done((bf16[4,512,512]{2,1,0:T(8,128)(2,1)}, bf16[4,512,512]{2,1,0:T(8,128)(2,1)S(1)}, u32[]{:S(2)}, u32[]{:S(2)}) %collective-permute-start.12) | collective-permute-done | bytes 2097184 | tf_op jit(solution)/shard_map/ppermute | solution.py:26
  54.9 2.6 %mix.1.refs_5_.refs_3_.refs_6_.refs_4_ = bf16[4,512,512]{2,1,0:T(8,128)(2,1)S(1)} custom-call(bf16[4,512,512]{2,1,0:T(8,128)(2,1)S(1)} %copy-done.9, bf16[4,512,512]{2,1,0:T(8,128)(2,1)} %copy-done.27), custom_call_target="tpu_custom_call" | custom-call | tf_op jit(solution)/shard_map/mix/pallas_call | solution.py:77
  57.6 1.8 collective-permute-start.3
  61.4 9.6 %collective-permute-done.3.refs_2_.refs_6_ = bf16[4,112,512]{2,1,0:T(8,128)(2,1)S(1)} collective-permute-done((bf16[4,112,512]{2,1,0:T(8,128)(2,1)S(1)}, bf16[4,112,512]{2,1,0:T(8,128)(2,1)S(1)}, u32[]{:S(2)}, u32[]{:S(2)}) %collective-permute-start.3) | collective-permute-done | bytes 458784 | tf_op jit(solution)/shard_map/ppermute | solution.py:41
  72.8 7.7 %collective-permute-done.9.refs_5_ = bf16[4,112,512]{2,1,0:T(8,128)(2,1)} collective-permute-done((bf16[4,112,512]{2,1,0:T(8,128)(2,1)S(1)}, bf16[4,112,512]{2,1,0:T(8,128)(2,1)}, u32[]{:S(2)}, u32[]{:S(2)}) %collective-permute-start.9) | collective-permute-done | bytes 458784 | tf_op jit(solution)/shard_map/ppermute | solution.py:41
  84.0 1.7 collective-permute-start.10
  85.7 8.3 %collective-permute-done.4.refs_1_.refs_8_ = bf16[4,112,512]{2,1,0:T(8,128)(2,1)} collective-permute-done((bf16[4,112,512]{2,1,0:T(8,128)(2,1)S(1)}, bf16[4,112,512]{2,1,0:T(8,128)(2,1)}, u32[]{:S(2)}, u32[]{:S(2)}) %collective-permute-start.4) | collective-permute-done | bytes 458784 | tf_op jit(solution)/shard_map/ppermute | solution.py:41
  94.8 7.8 %collective-permute-done.10.refs_3_ = bf16[4,112,512]{2,1,0:T(8,128)(2,1)} collective-permute-done((bf16[4,112,512]{2,1,0:T(8,128)(2,1)}, bf16[4,112,512]{2,1,0:T(8,128)(2,1)}, u32[]{:S(2)}, u32[]{:S(2)}) %collective-permute-start.10) | collective-permute-done | bytes 458784 | tf_op jit(solution)/shard_map/ppermute | solution.py:41
  107.0 4.4 %partial.8.refs_0_ = bf16[336,512]{1,0:T(8,128)(2,1)S(1)} custom-call(bf16[4,112,512]{2,1,0:T(8,128)(2,1)S(1)} %get-tuple-element.22.refs_0_.refs_4_, bf16[4,112,512]{2,1,0:T(8,128)(2,1)S(1)} %collective-permute-done.refs_1_.refs_5_, bf16[4,112,512]{2,1,0:T(8,128)(2,1)S(1)} %collective-permute-done.3.refs_2_.refs_6_, ...), custom_call_target="tpu_custom_call" | custom-call | tf_op jit(solution)/shard_map/partial/pallas_call | solution.py:122
  113.7 4.2 %partial.9.refs_1_ = bf16[224,512]{1,0:T(8,128)(2,1)S(1)} custom-call(bf16[4,112,512]{2,1,0:T(8,128)(2,1)} %collective-permute-done.1.refs_0_.refs_7_, bf16[4,112,512]{2,1,0:T(8,128)(2,1)} %collective-permute-done.4.refs_1_.refs_8_, bf16[4,112,512]{2,1,0:T(8,128)(2,1)S(1)} %collective-permute-done.7.refs_2_, ...), custom_call_target="tpu_custom_call" | custom-call | tf_op jit(solution)/shard_map/partial/pallas_call | solution.py:122
  121.6 3.9 %partial.11.far = bf16[224,512]{1,0:T(8,128)(2,1)S(1)} custom-call(bf16[4,112,512]{2,1,0:T(8,128)(2,1)} %collective-permute-done.1.refs_0_.refs_7_, bf16[4,112,512]{2,1,0:T(8,128)(2,1)} %collective-permute-done.4.refs_1_.refs_8_, bf16[4,112,512]{2,1,0:T(8,128)(2,1)S(1)} %copy-done.15, bf16[4,112,512]{2,1,0:T(8,128)(2,1)} %collective-permute-done.10.refs_3_, ...), custom_call_target="tpu_custom_call" | custom-call | tf_op jit(solution)/shard_map/partial/pallas_call | solution.py:122
  127.7 4.0 %partial.10.far = bf16[336,512]{1,0:T(8,128)(2,1)S(1)} custom-call(bf16[4,112,512]{2,1,0:T(8,128)(2,1)S(1)} %get-tuple-element.22.refs_0_.refs_4_, bf16[4,112,512]{2,1,0:T(8,128)(2,1)S(1)} %collective-permute-done.refs_1_.refs_5_, bf16[4,112,512]{2,1,0:T(8,128)(2,1)S(1)} %copy-done.3, bf16[4,112,512]{2,1,0:T(8,128)(2,1)S(1)} %get-tuple-element.21.refs_3_, ...), custom_call_target="tpu_custom_call" | custom-call | tf_op jit(solution)/shard_map/partial/pallas_call | solution.py:122
  131.7 2.3 %collective-permute-done.28.near_sent = bf16[224,512]{1,0:T(8,128)(2,1)S(1)} collective-permute-done((bf16[224,512]{1,0:T(8,128)(2,1)}, bf16[224,512]{1,0:T(8,128)(2,1)S(1)}, u32[]{:S(2)}, u32[]{:S(2)}) %collective-permute-start.28) | collective-permute-done | bytes 229408 | tf_op jit(solution)/shard_map/ppermute | solution.py:26
  136.7 2.8 %collective-permute-start.18 = (bf16[4,112,512]{2,1,0:T(8,128)(2,1)}, bf16[4,112,512]{2,1,0:T(8,128)(2,1)}, u32[]{:S(2)}, u32[]{:S(2)}) collective-permute-start(bf16[4,112,512]{2,1,0:T(8,128)(2,1)} %collective-permute-done.11.refs_3_), channel_id=1, source_target_pairs={{0,4},{2,6},{8,0},{10,2},{16,8},{18,10},{24,16},{26,18},{28,24},{3... | collective-permute-start | bytes 1376264 | tf_op jit(solution)/shard_map/ppermute | solution.py:41
  139.5 4.3 %collective-permute-done.27.far_sent = bf16[336,512]{1,0:T(8,128)(2,1)S(1)} collective-permute-done((bf16[336,512]{1,0:T(8,128)(2,1)S(1)}, bf16[336,512]{1,0:T(8,128)(2,1)S(1)}, u32[]{:S(2)}, u32[]{:S(2)}) %collective-permute-start.27) | collective-permute-done | bytes 344096 | tf_op jit(solution)/shard_map/ppermute | solution.py:26
  145.5 6.3 %partial.6 = (bf16[224,512]{1,0:T(8,128)(2,1)S(1)}, bf16[224,512]{1,0:T(8,128)(2,1)S(1)}) custom-call(bf16[4,112,512]{2,1,0:T(8,128)(2,1)} %collective-permute-done.2.refs_0_.refs_4_, bf16[4,112,512]{2,1,0:T(8,128)(2,1)} %collective-permute-done.5.refs_1_.refs_5_, bf16[4,112,512]{2,1,0:T(8,128)(2,1)} %collective-permute-done.8.refs_2_, ...), custom_call_target="tpu_custom_call" | custom-call | tf_op jit(solution)/shard_map/partial/pallas_call | solution.py:122
  153.9 4.9 %partial.7 = (bf16[112,512]{1,0:T(8,128)(2,1)S(1)}, bf16[112,512]{1,0:T(8,128)(2,1)S(1)}) custom-call(bf16[4,112,512]{2,1,0:T(8,128)(2,1)S(1)} %collective-permute-done.17.refs_0_.refs_6_, bf16[4,112,512]{2,1,0:T(8,128)(2,1)} %collective-permute-done.18.refs_1_, bf16[4,512,512]{2,1,0:T(8,128)(2,1)} %get-tuple-element.13.refs_4_.refs_2_.refs_6_, ...), custom_call_target="tpu_custom_call" | custom-call | tf_op jit(solution)/shard_map/partial/pallas_call | solution.py:122
  161.8 3.4 %collective-permute-done.16.far_sent = bf16[224,512]{1,0:T(8,128)(2,1)S(1)} collective-permute-done((bf16[224,512]{1,0:T(8,128)(2,1)S(1)}, bf16[224,512]{1,0:T(8,128)(2,1)S(1)}, u32[]{:S(2)}, u32[]{:S(2)}) %collective-permute-start.16) | collective-permute-done | bytes 229408 | tf_op jit(solution)/shard_map/ppermute | solution.py:26
  167.4 2.6 %collective-permute-done.20.far_sent = bf16[112,512]{1,0:T(8,128)(2,1)S(1)} collective-permute-done((bf16[112,512]{1,0:T(8,128)(2,1)S(1)}, bf16[112,512]{1,0:T(8,128)(2,1)S(1)}, u32[]{:S(2)}, u32[]{:S(2)}) %collective-permute-start.20) | collective-permute-done | bytes 114720 | tf_op jit(solution)/shard_map/ppermute | solution.py:26
  179.2 12.6 %residual.2.refs_10_ = f32[4,1024,512]{2,1,0:T(8,128)} custom-call(s32[1]{0:T(128)} %bitcast.tile, bf16[2,336,512]{2,1,0:T(8,128)(2,1)} %copy-done.7, bf16[2,224,512]{2,1,0:T(8,128)(2,1)S(1)} %join.7.refs_1_, bf16[2,336,512]{2,1,0:T(8,128)(2,1)} %copy-done.28, bf16[2,224,512]{2,1,0:T(8,128)(2,1)S(1)} %copy-done.26, ...), custom_call_target="tpu_custom_call" | custom-call | tf_op jit(solution)/shard_map/residual/pallas_call | solution.py:219
  191.8 10.9 %residual.3 = bf16[4,1024,512]{2,1,0:T(8,128)(2,1)} custom-call(s32[1]{0:T(128)} %bitcast.tile, bf16[2,224,512]{2,1,0:T(8,128)(2,1)S(1)} %join.4.refs_0_, bf16[2,112,512]{2,1,0:T(8,128)(2,1)S(1)} %join.5.refs_1_, bf16[2,224,512]{2,1,0:T(8,128)(2,1)} %collective-permute-done.21.refs_2_, bf16[2,112,512]{2,1,0:T(8,128)(2,1)} %collective-permute-done.22.refs_3_, ...), custom_call_target="tpu_custom_call" | custom-call | tf_op jit(solution)/shard_map/residual/pallas_call | solution.py:219
  (136 shorter events, 48.6 us)
Async XLA Ops:
  3.1 48.8 %collective-permute-start.12 = (bf16[4,512,512]{2,1,0:T(8,128)(2,1)}, bf16[4,512,512]{2,1,0:T(8,128)(2,1)S(1)}, u32[]{:S(2)}, u32[]{:S(2)}) collective-permute-start(bf16[4,512,512]{2,1,0:T(8,128)(2,1)} %constant_dynamic-slice_fusion), channel_id=1, source_target_pairs={{0,1},{1,0},{2,3},{3,2},{4,5},{5,4},{6,7},{7,6},{8,9},{9,8},{10,11... | collective-permute-start | bytes 6291464 | tf_op jit(solution)/shard_map/ppermute | solution.py:26
  11.9 93.5 %collective-permute-start.13 = (bf16[4,512,512]{2,1,0:T(8,128)(2,1)}, bf16[4,512,512]{2,1,0:T(8,128)(2,1)}, u32[]{:S(2)}, u32[]{:S(2)}) collective-permute-start(bf16[4,512,512]{2,1,0:T(8,128)(2,1)} %get-tuple-element.13.refs_4_.refs_2_.refs_6_), channel_id=1, source_target_pairs={{0,2},{2,0},{4,6},{6,4},{8,10},{10,8},{12,14},{14,12},{16,18},{18,... | collective-permute-start | bytes 6291464 | tf_op jit(solution)/shard_map/ppermute | solution.py:26
  13.1 46.5 %collective-permute-start = (bf16[4,112,512]{2,1,0:T(8,128)(2,1)S(1)}, bf16[4,112,512]{2,1,0:T(8,128)(2,1)S(1)}, u32[]{:S(2)}, u32[]{:S(2)}) collective-permute-start(bf16[4,112,512]{2,1,0:T(8,128)(2,1)S(1)} %get-tuple-element.22.refs_0_.refs_4_), channel_id=1, source_target_pairs={{0,8},{2,10},{8,16},{10,18},{16,24},{18,26},{24,28},{26,30},{28,20... | collective-permute-start | bytes 1376264 | tf_op jit(solution)/shard_map/ppermute | solution.py:41
  57.5 62.5 %collective-permute-start.14 = (bf16[4,512,512]{2,1,0:T(8,128)(2,1)S(1)}, bf16[4,512,512]{2,1,0:T(8,128)(2,1)}, u32[]{:S(2)}, u32[]{:S(2)}) collective-permute-start(bf16[4,512,512]{2,1,0:T(8,128)(2,1)S(1)} %mix.1.refs_5_.refs_3_.refs_6_.refs_4_), channel_id=1, source_target_pairs={{0,2},{2,0},{4,6},{6,4},{8,10},{10,8},{12,14},{14,12},{16,18},{18,... | collective-permute-start | bytes 6291464 | tf_op jit(solution)/shard_map/ppermute | solution.py:26
  59.7 20.8 %collective-permute-start.9 = (bf16[4,112,512]{2,1,0:T(8,128)(2,1)S(1)}, bf16[4,112,512]{2,1,0:T(8,128)(2,1)}, u32[]{:S(2)}, u32[]{:S(2)}) collective-permute-start(bf16[4,112,512]{2,1,0:T(8,128)(2,1)S(1)} %get-tuple-element.21.refs_3_), channel_id=1, source_target_pairs={{0,4},{2,6},{8,0},{10,2},{16,8},{18,10},{24,16},{26,18},{28,24},{3... | collective-permute-start | bytes 1376264 | tf_op jit(solution)/shard_map/ppermute | solution.py:41
  84.0 18.6 %collective-permute-start.10 = (bf16[4,112,512]{2,1,0:T(8,128)(2,1)}, bf16[4,112,512]{2,1,0:T(8,128)(2,1)}, u32[]{:S(2)}, u32[]{:S(2)}) collective-permute-start(bf16[4,112,512]{2,1,0:T(8,128)(2,1)} %collective-permute-done.9.refs_5_), channel_id=1, source_target_pairs={{0,4},{2,6},{8,0},{10,2},{16,8},{18,10},{24,16},{26,18},{28,24},{3... | collective-permute-start | bytes 1376264 | tf_op jit(solution)/shard_map/ppermute | solution.py:41
  94.8 23.7 %collective-permute-start.34 = (bf16[4,112,512]{2,1,0:T(8,128)(2,1)}, bf16[4,112,512]{2,1,0:T(8,128)(2,1)}, u32[]{:S(2)}, u32[]{:S(2)}) collective-permute-start(bf16[4,112,512]{2,1,0:T(8,128)(2,1)} %collective-permute-done.9.refs_5_), channel_id=1, source_target_pairs={{0,2},{2,0},{4,6},{6,4},{8,10},{10,8},{12,14},{14,12},{16,18},{18,... | collective-permute-start | bytes 1376264 | tf_op jit(solution)/shard_map/ppermute | solution.py:26
  102.6 22.9 %collective-permute-start.2 = (bf16[4,112,512]{2,1,0:T(8,128)(2,1)}, bf16[4,112,512]{2,1,0:T(8,128)(2,1)}, u32[]{:S(2)}, u32[]{:S(2)}) collective-permute-start(bf16[4,112,512]{2,1,0:T(8,128)(2,1)} %collective-permute-done.1.refs_0_.refs_7_), channel_id=1, source_target_pairs={{0,8},{2,10},{8,16},{10,18},{16,24},{18,26},{24,28},{26,30},{28,20... | collective-permute-start | bytes 1376264 | tf_op jit(solution)/shard_map/ppermute | solution.py:41
  105.0 22.1 %collective-permute-start.5 = (bf16[4,112,512]{2,1,0:T(8,128)(2,1)}, bf16[4,112,512]{2,1,0:T(8,128)(2,1)}, u32[]{:S(2)}, u32[]{:S(2)}) collective-permute-start(bf16[4,112,512]{2,1,0:T(8,128)(2,1)} %collective-permute-done.4.refs_1_.refs_8_), channel_id=1, source_target_pairs={{0,4},{2,6},{8,0},{10,2},{16,8},{18,10},{24,16},{26,18},{28,24},{3... | collective-permute-start | bytes 1376264 | tf_op jit(solution)/shard_map/ppermute | solution.py:41
  105.4 22.3 %collective-permute-start.11 = (bf16[4,112,512]{2,1,0:T(8,128)(2,1)}, bf16[4,112,512]{2,1,0:T(8,128)(2,1)}, u32[]{:S(2)}, u32[]{:S(2)}) collective-permute-start(bf16[4,112,512]{2,1,0:T(8,128)(2,1)} %collective-permute-done.10.refs_3_), channel_id=1, source_target_pairs={{0,4},{2,6},{8,0},{10,2},{16,8},{18,10},{24,16},{26,18},{28,24},{3... | collective-permute-start | bytes 1376264 | tf_op jit(solution)/shard_map/ppermute | solution.py:41
  118.5 16.0 %collective-permute-start.26 = (bf16[336,512]{1,0:T(8,128)(2,1)}, bf16[336,512]{1,0:T(8,128)(2,1)S(1)}, u32[]{:S(2)}, u32[]{:S(2)}) collective-permute-start(bf16[336,512]{1,0:T(8,128)(2,1)} %get-tuple-element.19.near), channel_id=1, source_target_pairs={{0,1},{1,0},{2,3},{3,2},{4,5},{5,4},{6,7},{7,6},{8,9},{9,8},{10,11... | collective-permute-start | bytes 1032200 | tf_op jit(solution)/shard_map/ppermute | solution.py:26
  120.0 13.9 %collective-permute-start.28 = (bf16[224,512]{1,0:T(8,128)(2,1)}, bf16[224,512]{1,0:T(8,128)(2,1)S(1)}, u32[]{:S(2)}, u32[]{:S(2)}) collective-permute-start(bf16[224,512]{1,0:T(8,128)(2,1)} %get-tuple-element.20.near), channel_id=1, source_target_pairs={{0,1},{1,0},{2,3},{3,2},{4,5},{5,4},{6,7},{7,6},{8,9},{9,8},{10,11... | collective-permute-start | bytes 688136 | tf_op jit(solution)/shard_map/ppermute | solution.py:26
  127.1 17.0 %collective-permute-start.8 = (bf16[4,112,512]{2,1,0:T(8,128)(2,1)S(1)}, bf16[4,112,512]{2,1,0:T(8,128)(2,1)}, u32[]{:S(2)}, u32[]{:S(2)}) collective-permute-start(bf16[4,112,512]{2,1,0:T(8,128)(2,1)S(1)} %copy-done.16), channel_id=1, source_target_pairs={{0,8},{2,10},{8,16},{10,18},{16,24},{18,26},{24,28},{26,30},{28,20... | collective-permute-start | bytes 1376264 | tf_op jit(solution)/shard_map/ppermute | solution.py:41
  127.6 17.1 %collective-permute-start.35 = (bf16[4,112,512]{2,1,0:T(8,128)(2,1)S(1)}, bf16[4,112,512]{2,1,0:T(8,128)(2,1)S(1)}, u32[]{:S(2)}, u32[]{:S(2)}) collective-permute-start(bf16[4,112,512]{2,1,0:T(8,128)(2,1)S(1)} %copy-done.16), channel_id=1, source_target_pairs={{0,2},{2,0},{4,6},{6,4},{8,10},{10,8},{12,14},{14,12},{16,18},{18,... | collective-permute-start | bytes 1376264 | tf_op jit(solution)/shard_map/ppermute | solution.py:26
  134.0 17.8 %collective-permute-start.17 = (bf16[4,112,512]{2,1,0:T(8,128)(2,1)}, bf16[4,112,512]{2,1,0:T(8,128)(2,1)S(1)}, u32[]{:S(2)}, u32[]{:S(2)}) collective-permute-start(bf16[4,112,512]{2,1,0:T(8,128)(2,1)} %collective-permute-done.2.refs_0_.refs_4_), channel_id=1, source_target_pairs={{0,8},{2,10},{8,16},{10,18},{16,24},{18,26},{24,28},{26,30},{28,20... | collective-permute-start | bytes 1376264 | tf_op jit(solution)/shard_map/ppermute | solution.py:41
  136.7 16.7 %collective-permute-start.18 = (bf16[4,112,512]{2,1,0:T(8,128)(2,1)}, bf16[4,112,512]{2,1,0:T(8,128)(2,1)}, u32[]{:S(2)}, u32[]{:S(2)}) collective-permute-start(bf16[4,112,512]{2,1,0:T(8,128)(2,1)} %collective-permute-done.11.refs_3_), channel_id=1, source_target_pairs={{0,4},{2,6},{8,0},{10,2},{16,8},{18,10},{24,16},{26,18},{28,24},{3... | collective-permute-start | bytes 1376264 | tf_op jit(solution)/shard_map/ppermute | solution.py:41
  143.8 23.0 %collective-permute-start.36 = (bf16[4,112,512]{2,1,0:T(8,128)(2,1)}, bf16[4,112,512]{2,1,0:T(8,128)(2,1)S(1)}, u32[]{:S(2)}, u32[]{:S(2)}) collective-permute-start(bf16[4,112,512]{2,1,0:T(8,128)(2,1)} %collective-permute-done.10.refs_3_), channel_id=1, source_target_pairs={{0,2},{2,0},{4,6},{6,4},{8,10},{10,8},{12,14},{14,12},{16,18},{18,... | collective-permute-start | bytes 1376264 | tf_op jit(solution)/shard_map/ppermute | solution.py:26
  144.1 27.2 %collective-permute-start.30 = (bf16[2,336,512]{2,1,0:T(8,128)(2,1)S(1)}, bf16[2,336,512]{2,1,0:T(8,128)(2,1)S(1)}, u32[]{:S(2)}, u32[]{:S(2)}) collective-permute-start(bf16[2,336,512]{2,1,0:T(8,128)(2,1)S(1)} %join.6.refs_0_), channel_id=1, source_target_pairs={{0,2},{2,0},{4,6},{6,4},{8,10},{10,8},{12,14},{14,12},{16,18},{18,... | collective-permute-start | bytes 2064392 | tf_op jit(solution)/shard_map/ppermute | solution.py:26
  145.5 24.5 %collective-permute-start.31 = (bf16[2,224,512]{2,1,0:T(8,128)(2,1)S(1)}, bf16[2,224,512]{2,1,0:T(8,128)(2,1)S(1)}, u32[]{:S(2)}, u32[]{:S(2)}) collective-permute-start(bf16[2,224,512]{2,1,0:T(8,128)(2,1)S(1)} %join.7.refs_1_), channel_id=1, source_target_pairs={{0,2},{2,0},{4,6},{6,4},{8,10},{10,8},{12,14},{14,12},{16,18},{18,... | collective-permute-start | bytes 1376264 | tf_op jit(solution)/shard_map/ppermute | solution.py:26
  166.8 24.9 %collective-permute-start.23 = (bf16[4,112,512]{2,1,0:T(8,128)(2,1)}, bf16[4,112,512]{2,1,0:T(8,128)(2,1)}, u32[]{:S(2)}, u32[]{:S(2)}) collective-permute-start(bf16[4,112,512]{2,1,0:T(8,128)(2,1)} %collective-permute-done.8.refs_2_), channel_id=1, source_target_pairs={{0,2},{2,0},{4,6},{6,4},{8,10},{10,8},{12,14},{14,12},{16,18},{18,... | collective-permute-start | bytes 1376264 | tf_op jit(solution)/shard_map/ppermute | solution.py:26
  167.3 24.4 %collective-permute-start.24 = (bf16[4,112,512]{2,1,0:T(8,128)(2,1)}, bf16[4,112,512]{2,1,0:T(8,128)(2,1)}, u32[]{:S(2)}, u32[]{:S(2)}) collective-permute-start(bf16[4,112,512]{2,1,0:T(8,128)(2,1)} %collective-permute-done.11.refs_3_), channel_id=1, source_target_pairs={{0,2},{2,0},{4,6},{6,4},{8,10},{10,8},{12,14},{14,12},{16,18},{18,... | collective-permute-start | bytes 1376264 | tf_op jit(solution)/shard_map/ppermute | solution.py:26
  170.0 21.8 %collective-permute-start.25 = (bf16[4,112,512]{2,1,0:T(8,128)(2,1)}, bf16[4,112,512]{2,1,0:T(8,128)(2,1)}, u32[]{:S(2)}, u32[]{:S(2)}) collective-permute-start(bf16[4,112,512]{2,1,0:T(8,128)(2,1)} %collective-permute-done.18.refs_1_), channel_id=1, source_target_pairs={{0,2},{2,0},{4,6},{6,4},{8,10},{10,8},{12,14},{14,12},{16,18},{18,... | collective-permute-start | bytes 1376264 | tf_op jit(solution)/shard_map/ppermute | solution.py:26
  170.8 20.9 %collective-permute-start.21 = (bf16[2,224,512]{2,1,0:T(8,128)(2,1)S(1)}, bf16[2,224,512]{2,1,0:T(8,128)(2,1)}, u32[]{:S(2)}, u32[]{:S(2)}) collective-permute-start(bf16[2,224,512]{2,1,0:T(8,128)(2,1)S(1)} %join.4.refs_0_), channel_id=1, source_target_pairs={{0,2},{2,0},{4,6},{6,4},{8,10},{10,8},{12,14},{14,12},{16,18},{18,... | collective-permute-start | bytes 1376264 | tf_op jit(solution)/shard_map/ppermute | solution.py:26
  172.3 19.5 %collective-permute-start.22 = (bf16[2,112,512]{2,1,0:T(8,128)(2,1)S(1)}, bf16[2,112,512]{2,1,0:T(8,128)(2,1)}, u32[]{:S(2)}, u32[]{:S(2)}) collective-permute-start(bf16[2,112,512]{2,1,0:T(8,128)(2,1)S(1)} %join.5.refs_1_), channel_id=1, source_target_pairs={{0,2},{2,0},{4,6},{6,4},{8,10},{10,8},{12,14},{14,12},{16,18},{18,... | collective-permute-start | bytes 688136 | tf_op jit(solution)/shard_map/ppermute | solution.py:26
  (45 other events, 378.2 us)

commit v2 on v0

v2 whole, which is shorter than its diff:
```python
import functools

import jax
import jax.numpy as jnp
from jax import lax
from jax.experimental import pallas as pl
from jax.experimental.pallas import tpu as pltpu
from jax.sharding import PartitionSpec as P

OCC = 8
BF16, F32 = jnp.bfloat16, jnp.float32
VMEM_LIMIT = 20 * 2**20
WORK = pl.CostEstimate(flops=1, bytes_accessed=1, transcendentals=0)
RING = 20
WHOLE = pl.BlockSpec(memory_space=pltpu.VMEM)
ANYWHERE = pl.BlockSpec(memory_space=pl.ANY)


def kernel_call(
    body, name, grid, in_specs, out_specs, out_shapes, scratch=(), tile=None, after=(), far=(), out=pltpu.VMEM
):
    scalars = 0 if tile is None else 1
    extra = len(after)

    def kernel(*refs):
        keep = scalars + len(in_specs)
        body(*refs[:keep], *refs[keep + extra :])

    def call(*args):
        held = [
            a if n in far else pltpu.with_memory_space_constraint(a, pltpu.VMEM)
            for n, a in enumerate((*args, *after))
        ]
        return pl.pallas_call(
            kernel,
            grid_spec=pltpu.PrefetchScalarGridSpec(
                num_scalar_prefetch=scalars,
                grid=grid,
                in_specs=[*in_specs, *[ANYWHERE] * extra],
                out_specs=list(out_specs),
                scratch_shapes=list(scratch),
            ),
            out_shape=[out(shape, kind) for shape, kind in out_shapes],
            compiler_params=pltpu.CompilerParams(
                dimension_semantics=("arbitrary",) * len(grid), vmem_limit_bytes=VMEM_LIMIT
            ),
            cost_estimate=WORK,
            name=name,
        )(*([] if tile is None else [tile]), *held)

    return call


def swap(x, axis, bit):
    return lax.ppermute(x, axis, [(i, i ^ 1 << bit) for i in range(lax.axis_size(axis))])


def ring_of(count, groups):
    places = count // groups
    return list(range(0, places, 2)) + list(range(places - 1, 0, -2))


def along_ring(x, step, groups):
    order = ring_of(lax.axis_size("pair"), groups)
    pairs = [
        (a * groups + g, order[(n + step) % len(order)] * groups + g)
        for n, a in enumerate(order)
        for g in range(groups)
    ]
    return lax.ppermute(x, "pair", pairs)


def turn_kernel(where, own, other, near, far):
    x = own[0].astype(F32)
    near[0] = (2.0 * x.T - x).astype(BF16)
    far[0] = other[0].T


def turn(where, amplitudes, part, count, after=()):
    _, rows, width = amplitudes.shape
    block = (1, width, width)
    return kernel_call(
        turn_kernel,
        "turn",
        (count,),
        [
            pl.BlockSpec(block, lambda j, t: (j + part * count, t[0], 0)),
            pl.BlockSpec(block, lambda j, t: (j + part * count, 1 - t[0], 0)),
        ],
        [pl.BlockSpec(block, lambda j, t: (j, 0, 0))] * 2,
        [((count, width, width), BF16)] * 2,
        tile=where,
        after=after,
        far=(0, 1),
    )(amplitudes, amplitudes)


def mix_kernel(parts, *refs):
    far, arrived, out = refs[:parts], refs[parts:-1], refs[-1]
    for j, f in enumerate(far):
        start = 0
        for r in arrived:
            rows = pl.ds(start, r.shape[1])
            out[j, rows] = (2.0 * f[0, rows].astype(F32) - r[j].astype(F32)).astype(BF16)
            start += r.shape[1]


def mix(far, arrived, after=()):
    shape = (len(far),) + far[0].shape[1:]
    (out,) = kernel_call(
        functools.partial(mix_kernel, len(far)),
        "mix",
        (1,),
        [WHOLE] * (len(far) + len(arrived)),
        [WHOLE],
        [(shape, BF16)],
        after=after,
    )(*far, *arrived)
    return out


def partial_kernel(shards, parts, joined, where, *refs):
    same, cross = refs[:shards], refs[shards : 2 * shards]
    refs = refs[2 * shards :]
    arrays = sum(parts)
    mine, theirs, refs = refs[:arrays], refs[arrays : 2 * arrays], refs[2 * arrays :]
    out, total = refs[0], refs[-1]
    j = pl.program_id(0)
    left = jnp.concatenate([r[0] for r in same], axis=0)
    right = jnp.concatenate([r[0] for r in cross], axis=0)
    if joined:
        refs[1][0] = left
        refs[2][0] = right
    at = 0
    for h, split in enumerate(parts):
        for part in range(split):

            @pl.when(j // (pl.num_programs(0) // split) == part)
            def _():
                value = jnp.dot(left, mine[at + part][0], preferred_element_type=F32)
                value += jnp.dot(right, theirs[at + part][0], preferred_element_type=F32)
                before = jnp.where(j == 0, 0.0, total[h])
                total[h] = value + before

        at += split

    @pl.when(j == pl.num_programs(0) - 1)
    def _():
        out[...] = total[...].astype(BF16)


def partial(where, same, cross, mine, theirs, joined=False, after=()):
    mine = [m if isinstance(m, list) else [m] for m in mine]
    theirs = [m if isinstance(m, list) else [m] for m in theirs]
    parts = [len(m) for m in mine]
    shards, halves = len(same), len(mine)
    count = sum(m.shape[0] for m in mine[0])
    width, columns = mine[0][0].shape[1:]
    depths = [v.shape[1] for v in same]
    rows = sum(depths)
    by_j = lambda n, m: pl.BlockSpec((1, n, m), lambda j, t: (j, 0, 0))

    def shard_spec(v, other):
        if v.shape[0] == count:
            return by_j(v.shape[1], width)
        if other:
            return pl.BlockSpec((1, v.shape[1], width), lambda j, t: (j + count * (1 - t[1]), 0, 0))
        return pl.BlockSpec((1, v.shape[1], width), lambda j, t: (j + count * t[1], 0, 0))

    def half_spec(part, split):
        block = count // split
        return pl.BlockSpec(
            (1, width, columns),
            lambda j, t: (jnp.clip(j - part * block, 0, block - 1), 0, 0),
        )

    out_shapes = [((halves, rows, columns), BF16)]
    out_specs = [pl.BlockSpec((halves, rows, columns), lambda j, t: (0, 0, 0))]
    if joined:
        out_shapes += [((count, rows, width), BF16)] * 2
        out_specs += [by_j(rows, width)] * 2
    return kernel_call(
        functools.partial(partial_kernel, shards, parts, joined),
        "partial",
        (count,),
        [shard_spec(v, False) for v in same]
        + [shard_spec(v, True) for v in cross]
        + [half_spec(part, split) for split in parts * 2 for part in range(split)],
        out_specs,
        out_shapes,
        [pltpu.VMEM((halves, rows, columns), F32)],
        tile=where,
        after=after,
    )(*same, *cross, *sum(mine, []), *sum(theirs, []))


def pick_kernel(where, forth, back, same, cross):
    same[...] = forth[...]
    cross[...] = back[...]


def pick(where, forth, back, after=()):
    block = (forth.shape[0] // 2,) + forth.shape[1:]
    return kernel_call(
        pick_kernel,
        "pick",
        (1,),
        [
            pl.BlockSpec(block, lambda k, t: (t[1], 0, 0)),
            pl.BlockSpec(block, lambda k, t: (1 - t[1], 0, 0)),
        ],
        [pl.BlockSpec(block, lambda k, t: (0, 0, 0))] * 2,
        [(block, BF16)] * 2,
        tile=where,
        after=after,
    )(forth, back)


def nothing(*refs):
    pass


def wall(*arrays, cost=0.1):
    held = [pltpu.with_memory_space_constraint(a, pltpu.VMEM) for a in arrays]
    return pl.pallas_call(
        nothing,
        in_specs=[ANYWHERE] * len(held),
        out_specs=ANYWHERE,
        out_shape=pltpu.VMEM((8, 128), F32),
        compiler_params=pltpu.CompilerParams(vmem_limit_bytes=2**20),
        cost_estimate=pl.CostEstimate(flops=int(cost * 10**9), bytes_accessed=1, transcendentals=0),
        name="wall",
    )(*held)


def gate(value, after):
    held = [pltpu.with_memory_space_constraint(a, pltpu.VMEM) for a in (value, *after)]
    return pl.pallas_call(
        nothing,
        in_specs=[ANYWHERE] * len(held),
        out_specs=ANYWHERE,
        out_shape=pltpu.VMEM(value.shape, value.dtype),
        input_output_aliases={0: 0},
        compiler_params=pltpu.CompilerParams(vmem_limit_bytes=2**20),
        cost_estimate=WORK,
        name="gate",
    )(*held)


def join(near, near_sent, far, far_sent, after=()):
    arrays = [v for v, _ in near + far_sent + far + near_sent]
    rows, columns = sum(v.shape[1] for v, _ in near), near[0][0].shape[2]
    n, f, fs = len(near), len(far), len(far_sent)

    def body(*refs):
        at = lambda first, items: [(refs[first + k], h) for k, (_, h) in enumerate(items)]
        own_near, got_far = at(0, near), at(n, far_sent)
        own_far, got_near = at(n + fs, far), at(n + fs + f, near_sent)
        out = refs[-1]
        for h, own, got in ((0, own_near, got_far), (1, own_far, got_near)):
            left = jnp.concatenate([r[k] for r, k in own], axis=0)
            right = jnp.concatenate([r[k] for r, k in got], axis=0)
            out[h] = (left.astype(F32) + right.astype(F32)).astype(BF16)

    whole = lambda shape: pl.BlockSpec(shape, lambda k: (0, 0, 0))
    (out,) = kernel_call(
        body,
        "join",
        (1,),
        [whole(v.shape) for v in arrays],
        [whole((2, rows, columns))],
        [((2, rows, columns), BF16)],
        after=after,
    )(*arrays)
    return out


def residual_kernel(chunks, shards, first, where, *refs):
    middles, vectors = refs[:chunks], refs[chunks : chunks + shards]
    rest, out, turned = refs[chunks + shards : -2], refs[-2], refs[-1]
    j = pl.program_id(0)
    columns = middles[0].shape[2]

    @pl.when(j == 0)
    def _():
        for h in range(2):
            rows = pl.ds(pl.multiple_of(lax.rem(where[0] + h, 2) * columns, columns), columns)
            turned[rows] = jnp.concatenate([m[h] for m in middles], axis=0).T

    if first:
        values, row_energy, column_energy, first_energy, second_energy = rest
        own = first_energy[where[2]] + second_energy[where[1] * pl.num_programs(0) + j]
        rows = jnp.broadcast_to(row_energy[...] - own, (128, row_energy.shape[1])).T[:, :1]
        total = (rows + column_energy[0]) * values[0].astype(F32)
    else:
        total = rest[0][j]
    right = jnp.concatenate([v[j] for v in vectors], axis=0)
    total += jnp.dot(turned[...], right, preferred_element_type=F32)
    out[0] = total.astype(out.dtype)


def residual(where, middles, vectors, first=None, before=None, last=True, after=()):
    count, _, width = vectors[0].shape
    rows = 2 * middles[0].shape[2]
    depth = sum(m.shape[1] for m in middles)
    by_j = pl.BlockSpec((1, rows, width), lambda j, t: (j, 0, 0))
    in_specs = [WHOLE] * (len(middles) + len(vectors))
    args = [*middles, *vectors]
    if first is not None:
        in_specs += [
            by_j,
            pl.BlockSpec((1, rows), lambda j, t: (0, 0)),
            pl.BlockSpec((1, 1, width), lambda j, t: (t[0], 0, 0)),
            pl.BlockSpec(memory_space=pltpu.SMEM),
            pl.BlockSpec(memory_space=pltpu.SMEM),
        ]
        args += first
    else:
        in_specs += [WHOLE]
        args += [before]
    (out,) = kernel_call(
        functools.partial(residual_kernel, len(middles), len(vectors), first is not None),
        "residual",
        (count,),
        in_specs,
        [by_j],
        [((count, rows, width), BF16 if last else F32)],
        [pltpu.VMEM((rows, depth), BF16)],
        tile=where,
        after=after,
        far=range(len(middles) + len(vectors), len(args)) if first is not None else (),
        out=pltpu.HBM if last else pltpu.VMEM,
    )(*args)
    return out


def two_tiles(amplitudes, cholesky, energy_first, energy_second, energy_virtual):
    count, virtual, width = amplitudes.shape
    groups = OCC // count
    places = lax.axis_size("pair") // groups
    place, group = lax.axis_index("pair") // groups, lax.axis_index("pair") % groups
    y = lax.axis_index("virt")
    where = jnp.stack([y, group, place]).astype(jnp.int32)
    ring = functools.partial(along_ring, groups=groups)
    to_core = functools.partial(swap, axis="pair", bit=0)
    to_tile = functools.partial(swap, axis="virt", bit=0)

    vectors = [jnp.swapaxes(cholesky, 1, 2)]
    forth, back = vectors[0], vectors[0]
    for step in range(1, places // 2):
        forth, back = ring(forth, 1), ring(back, -1)
        vectors += [forth, back]

    cut = width * 7 // 16 // 16 * 16
    sent, start = [], 0
    for rows in (cut, cut, width - 2 * cut):
        at = (0, (1 - y) * width + start, 0)
        sent.append(lax.dynamic_slice(amplitudes, at, (count, rows, width)))
        start += rows
    arrived = [to_tile(v) for v in sent]
    diagonal = [
        amplitudes,
        energy_virtual.reshape(1, virtual),
        energy_virtual.reshape(2, 1, width),
        energy_first,
        energy_second,
    ]
    near, near_theirs, far_turned = [], [], []
    held = []
    for j in range(count):
        v, w = turn(where, amplitudes, j, 1, after=held)
        near.append(v)
        far_turned.append(w)
        near_theirs.append(to_core(v))
        if j == count // 2 - 1:
            wall_1 = wall(*vectors[1:3], arrived[0], *near_theirs, cost=RING)
            held = [wall_1]
    wall_2 = wall(*vectors[3:5], arrived[1], *near_theirs[count // 2 :], cost=RING)
    near, near_theirs = [near], [near_theirs]
    n_1, same_1, cross_1 = partial(
        where, vectors[:3], vectors[:3], near, near_theirs, joined=True, after=[wall_2]
    )
    n_1_sent = to_tile(n_1)
    far = mix(far_turned, arrived, after=[n_1])
    far_theirs = to_core(far)
    n_2, same_2, cross_2 = partial(
        where, vectors[3:5], vectors[3:5], near, near_theirs, joined=True, after=[far]
    )
    n_2_sent = to_tile(n_2)
    (f_1,) = partial(where, [same_1], [cross_1], [far], [far_theirs], after=[n_2])
    f_1_sent = to_tile(f_1)
    handed_1, handed_2 = to_core(cross_1), to_core(cross_2)
    (f_2,) = partial(where, [same_2], [cross_2], [far], [far_theirs], after=[f_1, n_1_sent])
    f_2_sent = to_tile(f_2)
    picked = pick(where, *vectors[5:7], after=[f_2])
    same_c, cross_c = ring(picked[0], 1), ring(picked[1], -1)
    wall_3 = wall(*picked, handed_1, cost=RING)
    halves, halves_theirs = near + [far], near_theirs + [far_theirs]
    p_b, same_b, cross_b = partial(
        where, vectors[5:7], vectors[5:7], halves, halves_theirs, joined=True, after=[wall_3]
    )
    p_b_sent = to_tile(p_b)
    handed_b = to_core(cross_b)
    m_a = join(
        [(n_1, 0), (n_2, 0)],
        [(n_1_sent, 0), (n_2_sent, 0)],
        [(f_1, 0), (f_2, 0)],
        [(f_1_sent, 0), (f_2_sent, 0)],
        after=[p_b, handed_2],
    )
    m_a_theirs = to_core(m_a)
    wall_4 = wall(same_c, cross_c, m_a, cost=RING)
    (p_c,) = partial(where, [same_c], [cross_c], halves, halves_theirs, after=[wall_4])
    p_c_sent = to_tile(p_c)
    handed_c = to_core(cross_c)
    m_b = join([(p_b, 0)], [(p_b_sent, 0)], [(p_b, 1)], [(p_b_sent, 1)], after=[p_c])
    m_b_theirs = to_core(m_b)
    started = residual(
        where,
        [m_a, m_a_theirs],
        [same_1, same_2, handed_1, handed_2],
        first=diagonal,
        last=False,
        after=[m_b],
    )
    m_c = join([(p_c, 0)], [(p_c_sent, 0)], [(p_c, 1)], [(p_c_sent, 1)], after=[started])
    m_c_theirs = to_core(m_c)
    return residual(
        where,
        [m_b, m_b_theirs, m_c, m_c_theirs],
        [same_b, handed_b, same_c, handed_c],
        before=started,
    )


def from_partner(x, axis, bit):
    return lax.ppermute(x, axis, [(i, i ^ 1 << bit) for i in range(lax.axis_size(axis))])


def any_tiles(amplitudes, cholesky, energy_first, energy_second, energy_virtual):
    pair_count, virtual_count, local_virtual = amplitudes.shape
    tiles_count = lax.axis_size("virt")
    first_count = max(pair_count // OCC, 1)
    second_count = pair_count // first_count
    offset = lax.axis_index("pair") * pair_count
    first_start = offset // OCC
    second_start = offset % OCC
    column_start = lax.axis_index("virt") * local_virtual
    blocks = amplitudes.reshape(pair_count, tiles_count, local_virtual, local_virtual)
    arrived = lax.all_to_all(blocks, "virt", split_axis=1, concat_axis=1, tiled=True)
    mirrored = jnp.swapaxes(arrived, 2, 3).reshape(pair_count, virtual_count, local_virtual)
    combined = (2.0 * amplitudes.astype(F32) - mirrored.astype(F32)).astype(BF16)
    combined = combined.reshape(first_count, second_count, virtual_count, local_virtual)
    vectors = lax.all_gather(cholesky, "pair", axis=2, tiled=True)
    chosen = lax.dynamic_slice_in_dim(vectors, second_start, second_count, 0)
    partial_value = jnp.einsum("ilad,ldq->iaq", combined, chosen, preferred_element_type=F32)
    collected = lax.psum(partial_value.astype(BF16), "virt").astype(F32)
    for bit in range((OCC // second_count).bit_length() - 1):
        collected = collected + from_partner(collected.astype(BF16), "pair", bit).astype(F32)
    reduced = collected.astype(BF16)
    cycle_term = jnp.einsum("iaq,lbq->ilab", reduced, chosen, preferred_element_type=F32)
    first_energy = lax.dynamic_slice_in_dim(energy_first, first_start, first_count, 0)
    second_energy = lax.dynamic_slice_in_dim(energy_second, second_start, second_count, 0)
    column_energy = lax.dynamic_slice_in_dim(energy_virtual, column_start, local_virtual, 0)
    virtual_pairs = energy_virtual[:, None] + column_energy[None, :]
    diagonal = (
        virtual_pairs[None, None, :, :]
        - first_energy[:, None, None, None]
        - second_energy[None, :, None, None]
    )
    values = amplitudes.reshape(first_count, second_count, virtual_count, local_virtual)
    result = diagonal * values.astype(F32) + cycle_term
    return result.reshape(pair_count, virtual_count, local_virtual).astype(BF16)


def on_device(amplitudes, *others):
    ring = lax.axis_size("pair") * amplitudes.shape[0] // OCC
    fits = lax.axis_size("virt") == 2 and amplitudes.shape[0] * 2 == OCC and ring == 8
    return (two_tiles if fits else any_tiles)(amplitudes, *others)


def solution(mesh):
    return jax.shard_map(
        on_device,
        mesh=mesh,
        in_specs=(P("pair", None, "virt"), P(None, "virt", "pair"), P(), P(), P()),
        out_specs=P("pair", None, "virt"),
        check_vma=False,
    )
```

time: 298 us -> 120 us (0.40)
  waiting for transfers between devices: 190 us -> 43 us
  Pallas kernels: 0 us -> 45.4 us
  local copies, waits for them, and re-layouts: 47 us -> 8.64 us
  matrix products: 31.5 us -> 0 us
  starting transfers between devices: 6.12 us -> 22.3 us
  between operations: 13.5 us -> 0.42 us
  other arithmetic: 9.11 us -> 0.08 us
    psum x1 -> x0, waiting for transfers between devices: 95.7 us -> none  [on_device(): tile_sum = lax.psum(partial_value.astype(jnp.bfloat16), 'virt')]
    all_gather x1 -> x0, waiting for transfers between devices: 50.3 us -> none  [on_device(): vectors = lax.all_gather(cholesky, 'pair', axis=2, tiled=True)]
    pallas_call x0 -> x21, Pallas kernels: none -> 45.4 us  [the longest x17 45.4 us: call(): pl.pallas_call(kernel, grid_spec=pltpu.PrefetchScalarGridSpec(num_scalar_...]
    all_to_all x1 -> x0, waiting for transfers between devices: 42.5 us -> none  [on_device(): lax.all_to_all(blocks, 'virt', split_axis=1, concat_axis=1, tiled=True)]
    ppermute x2 -> x29, waiting for transfers between devices: 1.72 us -> 43 us  [the longest x21 25.5 us: swap(): lax.ppermute(x, axis, [(i, i ^ 1 << bit) for i in range(lax.axis_size(axi...]
    dot_general x3 -> x0, matrix products: 31.5 us -> none  [the longest x2 21 us: on_device(): jnp.einsum('ilad,ldq->iaq', combined, picked, preferred_element_type=jnp....]
    ppermute x2 -> x29, starting transfers between devices: 0.51 us -> 22.3 us  [the longest x21 13.2 us: swap(): lax.ppermute(x, axis, [(i, i ^ 1 << bit) for i in range(lax.axis_size(axi...]
    unnamed x21 -> x32, local copies, waits for them, and re-layouts: 21.3 us -> 4.83 us
  transfers between devices with their start and end apart: 5 -> 29, of which waited for: 4 -> 9; matrix products, arithmetic and copies ran while one was open for 8% -> 3% of each run, Pallas kernels for 0% -> 31%
where the time goes in v2:
time: 120 us
  Pallas kernels  45.4 us (38%)
  waiting for transfers between devices  43 us (36%)
  starting transfers between devices  22.3 us (19%)
  local copies, waits for them, and re-layouts  8.64 us (7%)
    pallas_call x17, Pallas kernels, call(): pl.pallas_call(kernel, grid_spec=pltpu.PrefetchScalarGridSpec(num_scalar_...  45.4 us
    ppermute x21, waiting for transfers between devices, swap(): lax.ppermute(x, axis, [(i, i ^ 1 << bit) for i in range(lax.axis_size(axi...  25.5 us
    ppermute x8, waiting for transfers between devices, along_ring(): return lax.ppermute(x, 'pair', pairs)  17.6 us
    ppermute x21, starting transfers between devices, swap(): lax.ppermute(x, axis, [(i, i ^ 1 << bit) for i in range(lax.axis_size(axi...  13.2 us
    ppermute x8, starting transfers between devices, along_ring(): return lax.ppermute(x, 'pair', pairs)  9.16 us
    unnamed x32, local copies, waits for them, and re-layouts  4.83 us
    dynamic_slice x2, local copies, waits for them, and re-layouts, two_tiles(): sent.append(lax.dynamic_slice(amplitudes, at, (count, rows, width)))  3.81 us
  transfers between devices with their start and end apart: 29, of which 9 were waited for; matrix products, arithmetic and copies ran while one was open for 3% of the time, Pallas kernels for 31%

profile of v2, /device:TPU:0, one launch (start us, length us, event | category | flops | bytes accessed | tf_op | source)
XLA Modules:
  0.0 119.9 jit_solution(215811894370409610)
XLA Ops:
  0.0 3.0 %collective-permute-start = (bf16[8,112,512]{2,1,0:T(8,128)(2,1)}, bf16[8,112,512]{2,1,0:T(8,128)(2,1)}, u32[]{:S(2)}, u32[]{:S(2)}) collective-permute-start(bf16[8,112,512]{2,1,0:T(8,128)(2,1)} %bitcast.6), channel_id=1, source_target_pairs={{0,8},{2,10},{8,16},{10,18},{16,24},{18,26},{24,28},{26,30},{28,20... | collective-permute-start | bytes 2752520 | tf_op jit(solution)/shard_map/ppermute | solution.py:70
  3.0 2.8 %constant_dynamic-slice_fusion.1 = (bf16[4,224,512]{2,1,0:T(8,128)(2,1)}, bf16[4,224,512]{2,1,0:T(8,128)(2,1)}) fusion(bf16[4,1024,512]{2,1,0:T(8,128)(2,1)} %refs_7_.1, s32[]{:T(128)S(6)} %select_n.23, s32[]{:T(128)S(6)} %select_n.22), kind=kLoop, calls=%fused_computation.1 | loop fusion | bytes 3670024 | tf_op jit(solution)/shard_map/dynamic_slice | solution.py:358
  5.9 2.0 %collective-permute-start.6 = (bf16[4,224,512]{2,1,0:T(8,128)(2,1)}, bf16[4,224,512]{2,1,0:T(8,128)(2,1)S(1)}, u32[]{:S(2)}, u32[]{:S(2)}) collective-permute-start(bf16[4,224,512]{2,1,0:T(8,128)(2,1)} %get-tuple-element.44), channel_id=1, source_target_pairs={{0,1},{1,0},{2,3},{3,2},{4,5},{5,4},{6,7},{7,6},{8,9},{9,8},{10,11... | collective-permute-start | bytes 2752520 | tf_op jit(solution)/shard_map/ppermute | solution.py:55
  7.9 2.2 %copy-done = bf16[4,1024,512]{2,1,0:T(8,128)(2,1)S(1)} copy-done((bf16[4,1024,512]{2,1,0:T(8,128)(2,1)S(1)}, bf16[4,1024,512]{2,1,0:T(8,128)(2,1)}, u32[]{:S(2)}) %copy-start) | copy-done | bytes 4194328
  13.4 10.2 %collective-permute-done.refs_0_.refs_2_.refs_5_ = bf16[8,112,512]{2,1,0:T(8,128)(2,1)} collective-permute-done((bf16[8,112,512]{2,1,0:T(8,128)(2,1)}, bf16[8,112,512]{2,1,0:T(8,128)(2,1)}, u32[]{:S(2)}, u32[]{:S(2)}) %collective-permute-start) | collective-permute-done | bytes 917536 | tf_op jit(solution)/shard_map/ppermute | solution.py:70
  23.6 1.8 %collective-permute-start.1 = (bf16[8,112,512]{2,1,0:T(8,128)(2,1)}, bf16[8,112,512]{2,1,0:T(8,128)(2,1)}, u32[]{:S(2)}, u32[]{:S(2)}) collective-permute-start(bf16[8,112,512]{2,1,0:T(8,128)(2,1)} %collective-permute-done.refs_0_.refs_2_.refs_5_), channel_id=1, source_target_pairs={{0,8},{2,10},{8,16},{10,18},{16,24},{18,26},{24,28},{26,30},{28,20... | collective-permute-start | bytes 2752520 | tf_op jit(solution)/shard_map/ppermute | solution.py:70
  25.6 3.7 %collective-permute-done.6.refs_2_.refs_4_ = bf16[4,224,512]{2,1,0:T(8,128)(2,1)S(1)} collective-permute-done((bf16[4,224,512]{2,1,0:T(8,128)(2,1)}, bf16[4,224,512]{2,1,0:T(8,128)(2,1)S(1)}, u32[]{:S(2)}, u32[]{:S(2)}) %collective-permute-start.6) | collective-permute-done | bytes 917536 | tf_op jit(solution)/shard_map/ppermute | solution.py:55
  34.5 13.2 %collective-permute-done.9.refs_2_.refs_5_ = bf16[4,224,512]{2,1,0:T(8,128)(2,1)} collective-permute-done((bf16[4,224,512]{2,1,0:T(8,128)(2,1)}, bf16[4,224,512]{2,1,0:T(8,128)(2,1)}, u32[]{:S(2)}, u32[]{:S(2)}) %collective-permute-start.9) | collective-permute-done | bytes 917536 | tf_op jit(solution)/shard_map/ppermute | solution.py:55
  47.7 1.7 %collective-permute-start.10 = (bf16[4,64,512]{2,1,0:T(8,128)(2,1)S(1)}, bf16[4,64,512]{2,1,0:T(8,128)(2,1)S(1)}, u32[]{:S(2)}, u32[]{:S(2)}) collective-permute-start(bf16[4,64,512]{2,1,0:T(8,128)(2,1)S(1)} %constant_dynamic-slice_fusion), channel_id=1, source_target_pairs={{0,1},{1,0},{2,3},{3,2},{4,5},{5,4},{6,7},{7,6},{8,9},{9,8},{10,11... | collective-permute-start | bytes 786440 | tf_op jit(solution)/shard_map/ppermute | solution.py:55
  49.4 5.3 %partial.6 = (bf16[1,336,512]{2,1,0:T(8,128)(2,1)S(1)}, bf16[4,336,512]{2,1,0:T(8,128)(2,1)S(1)}, bf16[4,336,512]{2,1,0:T(8,128)(2,1)S(1)}) custom-call(s32[3]{0:T(128)S(1)} %pad_add_fusion.refs_0_, bf16[8,112,512]{2,1,0:T(8,128)(2,1)S(1)} %bitcast.8, bf16[8,112,512]{2,1,0:T(8,128)(2,1)} %collective-permute-done.refs_0_.refs_2_.refs_5_, ...), custom_call_target="tpu_custom_call" | custom-call | flops 1 | bytes 1 | tf_op jit(solution)/shard_map/partial/pallas_call | solution.py:34
  54.8 1.8 %mix.1.refs_13_.refs_3_.refs_9_.refs_7_ = bf16[4,512,512]{2,1,0:T(8,128)(2,1)S(1)} custom-call(bf16[1,512,512]{2,1,0:T(8,128)(2,1)S(1)} %copy-done.6, bf16[1,512,512]{2,1,0:T(8,128)(2,1)S(1)} %copy-done.8, bf16[1,512,512]{2,1,0:T(8,128)(2,1)S(1)} %copy-done.10, bf16[1,512,512]{2,1,0:T(8,128)(2,1)S(1)} %copy-done.12, bf16[4,224,512]{2,1,0:T(8,128)(2,1)S(1)} %copy-done.4, ...), custom_call_target="tpu_custom_call" | custom-call | flops 1 | bytes 1 | tf_op jit(solution)/shard_map/mix/pallas_call | solution.py:34
  57.2 1.6 %collective-permute-start.2 = (bf16[8,112,512]{2,1,0:T(8,128)(2,1)}, bf16[8,112,512]{2,1,0:T(8,128)(2,1)S(1)}, u32[]{:S(2)}, u32[]{:S(2)}) collective-permute-start(bf16[8,112,512]{2,1,0:T(8,128)(2,1)} %collective-permute-done.1.refs_0_.refs_1_.refs_3_), channel_id=1, source_target_pairs={{0,8},{2,10},{8,16},{10,18},{16,24},{18,26},{24,28},{26,30},{28,20... | collective-permute-start | bytes 2752520 | tf_op jit(solution)/shard_map/ppermute | solution.py:70
  60.3 4.6 %partial.7 = (bf16[1,224,512]{2,1,0:T(8,128)(2,1)S(1)}, bf16[4,224,512]{2,1,0:T(8,128)(2,1)S(1)}, bf16[4,224,512]{2,1,0:T(8,128)(2,1)S(1)}) custom-call(s32[3]{0:T(128)S(1)} %pad_add_fusion.refs_0_, bf16[8,112,512]{2,1,0:T(8,128)(2,1)} %collective-permute-done.1.refs_0_.refs_1_.refs_3_, bf16[8,112,512]{2,1,0:T(8,128)(2,1)} %collective-permute-done.4.refs_1_.refs_2_.refs_4_, ...), custom_call_target="tpu_custom_call" | custom-call | flops 1 | bytes 1 | tf_op jit(solution)/shard_map/partial/pallas_call | solution.py:34
  65.9 2.9 %partial.8.refs_5_.refs_4_ = bf16[1,336,512]{2,1,0:T(8,128)(2,1)S(1)} custom-call(s32[3]{0:T(128)S(1)} %pad_add_fusion.refs_0_, bf16[4,336,512]{2,1,0:T(8,128)(2,1)S(1)} %get-tuple-element.35.refs_1_.refs_3_, bf16[4,336,512]{2,1,0:T(8,128)(2,1)S(1)} %get-tuple-element.36.refs_2_, bf16[4,512,512]{2,1,0:T(8,128)(2,1)S(1)} %mix.1.refs_13_.refs_3_.refs_9_.refs_7_, ...), custom_call_target="tpu_custom_call" | custom-call | flops 1 | bytes 1 | tf_op jit(solution)/shard_map/partial/pallas_call | solution.py:34
  68.8 1.4 %collective-permute-done.14.refs_6_ = bf16[1,336,512]{2,1,0:T(8,128)(2,1)S(1)} collective-permute-done((bf16[1,336,512]{2,1,0:T(8,128)(2,1)S(1)}, bf16[1,336,512]{2,1,0:T(8,128)(2,1)S(1)}, u32[]{:S(2)}, u32[]{:S(2)}) %collective-permute-start.14) | collective-permute-done | bytes 344096 | tf_op jit(solution)/shard_map/ppermute | solution.py:55
  70.2 2.3 %partial.9.refs_3_.refs_5_ = bf16[1,224,512]{2,1,0:T(8,128)(2,1)S(1)} custom-call(s32[3]{0:T(128)S(1)} %pad_add_fusion.refs_0_, bf16[4,224,512]{2,1,0:T(8,128)(2,1)S(1)} %get-tuple-element.33.refs_1_.refs_4_, bf16[4,224,512]{2,1,0:T(8,128)(2,1)S(1)} %get-tuple-element.34.refs_2_, bf16[4,512,512]{2,1,0:T(8,128)(2,1)S(1)} %mix.1.refs_13_.refs_3_.refs_9_.refs_7_, ...), custom_call_target="tpu_custom_call" | custom-call | flops 1 | bytes 1 | tf_op jit(solution)/shard_map/partial/pallas_call | solution.py:34
  72.6 7.2 %collective-permute-done.2.refs_1_.refs_3_ = bf16[8,112,512]{2,1,0:T(8,128)(2,1)S(1)} collective-permute-done((bf16[8,112,512]{2,1,0:T(8,128)(2,1)}, bf16[8,112,512]{2,1,0:T(8,128)(2,1)S(1)}, u32[]{:S(2)}, u32[]{:S(2)}) %collective-permute-start.2) | collective-permute-done | bytes 917536 | tf_op jit(solution)/shard_map/ppermute | solution.py:70
  82.8 1.6 %collective-permute-start.17 = (bf16[4,112,512]{2,1,0:T(8,128)(2,1)S(1)}, bf16[4,112,512]{2,1,0:T(8,128)(2,1)S(1)}, u32[]{:S(2)}, u32[]{:S(2)}) collective-permute-start(bf16[4,112,512]{2,1,0:T(8,128)(2,1)S(1)} %get-tuple-element.38.refs_0_), channel_id=1, source_target_pairs={{0,8},{2,10},{8,16},{10,18},{16,24},{18,26},{24,28},{26,30},{28,20... | collective-permute-start | bytes 1376264 | tf_op jit(solution)/shard_map/ppermute | solution.py:70
  84.9 5.4 %partial.10 = (bf16[2,224,512]{2,1,0:T(8,128)(2,1)S(1)}, bf16[4,224,512]{2,1,0:T(8,128)(2,1)S(1)}, bf16[4,224,512]{2,1,0:T(8,128)(2,1)S(1)}) custom-call(s32[3]{0:T(128)S(1)} %pad_add_fusion.refs_0_, bf16[8,112,512]{2,1,0:T(8,128)(2,1)S(1)} %collective-permute-done.2.refs_1_.refs_3_, bf16[8,112,512]{2,1,0:T(8,128)(2,1)S(1)} %collective-permute-done.5.refs_2_.refs_4_, ...), custom_call_target="tpu_custom_call" | custom-call | flops 1 | bytes 1 | tf_op jit(solution)/shard_map/partial/pallas_call | solution.py:34
  91.2 4.4 %collective-permute-done.20.refs_3_ = bf16[1,224,512]{2,1,0:T(8,128)(2,1)S(1)} collective-permute-done((bf16[1,224,512]{2,1,0:T(8,128)(2,1)S(1)}, bf16[1,224,512]{2,1,0:T(8,128)(2,1)S(1)}, u32[]{:S(2)}, u32[]{:S(2)}) %collective-permute-start.20) | collective-permute-done | bytes 229408 | tf_op jit(solution)/shard_map/ppermute | solution.py:55
  96.5 4.7 %partial.11.refs_4_.refs_0_.refs_2_ = bf16[2,112,512]{2,1,0:T(8,128)(2,1)S(1)} custom-call(s32[3]{0:T(128)S(1)} %pad_add_fusion.refs_0_, bf16[4,112,512]{2,1,0:T(8,128)(2,1)S(1)} %collective-permute-done.17.refs_0_.refs_1_.refs_7_, bf16[4,112,512]{2,1,0:T(8,128)(2,1)S(1)} %collective-permute-done.18.refs_1_.refs_2_, ...), custom_call_target="tpu_custom_call" | custom-call | flops 1 | bytes 1 | tf_op jit(solution)/shard_map/partial/pallas_call | solution.py:34
  104.4 7.9 %residual.2.refs_4_.refs_9_ = f32[4,1024,512]{2,1,0:T(8,128)S(1)} custom-call(s32[3]{0:T(128)S(1)} %pad_add_fusion.refs_0_, bf16[2,560,512]{2,1,0:T(8,128)(2,1)S(1)} %join.3.refs_2_.refs_1_, bf16[2,560,512]{2,1,0:T(8,128)(2,1)S(1)} %collective-permute-done.25.refs_2_, bf16[4,336,512]{2,1,0:T(8,128)(2,1)S(1)} %get-tuple-element.35.refs_1_.refs_3_, ...), custom_call_target="tpu_custom_call" | custom-call | flops 1 | bytes 1 | tf_op jit(solution)/shard_map/residual/pallas_call | solution.py:34
  112.6 1.4 %collective-permute-done.26.refs_4_ = bf16[2,112,512]{2,1,0:T(8,128)(2,1)S(1)} collective-permute-done((bf16[2,112,512]{2,1,0:T(8,128)(2,1)S(1)}, bf16[2,112,512]{2,1,0:T(8,128)(2,1)S(1)}, u32[]{:S(2)}, u32[]{:S(2)}) %collective-permute-start.26) | collective-permute-done | bytes 229408 | tf_op jit(solution)/shard_map/ppermute | solution.py:55
  113.9 6.0 %residual.3 = bf16[4,1024,512]{2,1,0:T(8,128)(2,1)} custom-call(s32[3]{0:T(128)S(1)} %pad_add_fusion.refs_0_, bf16[2,224,512]{2,1,0:T(8,128)(2,1)S(1)} %join.4.refs_12_.refs_1_, bf16[2,224,512]{2,1,0:T(8,128)(2,1)S(1)} %collective-permute-done.23.refs_2_, bf16[2,112,512]{2,1,0:T(8,128)(2,1)S(1)} %join.5.refs_3_, ...), custom_call_target="tpu_custom_call" | custom-call | flops 1 | bytes 1 | tf_op jit(solution)/shard_map/residual/pallas_call | solution.py:34
  (90 shorter events, 20.4 us)
Async XLA Ops:
  0.0 23.6 %collective-permute-start = (bf16[8,112,512]{2,1,0:T(8,128)(2,1)}, bf16[8,112,512]{2,1,0:T(8,128)(2,1)}, u32[]{:S(2)}, u32[]{:S(2)}) collective-permute-start(bf16[8,112,512]{2,1,0:T(8,128)(2,1)} %bitcast.6), channel_id=1, source_target_pairs={{0,8},{2,10},{8,16},{10,18},{16,24},{18,26},{24,28},{26,30},{28,20... | collective-permute-start | bytes 2752520 | tf_op jit(solution)/shard_map/ppermute | solution.py:70
  3.0 22.4 %collective-permute-start.3 = (bf16[8,112,512]{2,1,0:T(8,128)(2,1)}, bf16[8,112,512]{2,1,0:T(8,128)(2,1)}, u32[]{:S(2)}, u32[]{:S(2)}) collective-permute-start(bf16[8,112,512]{2,1,0:T(8,128)(2,1)} %bitcast.7), channel_id=1, source_target_pairs={{0,4},{2,6},{8,0},{10,2},{16,8},{18,10},{24,16},{26,18},{28,24},{3... | collective-permute-start | bytes 2752520 | tf_op jit(solution)/shard_map/ppermute | solution.py:70
  5.9 23.5 %collective-permute-start.6 = (bf16[4,224,512]{2,1,0:T(8,128)(2,1)}, bf16[4,224,512]{2,1,0:T(8,128)(2,1)S(1)}, u32[]{:S(2)}, u32[]{:S(2)}) collective-permute-start(bf16[4,224,512]{2,1,0:T(8,128)(2,1)} %get-tuple-element.44), channel_id=1, source_target_pairs={{0,1},{1,0},{2,3},{3,2},{4,5},{5,4},{6,7},{7,6},{8,9},{9,8},{10,11... | collective-permute-start | bytes 2752520 | tf_op jit(solution)/shard_map/ppermute | solution.py:55
  12.8 12.8 %collective-permute-start.8 = (bf16[1,512,512]{2,1,0:T(8,128)(2,1)S(1)}, bf16[1,512,512]{2,1,0:T(8,128)(2,1)S(1)}, u32[]{:S(2)}, u32[]{:S(2)}) collective-permute-start(bf16[1,512,512]{2,1,0:T(8,128)(2,1)S(1)} %get-tuple-element.25.refs_8_.refs_6_.refs_4_), channel_id=1, source_target_pairs={{0,2},{2,0},{4,6},{6,4},{8,10},{10,8},{12,14},{14,12},{16,18},{18,... | collective-permute-start | bytes 1572872 | tf_op jit(solution)/shard_map/ppermute | solution.py:55
  13.3 34.3 %collective-permute-start.9 = (bf16[4,224,512]{2,1,0:T(8,128)(2,1)}, bf16[4,224,512]{2,1,0:T(8,128)(2,1)}, u32[]{:S(2)}, u32[]{:S(2)}) collective-permute-start(bf16[4,224,512]{2,1,0:T(8,128)(2,1)} %get-tuple-element.43), channel_id=1, source_target_pairs={{0,1},{1,0},{2,3},{3,2},{4,5},{5,4},{6,7},{7,6},{8,9},{9,8},{10,11... | collective-permute-start | bytes 2752520 | tf_op jit(solution)/shard_map/ppermute | solution.py:55
  23.6 25.8 %collective-permute-start.1 = (bf16[8,112,512]{2,1,0:T(8,128)(2,1)}, bf16[8,112,512]{2,1,0:T(8,128)(2,1)}, u32[]{:S(2)}, u32[]{:S(2)}) collective-permute-start(bf16[8,112,512]{2,1,0:T(8,128)(2,1)} %collective-permute-done.refs_0_.refs_2_.refs_5_), channel_id=1, source_target_pairs={{0,8},{2,10},{8,16},{10,18},{16,24},{18,26},{24,28},{26,30},{28,20... | collective-permute-start | bytes 2752520 | tf_op jit(solution)/shard_map/ppermute | solution.py:70
  25.4 23.9 %collective-permute-start.4 = (bf16[8,112,512]{2,1,0:T(8,128)(2,1)}, bf16[8,112,512]{2,1,0:T(8,128)(2,1)}, u32[]{:S(2)}, u32[]{:S(2)}) collective-permute-start(bf16[8,112,512]{2,1,0:T(8,128)(2,1)} %collective-permute-done.3.refs_1_.refs_3_.refs_6_), channel_id=1, source_target_pairs={{0,4},{2,6},{8,0},{10,2},{16,8},{18,10},{24,16},{26,18},{28,24},{3... | collective-permute-start | bytes 2752520 | tf_op jit(solution)/shard_map/ppermute | solution.py:70
  33.0 16.3 %collective-permute-start.11 = (bf16[1,512,512]{2,1,0:T(8,128)(2,1)S(1)}, bf16[1,512,512]{2,1,0:T(8,128)(2,1)}, u32[]{:S(2)}, u32[]{:S(2)}) collective-permute-start(bf16[1,512,512]{2,1,0:T(8,128)(2,1)S(1)} %get-tuple-element.26.refs_9_.refs_7_.refs_5_), channel_id=1, source_target_pairs={{0,2},{2,0},{4,6},{6,4},{8,10},{10,8},{12,14},{14,12},{16,18},{18,... | collective-permute-start | bytes 1572872 | tf_op jit(solution)/shard_map/ppermute | solution.py:55
  33.0 16.3 %collective-permute-start.12 = (bf16[1,512,512]{2,1,0:T(8,128)(2,1)S(1)}, bf16[1,512,512]{2,1,0:T(8,128)(2,1)}, u32[]{:S(2)}, u32[]{:S(2)}) collective-permute-start(bf16[1,512,512]{2,1,0:T(8,128)(2,1)S(1)} %get-tuple-element.27.refs_10_.refs_8_.refs_6_), channel_id=1, source_target_pairs={{0,2},{2,0},{4,6},{6,4},{8,10},{10,8},{12,14},{14,12},{16,18},{18,... | collective-permute-start | bytes 1572872 | tf_op jit(solution)/shard_map/ppermute | solution.py:55
  56.7 27.7 %collective-permute-start.15 = (bf16[4,336,512]{2,1,0:T(8,128)(2,1)S(1)}, bf16[4,336,512]{2,1,0:T(8,128)(2,1)S(1)}, u32[]{:S(2)}, u32[]{:S(2)}) collective-permute-start(bf16[4,336,512]{2,1,0:T(8,128)(2,1)S(1)} %get-tuple-element.36.refs_2_), channel_id=1, source_target_pairs={{0,2},{2,0},{4,6},{6,4},{8,10},{10,8},{12,14},{14,12},{16,18},{18,... | collective-permute-start | bytes 4128776 | tf_op jit(solution)/shard_map/ppermute | solution.py:55
  57.2 22.5 %collective-permute-start.2 = (bf16[8,112,512]{2,1,0:T(8,128)(2,1)}, bf16[8,112,512]{2,1,0:T(8,128)(2,1)S(1)}, u32[]{:S(2)}, u32[]{:S(2)}) collective-permute-start(bf16[8,112,512]{2,1,0:T(8,128)(2,1)} %collective-permute-done.1.refs_0_.refs_1_.refs_3_), channel_id=1, source_target_pairs={{0,8},{2,10},{8,16},{10,18},{16,24},{18,26},{24,28},{26,30},{28,20... | collective-permute-start | bytes 2752520 | tf_op jit(solution)/shard_map/ppermute | solution.py:70
  58.8 22.3 %collective-permute-start.5 = (bf16[8,112,512]{2,1,0:T(8,128)(2,1)}, bf16[8,112,512]{2,1,0:T(8,128)(2,1)S(1)}, u32[]{:S(2)}, u32[]{:S(2)}) collective-permute-start(bf16[8,112,512]{2,1,0:T(8,128)(2,1)} %collective-permute-done.4.refs_1_.refs_2_.refs_4_), channel_id=1, source_target_pairs={{0,4},{2,6},{8,0},{10,2},{16,8},{18,10},{24,16},{26,18},{28,24},{3... | collective-permute-start | bytes 2752520 | tf_op jit(solution)/shard_map/ppermute | solution.py:70
  59.2 11.0 %collective-permute-start.14 = (bf16[1,336,512]{2,1,0:T(8,128)(2,1)S(1)}, bf16[1,336,512]{2,1,0:T(8,128)(2,1)S(1)}, u32[]{:S(2)}, u32[]{:S(2)}) collective-permute-start(bf16[1,336,512]{2,1,0:T(8,128)(2,1)S(1)} %get-tuple-element.32.refs_7_.refs_0_), channel_id=1, source_target_pairs={{0,1},{1,0},{2,3},{3,2},{4,5},{5,4},{6,7},{7,6},{8,9},{9,8},{10,11... | collective-permute-start | bytes 1032200 | tf_op jit(solution)/shard_map/ppermute | solution.py:55
  64.9 17.8 %collective-permute-start.21 = (bf16[1,224,512]{2,1,0:T(8,128)(2,1)S(1)}, bf16[1,224,512]{2,1,0:T(8,128)(2,1)S(1)}, u32[]{:S(2)}, u32[]{:S(2)}) collective-permute-start(bf16[1,224,512]{2,1,0:T(8,128)(2,1)S(1)} %get-tuple-element.37.refs_5_.refs_1_), channel_id=1, source_target_pairs={{0,1},{1,0},{2,3},{3,2},{4,5},{5,4},{6,7},{7,6},{8,9},{9,8},{10,11... | collective-permute-start | bytes 688136 | tf_op jit(solution)/shard_map/ppermute | solution.py:55
  70.2 20.0 %collective-permute-start.22 = (bf16[4,224,512]{2,1,0:T(8,128)(2,1)S(1)}, bf16[4,224,512]{2,1,0:T(8,128)(2,1)S(1)}, u32[]{:S(2)}, u32[]{:S(2)}) collective-permute-start(bf16[4,224,512]{2,1,0:T(8,128)(2,1)S(1)} %get-tuple-element.34.refs_2_), channel_id=1, source_target_pairs={{0,2},{2,0},{4,6},{6,4},{8,10},{10,8},{12,14},{14,12},{16,18},{18,... | collective-permute-start | bytes 2752520 | tf_op jit(solution)/shard_map/ppermute | solution.py:55
  79.7 15.9 %collective-permute-start.19 = (bf16[1,336,512]{2,1,0:T(8,128)(2,1)S(1)}, bf16[1,336,512]{2,1,0:T(8,128)(2,1)S(1)}, u32[]{:S(2)}, u32[]{:S(2)}) collective-permute-start(bf16[1,336,512]{2,1,0:T(8,128)(2,1)S(1)} %partial.8.refs_5_.refs_4_), channel_id=1, source_target_pairs={{0,1},{1,0},{2,3},{3,2},{4,5},{5,4},{6,7},{7,6},{8,9},{9,8},{10,11... | collective-permute-start | bytes 1032200 | tf_op jit(solution)/shard_map/ppermute | solution.py:55
  81.0 14.6 %collective-permute-start.20 = (bf16[1,224,512]{2,1,0:T(8,128)(2,1)S(1)}, bf16[1,224,512]{2,1,0:T(8,128)(2,1)S(1)}, u32[]{:S(2)}, u32[]{:S(2)}) collective-permute-start(bf16[1,224,512]{2,1,0:T(8,128)(2,1)S(1)} %partial.9.refs_3_.refs_5_), channel_id=1, source_target_pairs={{0,1},{1,0},{2,3},{3,2},{4,5},{5,4},{6,7},{7,6},{8,9},{9,8},{10,11... | collective-permute-start | bytes 688136 | tf_op jit(solution)/shard_map/ppermute | solution.py:55
  82.8 13.7 %collective-permute-start.17 = (bf16[4,112,512]{2,1,0:T(8,128)(2,1)S(1)}, bf16[4,112,512]{2,1,0:T(8,128)(2,1)S(1)}, u32[]{:S(2)}, u32[]{:S(2)}) collective-permute-start(bf16[4,112,512]{2,1,0:T(8,128)(2,1)S(1)} %get-tuple-element.38.refs_0_), channel_id=1, source_target_pairs={{0,8},{2,10},{8,16},{10,18},{16,24},{18,26},{24,28},{26,30},{28,20... | collective-permute-start | bytes 1376264 | tf_op jit(solution)/shard_map/ppermute | solution.py:70
  84.4 12.1 %collective-permute-start.18 = (bf16[4,112,512]{2,1,0:T(8,128)(2,1)S(1)}, bf16[4,112,512]{2,1,0:T(8,128)(2,1)S(1)}, u32[]{:S(2)}, u32[]{:S(2)}) collective-permute-start(bf16[4,112,512]{2,1,0:T(8,128)(2,1)S(1)} %get-tuple-element.39.refs_1_), channel_id=1, source_target_pairs={{0,4},{2,6},{8,0},{10,2},{16,8},{18,10},{24,16},{26,18},{28,24},{3... | collective-permute-start | bytes 1376264 | tf_op jit(solution)/shard_map/ppermute | solution.py:70
  90.2 13.4 %collective-permute-start.16 = (bf16[2,224,512]{2,1,0:T(8,128)(2,1)S(1)}, bf16[2,224,512]{2,1,0:T(8,128)(2,1)S(1)}, u32[]{:S(2)}, u32[]{:S(2)}) collective-permute-start(bf16[2,224,512]{2,1,0:T(8,128)(2,1)S(1)} %get-tuple-element.40.refs_8_.refs_0_.refs_2_), channel_id=1, source_target_pairs={{0,1},{1,0},{2,3},{3,2},{4,5},{5,4},{6,7},{7,6},{8,9},{9,8},{10,11... | collective-permute-start | bytes 1376264 | tf_op jit(solution)/shard_map/ppermute | solution.py:55
  95.6 16.9 %collective-permute-start.27 = (bf16[4,224,512]{2,1,0:T(8,128)(2,1)S(1)}, bf16[4,224,512]{2,1,0:T(8,128)(2,1)S(1)}, u32[]{:S(2)}, u32[]{:S(2)}) collective-permute-start(bf16[4,224,512]{2,1,0:T(8,128)(2,1)S(1)} %get-tuple-element.42), channel_id=1, source_target_pairs={{0,2},{2,0},{4,6},{6,4},{8,10},{10,8},{12,14},{14,12},{16,18},{18,... | collective-permute-start | bytes 2752520 | tf_op jit(solution)/shard_map/ppermute | solution.py:55
  101.2 11.1 %collective-permute-start.24 = (bf16[2,112,512]{2,1,0:T(8,128)(2,1)S(1)}, bf16[2,112,512]{2,1,0:T(8,128)(2,1)S(1)}, u32[]{:S(2)}, u32[]{:S(2)}) collective-permute-start(bf16[2,112,512]{2,1,0:T(8,128)(2,1)S(1)} %partial.11.refs_4_.refs_0_.refs_2_), channel_id=1, source_target_pairs={{0,1},{1,0},{2,3},{3,2},{4,5},{5,4},{6,7},{7,6},{8,9},{9,8},{10,11... | collective-permute-start | bytes 688136 | tf_op jit(solution)/shard_map/ppermute | solution.py:55
  103.8 8.8 %collective-permute-start.23 = (bf16[2,224,512]{2,1,0:T(8,128)(2,1)S(1)}, bf16[2,224,512]{2,1,0:T(8,128)(2,1)S(1)}, u32[]{:S(2)}, u32[]{:S(2)}) collective-permute-start(bf16[2,224,512]{2,1,0:T(8,128)(2,1)S(1)} %join.4.refs_12_.refs_1_), channel_id=1, source_target_pairs={{0,2},{2,0},{4,6},{6,4},{8,10},{10,8},{12,14},{14,12},{16,18},{18,... | collective-permute-start | bytes 1376264 | tf_op jit(solution)/shard_map/ppermute | solution.py:55
  103.9 8.7 %collective-permute-start.28 = (bf16[4,112,512]{2,1,0:T(8,128)(2,1)S(1)}, bf16[4,112,512]{2,1,0:T(8,128)(2,1)S(1)}, u32[]{:S(2)}, u32[]{:S(2)}) collective-permute-start(bf16[4,112,512]{2,1,0:T(8,128)(2,1)S(1)} %collective-permute-done.18.refs_1_.refs_2_), channel_id=1, source_target_pairs={{0,2},{2,0},{4,6},{6,4},{8,10},{10,8},{12,14},{14,12},{16,18},{18,... | collective-permute-start | bytes 1376264 | tf_op jit(solution)/shard_map/ppermute | solution.py:55
  (21 other events, 93.6 us)

commit v3 on v2

--- a/solution.py
+++ b/solution.py
@@ -11,7 +11,7 @@
 BF16, F32 = jnp.bfloat16, jnp.float32
 VMEM_LIMIT = 20 * 2**20
 WORK = pl.CostEstimate(flops=1, bytes_accessed=1, transcendentals=0)
-RING = 20
+WALLS = (1, 1, 1, 6, 12)
 WHOLE = pl.BlockSpec(memory_space=pltpu.VMEM)
 ANYWHERE = pl.BlockSpec(memory_space=pl.ANY)
 
@@ -28,7 +28,7 @@
 
     def call(*args):
         held = [
-            a if n in far else pltpu.with_memory_space_constraint(a, pltpu.VMEM)
+            pltpu.with_memory_space_constraint(a, pltpu.HBM if n in far else pltpu.VMEM)
             for n, a in enumerate((*args, *after))
         ]
         return pl.pallas_call(
@@ -70,45 +70,83 @@
     return lax.ppermute(x, "pair", pairs)
 
 
-def turn_kernel(where, own, other, near, far):
-    x = own[0].astype(F32)
-    near[0] = (2.0 * x.T - x).astype(BF16)
+def turn_kernel(where, own, own_rows, other, near, far):
+    near[0] = (2.0 * own[0].astype(F32).T - own_rows[0].astype(F32)).astype(BF16)
     far[0] = other[0].T
 
 
-def turn(where, amplitudes, part, count, after=()):
-    _, rows, width = amplitudes.shape
-    block = (1, width, width)
+def turn(where, amplitudes, part, parts, after=()):
+    count, _, width = amplitudes.shape
+    rows = width // parts
+    block = (1, width, rows)
+    out = pl.BlockSpec((1, rows, width), lambda j, t: (j, 0, 0))
     return kernel_call(
         turn_kernel,
         "turn",
         (count,),
         [
-            pl.BlockSpec(block, lambda j, t: (j + part * count, t[0], 0)),
-            pl.BlockSpec(block, lambda j, t: (j + part * count, 1 - t[0], 0)),
+            pl.BlockSpec(block, lambda j, t: (j, t[0], part)),
+            pl.BlockSpec((1, rows, width), lambda j, t: (j, t[0] * parts + part, 0)),
+            pl.BlockSpec(block, lambda j, t: (j, 1 - t[0], part)),
         ],
-        [pl.BlockSpec(block, lambda j, t: (j, 0, 0))] * 2,
-        [((count, width, width), BF16)] * 2,
+        [out] * 2,
+        [((count, rows, width), BF16)] * 2,
         tile=where,
         after=after,
-        far=(0, 1),
-    )(amplitudes, amplitudes)
-
-
-def mix_kernel(parts, *refs):
+        far=(0, 1, 2),
+    )(amplitudes, amplitudes, amplitudes)
+
+
+def cut_kernel(starts, where, *refs):
+    outs, done = refs[-1 - len(starts) : -1], refs[-1]
+    copies = []
+    for n, (start, out) in enumerate(zip(starts, outs)):
+        at = pl.multiple_of((1 - where[0]) * out.shape[2] + start, 16)
+        source = refs[0].at[:, pl.ds(at, out.shape[1]), :]
+        copies.append(pltpu.make_async_copy(source, out, done.at[n]))
+    for copy in copies:
+        copy.start()
+    for copy in copies:
+        copy.wait()
+
+
+def cut(where, amplitudes, pieces, after=()):
+    count, _, width = amplitudes.shape
+    return kernel_call(
+        functools.partial(cut_kernel, [start for start, _ in pieces]),
+        "cut",
+        (1,),
+        [ANYWHERE],
+        [WHOLE] * len(pieces),
+        [((count, rows, width), BF16) for _, rows in pieces],
+        [pltpu.SemaphoreType.DMA((len(pieces),))],
+        tile=where,
+        after=after,
+        far=(0,),
+    )(amplitudes)
+
+
+def mix_kernel(parts, start, *refs):
     far, arrived, out = refs[:parts], refs[parts:-1], refs[-1]
-    for j, f in enumerate(far):
-        start = 0
-        for r in arrived:
-            rows = pl.ds(start, r.shape[1])
-            out[j, rows] = (2.0 * f[0, rows].astype(F32) - r[j].astype(F32)).astype(BF16)
-            start += r.shape[1]
-
-
-def mix(far, arrived, after=()):
-    shape = (len(far),) + far[0].shape[1:]
+    step = far[0].shape[1]
+    first = 0
+    for r in arrived:
+        rows = r.shape[1]
+        while rows:
+            part, at = divmod(start + first, step)
+            here = min(rows, step - at)
+            came = r.shape[1] - rows
+            value = 2.0 * far[part][:, at : at + here].astype(F32)
+            value -= r[:, came : came + here].astype(F32)
+            out[:, first : first + here] = value.astype(BF16)
+            first, rows = first + here, rows - here
+
+
+def mix(far, arrived, start, after=()):
+    count, _, width = far[0].shape
+    shape = (count, sum(r.shape[1] for r in arrived), width)
     (out,) = kernel_call(
-        functools.partial(mix_kernel, len(far)),
+        functools.partial(mix_kernel, len(far), start),
         "mix",
         (1,),
         [WHOLE] * (len(far) + len(arrived)),
@@ -119,29 +157,27 @@
     return out
 
 
-def partial_kernel(shards, parts, joined, where, *refs):
+def partial_kernel(shards, parts, joined, extras, where, *refs):
     same, cross = refs[:shards], refs[shards : 2 * shards]
     refs = refs[2 * shards :]
     arrays = sum(parts)
     mine, theirs, refs = refs[:arrays], refs[arrays : 2 * arrays], refs[2 * arrays :]
+    extra_refs, refs = refs[:extras], refs[extras:]
     out, total = refs[0], refs[-1]
     j = pl.program_id(0)
     left = jnp.concatenate([r[0] for r in same], axis=0)
     right = jnp.concatenate([r[0] for r in cross], axis=0)
-    if joined:
-        refs[1][0] = left
-        refs[2][0] = right
+    extra = list(extra_refs)
+    for n in range(joined):
+        before = [extra.pop(0)[0]] if extra_refs else []
+        refs[1 + n][0] = jnp.concatenate([*before, (left, right)[n - joined]], axis=0)
+    first = j == 0
     at = 0
     for h, split in enumerate(parts):
-        for part in range(split):
-
-            @pl.when(j // (pl.num_programs(0) // split) == part)
-            def _():
-                value = jnp.dot(left, mine[at + part][0], preferred_element_type=F32)
-                value += jnp.dot(right, theirs[at + part][0], preferred_element_type=F32)
-                before = jnp.where(j == 0, 0.0, total[h])
-                total[h] = value + before
-
+        whole = [jnp.concatenate([r[0] for r in v[at : at + split]], axis=0) for v in (mine, theirs)]
+        value = jnp.dot(left, whole[0], preferred_element_type=F32)
+        value += jnp.dot(right, whole[1], preferred_element_type=F32)
+        total[h] = value + jnp.where(first, 0.0, total[h])
         at += split
 
     @pl.when(j == pl.num_programs(0) - 1)
@@ -149,13 +185,11 @@
         out[...] = total[...].astype(BF16)
 
 
-def partial(where, same, cross, mine, theirs, joined=False, after=()):
-    mine = [m if isinstance(m, list) else [m] for m in mine]
-    theirs = [m if isinstance(m, list) else [m] for m in theirs]
+def partial(where, same, cross, mine, theirs, joined=0, behind=(), after=()):
     parts = [len(m) for m in mine]
     shards, halves = len(same), len(mine)
-    count = sum(m.shape[0] for m in mine[0])
-    width, columns = mine[0][0].shape[1:]
+    count, _, columns = mine[0][0].shape
+    width = same[0].shape[2]
     depths = [v.shape[1] for v in same]
     rows = sum(depths)
     by_j = lambda n, m: pl.BlockSpec((1, n, m), lambda j, t: (j, 0, 0))
@@ -167,31 +201,26 @@
             return pl.BlockSpec((1, v.shape[1], width), lambda j, t: (j + count * (1 - t[1]), 0, 0))
         return pl.BlockSpec((1, v.shape[1], width), lambda j, t: (j + count * t[1], 0, 0))
 
-    def half_spec(part, split):
-        block = count // split
-        return pl.BlockSpec(
-            (1, width, columns),
-            lambda j, t: (jnp.clip(j - part * block, 0, block - 1), 0, 0),
-        )
-
     out_shapes = [((halves, rows, columns), BF16)]
     out_specs = [pl.BlockSpec((halves, rows, columns), lambda j, t: (0, 0, 0))]
-    if joined:
-        out_shapes += [((count, rows, width), BF16)] * 2
-        out_specs += [by_j(rows, width)] * 2
+    for n in range(joined):
+        more = rows + (behind[n].shape[1] if behind else 0)
+        out_shapes.append(((count, more, width), BF16))
+        out_specs.append(by_j(more, width))
     return kernel_call(
-        functools.partial(partial_kernel, shards, parts, joined),
+        functools.partial(partial_kernel, shards, parts, joined, len(behind)),
         "partial",
         (count,),
         [shard_spec(v, False) for v in same]
         + [shard_spec(v, True) for v in cross]
-        + [half_spec(part, split) for split in parts * 2 for part in range(split)],
+        + [by_j(m.shape[1], columns) for v in (mine, theirs) for m in sum(v, [])]
+        + [by_j(v.shape[1], width) for v in behind],
         out_specs,
         out_shapes,
         [pltpu.VMEM((halves, rows, columns), F32)],
         tile=where,
         after=after,
-    )(*same, *cross, *sum(mine, []), *sum(theirs, []))
+    )(*same, *cross, *sum(mine, []), *sum(theirs, []), *behind)
 
 
 def pick_kernel(where, forth, back, same, cross):
@@ -345,19 +374,19 @@
     to_core = functools.partial(swap, axis="pair", bit=0)
     to_tile = functools.partial(swap, axis="virt", bit=0)
 
-    vectors = [jnp.swapaxes(cholesky, 1, 2)]
-    forth, back = vectors[0], vectors[0]
+    unit = width // 32
+    pieces = [(0, 15 * unit), (15 * unit, 13 * unit), (28 * unit, 4 * unit)]
+    sent = cut(where, amplitudes, pieces[:1])
+    sent += cut(where, amplitudes, pieces[1:], after=sent)
+    arrived = [to_tile(v) for v in sent]
+
+    own = jnp.swapaxes(cholesky, 1, 2)
+    vectors = [own]
+    forth, back = own, own
     for step in range(1, places // 2):
         forth, back = ring(forth, 1), ring(back, -1)
         vectors += [forth, back]
 
-    cut = width * 7 // 16 // 16 * 16
-    sent, start = [], 0
-    for rows in (cut, cut, width - 2 * cut):
-        at = (0, (1 - y) * width + start, 0)
-        sent.append(lax.dynamic_slice(amplitudes, at, (count, rows, width)))
-        start += rows
-    arrived = [to_tile(v) for v in sent]
     diagonal = [
         amplitudes,
         energy_virtual.reshape(1, virtual),
@@ -366,71 +395,71 @@
         energy_second,
     ]
     near, near_theirs, far_turned = [], [], []
-    held = []
-    for j in range(count):
-        v, w = turn(where, amplitudes, j, 1, after=held)
+    held = sent[1:]
+    parts = 4
+    for part in range(parts):
+        v, w = turn(where, amplitudes, part, parts, after=held)
         near.append(v)
         far_turned.append(w)
         near_theirs.append(to_core(v))
-        if j == count // 2 - 1:
-            wall_1 = wall(*vectors[1:3], arrived[0], *near_theirs, cost=RING)
+        if part == parts // 2 - 1:
+            wall_1 = wall(*vectors[1:3], arrived[0], *near_theirs, cost=WALLS[0])
             held = [wall_1]
-    wall_2 = wall(*vectors[3:5], arrived[1], *near_theirs[count // 2 :], cost=RING)
+    wall_2 = wall(*vectors[3:5], arrived[1], *near_theirs[parts // 2 :], cost=WALLS[1])
+    far_0 = mix(far_turned, arrived[:2], 0, after=[wall_2])
+    far_0_theirs = to_core(far_0)
     near, near_theirs = [near], [near_theirs]
-    n_1, same_1, cross_1 = partial(
-        where, vectors[:3], vectors[:3], near, near_theirs, joined=True, after=[wall_2]
-    )
-    n_1_sent = to_tile(n_1)
-    far = mix(far_turned, arrived, after=[n_1])
-    far_theirs = to_core(far)
-    n_2, same_2, cross_2 = partial(
-        where, vectors[3:5], vectors[3:5], near, near_theirs, joined=True, after=[far]
-    )
-    n_2_sent = to_tile(n_2)
-    (f_1,) = partial(where, [same_1], [cross_1], [far], [far_theirs], after=[n_2])
-    f_1_sent = to_tile(f_1)
-    handed_1, handed_2 = to_core(cross_1), to_core(cross_2)
-    (f_2,) = partial(where, [same_2], [cross_2], [far], [far_theirs], after=[f_1, n_1_sent])
-    f_2_sent = to_tile(f_2)
-    picked = pick(where, *vectors[5:7], after=[f_2])
+    n_a, same_a, cross_a = partial(
+        where, vectors[:5], vectors[:5], near, near_theirs, joined=2, after=[far_0]
+    )
+    n_a_sent = to_tile(n_a)
+    far_1 = mix(far_turned, arrived[2:], far_0.shape[1], after=[n_a])
+    far_1_theirs = to_core(far_1)
+    far, far_theirs = [far_0, far_1], [far_0_theirs, far_1_theirs]
+    f_a, cross_a = partial(where, [same_a], [cross_a], [far], [far_theirs], joined=1)
+    f_a_sent = to_tile(f_a)
+    handed_a = to_core(cross_a)
+    picked = pick(where, *vectors[5:7], after=[f_a, n_a_sent])
     same_c, cross_c = ring(picked[0], 1), ring(picked[1], -1)
-    wall_3 = wall(*picked, handed_1, cost=RING)
+    wall_3 = wall(*picked, cost=WALLS[2])
     halves, halves_theirs = near + [far], near_theirs + [far_theirs]
     p_b, same_b, cross_b = partial(
-        where, vectors[5:7], vectors[5:7], halves, halves_theirs, joined=True, after=[wall_3]
+        where, vectors[5:7], vectors[5:7], halves, halves_theirs, joined=2, after=[wall_3]
     )
     p_b_sent = to_tile(p_b)
-    handed_b = to_core(cross_b)
-    m_a = join(
-        [(n_1, 0), (n_2, 0)],
-        [(n_1_sent, 0), (n_2_sent, 0)],
-        [(f_1, 0), (f_2, 0)],
-        [(f_1_sent, 0), (f_2_sent, 0)],
-        after=[p_b, handed_2],
-    )
+    m_a = join([(n_a, 0)], [(n_a_sent, 0)], [(f_a, 0)], [(f_a_sent, 0)], after=[p_b])
     m_a_theirs = to_core(m_a)
-    wall_4 = wall(same_c, cross_c, m_a, cost=RING)
-    (p_c,) = partial(where, [same_c], [cross_c], halves, halves_theirs, after=[wall_4])
+    wall_4 = wall(same_c, cross_c, m_a, cost=WALLS[3])
+    p_c, same_d, cross_d = partial(
+        where,
+        [same_c],
+        [cross_c],
+        halves,
+        halves_theirs,
+        joined=2,
+        behind=[same_b, cross_b],
+        after=[wall_4],
+    )
     p_c_sent = to_tile(p_c)
-    handed_c = to_core(cross_c)
-    m_b = join([(p_b, 0)], [(p_b_sent, 0)], [(p_b, 1)], [(p_b_sent, 1)], after=[p_c])
-    m_b_theirs = to_core(m_b)
+    handed_d = to_core(cross_d)
+    wall_5 = wall(p_c, p_b_sent, cost=WALLS[4])
     started = residual(
         where,
         [m_a, m_a_theirs],
-        [same_1, same_2, handed_1, handed_2],
+        [same_a, handed_a],
         first=diagonal,
         last=False,
-        after=[m_b],
-    )
-    m_c = join([(p_c, 0)], [(p_c_sent, 0)], [(p_c, 1)], [(p_c_sent, 1)], after=[started])
-    m_c_theirs = to_core(m_c)
-    return residual(
-        where,
-        [m_b, m_b_theirs, m_c, m_c_theirs],
-        [same_b, handed_b, same_c, handed_c],
-        before=started,
-    )
+        after=[wall_5],
+    )
+    m_d = join(
+        [(p_b, 0), (p_c, 0)],
+        [(p_b_sent, 0), (p_c_sent, 0)],
+        [(p_b, 1), (p_c, 1)],
+        [(p_b_sent, 1), (p_c_sent, 1)],
+        after=[started],
+    )
+    m_d_theirs = to_core(m_d)
+    return residual(where, [m_d, m_d_theirs], [same_d, handed_d], before=started)
 
 
 def from_partner(x, axis, bit):

time: 120 us -> 110 us (0.917)
  local copies, waits for them, and re-layouts: 8.64 us -> 0.01 us
  waiting for transfers between devices: 43 us -> 41.3 us
    ppermute x8, waiting for transfers between devices: 17.6 us -> 10.5 us  [along_ring(): return lax.ppermute(x, 'pair', pairs)]
    ppermute x21 -> x17, waiting for transfers between devices: 25.5 us -> 30.8 us  [swap(): lax.ppermute(x, axis, [(i, i ^ 1 << bit) for i in range(lax.axis_size(axi...]
    unnamed x32 -> x2, local copies, waits for them, and re-layouts: 4.83 us -> 0.01 us
    dynamic_slice x2 -> x0, local copies, waits for them, and re-layouts: 3.81 us -> none  [two_tiles(): sent.append(lax.dynamic_slice(amplitudes, at, (count, rows, width)))]
    ppermute x21 -> x17, starting transfers between devices: 13.2 us -> 13.1 us  [swap(): lax.ppermute(x, axis, [(i, i ^ 1 << bit) for i in range(lax.axis_size(axi...]
  transfers between devices with their start and end apart: 29 -> 25, of which waited for: 9 -> 12; matrix products, arithmetic and copies ran while one was open for 3% -> 0% of each run, Pallas kernels for 31% -> 36%
where the time goes in v3:
time: 110 us
  Pallas kernels  45.8 us (42%)
  waiting for transfers between devices  41.3 us (38%)
  starting transfers between devices  22.4 us (20%)
    pallas_call x17, Pallas kernels, call(): pl.pallas_call(kernel, grid_spec=pltpu.PrefetchScalarGridSpec(num_scalar_...  45.8 us
    ppermute x17, waiting for transfers between devices, swap(): lax.ppermute(x, axis, [(i, i ^ 1 << bit) for i in range(lax.axis_size(axi...  30.8 us
    ppermute x17, starting transfers between devices, swap(): lax.ppermute(x, axis, [(i, i ^ 1 << bit) for i in range(lax.axis_size(axi...  13.1 us
    ppermute x8, waiting for transfers between devices, along_ring(): return lax.ppermute(x, 'pair', pairs)  10.5 us
    ppermute x8, starting transfers between devices, along_ring(): return lax.ppermute(x, 'pair', pairs)  9.21 us
  transfers between devices with their start and end apart: 25, of which 12 were waited for; matrix products, arithmetic and copies ran while one was open for 0% of the time, Pallas kernels for 36%

profile of v3, /device:TPU:0, one launch (start us, length us, event | category | flops | bytes accessed | tf_op | source)
XLA Modules:
  0.0 109.7 jit_solution(11001573325415802425)
XLA Ops:
  0.0 3.0 %collective-permute-start = (bf16[8,112,512]{2,1,0:T(8,128)(2,1)}, bf16[8,112,512]{2,1,0:T(8,128)(2,1)S(1)}, u32[]{:S(2)}, u32[]{:S(2)}) collective-permute-start(bf16[8,112,512]{2,1,0:T(8,128)(2,1)} %bitcast.6), channel_id=1, source_target_pairs={{0,8},{2,10},{8,16},{10,18},{16,24},{18,26},{24,28},{26,30},{28,20... | collective-permute-start | bytes 2752520 | tf_op jit(solution)/shard_map/ppermute | solution.py:70
  4.9 2.0 %collective-permute-start.6 = (bf16[4,240,512]{2,1,0:T(8,128)(2,1)S(1)}, bf16[4,240,512]{2,1,0:T(8,128)(2,1)S(1)}, u32[]{:S(2)}, u32[]{:S(2)}) collective-permute-start(bf16[4,240,512]{2,1,0:T(8,128)(2,1)S(1)} %cut.2.refs_2_), channel_id=1, source_target_pairs={{0,1},{1,0},{2,3},{3,2},{4,5},{5,4},{6,7},{7,6},{8,9},{9,8},{10,11... | collective-permute-start | bytes 2949128 | tf_op jit(solution)/shard_map/ppermute | solution.py:55
  8.7 3.2 %turn.4 = (bf16[4,128,512]{2,1,0:T(8,128)(2,1)S(1)}, bf16[4,128,512]{2,1,0:T(8,128)(2,1)S(1)}) custom-call(s32[3]{0:T(128)S(1)} %pad_add_fusion.refs_0_, bf16[4,1024,512]{2,1,0:T(8,128)(2,1)} %refs_5_.1, bf16[4,1024,512]{2,1,0:T(8,128)(2,1)} %refs_5_.1, bf16[4,1024,512]{2,1,0:T(8,128)(2,1)} %refs_5_.1, bf16[4,208,512]{2,1,0:T(8,128)(2,1)S(1)} %get-tuple-element.28.refs_4_, ...), custom_call_target="tpu_custom_call" | custom-call | flops 1 | bytes 1 | tf_op jit(solution)/shard_map/turn/pallas_call | solution.py:34
  11.9 3.2 %turn.5 = (bf16[4,128,512]{2,1,0:T(8,128)(2,1)S(1)}, bf16[4,128,512]{2,1,0:T(8,128)(2,1)S(1)}) custom-call(s32[3]{0:T(128)S(1)} %pad_add_fusion.refs_0_, bf16[4,1024,512]{2,1,0:T(8,128)(2,1)} %refs_5_.1, bf16[4,1024,512]{2,1,0:T(8,128)(2,1)} %refs_5_.1, bf16[4,1024,512]{2,1,0:T(8,128)(2,1)} %refs_5_.1, bf16[4,208,512]{2,1,0:T(8,128)(2,1)S(1)} %get-tuple-element.28.refs_4_, ...), custom_call_target="tpu_custom_call" | custom-call | flops 1 | bytes 1 | tf_op jit(solution)/shard_map/turn/pallas_call | solution.py:34
  15.7 7.8 %collective-permute-done.refs_0_.refs_2_.refs_7_ = bf16[8,112,512]{2,1,0:T(8,128)(2,1)S(1)} collective-permute-done((bf16[8,112,512]{2,1,0:T(8,128)(2,1)}, bf16[8,112,512]{2,1,0:T(8,128)(2,1)S(1)}, u32[]{:S(2)}, u32[]{:S(2)}) %collective-permute-start) | collective-permute-done | bytes 917536 | tf_op jit(solution)/shard_map/ppermute | solution.py:70
  23.5 1.8 %collective-permute-start.1 = (bf16[8,112,512]{2,1,0:T(8,128)(2,1)S(1)}, bf16[8,112,512]{2,1,0:T(8,128)(2,1)S(1)}, u32[]{:S(2)}, u32[]{:S(2)}) collective-permute-start(bf16[8,112,512]{2,1,0:T(8,128)(2,1)S(1)} %collective-permute-done.refs_0_.refs_2_.refs_7_), channel_id=1, source_target_pairs={{0,8},{2,10},{8,16},{10,18},{16,24},{18,26},{24,28},{26,30},{28,20... | collective-permute-start | bytes 2752520 | tf_op jit(solution)/shard_map/ppermute | solution.py:70
  25.5 1.8 %collective-permute-start.9 = (bf16[4,208,512]{2,1,0:T(8,128)(2,1)S(1)}, bf16[4,208,512]{2,1,0:T(8,128)(2,1)S(1)}, u32[]{:S(2)}, u32[]{:S(2)}) collective-permute-start(bf16[4,208,512]{2,1,0:T(8,128)(2,1)S(1)} %get-tuple-element.28.refs_4_), channel_id=1, source_target_pairs={{0,1},{1,0},{2,3},{3,2},{4,5},{5,4},{6,7},{7,6},{8,9},{9,8},{10,11... | collective-permute-start | bytes 2555912 | tf_op jit(solution)/shard_map/ppermute | solution.py:55
  27.3 2.1 %collective-permute-done.6.refs_2_.refs_4_ = bf16[4,240,512]{2,1,0:T(8,128)(2,1)S(1)} collective-permute-done((bf16[4,240,512]{2,1,0:T(8,128)(2,1)S(1)}, bf16[4,240,512]{2,1,0:T(8,128)(2,1)S(1)}, u32[]{:S(2)}, u32[]{:S(2)}) %collective-permute-start.6) | collective-permute-done | bytes 983072 | tf_op jit(solution)/shard_map/ppermute | solution.py:55
  29.4 3.2 %turn.7 = (bf16[4,128,512]{2,1,0:T(8,128)(2,1)S(1)}, bf16[4,128,512]{2,1,0:T(8,128)(2,1)S(1)}) custom-call(s32[3]{0:T(128)S(1)} %pad_add_fusion.refs_0_, bf16[4,1024,512]{2,1,0:T(8,128)(2,1)} %refs_5_.1, bf16[4,1024,512]{2,1,0:T(8,128)(2,1)} %refs_5_.1, bf16[4,1024,512]{2,1,0:T(8,128)(2,1)} %refs_5_.1, f32[8,128]{1,0:T(8,128)S(1)} %wall.5.refs_4_), custom_call_target="tpu_custom_call" | custom-call | flops 1 | bytes 1 | tf_op jit(solution)/shard_map/turn/pallas_call | solution.py:34
  32.6 3.2 %turn.6 = (bf16[4,128,512]{2,1,0:T(8,128)(2,1)S(1)}, bf16[4,128,512]{2,1,0:T(8,128)(2,1)S(1)}) custom-call(s32[3]{0:T(128)S(1)} %pad_add_fusion.refs_0_, bf16[4,1024,512]{2,1,0:T(8,128)(2,1)} %refs_5_.1, bf16[4,1024,512]{2,1,0:T(8,128)(2,1)} %refs_5_.1, bf16[4,1024,512]{2,1,0:T(8,128)(2,1)} %refs_5_.1, f32[8,128]{1,0:T(8,128)S(1)} %wall.5.refs_4_), custom_call_target="tpu_custom_call" | custom-call | flops 1 | bytes 1 | tf_op jit(solution)/shard_map/turn/pallas_call | solution.py:34
  36.3 10.1 %collective-permute-done.9.refs_2_.refs_5_ = bf16[4,208,512]{2,1,0:T(8,128)(2,1)S(1)} collective-permute-done((bf16[4,208,512]{2,1,0:T(8,128)(2,1)S(1)}, bf16[4,208,512]{2,1,0:T(8,128)(2,1)S(1)}, u32[]{:S(2)}, u32[]{:S(2)}) %collective-permute-start.9) | collective-permute-done | bytes 852000 | tf_op jit(solution)/shard_map/ppermute | solution.py:55
  47.1 1.8 %collective-permute-start.2 = (bf16[8,112,512]{2,1,0:T(8,128)(2,1)S(1)}, bf16[8,112,512]{2,1,0:T(8,128)(2,1)S(1)}, u32[]{:S(2)}, u32[]{:S(2)}) collective-permute-start(bf16[8,112,512]{2,1,0:T(8,128)(2,1)S(1)} %collective-permute-done.1.refs_0_.refs_4_.refs_9_), channel_id=1, source_target_pairs={{0,8},{2,10},{8,16},{10,18},{16,24},{18,26},{24,28},{26,30},{28,20... | collective-permute-start | bytes 2752520 | tf_op jit(solution)/shard_map/ppermute | solution.py:70
  50.8 3.7 %partial.4 = (bf16[1,560,512]{2,1,0:T(8,128)(2,1)S(1)}, bf16[4,560,512]{2,1,0:T(8,128)(2,1)S(1)}, bf16[4,560,512]{2,1,0:T(8,128)(2,1)S(1)}) custom-call(s32[3]{0:T(128)S(1)} %pad_add_fusion.refs_0_, bf16[8,112,512]{2,1,0:T(8,128)(2,1)S(1)} %bitcast.8, bf16[8,112,512]{2,1,0:T(8,128)(2,1)S(1)} %collective-permute-done.refs_0_.refs_2_.refs_7_, ...), custom_call_target="tpu_custom_call" | custom-call | flops 1 | bytes 1 | tf_op jit(solution)/shard_map/partial/pallas_call | solution.py:34
  54.9 2.7 %collective-permute-done.12.refs_4_ = bf16[4,64,512]{2,1,0:T(8,128)(2,1)S(1)} collective-permute-done((bf16[4,64,512]{2,1,0:T(8,128)(2,1)S(1)}, bf16[4,64,512]{2,1,0:T(8,128)(2,1)S(1)}, u32[]{:S(2)}, u32[]{:S(2)}) %collective-permute-start.12) | collective-permute-done | bytes 262176 | tf_op jit(solution)/shard_map/ppermute | solution.py:55
  59.3 3.7 %partial.5 = (bf16[1,560,512]{2,1,0:T(8,128)(2,1)S(1)}, bf16[4,560,512]{2,1,0:T(8,128)(2,1)S(1)}) custom-call(s32[3]{0:T(128)S(1)} %pad_add_fusion.refs_0_, bf16[4,560,512]{2,1,0:T(8,128)(2,1)S(1)} %get-tuple-element.39.refs_1_.refs_3_, bf16[4,560,512]{2,1,0:T(8,128)(2,1)S(1)} %get-tuple-element.40.refs_2_, ...), custom_call_target="tpu_custom_call" | custom-call | flops 1 | bytes 1 | tf_op jit(solution)/shard_map/partial/pallas_call | solution.py:34
  63.2 2.4 %collective-permute-start.18 = (bf16[1,560,512]{2,1,0:T(8,128)(2,1)S(1)}, bf16[1,560,512]{2,1,0:T(8,128)(2,1)S(1)}, u32[]{:S(2)}, u32[]{:S(2)}) collective-permute-start(bf16[1,560,512]{2,1,0:T(8,128)(2,1)S(1)} %get-tuple-element.41.refs_3_.refs_2_), channel_id=1, source_target_pairs={{0,1},{1,0},{2,3},{3,2},{4,5},{5,4},{6,7},{7,6},{8,9},{9,8},{10,11... | collective-permute-start | bytes 1720328 | tf_op jit(solution)/shard_map/ppermute | solution.py:55
  65.6 4.9 %collective-permute-done.15.refs_4_.refs_3_ = bf16[1,560,512]{2,1,0:T(8,128)(2,1)S(1)} collective-permute-done((bf16[1,560,512]{2,1,0:T(8,128)(2,1)S(1)}, bf16[1,560,512]{2,1,0:T(8,128)(2,1)S(1)}, u32[]{:S(2)}, u32[]{:S(2)}) %collective-permute-start.15) | collective-permute-done | bytes 573472 | tf_op jit(solution)/shard_map/ppermute | solution.py:55
  74.0 3.3 %partial.6 = (bf16[2,224,512]{2,1,0:T(8,128)(2,1)S(1)}, bf16[4,224,512]{2,1,0:T(8,128)(2,1)S(1)}, bf16[4,224,512]{2,1,0:T(8,128)(2,1)S(1)}) custom-call(s32[3]{0:T(128)S(1)} %pad_add_fusion.refs_0_, bf16[8,112,512]{2,1,0:T(8,128)(2,1)S(1)} %collective-permute-done.2.refs_1_.refs_3_, bf16[8,112,512]{2,1,0:T(8,128)(2,1)S(1)} %collective-permute-done.5.refs_2_.refs_4_, ...), custom_call_target="tpu_custom_call" | custom-call | flops 1 | bytes 1 | tf_op jit(solution)/shard_map/partial/pallas_call | solution.py:34
  78.9 3.9 %collective-permute-done.18.refs_1_ = bf16[1,560,512]{2,1,0:T(8,128)(2,1)S(1)} collective-permute-done((bf16[1,560,512]{2,1,0:T(8,128)(2,1)S(1)}, bf16[1,560,512]{2,1,0:T(8,128)(2,1)S(1)}, u32[]{:S(2)}, u32[]{:S(2)}) %collective-permute-start.18) | collective-permute-done | bytes 573472 | tf_op jit(solution)/shard_map/ppermute | solution.py:55
  85.0 2.5 %partial.7 = (bf16[2,112,512]{2,1,0:T(8,128)(2,1)S(1)}, bf16[4,336,512]{2,1,0:T(8,128)(2,1)S(1)}, bf16[4,336,512]{2,1,0:T(8,128)(2,1)S(1)}) custom-call(s32[3]{0:T(128)S(1)} %pad_add_fusion.refs_0_, bf16[4,112,512]{2,1,0:T(8,128)(2,1)S(1)} %collective-permute-done.16.refs_0_.refs_1_, bf16[4,112,512]{2,1,0:T(8,128)(2,1)S(1)} %collective-permute-done.17.refs_1_.refs_2_, ...), custom_call_target="tpu_custom_call" | custom-call | flops 1 | bytes 1 | tf_op jit(solution)/shard_map/partial/pallas_call | solution.py:34
  89.2 3.5 %collective-permute-done.19.refs_1_.refs_2_.refs_6_ = bf16[2,224,512]{2,1,0:T(8,128)(2,1)S(1)} collective-permute-done((bf16[2,224,512]{2,1,0:T(8,128)(2,1)S(1)}, bf16[2,224,512]{2,1,0:T(8,128)(2,1)S(1)}, u32[]{:S(2)}, u32[]{:S(2)}) %collective-permute-start.19) | collective-permute-done | bytes 458784 | tf_op jit(solution)/shard_map/ppermute | solution.py:55
  92.6 8.7 %residual.2.refs_8_.refs_5_ = f32[4,1024,512]{2,1,0:T(8,128)S(1)} custom-call(s32[3]{0:T(128)S(1)} %pad_add_fusion.refs_0_, bf16[2,560,512]{2,1,0:T(8,128)(2,1)S(1)} %join.2.refs_2_.refs_1_, bf16[2,560,512]{2,1,0:T(8,128)(2,1)S(1)} %collective-permute-done.21.refs_2_, bf16[4,560,512]{2,1,0:T(8,128)(2,1)S(1)} %get-tuple-element.39.refs_1_.refs_3_, ...), custom_call_target="tpu_custom_call" | custom-call | flops 1 | bytes 1 | tf_op jit(solution)/shard_map/residual/pallas_call | solution.py:34
  101.6 2.1 %collective-permute-done.23.refs_2_ = bf16[2,336,512]{2,1,0:T(8,128)(2,1)S(1)} collective-permute-done((bf16[2,336,512]{2,1,0:T(8,128)(2,1)S(1)}, bf16[2,336,512]{2,1,0:T(8,128)(2,1)S(1)}, u32[]{:S(2)}, u32[]{:S(2)}) %collective-permute-start.23) | collective-permute-done | bytes 688160 | tf_op jit(solution)/shard_map/ppermute | solution.py:55
  103.7 6.0 %residual.3 = bf16[4,1024,512]{2,1,0:T(8,128)(2,1)} custom-call(s32[3]{0:T(128)S(1)} %pad_add_fusion.refs_0_, bf16[2,336,512]{2,1,0:T(8,128)(2,1)S(1)} %join.3.refs_1_, bf16[2,336,512]{2,1,0:T(8,128)(2,1)S(1)} %collective-permute-done.23.refs_2_, bf16[4,336,512]{2,1,0:T(8,128)(2,1)S(1)} %get-tuple-element.49.refs_3_, ...), custom_call_target="tpu_custom_call" | custom-call | flops 1 | bytes 1 | tf_op jit(solution)/shard_map/residual/pallas_call | solution.py:34
  (51 shorter events, 19.0 us)
Async XLA Ops:
  0.0 23.5 %collective-permute-start = (bf16[8,112,512]{2,1,0:T(8,128)(2,1)}, bf16[8,112,512]{2,1,0:T(8,128)(2,1)S(1)}, u32[]{:S(2)}, u32[]{:S(2)}) collective-permute-start(bf16[8,112,512]{2,1,0:T(8,128)(2,1)} %bitcast.6), channel_id=1, source_target_pairs={{0,8},{2,10},{8,16},{10,18},{16,24},{18,26},{24,28},{26,30},{28,20... | collective-permute-start | bytes 2752520 | tf_op jit(solution)/shard_map/ppermute | solution.py:70
  3.0 22.3 %collective-permute-start.3 = (bf16[8,112,512]{2,1,0:T(8,128)(2,1)}, bf16[8,112,512]{2,1,0:T(8,128)(2,1)S(1)}, u32[]{:S(2)}, u32[]{:S(2)}) collective-permute-start(bf16[8,112,512]{2,1,0:T(8,128)(2,1)} %bitcast.7), channel_id=1, source_target_pairs={{0,4},{2,6},{8,0},{10,2},{16,8},{18,10},{24,16},{26,18},{28,24},{3... | collective-permute-start | bytes 2752520 | tf_op jit(solution)/shard_map/ppermute | solution.py:70
  4.9 24.5 %collective-permute-start.6 = (bf16[4,240,512]{2,1,0:T(8,128)(2,1)S(1)}, bf16[4,240,512]{2,1,0:T(8,128)(2,1)S(1)}, u32[]{:S(2)}, u32[]{:S(2)}) collective-permute-start(bf16[4,240,512]{2,1,0:T(8,128)(2,1)S(1)} %cut.2.refs_2_), channel_id=1, source_target_pairs={{0,1},{1,0},{2,3},{3,2},{4,5},{5,4},{6,7},{7,6},{8,9},{9,8},{10,11... | collective-permute-start | bytes 2949128 | tf_op jit(solution)/shard_map/ppermute | solution.py:55
  11.9 13.7 %collective-permute-start.7 = (bf16[4,128,512]{2,1,0:T(8,128)(2,1)S(1)}, bf16[4,128,512]{2,1,0:T(8,128)(2,1)S(1)}, u32[]{:S(2)}, u32[]{:S(2)}) collective-permute-start(bf16[4,128,512]{2,1,0:T(8,128)(2,1)S(1)} %get-tuple-element.30.refs_11_.refs_5_.refs_3_), channel_id=1, source_target_pairs={{0,2},{2,0},{4,6},{6,4},{8,10},{10,8},{12,14},{14,12},{16,18},{18,... | collective-permute-start | bytes 1572872 | tf_op jit(solution)/shard_map/ppermute | solution.py:55
  15.1 12.2 %collective-permute-start.8 = (bf16[4,128,512]{2,1,0:T(8,128)(2,1)S(1)}, bf16[4,128,512]{2,1,0:T(8,128)(2,1)S(1)}, u32[]{:S(2)}, u32[]{:S(2)}) collective-permute-start(bf16[4,128,512]{2,1,0:T(8,128)(2,1)S(1)} %get-tuple-element.31.refs_12_.refs_6_.refs_4_), channel_id=1, source_target_pairs={{0,2},{2,0},{4,6},{6,4},{8,10},{10,8},{12,14},{14,12},{16,18},{18,... | collective-permute-start | bytes 1572872 | tf_op jit(solution)/shard_map/ppermute | solution.py:55
  23.5 22.9 %collective-permute-start.1 = (bf16[8,112,512]{2,1,0:T(8,128)(2,1)S(1)}, bf16[8,112,512]{2,1,0:T(8,128)(2,1)S(1)}, u32[]{:S(2)}, u32[]{:S(2)}) collective-permute-start(bf16[8,112,512]{2,1,0:T(8,128)(2,1)S(1)} %collective-permute-done.refs_0_.refs_2_.refs_7_), channel_id=1, source_target_pairs={{0,8},{2,10},{8,16},{10,18},{16,24},{18,26},{24,28},{26,30},{28,20... | collective-permute-start | bytes 2752520 | tf_op jit(solution)/shard_map/ppermute | solution.py:70
  25.3 21.1 %collective-permute-start.4 = (bf16[8,112,512]{2,1,0:T(8,128)(2,1)S(1)}, bf16[8,112,512]{2,1,0:T(8,128)(2,1)S(1)}, u32[]{:S(2)}, u32[]{:S(2)}) collective-permute-start(bf16[8,112,512]{2,1,0:T(8,128)(2,1)S(1)} %collective-permute-done.3.refs_1_.refs_3_.refs_8_), channel_id=1, source_target_pairs={{0,4},{2,6},{8,0},{10,2},{16,8},{18,10},{24,16},{26,18},{28,24},{3... | collective-permute-start | bytes 2752520 | tf_op jit(solution)/shard_map/ppermute | solution.py:70
  25.5 20.9 %collective-permute-start.9 = (bf16[4,208,512]{2,1,0:T(8,128)(2,1)S(1)}, bf16[4,208,512]{2,1,0:T(8,128)(2,1)S(1)}, u32[]{:S(2)}, u32[]{:S(2)}) collective-permute-start(bf16[4,208,512]{2,1,0:T(8,128)(2,1)S(1)} %get-tuple-element.28.refs_4_), channel_id=1, source_target_pairs={{0,1},{1,0},{2,3},{3,2},{4,5},{5,4},{6,7},{7,6},{8,9},{9,8},{10,11... | collective-permute-start | bytes 2555912 | tf_op jit(solution)/shard_map/ppermute | solution.py:55
  35.7 10.7 %collective-permute-start.11 = (bf16[4,128,512]{2,1,0:T(8,128)(2,1)S(1)}, bf16[4,128,512]{2,1,0:T(8,128)(2,1)S(1)}, u32[]{:S(2)}, u32[]{:S(2)}) collective-permute-start(bf16[4,128,512]{2,1,0:T(8,128)(2,1)S(1)} %get-tuple-element.33.refs_14_.refs_8_.refs_6_), channel_id=1, source_target_pairs={{0,2},{2,0},{4,6},{6,4},{8,10},{10,8},{12,14},{14,12},{16,18},{18,... | collective-permute-start | bytes 1572872 | tf_op jit(solution)/shard_map/ppermute | solution.py:55
  35.8 10.6 %collective-permute-start.10 = (bf16[4,128,512]{2,1,0:T(8,128)(2,1)S(1)}, bf16[4,128,512]{2,1,0:T(8,128)(2,1)S(1)}, u32[]{:S(2)}, u32[]{:S(2)}) collective-permute-start(bf16[4,128,512]{2,1,0:T(8,128)(2,1)S(1)} %get-tuple-element.32.refs_13_.refs_7_.refs_5_), channel_id=1, source_target_pairs={{0,2},{2,0},{4,6},{6,4},{8,10},{10,8},{12,14},{14,12},{16,18},{18,... | collective-permute-start | bytes 1572872 | tf_op jit(solution)/shard_map/ppermute | solution.py:55
  47.0 12.3 %collective-permute-start.13 = (bf16[4,448,512]{2,1,0:T(8,128)(2,1)S(1)}, bf16[4,448,512]{2,1,0:T(8,128)(2,1)S(1)}, u32[]{:S(2)}, u32[]{:S(2)}) collective-permute-start(bf16[4,448,512]{2,1,0:T(8,128)(2,1)S(1)} %mix.2.refs_19_.refs_3_.refs_9_.refs_7_), channel_id=1, source_target_pairs={{0,2},{2,0},{4,6},{6,4},{8,10},{10,8},{12,14},{14,12},{16,18},{18,... | collective-permute-start | bytes 5505032 | tf_op jit(solution)/shard_map/ppermute | solution.py:55
  47.1 23.4 %collective-permute-start.2 = (bf16[8,112,512]{2,1,0:T(8,128)(2,1)S(1)}, bf16[8,112,512]{2,1,0:T(8,128)(2,1)S(1)}, u32[]{:S(2)}, u32[]{:S(2)}) collective-permute-start(bf16[8,112,512]{2,1,0:T(8,128)(2,1)S(1)} %collective-permute-done.1.refs_0_.refs_4_.refs_9_), channel_id=1, source_target_pairs={{0,8},{2,10},{8,16},{10,18},{16,24},{18,26},{24,28},{26,30},{28,20... | collective-permute-start | bytes 2752520 | tf_op jit(solution)/shard_map/ppermute | solution.py:70
  48.9 22.4 %collective-permute-start.5 = (bf16[8,112,512]{2,1,0:T(8,128)(2,1)S(1)}, bf16[8,112,512]{2,1,0:T(8,128)(2,1)S(1)}, u32[]{:S(2)}, u32[]{:S(2)}) collective-permute-start(bf16[8,112,512]{2,1,0:T(8,128)(2,1)S(1)} %collective-permute-done.4.refs_1_.refs_5_.refs_10_), channel_id=1, source_target_pairs={{0,4},{2,6},{8,0},{10,2},{16,8},{18,10},{24,16},{26,18},{28,24},{3... | collective-permute-start | bytes 2752520 | tf_op jit(solution)/shard_map/ppermute | solution.py:70
  49.2 8.5 %collective-permute-start.12 = (bf16[4,64,512]{2,1,0:T(8,128)(2,1)S(1)}, bf16[4,64,512]{2,1,0:T(8,128)(2,1)S(1)}, u32[]{:S(2)}, u32[]{:S(2)}) collective-permute-start(bf16[4,64,512]{2,1,0:T(8,128)(2,1)S(1)} %get-tuple-element.29.refs_5_), channel_id=1, source_target_pairs={{0,1},{1,0},{2,3},{3,2},{4,5},{5,4},{6,7},{7,6},{8,9},{9,8},{10,11... | collective-permute-start | bytes 786440 | tf_op jit(solution)/shard_map/ppermute | solution.py:55
  54.5 16.0 %collective-permute-start.15 = (bf16[1,560,512]{2,1,0:T(8,128)(2,1)S(1)}, bf16[1,560,512]{2,1,0:T(8,128)(2,1)S(1)}, u32[]{:S(2)}, u32[]{:S(2)}) collective-permute-start(bf16[1,560,512]{2,1,0:T(8,128)(2,1)S(1)} %get-tuple-element.38.refs_5_.refs_0_), channel_id=1, source_target_pairs={{0,1},{1,0},{2,3},{3,2},{4,5},{5,4},{6,7},{7,6},{8,9},{9,8},{10,11... | collective-permute-start | bytes 1720328 | tf_op jit(solution)/shard_map/ppermute | solution.py:55
  63.0 29.6 %collective-permute-start.22 = (bf16[4,560,512]{2,1,0:T(8,128)(2,1)S(1)}, bf16[4,560,512]{2,1,0:T(8,128)(2,1)S(1)}, u32[]{:S(2)}, u32[]{:S(2)}) collective-permute-start(bf16[4,560,512]{2,1,0:T(8,128)(2,1)S(1)} %get-tuple-element.48), channel_id=1, source_target_pairs={{0,2},{2,0},{4,6},{6,4},{8,10},{10,8},{12,14},{14,12},{16,18},{18,... | collective-permute-start | bytes 6881288 | tf_op jit(solution)/shard_map/ppermute | solution.py:55
  63.2 19.6 %collective-permute-start.18 = (bf16[1,560,512]{2,1,0:T(8,128)(2,1)S(1)}, bf16[1,560,512]{2,1,0:T(8,128)(2,1)S(1)}, u32[]{:S(2)}, u32[]{:S(2)}) collective-permute-start(bf16[1,560,512]{2,1,0:T(8,128)(2,1)S(1)} %get-tuple-element.41.refs_3_.refs_2_), channel_id=1, source_target_pairs={{0,1},{1,0},{2,3},{3,2},{4,5},{5,4},{6,7},{7,6},{8,9},{9,8},{10,11... | collective-permute-start | bytes 1720328 | tf_op jit(solution)/shard_map/ppermute | solution.py:55
  71.9 11.8 %collective-permute-start.16 = (bf16[4,112,512]{2,1,0:T(8,128)(2,1)S(1)}, bf16[4,112,512]{2,1,0:T(8,128)(2,1)S(1)}, u32[]{:S(2)}, u32[]{:S(2)}) collective-permute-start(bf16[4,112,512]{2,1,0:T(8,128)(2,1)S(1)} %get-tuple-element.42.refs_0_), channel_id=1, source_target_pairs={{0,8},{2,10},{8,16},{10,18},{16,24},{18,26},{24,28},{26,30},{28,20... | collective-permute-start | bytes 1376264 | tf_op jit(solution)/shard_map/ppermute | solution.py:70
  73.5 11.5 %collective-permute-start.17 = (bf16[4,112,512]{2,1,0:T(8,128)(2,1)S(1)}, bf16[4,112,512]{2,1,0:T(8,128)(2,1)S(1)}, u32[]{:S(2)}, u32[]{:S(2)}) collective-permute-start(bf16[4,112,512]{2,1,0:T(8,128)(2,1)S(1)} %get-tuple-element.43.refs_1_), channel_id=1, source_target_pairs={{0,4},{2,6},{8,0},{10,2},{16,8},{18,10},{24,16},{26,18},{28,24},{3... | collective-permute-start | bytes 1376264 | tf_op jit(solution)/shard_map/ppermute | solution.py:70
  77.3 15.3 %collective-permute-start.19 = (bf16[2,224,512]{2,1,0:T(8,128)(2,1)S(1)}, bf16[2,224,512]{2,1,0:T(8,128)(2,1)S(1)}, u32[]{:S(2)}, u32[]{:S(2)}) collective-permute-start(bf16[2,224,512]{2,1,0:T(8,128)(2,1)S(1)} %get-tuple-element.44.refs_4_.refs_0_), channel_id=1, source_target_pairs={{0,1},{1,0},{2,3},{3,2},{4,5},{5,4},{6,7},{7,6},{8,9},{9,8},{10,11... | collective-permute-start | bytes 1376264 | tf_op jit(solution)/shard_map/ppermute | solution.py:55
  83.0 9.6 %collective-permute-start.21 = (bf16[2,560,512]{2,1,0:T(8,128)(2,1)S(1)}, bf16[2,560,512]{2,1,0:T(8,128)(2,1)S(1)}, u32[]{:S(2)}, u32[]{:S(2)}) collective-permute-start(bf16[2,560,512]{2,1,0:T(8,128)(2,1)S(1)} %join.2.refs_2_.refs_1_), channel_id=1, source_target_pairs={{0,2},{2,0},{4,6},{6,4},{8,10},{10,8},{12,14},{14,12},{16,18},{18,... | collective-permute-start | bytes 3440648 | tf_op jit(solution)/shard_map/ppermute | solution.py:55
  87.6 13.8 %collective-permute-start.20 = (bf16[2,112,512]{2,1,0:T(8,128)(2,1)S(1)}, bf16[2,112,512]{2,1,0:T(8,128)(2,1)S(1)}, u32[]{:S(2)}, u32[]{:S(2)}) collective-permute-start(bf16[2,112,512]{2,1,0:T(8,128)(2,1)S(1)} %get-tuple-element.47.refs_0_.refs_1_.refs_5_), channel_id=1, source_target_pairs={{0,1},{1,0},{2,3},{3,2},{4,5},{5,4},{6,7},{7,6},{8,9},{9,8},{10,11... | collective-permute-start | bytes 688136 | tf_op jit(solution)/shard_map/ppermute | solution.py:55
  89.2 12.4 %collective-permute-start.24 = (bf16[4,336,512]{2,1,0:T(8,128)(2,1)S(1)}, bf16[4,336,512]{2,1,0:T(8,128)(2,1)S(1)}, u32[]{:S(2)}, u32[]{:S(2)}) collective-permute-start(bf16[4,336,512]{2,1,0:T(8,128)(2,1)S(1)} %get-tuple-element.50), channel_id=1, source_target_pairs={{0,2},{2,0},{4,6},{6,4},{8,10},{10,8},{12,14},{14,12},{16,18},{18,... | collective-permute-start | bytes 4128776 | tf_op jit(solution)/shard_map/ppermute | solution.py:55
  101.5 2.2 %collective-permute-start.23 = (bf16[2,336,512]{2,1,0:T(8,128)(2,1)S(1)}, bf16[2,336,512]{2,1,0:T(8,128)(2,1)S(1)}, u32[]{:S(2)}, u32[]{:S(2)}) collective-permute-start(bf16[2,336,512]{2,1,0:T(8,128)(2,1)S(1)} %join.3.refs_1_), channel_id=1, source_target_pairs={{0,2},{2,0},{4,6},{6,4},{8,10},{10,8},{12,14},{14,12},{16,18},{18,... | collective-permute-start | bytes 2064392 | tf_op jit(solution)/shard_map/ppermute | solution.py:55
  (2 other events, 6.0 us)

commit v4 on v3

--- a/solution.py
+++ b/solution.py
@@ -11,7 +11,7 @@
 BF16, F32 = jnp.bfloat16, jnp.float32
 VMEM_LIMIT = 20 * 2**20
 WORK = pl.CostEstimate(flops=1, bytes_accessed=1, transcendentals=0)
-WALLS = (1, 1, 1, 6, 12)
+WALLS = (1, 1, 1, 1, 16)
 WHOLE = pl.BlockSpec(memory_space=pltpu.VMEM)
 ANYWHERE = pl.BlockSpec(memory_space=pl.ANY)
 
@@ -28,7 +28,7 @@
 
     def call(*args):
         held = [
-            pltpu.with_memory_space_constraint(a, pltpu.HBM if n in far else pltpu.VMEM)
+            a if a.ndim == 1 else pltpu.with_memory_space_constraint(a, pltpu.HBM if n in far else pltpu.VMEM)
             for n, a in enumerate((*args, *after))
         ]
         return pl.pallas_call(
@@ -162,27 +162,28 @@
     refs = refs[2 * shards :]
     arrays = sum(parts)
     mine, theirs, refs = refs[:arrays], refs[arrays : 2 * arrays], refs[2 * arrays :]
-    extra_refs, refs = refs[:extras], refs[extras:]
-    out, total = refs[0], refs[-1]
-    j = pl.program_id(0)
-    left = jnp.concatenate([r[0] for r in same], axis=0)
-    right = jnp.concatenate([r[0] for r in cross], axis=0)
-    extra = list(extra_refs)
-    for n in range(joined):
-        before = [extra.pop(0)[0]] if extra_refs else []
-        refs[1 + n][0] = jnp.concatenate([*before, (left, right)[n - joined]], axis=0)
-    first = j == 0
-    at = 0
-    for h, split in enumerate(parts):
-        whole = [jnp.concatenate([r[0] for r in v[at : at + split]], axis=0) for v in (mine, theirs)]
-        value = jnp.dot(left, whole[0], preferred_element_type=F32)
-        value += jnp.dot(right, whole[1], preferred_element_type=F32)
-        total[h] = value + jnp.where(first, 0.0, total[h])
-        at += split
-
-    @pl.when(j == pl.num_programs(0) - 1)
-    def _():
-        out[...] = total[...].astype(BF16)
+    extra, outs = refs[:extras], refs[extras:]
+    count = mine[0].shape[0]
+
+    def together(arrays, j, group=0):
+        pieces = [r[j + (group * count if r.shape[0] > count else 0)] for r in arrays]
+        return jnp.concatenate(pieces, axis=0) if len(pieces) > 1 else pieces[0]
+
+    totals = [None] * len(parts)
+    for j in range(count):
+        left, right = together(same, j, where[1]), together(cross, j, 1 - where[1])
+        for n in range(joined):
+            value = (left, right)[n - joined]
+            outs[1 + n][j] = jnp.concatenate([extra[n][j], value], axis=0) if extras else value
+        at = 0
+        for h, split in enumerate(parts):
+            for shard, half in ((left, mine), (right, theirs)):
+                half = together(half[at : at + split], j)
+                value = jnp.dot(shard, half, preferred_element_type=F32)
+                totals[h] = value if totals[h] is None else totals[h] + value
+            at += split
+    for h, total in enumerate(totals):
+        outs[0][h] = total.astype(BF16)
 
 
 def partial(where, same, cross, mine, theirs, joined=0, behind=(), after=()):
@@ -190,37 +191,22 @@
     shards, halves = len(same), len(mine)
     count, _, columns = mine[0][0].shape
     width = same[0].shape[2]
-    depths = [v.shape[1] for v in same]
-    rows = sum(depths)
-    by_j = lambda n, m: pl.BlockSpec((1, n, m), lambda j, t: (j, 0, 0))
-
-    def shard_spec(v, other):
-        if v.shape[0] == count:
-            return by_j(v.shape[1], width)
-        if other:
-            return pl.BlockSpec((1, v.shape[1], width), lambda j, t: (j + count * (1 - t[1]), 0, 0))
-        return pl.BlockSpec((1, v.shape[1], width), lambda j, t: (j + count * t[1], 0, 0))
-
+    rows = sum(v.shape[1] for v in same)
+    args = [*same, *cross, *sum(mine, []), *sum(theirs, []), *behind]
     out_shapes = [((halves, rows, columns), BF16)]
-    out_specs = [pl.BlockSpec((halves, rows, columns), lambda j, t: (0, 0, 0))]
     for n in range(joined):
         more = rows + (behind[n].shape[1] if behind else 0)
         out_shapes.append(((count, more, width), BF16))
-        out_specs.append(by_j(more, width))
     return kernel_call(
         functools.partial(partial_kernel, shards, parts, joined, len(behind)),
         "partial",
-        (count,),
-        [shard_spec(v, False) for v in same]
-        + [shard_spec(v, True) for v in cross]
-        + [by_j(m.shape[1], columns) for v in (mine, theirs) for m in sum(v, [])]
-        + [by_j(v.shape[1], width) for v in behind],
-        out_specs,
+        (1,),
+        [WHOLE] * len(args),
+        [WHOLE] * len(out_shapes),
         out_shapes,
-        [pltpu.VMEM((halves, rows, columns), F32)],
         tile=where,
         after=after,
-    )(*same, *cross, *sum(mine, []), *sum(theirs, []), *behind)
+    )(*args)
 
 
 def pick_kernel(where, forth, back, same, cross):
@@ -276,91 +262,123 @@
     )(*held)
 
 
-def join(near, near_sent, far, far_sent, after=()):
-    arrays = [v for v, _ in near + far_sent + far + near_sent]
-    rows, columns = sum(v.shape[1] for v, _ in near), near[0][0].shape[2]
-    n, f, fs = len(near), len(far), len(far_sent)
-
-    def body(*refs):
-        at = lambda first, items: [(refs[first + k], h) for k, (_, h) in enumerate(items)]
-        own_near, got_far = at(0, near), at(n, far_sent)
-        own_far, got_near = at(n + fs, far), at(n + fs + f, near_sent)
-        out = refs[-1]
-        for h, own, got in ((0, own_near, got_far), (1, own_far, got_near)):
-            left = jnp.concatenate([r[k] for r, k in own], axis=0)
-            right = jnp.concatenate([r[k] for r, k in got], axis=0)
-            out[h] = (left.astype(F32) + right.astype(F32)).astype(BF16)
-
-    whole = lambda shape: pl.BlockSpec(shape, lambda k: (0, 0, 0))
+def join_kernel(counts, *refs):
+    out, at = refs[-1], 0
+    for h, count in enumerate(counts):
+        own, sent = refs[at : at + count], refs[at + count : at + 2 * count]
+        at += 2 * count
+        left, right = [
+            jnp.concatenate([r[...] for r in v], axis=0) if count > 1 else v[0][...]
+            for v in (own, sent)
+        ]
+        out[h] = (left.astype(F32) + right.astype(F32)).astype(BF16)
+
+
+def join(*halves, after=()):
+    args, in_specs = [], []
+    for pairs in halves:
+        for side in range(2):
+            for pair in pairs:
+                v, h = pair[side]
+                args.append(v)
+                in_specs.append(pl.BlockSpec((None,) + v.shape[1:], functools.partial(lambda h, k: (h, 0, 0), h)))
+    rows = sum(pair[0][0].shape[1] for pair in halves[0])
+    shape = (len(halves), rows, args[0].shape[2])
     (out,) = kernel_call(
-        body,
+        functools.partial(join_kernel, [len(pairs) for pairs in halves]),
         "join",
         (1,),
-        [whole(v.shape) for v in arrays],
-        [whole((2, rows, columns))],
-        [((2, rows, columns), BF16)],
-        after=after,
-    )(*arrays)
+        in_specs,
+        [WHOLE],
+        [(shape, BF16)],
+        after=after,
+    )(*args)
     return out
 
 
-def residual_kernel(chunks, shards, first, where, *refs):
-    middles, vectors = refs[:chunks], refs[chunks : chunks + shards]
-    rest, out, turned = refs[chunks + shards : -2], refs[-2], refs[-1]
-    j = pl.program_id(0)
+def joined_rows(pieces):
+    return jnp.concatenate(pieces, axis=0) if len(pieces) > 1 else pieces[0]
+
+
+def diagonal_kernel(where, values, energy, first_energy, second_energy, own, off, held, done):
+    count, columns, width = own.shape
+    copies = []
+    for h in range(2):
+        tile = lax.rem(where[0] + h, 2)
+        rows = pl.ds(pl.multiple_of(tile * columns, 16), columns)
+        for j in range(count):
+            copies.append(pltpu.make_async_copy(values.at[j, rows], held.at[h, j], done.at[h, j]))
+            copies[-1].start()
+    for h, out in enumerate((own, off)):
+        row_energy = energy[lax.rem(where[0] + h, 2)]
+        row_energy = jnp.broadcast_to(row_energy, (128, columns)).T[:, :1]
+        for j in range(count):
+            occupied = first_energy[where[2]] + second_energy[where[1] * count + j]
+            copies[h * count + j].wait()
+            out[j] = (row_energy - occupied + energy[where[0]]) * held[h, j].astype(F32)
+
+
+def diagonal(where, amplitudes, energy_virtual, energy_first, energy_second, after=()):
+    count, rows, width = amplitudes.shape
+    block = (count, rows // 2, width)
+    return kernel_call(
+        diagonal_kernel,
+        "diagonal",
+        (1,),
+        [ANYWHERE, WHOLE] + [pl.BlockSpec(memory_space=pltpu.SMEM)] * 2,
+        [WHOLE] * 2,
+        [(block, F32)] * 2,
+        [pltpu.VMEM((2,) + block, BF16), pltpu.SemaphoreType.DMA((2, count))],
+        tile=where,
+        after=after,
+        far=(0,),
+    )(amplitudes, energy_virtual.reshape(2, 1, width), energy_first, energy_second)
+
+
+def residual_kernel(chunks, shards, halves, last, where, *refs):
+    middles, vectors, refs = refs[:chunks], refs[chunks : chunks + shards], refs[chunks + shards :]
+    count, _, width = vectors[0].shape
+    before, outs = refs[: len(halves)], refs[len(halves) :]
+    if last:
+        out, held, done = outs
     columns = middles[0].shape[2]
-
-    @pl.when(j == 0)
-    def _():
-        for h in range(2):
-            rows = pl.ds(pl.multiple_of(lax.rem(where[0] + h, 2) * columns, columns), columns)
-            turned[rows] = jnp.concatenate([m[h] for m in middles], axis=0).T
-
-    if first:
-        values, row_energy, column_energy, first_energy, second_energy = rest
-        own = first_energy[where[2]] + second_energy[where[1] * pl.num_programs(0) + j]
-        rows = jnp.broadcast_to(row_energy[...] - own, (128, row_energy.shape[1])).T[:, :1]
-        total = (rows + column_energy[0]) * values[0].astype(F32)
-    else:
-        total = rest[0][j]
-    right = jnp.concatenate([v[j] for v in vectors], axis=0)
-    total += jnp.dot(turned[...], right, preferred_element_type=F32)
-    out[0] = total.astype(out.dtype)
-
-
-def residual(where, middles, vectors, first=None, before=None, last=True, after=()):
+    copies = []
+    for n, h in enumerate(halves):
+        rows = pl.ds(pl.multiple_of(lax.rem(where[0] + h, 2) * columns, 16), columns)
+        left = joined_rows([m[h if m.shape[0] > 1 else 0] for m in middles]).T
+        for j in range(count):
+            total = jnp.dot(left, joined_rows([v[j] for v in vectors]), preferred_element_type=F32)
+            total += before[n][j]
+            if last:
+                held[n, j] = total.astype(BF16)
+                copies.append(pltpu.make_async_copy(held.at[n, j], out.at[j, rows], done.at[n, j]))
+                copies[-1].start()
+            else:
+                outs[n][j] = total
+    for copy in copies:
+        copy.wait()
+
+
+def residual(where, middles, vectors, halves, before, last=False, after=()):
     count, _, width = vectors[0].shape
-    rows = 2 * middles[0].shape[2]
-    depth = sum(m.shape[1] for m in middles)
-    by_j = pl.BlockSpec((1, rows, width), lambda j, t: (j, 0, 0))
-    in_specs = [WHOLE] * (len(middles) + len(vectors))
-    args = [*middles, *vectors]
-    if first is not None:
-        in_specs += [
-            by_j,
-            pl.BlockSpec((1, rows), lambda j, t: (0, 0)),
-            pl.BlockSpec((1, 1, width), lambda j, t: (t[0], 0, 0)),
-            pl.BlockSpec(memory_space=pltpu.SMEM),
-            pl.BlockSpec(memory_space=pltpu.SMEM),
-        ]
-        args += first
-    else:
-        in_specs += [WHOLE]
-        args += [before]
-    (out,) = kernel_call(
-        functools.partial(residual_kernel, len(middles), len(vectors), first is not None),
+    block = (count, middles[0].shape[2], width)
+    args = [*middles, *vectors, *before]
+    out_shapes, scratch = [(block, F32)] * len(halves), []
+    if last:
+        out_shapes = [((count, 2 * block[1], width), BF16)]
+        scratch = [pltpu.VMEM((2,) + block, BF16), pltpu.SemaphoreType.DMA((2, count))]
+    return kernel_call(
+        functools.partial(residual_kernel, len(middles), len(vectors), halves, last),
         "residual",
-        (count,),
-        in_specs,
-        [by_j],
-        [((count, rows, width), BF16 if last else F32)],
-        [pltpu.VMEM((rows, depth), BF16)],
+        (1,),
+        [WHOLE] * len(args),
+        [ANYWHERE if last else WHOLE] * len(out_shapes),
+        out_shapes,
+        scratch,
         tile=where,
         after=after,
-        far=range(len(middles) + len(vectors), len(args)) if first is not None else (),
         out=pltpu.HBM if last else pltpu.VMEM,
     )(*args)
-    return out
 
 
 def two_tiles(amplitudes, cholesky, energy_first, energy_second, energy_virtual):
@@ -387,13 +405,6 @@
         forth, back = ring(forth, 1), ring(back, -1)
         vectors += [forth, back]
 
-    diagonal = [
-        amplitudes,
-        energy_virtual.reshape(1, virtual),
-        energy_virtual.reshape(2, 1, width),
-        energy_first,
-        energy_second,
-    ]
     near, near_theirs, far_turned = [], [], []
     held = sent[1:]
     parts = 4
@@ -405,7 +416,10 @@
         if part == parts // 2 - 1:
             wall_1 = wall(*vectors[1:3], arrived[0], *near_theirs, cost=WALLS[0])
             held = [wall_1]
-    wall_2 = wall(*vectors[3:5], arrived[1], *near_theirs[parts // 2 :], cost=WALLS[1])
+    begun = diagonal(
+        where, amplitudes, energy_virtual, energy_first, energy_second, after=near
+    )
+    wall_2 = wall(*vectors[3:5], arrived[1], *near_theirs[parts // 2 :], *begun, cost=WALLS[1])
     far_0 = mix(far_turned, arrived[:2], 0, after=[wall_2])
     far_0_theirs = to_core(far_0)
     near, near_theirs = [near], [near_theirs]
@@ -427,9 +441,12 @@
         where, vectors[5:7], vectors[5:7], halves, halves_theirs, joined=2, after=[wall_3]
     )
     p_b_sent = to_tile(p_b)
-    m_a = join([(n_a, 0)], [(n_a_sent, 0)], [(f_a, 0)], [(f_a_sent, 0)], after=[p_b])
+    m_off = join([((f_a, 0), (n_a_sent, 0))], after=[p_b])
+    (begun_off,) = residual(where, [m_off], [same_a], [1], begun[1:])
+    m_a = join([((n_a, 0), (f_a_sent, 0))], [((f_a, 0), (n_a_sent, 0))], after=[begun_off])
     m_a_theirs = to_core(m_a)
-    wall_4 = wall(same_c, cross_c, m_a, cost=WALLS[3])
+    (begun_own,) = residual(where, [m_a], [same_a], [0], begun[:1])
+    wall_4 = wall(same_c, cross_c, begun_own, cost=WALLS[3])
     p_c, same_d, cross_d = partial(
         where,
         [same_c],
@@ -443,23 +460,21 @@
     p_c_sent = to_tile(p_c)
     handed_d = to_core(cross_d)
     wall_5 = wall(p_c, p_b_sent, cost=WALLS[4])
-    started = residual(
+    begun = residual(
         where,
-        [m_a, m_a_theirs],
-        [same_a, handed_a],
-        first=diagonal,
-        last=False,
+        [m_a_theirs],
+        [handed_a],
+        [0, 1],
+        [begun_own, begun_off],
         after=[wall_5],
     )
     m_d = join(
-        [(p_b, 0), (p_c, 0)],
-        [(p_b_sent, 0), (p_c_sent, 0)],
-        [(p_b, 1), (p_c, 1)],
-        [(p_b_sent, 1), (p_c_sent, 1)],
-        after=[started],
+        *[[((p_b, h), (p_b_sent, 1 - h)), ((p_c, h), (p_c_sent, 1 - h))] for h in range(2)],
+        after=begun,
     )
     m_d_theirs = to_core(m_d)
-    return residual(where, [m_d, m_d_theirs], [same_d, handed_d], before=started)
+    (out,) = residual(where, [m_d, m_d_theirs], [same_d, handed_d], [0, 1], begun, last=True)
+    return out
 
 
 def from_partner(x, axis, bit):

time: 110 us -> 104 us (0.945)
  waiting for transfers between devices: 41.3 us -> 35.2 us
    ppermute x17, waiting for transfers between devices: 30.8 us -> 26.6 us  [swap(): lax.ppermute(x, axis, [(i, i ^ 1 << bit) for i in range(lax.axis_size(axi...]
    ppermute x8, waiting for transfers between devices: 10.5 us -> 8.58 us  [along_ring(): return lax.ppermute(x, 'pair', pairs)]
    pallas_call x17 -> x21, Pallas kernels: 45.8 us -> 46.1 us  [call(): pl.pallas_call(kernel, grid_spec=pltpu.PrefetchScalarGridSpec(num_scalar_...]
  transfers between devices with their start and end apart: 25 -> 25, of which waited for: 12 -> 10; matrix products, arithmetic and copies ran while one was open for 0% -> 0% of each run, Pallas kernels for 36% -> 39%
where the time goes in v4:
time: 104 us
  Pallas kernels  46.1 us (44%)
  waiting for transfers between devices  35.2 us (34%)
  starting transfers between devices  22.2 us (21%)
    pallas_call x21, Pallas kernels, call(): pl.pallas_call(kernel, grid_spec=pltpu.PrefetchScalarGridSpec(num_scalar_...  46.1 us
    ppermute x17, waiting for transfers between devices, swap(): lax.ppermute(x, axis, [(i, i ^ 1 << bit) for i in range(lax.axis_size(axi...  26.6 us
    ppermute x17, starting transfers between devices, swap(): lax.ppermute(x, axis, [(i, i ^ 1 << bit) for i in range(lax.axis_size(axi...  13 us
    ppermute x8, starting transfers between devices, along_ring(): return lax.ppermute(x, 'pair', pairs)  9.21 us
    ppermute x8, waiting for transfers between devices, along_ring(): return lax.ppermute(x, 'pair', pairs)  8.58 us
  transfers between devices with their start and end apart: 25, of which 10 were waited for; matrix products, arithmetic and copies ran while one was open for 0% of the time, Pallas kernels for 39%

profile of v4, /device:TPU:0, one launch (start us, length us, event | category | flops | bytes accessed | tf_op | source)
XLA Modules:
  0.0 104.0 jit_solution(13322411373451774417)
XLA Ops:
  0.0 3.0 %collective-permute-start = (bf16[8,112,512]{2,1,0:T(8,128)(2,1)}, bf16[8,112,512]{2,1,0:T(8,128)(2,1)S(1)}, u32[]{:S(2)}, u32[]{:S(2)}) collective-permute-start(bf16[8,112,512]{2,1,0:T(8,128)(2,1)} %bitcast.5), channel_id=1, source_target_pairs={{0,8},{2,10},{8,16},{10,18},{16,24},{18,26},{24,28},{26,30},{28,20... | collective-permute-start | bytes 2752520 | tf_op jit(solution)/shard_map/ppermute | solution.py:70
  4.9 2.0 %collective-permute-start.6 = (bf16[4,240,512]{2,1,0:T(8,128)(2,1)S(1)}, bf16[4,240,512]{2,1,0:T(8,128)(2,1)S(1)}, u32[]{:S(2)}, u32[]{:S(2)}) collective-permute-start(bf16[4,240,512]{2,1,0:T(8,128)(2,1)S(1)} %cut.2.refs_2_), channel_id=1, source_target_pairs={{0,1},{1,0},{2,3},{3,2},{4,5},{5,4},{6,7},{7,6},{8,9},{9,8},{10,11... | collective-permute-start | bytes 2949128 | tf_op jit(solution)/shard_map/ppermute | solution.py:55
  8.7 3.2 %turn.4 = (bf16[4,128,512]{2,1,0:T(8,128)(2,1)S(1)}, bf16[4,128,512]{2,1,0:T(8,128)(2,1)S(1)}) custom-call(s32[3]{0:T(128)S(1)} %pad_add_fusion.refs_0_, bf16[4,1024,512]{2,1,0:T(8,128)(2,1)} %refs_1_.13, bf16[4,1024,512]{2,1,0:T(8,128)(2,1)} %refs_1_.13, bf16[4,1024,512]{2,1,0:T(8,128)(2,1)} %refs_1_.13, ...), custom_call_target="tpu_custom_call" | custom-call | flops 1 | bytes 1 | tf_op jit(solution)/shard_map/turn/pallas_call | solution.py:34
  11.9 3.2 %turn.5 = (bf16[4,128,512]{2,1,0:T(8,128)(2,1)S(1)}, bf16[4,128,512]{2,1,0:T(8,128)(2,1)S(1)}) custom-call(s32[3]{0:T(128)S(1)} %pad_add_fusion.refs_0_, bf16[4,1024,512]{2,1,0:T(8,128)(2,1)} %refs_1_.13, bf16[4,1024,512]{2,1,0:T(8,128)(2,1)} %refs_1_.13, bf16[4,1024,512]{2,1,0:T(8,128)(2,1)} %refs_1_.13, ...), custom_call_target="tpu_custom_call" | custom-call | flops 1 | bytes 1 | tf_op jit(solution)/shard_map/turn/pallas_call | solution.py:34
  15.7 7.8 %collective-permute-done.refs_0_.refs_2_.refs_7_ = bf16[8,112,512]{2,1,0:T(8,128)(2,1)S(1)} collective-permute-done((bf16[8,112,512]{2,1,0:T(8,128)(2,1)}, bf16[8,112,512]{2,1,0:T(8,128)(2,1)S(1)}, u32[]{:S(2)}, u32[]{:S(2)}) %collective-permute-start) | collective-permute-done | bytes 917536 | tf_op jit(solution)/shard_map/ppermute | solution.py:70
  23.5 1.8 %collective-permute-start.1 = (bf16[8,112,512]{2,1,0:T(8,128)(2,1)S(1)}, bf16[8,112,512]{2,1,0:T(8,128)(2,1)S(1)}, u32[]{:S(2)}, u32[]{:S(2)}) collective-permute-start(bf16[8,112,512]{2,1,0:T(8,128)(2,1)S(1)} %collective-permute-done.refs_0_.refs_2_.refs_7_), channel_id=1, source_target_pairs={{0,8},{2,10},{8,16},{10,18},{16,24},{18,26},{24,28},{26,30},{28,20... | collective-permute-start | bytes 2752520 | tf_op jit(solution)/shard_map/ppermute | solution.py:70
  27.3 2.1 %collective-permute-done.6.refs_2_.refs_4_ = bf16[4,240,512]{2,1,0:T(8,128)(2,1)S(1)} collective-permute-done((bf16[4,240,512]{2,1,0:T(8,128)(2,1)S(1)}, bf16[4,240,512]{2,1,0:T(8,128)(2,1)S(1)}, u32[]{:S(2)}, u32[]{:S(2)}) %collective-permute-start.6) | collective-permute-done | bytes 983072 | tf_op jit(solution)/shard_map/ppermute | solution.py:55
  29.4 3.2 %turn.7 = (bf16[4,128,512]{2,1,0:T(8,128)(2,1)S(1)}, bf16[4,128,512]{2,1,0:T(8,128)(2,1)S(1)}) custom-call(s32[3]{0:T(128)S(1)} %pad_add_fusion.refs_0_, bf16[4,1024,512]{2,1,0:T(8,128)(2,1)} %refs_1_.13, bf16[4,1024,512]{2,1,0:T(8,128)(2,1)} %refs_1_.13, bf16[4,1024,512]{2,1,0:T(8,128)(2,1)} %refs_1_.13, f32[8,128]{1,0:T(8,128)S(1)} %wall.5.refs_4_), custom_call_target="tpu_custom_call" | custom-call | flops 1 | bytes 1 | tf_op jit(solution)/shard_map/turn/pallas_call | solution.py:34
  32.6 3.2 %turn.6 = (bf16[4,128,512]{2,1,0:T(8,128)(2,1)S(1)}, bf16[4,128,512]{2,1,0:T(8,128)(2,1)S(1)}) custom-call(s32[3]{0:T(128)S(1)} %pad_add_fusion.refs_0_, bf16[4,1024,512]{2,1,0:T(8,128)(2,1)} %refs_1_.13, bf16[4,1024,512]{2,1,0:T(8,128)(2,1)} %refs_1_.13, bf16[4,1024,512]{2,1,0:T(8,128)(2,1)} %refs_1_.13, f32[8,128]{1,0:T(8,128)S(1)} %wall.5.refs_4_), custom_call_target="tpu_custom_call" | custom-call | flops 1 | bytes 1 | tf_op jit(solution)/shard_map/turn/pallas_call | solution.py:34
  36.4 3.7 %diagonal.1 = (f32[4,512,512]{2,1,0:T(8,128)S(1)}, f32[4,512,512]{2,1,0:T(8,128)S(1)}) custom-call(s32[3]{0:T(128)S(1)} %pad_add_fusion.refs_0_, bf16[4,1024,512]{2,1,0:T(8,128)(2,1)} %refs_1_.13, f32[2,1,512]{2,1,0:T(1,128)S(1)} %bitcast.9, f32[8]{0:T(128)S(1)} %copy-done.2, f32[8]{0:T(128)S(1)} %copy-done.3, ...), custom_call_target="tpu_custom_call" | custom-call | flops 1 | bytes 1 | tf_op jit(solution)/shard_map/diagonal/pallas_call | solution.py:34
  40.1 6.4 %collective-permute-done.9.refs_2_.refs_5_ = bf16[4,208,512]{2,1,0:T(8,128)(2,1)S(1)} collective-permute-done((bf16[4,208,512]{2,1,0:T(8,128)(2,1)S(1)}, bf16[4,208,512]{2,1,0:T(8,128)(2,1)S(1)}, u32[]{:S(2)}, u32[]{:S(2)}) %collective-permute-start.9) | collective-permute-done | bytes 852000 | tf_op jit(solution)/shard_map/ppermute | solution.py:55
  50.8 3.1 %partial.4 = (bf16[1,560,512]{2,1,0:T(8,128)(2,1)S(1)}, bf16[4,560,512]{2,1,0:T(8,128)(2,1)S(1)}, bf16[4,560,512]{2,1,0:T(8,128)(2,1)S(1)}) custom-call(s32[3]{0:T(128)S(1)} %pad_add_fusion.refs_0_, bf16[8,112,512]{2,1,0:T(8,128)(2,1)S(1)} %bitcast.7, bf16[8,112,512]{2,1,0:T(8,128)(2,1)S(1)} %collective-permute-done.refs_0_.refs_2_.refs_7_, ...), custom_call_target="tpu_custom_call" | custom-call | flops 1 | bytes 1 | tf_op jit(solution)/shard_map/partial/pallas_call | solution.py:34
  54.3 3.9 %collective-permute-done.12.refs_4_ = bf16[4,64,512]{2,1,0:T(8,128)(2,1)S(1)} collective-permute-done((bf16[4,64,512]{2,1,0:T(8,128)(2,1)S(1)}, bf16[4,64,512]{2,1,0:T(8,128)(2,1)S(1)}, u32[]{:S(2)}, u32[]{:S(2)}) %collective-permute-start.12) | collective-permute-done | bytes 262176 | tf_op jit(solution)/shard_map/ppermute | solution.py:55
  60.0 3.1 %partial.5 = (bf16[1,560,512]{2,1,0:T(8,128)(2,1)S(1)}, bf16[4,560,512]{2,1,0:T(8,128)(2,1)S(1)}) custom-call(s32[3]{0:T(128)S(1)} %pad_add_fusion.refs_0_, bf16[4,560,512]{2,1,0:T(8,128)(2,1)S(1)} %get-tuple-element.45.refs_1_.refs_2_, bf16[4,560,512]{2,1,0:T(8,128)(2,1)S(1)} %get-tuple-element.46.refs_2_, ...), custom_call_target="tpu_custom_call" | custom-call | flops 1 | bytes 1 | tf_op jit(solution)/shard_map/partial/pallas_call | solution.py:34
  65.0 5.5 %collective-permute-done.15.refs_4_.refs_1_.refs_3_ = bf16[1,560,512]{2,1,0:T(8,128)(2,1)S(1)} collective-permute-done((bf16[1,560,512]{2,1,0:T(8,128)(2,1)S(1)}, bf16[1,560,512]{2,1,0:T(8,128)(2,1)S(1)}, u32[]{:S(2)}, u32[]{:S(2)}) %collective-permute-start.15) | collective-permute-done | bytes 573472 | tf_op jit(solution)/shard_map/ppermute | solution.py:55
  74.0 2.6 %partial.6 = (bf16[2,224,512]{2,1,0:T(8,128)(2,1)S(1)}, bf16[4,224,512]{2,1,0:T(8,128)(2,1)S(1)}, bf16[4,224,512]{2,1,0:T(8,128)(2,1)S(1)}) custom-call(s32[3]{0:T(128)S(1)} %pad_add_fusion.refs_0_, bf16[8,112,512]{2,1,0:T(8,128)(2,1)S(1)} %collective-permute-done.2.refs_1_.refs_3_, bf16[8,112,512]{2,1,0:T(8,128)(2,1)S(1)} %collective-permute-done.5.refs_2_.refs_4_, ...), custom_call_target="tpu_custom_call" | custom-call | flops 1 | bytes 1 | tf_op jit(solution)/shard_map/partial/pallas_call | solution.py:34
  78.3 2.4 %residual.4.refs_4_ = f32[4,512,512]{2,1,0:T(8,128)S(1)} custom-call(s32[3]{0:T(128)S(1)} %pad_add_fusion.refs_0_, bf16[1,560,512]{2,1,0:T(8,128)(2,1)S(1)} %join.3.refs_1_, bf16[4,560,512]{2,1,0:T(8,128)(2,1)S(1)} %get-tuple-element.45.refs_1_.refs_2_, f32[4,512,512]{2,1,0:T(8,128)S(1)} %get-tuple-element.43.refs_6_.refs_3_), custom_call_target="tpu_custom_call" | custom-call | flops 1 | bytes 1 | tf_op jit(solution)/shard_map/residual/pallas_call | solution.py:34
  80.7 2.1 %collective-permute-done.18.refs_1_ = bf16[1,560,512]{2,1,0:T(8,128)(2,1)S(1)} collective-permute-done((bf16[1,560,512]{2,1,0:T(8,128)(2,1)S(1)}, bf16[1,560,512]{2,1,0:T(8,128)(2,1)S(1)}, u32[]{:S(2)}, u32[]{:S(2)}) %collective-permute-start.18) | collective-permute-done | bytes 573472 | tf_op jit(solution)/shard_map/ppermute | solution.py:55
  83.1 2.4 %residual.5.refs_2_.refs_3_ = f32[4,512,512]{2,1,0:T(8,128)S(1)} custom-call(s32[3]{0:T(128)S(1)} %pad_add_fusion.refs_0_, bf16[2,560,512]{2,1,0:T(8,128)(2,1)S(1)} %join.4.refs_1_, bf16[4,560,512]{2,1,0:T(8,128)(2,1)S(1)} %get-tuple-element.45.refs_1_.refs_2_, f32[4,512,512]{2,1,0:T(8,128)S(1)} %get-tuple-element.42.refs_5_.refs_3_), custom_call_target="tpu_custom_call" | custom-call | flops 1 | bytes 1 | tf_op jit(solution)/shard_map/residual/pallas_call | solution.py:34
  85.7 1.9 %partial.7 = (bf16[2,112,512]{2,1,0:T(8,128)(2,1)S(1)}, bf16[4,336,512]{2,1,0:T(8,128)(2,1)S(1)}, bf16[4,336,512]{2,1,0:T(8,128)(2,1)S(1)}) custom-call(s32[3]{0:T(128)S(1)} %pad_add_fusion.refs_0_, bf16[4,112,512]{2,1,0:T(8,128)(2,1)S(1)} %collective-permute-done.16.refs_0_.refs_1_, bf16[4,112,512]{2,1,0:T(8,128)(2,1)S(1)} %collective-permute-done.17.refs_1_.refs_2_, ...), custom_call_target="tpu_custom_call" | custom-call | flops 1 | bytes 1 | tf_op jit(solution)/shard_map/partial/pallas_call | solution.py:34
  89.6 2.9 %collective-permute-done.19.refs_1_.refs_2_.refs_6_ = bf16[2,224,512]{2,1,0:T(8,128)(2,1)S(1)} collective-permute-done((bf16[2,224,512]{2,1,0:T(8,128)(2,1)S(1)}, bf16[2,224,512]{2,1,0:T(8,128)(2,1)S(1)}, u32[]{:S(2)}, u32[]{:S(2)}) %collective-permute-start.19) | collective-permute-done | bytes 458784 | tf_op jit(solution)/shard_map/ppermute | solution.py:55
  92.5 4.0 %residual.6 = (f32[4,512,512]{2,1,0:T(8,128)S(1)}, f32[4,512,512]{2,1,0:T(8,128)S(1)}) custom-call(s32[3]{0:T(128)S(1)} %pad_add_fusion.refs_0_, bf16[2,560,512]{2,1,0:T(8,128)(2,1)S(1)} %collective-permute-done.21.refs_1_, bf16[4,560,512]{2,1,0:T(8,128)(2,1)S(1)} %collective-permute-done.22.refs_2_, f32[4,512,512]{2,1,0:T(8,128)S(1)} %residual.5.refs_2_.refs_3_, ...), custom_call_target="tpu_custom_call" | custom-call | flops 1 | bytes 1 | tf_op jit(solution)/shard_map/residual/pallas_call | solution.py:34
  96.8 2.1 %collective-permute-done.23.refs_2_ = bf16[2,336,512]{2,1,0:T(8,128)(2,1)S(1)} collective-permute-done((bf16[2,336,512]{2,1,0:T(8,128)(2,1)S(1)}, bf16[2,336,512]{2,1,0:T(8,128)(2,1)S(1)}, u32[]{:S(2)}, u32[]{:S(2)}) %collective-permute-start.23) | collective-permute-done | bytes 688160 | tf_op jit(solution)/shard_map/ppermute | solution.py:55
  98.9 4.9 %residual.7 = bf16[4,1024,512]{2,1,0:T(8,128)(2,1)} custom-call(s32[3]{0:T(128)S(1)} %pad_add_fusion.refs_0_, bf16[2,336,512]{2,1,0:T(8,128)(2,1)S(1)} %join.5.refs_1_, bf16[2,336,512]{2,1,0:T(8,128)(2,1)S(1)} %collective-permute-done.23.refs_2_, bf16[4,336,512]{2,1,0:T(8,128)(2,1)S(1)} %get-tuple-element.57.refs_3_, ...), custom_call_target="tpu_custom_call" | custom-call | flops 1 | bytes 1 | tf_op jit(solution)/shard_map/residual/pallas_call | solution.py:34
  (61 shorter events, 23.1 us)
Async XLA Ops:
  0.0 23.5 %collective-permute-start = (bf16[8,112,512]{2,1,0:T(8,128)(2,1)}, bf16[8,112,512]{2,1,0:T(8,128)(2,1)S(1)}, u32[]{:S(2)}, u32[]{:S(2)}) collective-permute-start(bf16[8,112,512]{2,1,0:T(8,128)(2,1)} %bitcast.5), channel_id=1, source_target_pairs={{0,8},{2,10},{8,16},{10,18},{16,24},{18,26},{24,28},{26,30},{28,20... | collective-permute-start | bytes 2752520 | tf_op jit(solution)/shard_map/ppermute | solution.py:70
  3.0 22.3 %collective-permute-start.3 = (bf16[8,112,512]{2,1,0:T(8,128)(2,1)}, bf16[8,112,512]{2,1,0:T(8,128)(2,1)S(1)}, u32[]{:S(2)}, u32[]{:S(2)}) collective-permute-start(bf16[8,112,512]{2,1,0:T(8,128)(2,1)} %bitcast.6), channel_id=1, source_target_pairs={{0,4},{2,6},{8,0},{10,2},{16,8},{18,10},{24,16},{26,18},{28,24},{3... | collective-permute-start | bytes 2752520 | tf_op jit(solution)/shard_map/ppermute | solution.py:70
  4.9 24.5 %collective-permute-start.6 = (bf16[4,240,512]{2,1,0:T(8,128)(2,1)S(1)}, bf16[4,240,512]{2,1,0:T(8,128)(2,1)S(1)}, u32[]{:S(2)}, u32[]{:S(2)}) collective-permute-start(bf16[4,240,512]{2,1,0:T(8,128)(2,1)S(1)} %cut.2.refs_2_), channel_id=1, source_target_pairs={{0,1},{1,0},{2,3},{3,2},{4,5},{5,4},{6,7},{7,6},{8,9},{9,8},{10,11... | collective-permute-start | bytes 2949128 | tf_op jit(solution)/shard_map/ppermute | solution.py:55
  11.9 13.7 %collective-permute-start.7 = (bf16[4,128,512]{2,1,0:T(8,128)(2,1)S(1)}, bf16[4,128,512]{2,1,0:T(8,128)(2,1)S(1)}, u32[]{:S(2)}, u32[]{:S(2)}) collective-permute-start(bf16[4,128,512]{2,1,0:T(8,128)(2,1)S(1)} %get-tuple-element.34.refs_5_.refs_11_.refs_3_), channel_id=1, source_target_pairs={{0,2},{2,0},{4,6},{6,4},{8,10},{10,8},{12,14},{14,12},{16,18},{18,... | collective-permute-start | bytes 1572872 | tf_op jit(solution)/shard_map/ppermute | solution.py:55
  15.1 12.2 %collective-permute-start.8 = (bf16[4,128,512]{2,1,0:T(8,128)(2,1)S(1)}, bf16[4,128,512]{2,1,0:T(8,128)(2,1)S(1)}, u32[]{:S(2)}, u32[]{:S(2)}) collective-permute-start(bf16[4,128,512]{2,1,0:T(8,128)(2,1)S(1)} %get-tuple-element.35.refs_6_.refs_12_.refs_4_), channel_id=1, source_target_pairs={{0,2},{2,0},{4,6},{6,4},{8,10},{10,8},{12,14},{14,12},{16,18},{18,... | collective-permute-start | bytes 1572872 | tf_op jit(solution)/shard_map/ppermute | solution.py:55
  23.5 22.9 %collective-permute-start.1 = (bf16[8,112,512]{2,1,0:T(8,128)(2,1)S(1)}, bf16[8,112,512]{2,1,0:T(8,128)(2,1)S(1)}, u32[]{:S(2)}, u32[]{:S(2)}) collective-permute-start(bf16[8,112,512]{2,1,0:T(8,128)(2,1)S(1)} %collective-permute-done.refs_0_.refs_2_.refs_7_), channel_id=1, source_target_pairs={{0,8},{2,10},{8,16},{10,18},{16,24},{18,26},{24,28},{26,30},{28,20... | collective-permute-start | bytes 2752520 | tf_op jit(solution)/shard_map/ppermute | solution.py:70
  25.3 21.1 %collective-permute-start.4 = (bf16[8,112,512]{2,1,0:T(8,128)(2,1)S(1)}, bf16[8,112,512]{2,1,0:T(8,128)(2,1)S(1)}, u32[]{:S(2)}, u32[]{:S(2)}) collective-permute-start(bf16[8,112,512]{2,1,0:T(8,128)(2,1)S(1)} %collective-permute-done.3.refs_1_.refs_3_.refs_8_), channel_id=1, source_target_pairs={{0,4},{2,6},{8,0},{10,2},{16,8},{18,10},{24,16},{26,18},{28,24},{3... | collective-permute-start | bytes 2752520 | tf_op jit(solution)/shard_map/ppermute | solution.py:70
  25.5 20.9 %collective-permute-start.9 = (bf16[4,208,512]{2,1,0:T(8,128)(2,1)S(1)}, bf16[4,208,512]{2,1,0:T(8,128)(2,1)S(1)}, u32[]{:S(2)}, u32[]{:S(2)}) collective-permute-start(bf16[4,208,512]{2,1,0:T(8,128)(2,1)S(1)} %get-tuple-element.32.refs_4_), channel_id=1, source_target_pairs={{0,1},{1,0},{2,3},{3,2},{4,5},{5,4},{6,7},{7,6},{8,9},{9,8},{10,11... | collective-permute-start | bytes 2555912 | tf_op jit(solution)/shard_map/ppermute | solution.py:55
  35.8 10.6 %collective-permute-start.11 = (bf16[4,128,512]{2,1,0:T(8,128)(2,1)S(1)}, bf16[4,128,512]{2,1,0:T(8,128)(2,1)S(1)}, u32[]{:S(2)}, u32[]{:S(2)}) collective-permute-start(bf16[4,128,512]{2,1,0:T(8,128)(2,1)S(1)} %get-tuple-element.37.refs_8_.refs_14_.refs_6_), channel_id=1, source_target_pairs={{0,2},{2,0},{4,6},{6,4},{8,10},{10,8},{12,14},{14,12},{16,18},{18,... | collective-permute-start | bytes 1572872 | tf_op jit(solution)/shard_map/ppermute | solution.py:55
  35.9 10.6 %collective-permute-start.10 = (bf16[4,128,512]{2,1,0:T(8,128)(2,1)S(1)}, bf16[4,128,512]{2,1,0:T(8,128)(2,1)S(1)}, u32[]{:S(2)}, u32[]{:S(2)}) collective-permute-start(bf16[4,128,512]{2,1,0:T(8,128)(2,1)S(1)} %get-tuple-element.36.refs_7_.refs_13_.refs_5_), channel_id=1, source_target_pairs={{0,2},{2,0},{4,6},{6,4},{8,10},{10,8},{12,14},{14,12},{16,18},{18,... | collective-permute-start | bytes 1572872 | tf_op jit(solution)/shard_map/ppermute | solution.py:55
  47.0 13.0 %collective-permute-start.13 = (bf16[4,448,512]{2,1,0:T(8,128)(2,1)S(1)}, bf16[4,448,512]{2,1,0:T(8,128)(2,1)S(1)}, u32[]{:S(2)}, u32[]{:S(2)}) collective-permute-start(bf16[4,448,512]{2,1,0:T(8,128)(2,1)S(1)} %mix.2.refs_19_.refs_3_.refs_9_.refs_7_), channel_id=1, source_target_pairs={{0,2},{2,0},{4,6},{6,4},{8,10},{10,8},{12,14},{14,12},{16,18},{18,... | collective-permute-start | bytes 5505032 | tf_op jit(solution)/shard_map/ppermute | solution.py:55
  47.1 23.5 %collective-permute-start.2 = (bf16[8,112,512]{2,1,0:T(8,128)(2,1)S(1)}, bf16[8,112,512]{2,1,0:T(8,128)(2,1)S(1)}, u32[]{:S(2)}, u32[]{:S(2)}) collective-permute-start(bf16[8,112,512]{2,1,0:T(8,128)(2,1)S(1)} %collective-permute-done.1.refs_0_.refs_4_.refs_9_), channel_id=1, source_target_pairs={{0,8},{2,10},{8,16},{10,18},{16,24},{18,26},{24,28},{26,30},{28,20... | collective-permute-start | bytes 2752520 | tf_op jit(solution)/shard_map/ppermute | solution.py:70
  48.9 22.4 %collective-permute-start.5 = (bf16[8,112,512]{2,1,0:T(8,128)(2,1)S(1)}, bf16[8,112,512]{2,1,0:T(8,128)(2,1)S(1)}, u32[]{:S(2)}, u32[]{:S(2)}) collective-permute-start(bf16[8,112,512]{2,1,0:T(8,128)(2,1)S(1)} %collective-permute-done.4.refs_1_.refs_5_.refs_10_), channel_id=1, source_target_pairs={{0,4},{2,6},{8,0},{10,2},{16,8},{18,10},{24,16},{26,18},{28,24},{3... | collective-permute-start | bytes 2752520 | tf_op jit(solution)/shard_map/ppermute | solution.py:70
  49.2 9.1 %collective-permute-start.12 = (bf16[4,64,512]{2,1,0:T(8,128)(2,1)S(1)}, bf16[4,64,512]{2,1,0:T(8,128)(2,1)S(1)}, u32[]{:S(2)}, u32[]{:S(2)}) collective-permute-start(bf16[4,64,512]{2,1,0:T(8,128)(2,1)S(1)} %get-tuple-element.33.refs_5_), channel_id=1, source_target_pairs={{0,1},{1,0},{2,3},{3,2},{4,5},{5,4},{6,7},{7,6},{8,9},{9,8},{10,11... | collective-permute-start | bytes 786440 | tf_op jit(solution)/shard_map/ppermute | solution.py:55
  53.9 16.6 %collective-permute-start.15 = (bf16[1,560,512]{2,1,0:T(8,128)(2,1)S(1)}, bf16[1,560,512]{2,1,0:T(8,128)(2,1)S(1)}, u32[]{:S(2)}, u32[]{:S(2)}) collective-permute-start(bf16[1,560,512]{2,1,0:T(8,128)(2,1)S(1)} %get-tuple-element.44.refs_5_.refs_0_), channel_id=1, source_target_pairs={{0,1},{1,0},{2,3},{3,2},{4,5},{5,4},{6,7},{7,6},{8,9},{9,8},{10,11... | collective-permute-start | bytes 1720328 | tf_op jit(solution)/shard_map/ppermute | solution.py:55
  63.0 29.5 %collective-permute-start.22 = (bf16[4,560,512]{2,1,0:T(8,128)(2,1)S(1)}, bf16[4,560,512]{2,1,0:T(8,128)(2,1)S(1)}, u32[]{:S(2)}, u32[]{:S(2)}) collective-permute-start(bf16[4,560,512]{2,1,0:T(8,128)(2,1)S(1)} %get-tuple-element.54), channel_id=1, source_target_pairs={{0,2},{2,0},{4,6},{6,4},{8,10},{10,8},{12,14},{14,12},{16,18},{18,... | collective-permute-start | bytes 6881288 | tf_op jit(solution)/shard_map/ppermute | solution.py:55
  63.2 19.6 %collective-permute-start.18 = (bf16[1,560,512]{2,1,0:T(8,128)(2,1)S(1)}, bf16[1,560,512]{2,1,0:T(8,128)(2,1)S(1)}, u32[]{:S(2)}, u32[]{:S(2)}) collective-permute-start(bf16[1,560,512]{2,1,0:T(8,128)(2,1)S(1)} %get-tuple-element.47.refs_3_.refs_0_.refs_2_), channel_id=1, source_target_pairs={{0,1},{1,0},{2,3},{3,2},{4,5},{5,4},{6,7},{7,6},{8,9},{9,8},{10,11... | collective-permute-start | bytes 1720328 | tf_op jit(solution)/shard_map/ppermute | solution.py:55
  71.9 13.7 %collective-permute-start.16 = (bf16[4,112,512]{2,1,0:T(8,128)(2,1)S(1)}, bf16[4,112,512]{2,1,0:T(8,128)(2,1)S(1)}, u32[]{:S(2)}, u32[]{:S(2)}) collective-permute-start(bf16[4,112,512]{2,1,0:T(8,128)(2,1)S(1)} %get-tuple-element.48.refs_0_), channel_id=1, source_target_pairs={{0,8},{2,10},{8,16},{10,18},{16,24},{18,26},{24,28},{26,30},{28,20... | collective-permute-start | bytes 1376264 | tf_op jit(solution)/shard_map/ppermute | solution.py:70
  73.5 12.1 %collective-permute-start.17 = (bf16[4,112,512]{2,1,0:T(8,128)(2,1)S(1)}, bf16[4,112,512]{2,1,0:T(8,128)(2,1)S(1)}, u32[]{:S(2)}, u32[]{:S(2)}) collective-permute-start(bf16[4,112,512]{2,1,0:T(8,128)(2,1)S(1)} %get-tuple-element.49.refs_1_), channel_id=1, source_target_pairs={{0,4},{2,6},{8,0},{10,2},{16,8},{18,10},{24,16},{26,18},{28,24},{3... | collective-permute-start | bytes 1376264 | tf_op jit(solution)/shard_map/ppermute | solution.py:70
  76.6 15.9 %collective-permute-start.19 = (bf16[2,224,512]{2,1,0:T(8,128)(2,1)S(1)}, bf16[2,224,512]{2,1,0:T(8,128)(2,1)S(1)}, u32[]{:S(2)}, u32[]{:S(2)}) collective-permute-start(bf16[2,224,512]{2,1,0:T(8,128)(2,1)S(1)} %get-tuple-element.50.refs_2_.refs_0_.refs_4_), channel_id=1, source_target_pairs={{0,1},{1,0},{2,3},{3,2},{4,5},{5,4},{6,7},{7,6},{8,9},{9,8},{10,11... | collective-permute-start | bytes 1376264 | tf_op jit(solution)/shard_map/ppermute | solution.py:55
  85.6 6.9 %collective-permute-start.21 = (bf16[2,560,512]{2,1,0:T(8,128)(2,1)S(1)}, bf16[2,560,512]{2,1,0:T(8,128)(2,1)S(1)}, u32[]{:S(2)}, u32[]{:S(2)}) collective-permute-start(bf16[2,560,512]{2,1,0:T(8,128)(2,1)S(1)} %join.4.refs_1_), channel_id=1, source_target_pairs={{0,2},{2,0},{4,6},{6,4},{8,10},{10,8},{12,14},{14,12},{16,18},{18,... | collective-permute-start | bytes 3440648 | tf_op jit(solution)/shard_map/ppermute | solution.py:55
  87.6 9.0 %collective-permute-start.20 = (bf16[2,112,512]{2,1,0:T(8,128)(2,1)S(1)}, bf16[2,112,512]{2,1,0:T(8,128)(2,1)S(1)}, u32[]{:S(2)}, u32[]{:S(2)}) collective-permute-start(bf16[2,112,512]{2,1,0:T(8,128)(2,1)S(1)} %get-tuple-element.53.refs_0_.refs_1_.refs_5_), channel_id=1, source_target_pairs={{0,1},{1,0},{2,3},{3,2},{4,5},{5,4},{6,7},{7,6},{8,9},{9,8},{10,11... | collective-permute-start | bytes 688136 | tf_op jit(solution)/shard_map/ppermute | solution.py:55
  89.4 7.4 %collective-permute-start.24 = (bf16[4,336,512]{2,1,0:T(8,128)(2,1)S(1)}, bf16[4,336,512]{2,1,0:T(8,128)(2,1)S(1)}, u32[]{:S(2)}, u32[]{:S(2)}) collective-permute-start(bf16[4,336,512]{2,1,0:T(8,128)(2,1)S(1)} %get-tuple-element.58), channel_id=1, source_target_pairs={{0,2},{2,0},{4,6},{6,4},{8,10},{10,8},{12,14},{14,12},{16,18},{18,... | collective-permute-start | bytes 4128776 | tf_op jit(solution)/shard_map/ppermute | solution.py:55
  96.7 2.2 %collective-permute-start.23 = (bf16[2,336,512]{2,1,0:T(8,128)(2,1)S(1)}, bf16[2,336,512]{2,1,0:T(8,128)(2,1)S(1)}, u32[]{:S(2)}, u32[]{:S(2)}) collective-permute-start(bf16[2,336,512]{2,1,0:T(8,128)(2,1)S(1)} %join.5.refs_1_), channel_id=1, source_target_pairs={{0,2},{2,0},{4,6},{6,4},{8,10},{10,8},{12,14},{14,12},{16,18},{18,... | collective-permute-start | bytes 2064392 | tf_op jit(solution)/shard_map/ppermute | solution.py:55
  (5 other events, 17.4 us)

commit v5 on v4

--- a/solution.py
+++ b/solution.py
@@ -10,14 +10,29 @@
 OCC = 8
 BF16, F32 = jnp.bfloat16, jnp.float32
 VMEM_LIMIT = 20 * 2**20
-WORK = pl.CostEstimate(flops=1, bytes_accessed=1, transcendentals=0)
 WALLS = (1, 1, 1, 1, 16)
+MIXED = 3
 WHOLE = pl.BlockSpec(memory_space=pltpu.VMEM)
 ANYWHERE = pl.BlockSpec(memory_space=pl.ANY)
 
 
+def estimate(cost):
+    return pl.CostEstimate(flops=int(cost * 10**9) + 1, bytes_accessed=1, transcendentals=0)
+
+
 def kernel_call(
-    body, name, grid, in_specs, out_specs, out_shapes, scratch=(), tile=None, after=(), far=(), out=pltpu.VMEM
+    body,
+    name,
+    grid,
+    in_specs,
+    out_specs,
+    out_shapes,
+    scratch=(),
+    tile=None,
+    after=(),
+    far=(),
+    out=pltpu.VMEM,
+    cost=0,
 ):
     scalars = 0 if tile is None else 1
     extra = len(after)
@@ -44,7 +59,7 @@
             compiler_params=pltpu.CompilerParams(
                 dimension_semantics=("arbitrary",) * len(grid), vmem_limit_bytes=VMEM_LIMIT
             ),
-            cost_estimate=WORK,
+            cost_estimate=estimate(cost),
             name=name,
         )(*([] if tile is None else [tile]), *held)
 
@@ -142,7 +157,7 @@
             first, rows = first + here, rows - here
 
 
-def mix(far, arrived, start, after=()):
+def mix(far, arrived, start, after=(), cost=0):
     count, _, width = far[0].shape
     shape = (count, sum(r.shape[1] for r in arrived), width)
     (out,) = kernel_call(
@@ -153,6 +168,7 @@
         [WHOLE],
         [(shape, BF16)],
         after=after,
+        cost=cost,
     )(*far, *arrived)
     return out
 
@@ -243,22 +259,8 @@
         out_specs=ANYWHERE,
         out_shape=pltpu.VMEM((8, 128), F32),
         compiler_params=pltpu.CompilerParams(vmem_limit_bytes=2**20),
-        cost_estimate=pl.CostEstimate(flops=int(cost * 10**9), bytes_accessed=1, transcendentals=0),
+        cost_estimate=estimate(cost),
         name="wall",
-    )(*held)
-
-
-def gate(value, after):
-    held = [pltpu.with_memory_space_constraint(a, pltpu.VMEM) for a in (value, *after)]
-    return pl.pallas_call(
-        nothing,
-        in_specs=[ANYWHERE] * len(held),
-        out_specs=ANYWHERE,
-        out_shape=pltpu.VMEM(value.shape, value.dtype),
-        input_output_aliases={0: 0},
-        compiler_params=pltpu.CompilerParams(vmem_limit_bytes=2**20),
-        cost_estimate=WORK,
-        name="gate",
     )(*held)
 
 
@@ -427,7 +429,7 @@
         where, vectors[:5], vectors[:5], near, near_theirs, joined=2, after=[far_0]
     )
     n_a_sent = to_tile(n_a)
-    far_1 = mix(far_turned, arrived[2:], far_0.shape[1], after=[n_a])
+    far_1 = mix(far_turned, arrived[2:], far_0.shape[1], after=[n_a], cost=MIXED)
     far_1_theirs = to_core(far_1)
     far, far_theirs = [far_0, far_1], [far_0_theirs, far_1_theirs]
     f_a, cross_a = partial(where, [same_a], [cross_a], [far], [far_theirs], joined=1)
@@ -459,7 +461,9 @@
     )
     p_c_sent = to_tile(p_c)
     handed_d = to_core(cross_d)
-    wall_5 = wall(p_c, p_b_sent, cost=WALLS[4])
+    m_b = join(*[[((p_b, h), (p_b_sent, 1 - h))] for h in range(2)], after=[p_c])
+    m_b_theirs = to_core(m_b)
+    wall_5 = wall(m_b, cost=WALLS[4])
     begun = residual(
         where,
         [m_a_theirs],
@@ -468,12 +472,10 @@
         [begun_own, begun_off],
         after=[wall_5],
     )
-    m_d = join(
-        *[[((p_b, h), (p_b_sent, 1 - h)), ((p_c, h), (p_c_sent, 1 - h))] for h in range(2)],
-        after=begun,
-    )
-    m_d_theirs = to_core(m_d)
-    (out,) = residual(where, [m_d, m_d_theirs], [same_d, handed_d], [0, 1], begun, last=True)
+    m_c = join(*[[((p_c, h), (p_c_sent, 1 - h))] for h in range(2)], after=begun)
+    m_c_theirs = to_core(m_c)
+    middles = [m_b, m_c, m_b_theirs, m_c_theirs]
+    (out,) = residual(where, middles, [same_d, handed_d], [0, 1], begun, last=True)
     return out
 
 

time: 104 us -> 103 us (level)
  starting transfers between devices: 22.2 us -> 20.5 us
    ppermute x17 -> x18, waiting for transfers between devices: 26.6 us -> 23.7 us  [swap(): lax.ppermute(x, axis, [(i, i ^ 1 << bit) for i in range(lax.axis_size(axi...]
    ppermute x8, waiting for transfers between devices: 8.58 us -> 11.5 us  [along_ring(): return lax.ppermute(x, 'pair', pairs)]
    ppermute x17 -> x18, starting transfers between devices: 13 us -> 11.3 us  [swap(): lax.ppermute(x, axis, [(i, i ^ 1 << bit) for i in range(lax.axis_size(axi...]
    pallas_call x21 -> x22, Pallas kernels: 46.1 us -> 46.1 us  [call(): pl.pallas_call(kernel, grid_spec=pltpu.PrefetchScalarGridSpec(num_scalar_...]
  transfers between devices with their start and end apart: 25 -> 26, of which waited for: 10 -> 13; matrix products, arithmetic and copies ran while one was open for 0% -> 0% of each run, Pallas kernels for 39% -> 40%
where the time goes in v5:
time: 103 us; the launch traced here: 102 us
  Pallas kernels  46.1 us (45%)
  waiting for transfers between devices  35.1 us (34%)
  starting transfers between devices  20.5 us (20%)
    pallas_call x22, Pallas kernels, call(): pl.pallas_call(kernel, grid_spec=pltpu.PrefetchScalarGridSpec(num_scalar_...  46.1 us
    ppermute x18, waiting for transfers between devices, swap(): lax.ppermute(x, axis, [(i, i ^ 1 << bit) for i in range(lax.axis_size(axi...  23.7 us
    ppermute x8, waiting for transfers between devices, along_ring(): return lax.ppermute(x, 'pair', pairs)  11.5 us
    ppermute x18, starting transfers between devices, swap(): lax.ppermute(x, axis, [(i, i ^ 1 << bit) for i in range(lax.axis_size(axi...  11.3 us
    ppermute x8, starting transfers between devices, along_ring(): return lax.ppermute(x, 'pair', pairs)  9.16 us
  transfers between devices with their start and end apart: 26, of which 13 were waited for; matrix products, arithmetic and copies ran while one was open for 0% of the time, Pallas kernels for 40%

profile of v5, /device:TPU:0, one launch (start us, length us, event | category | flops | bytes accessed | tf_op | source)
XLA Modules:
  0.0 102.2 jit_solution(14486463288610016336)
XLA Ops:
  0.0 3.0 %collective-permute-start = (bf16[8,112,512]{2,1,0:T(8,128)(2,1)}, bf16[8,112,512]{2,1,0:T(8,128)(2,1)S(1)}, u32[]{:S(2)}, u32[]{:S(2)}) collective-permute-start(bf16[8,112,512]{2,1,0:T(8,128)(2,1)} %bitcast.5), channel_id=1, source_target_pairs={{0,8},{2,10},{8,16},{10,18},{16,24},{18,26},{24,28},{26,30},{28,20... | collective-permute-start | bytes 2752520 | tf_op jit(solution)/shard_map/ppermute | solution.py:85
  4.9 2.0 %collective-permute-start.6 = (bf16[4,240,512]{2,1,0:T(8,128)(2,1)S(1)}, bf16[4,240,512]{2,1,0:T(8,128)(2,1)S(1)}, u32[]{:S(2)}, u32[]{:S(2)}) collective-permute-start(bf16[4,240,512]{2,1,0:T(8,128)(2,1)S(1)} %cut.2.refs_2_), channel_id=1, source_target_pairs={{0,1},{1,0},{2,3},{3,2},{4,5},{5,4},{6,7},{7,6},{8,9},{9,8},{10,11... | collective-permute-start | bytes 2949128 | tf_op jit(solution)/shard_map/ppermute | solution.py:70
  6.9 1.8 %cut.3 = (bf16[4,208,512]{2,1,0:T(8,128)(2,1)S(1)}, bf16[4,64,512]{2,1,0:T(8,128)(2,1)S(1)}) custom-call(s32[3]{0:T(128)S(1)} %pad_add_fusion.refs_0_, bf16[4,1024,512]{2,1,0:T(8,128)(2,1)} %refs_1_.13, bf16[4,240,512]{2,1,0:T(8,128)(2,1)S(1)} %cut.2.refs_2_), custom_call_target="tpu_custom_call" | custom-call | flops 1 | bytes 1 | tf_op jit(solution)/shard_map/cut/pallas_call | solution.py:49
  8.7 3.2 %turn.4 = (bf16[4,128,512]{2,1,0:T(8,128)(2,1)S(1)}, bf16[4,128,512]{2,1,0:T(8,128)(2,1)S(1)}) custom-call(s32[3]{0:T(128)S(1)} %pad_add_fusion.refs_0_, bf16[4,1024,512]{2,1,0:T(8,128)(2,1)} %refs_1_.13, bf16[4,1024,512]{2,1,0:T(8,128)(2,1)} %refs_1_.13, bf16[4,1024,512]{2,1,0:T(8,128)(2,1)} %refs_1_.13, ...), custom_call_target="tpu_custom_call" | custom-call | flops 1 | bytes 1 | tf_op jit(solution)/shard_map/turn/pallas_call | solution.py:49
  11.9 3.2 %turn.5 = (bf16[4,128,512]{2,1,0:T(8,128)(2,1)S(1)}, bf16[4,128,512]{2,1,0:T(8,128)(2,1)S(1)}) custom-call(s32[3]{0:T(128)S(1)} %pad_add_fusion.refs_0_, bf16[4,1024,512]{2,1,0:T(8,128)(2,1)} %refs_1_.13, bf16[4,1024,512]{2,1,0:T(8,128)(2,1)} %refs_1_.13, bf16[4,1024,512]{2,1,0:T(8,128)(2,1)} %refs_1_.13, ...), custom_call_target="tpu_custom_call" | custom-call | flops 1 | bytes 1 | tf_op jit(solution)/shard_map/turn/pallas_call | solution.py:49
  15.7 7.8 %collective-permute-done.refs_0_.refs_2_.refs_7_ = bf16[8,112,512]{2,1,0:T(8,128)(2,1)S(1)} collective-permute-done((bf16[8,112,512]{2,1,0:T(8,128)(2,1)}, bf16[8,112,512]{2,1,0:T(8,128)(2,1)S(1)}, u32[]{:S(2)}, u32[]{:S(2)}) %collective-permute-start) | collective-permute-done | bytes 917536 | tf_op jit(solution)/shard_map/ppermute | solution.py:85
  23.5 1.8 %collective-permute-start.1 = (bf16[8,112,512]{2,1,0:T(8,128)(2,1)S(1)}, bf16[8,112,512]{2,1,0:T(8,128)(2,1)S(1)}, u32[]{:S(2)}, u32[]{:S(2)}) collective-permute-start(bf16[8,112,512]{2,1,0:T(8,128)(2,1)S(1)} %collective-permute-done.refs_0_.refs_2_.refs_7_), channel_id=1, source_target_pairs={{0,8},{2,10},{8,16},{10,18},{16,24},{18,26},{24,28},{26,30},{28,20... | collective-permute-start | bytes 2752520 | tf_op jit(solution)/shard_map/ppermute | solution.py:85
  25.5 1.8 %collective-permute-start.9 = (bf16[4,208,512]{2,1,0:T(8,128)(2,1)S(1)}, bf16[4,208,512]{2,1,0:T(8,128)(2,1)S(1)}, u32[]{:S(2)}, u32[]{:S(2)}) collective-permute-start(bf16[4,208,512]{2,1,0:T(8,128)(2,1)S(1)} %get-tuple-element.32.refs_4_), channel_id=1, source_target_pairs={{0,1},{1,0},{2,3},{3,2},{4,5},{5,4},{6,7},{7,6},{8,9},{9,8},{10,11... | collective-permute-start | bytes 2555912 | tf_op jit(solution)/shard_map/ppermute | solution.py:70
  27.3 2.1 %collective-permute-done.6.refs_2_.refs_4_ = bf16[4,240,512]{2,1,0:T(8,128)(2,1)S(1)} collective-permute-done((bf16[4,240,512]{2,1,0:T(8,128)(2,1)S(1)}, bf16[4,240,512]{2,1,0:T(8,128)(2,1)S(1)}, u32[]{:S(2)}, u32[]{:S(2)}) %collective-permute-start.6) | collective-permute-done | bytes 983072 | tf_op jit(solution)/shard_map/ppermute | solution.py:70
  29.4 3.2 %turn.7 = (bf16[4,128,512]{2,1,0:T(8,128)(2,1)S(1)}, bf16[4,128,512]{2,1,0:T(8,128)(2,1)S(1)}) custom-call(s32[3]{0:T(128)S(1)} %pad_add_fusion.refs_0_, bf16[4,1024,512]{2,1,0:T(8,128)(2,1)} %refs_1_.13, bf16[4,1024,512]{2,1,0:T(8,128)(2,1)} %refs_1_.13, bf16[4,1024,512]{2,1,0:T(8,128)(2,1)} %refs_1_.13, f32[8,128]{1,0:T(8,128)S(1)} %wall.5.refs_4_), custom_call_target="tpu_custom_call" | custom-call | flops 1 | bytes 1 | tf_op jit(solution)/shard_map/turn/pallas_call | solution.py:49
  32.6 3.2 %turn.6 = (bf16[4,128,512]{2,1,0:T(8,128)(2,1)S(1)}, bf16[4,128,512]{2,1,0:T(8,128)(2,1)S(1)}) custom-call(s32[3]{0:T(128)S(1)} %pad_add_fusion.refs_0_, bf16[4,1024,512]{2,1,0:T(8,128)(2,1)} %refs_1_.13, bf16[4,1024,512]{2,1,0:T(8,128)(2,1)} %refs_1_.13, bf16[4,1024,512]{2,1,0:T(8,128)(2,1)} %refs_1_.13, f32[8,128]{1,0:T(8,128)S(1)} %wall.5.refs_4_), custom_call_target="tpu_custom_call" | custom-call | flops 1 | bytes 1 | tf_op jit(solution)/shard_map/turn/pallas_call | solution.py:49
  36.4 3.7 %diagonal.1 = (f32[4,512,512]{2,1,0:T(8,128)S(1)}, f32[4,512,512]{2,1,0:T(8,128)S(1)}) custom-call(s32[3]{0:T(128)S(1)} %pad_add_fusion.refs_0_, bf16[4,1024,512]{2,1,0:T(8,128)(2,1)} %refs_1_.13, f32[2,1,512]{2,1,0:T(1,128)S(1)} %bitcast.9, f32[8]{0:T(128)S(1)} %copy-done.2, f32[8]{0:T(128)S(1)} %copy-done.3, ...), custom_call_target="tpu_custom_call" | custom-call | flops 1 | bytes 1 | tf_op jit(solution)/shard_map/diagonal/pallas_call | solution.py:49
  40.1 6.4 %collective-permute-done.9.refs_2_.refs_5_ = bf16[4,208,512]{2,1,0:T(8,128)(2,1)S(1)} collective-permute-done((bf16[4,208,512]{2,1,0:T(8,128)(2,1)S(1)}, bf16[4,208,512]{2,1,0:T(8,128)(2,1)S(1)}, u32[]{:S(2)}, u32[]{:S(2)}) %collective-permute-start.9) | collective-permute-done | bytes 852000 | tf_op jit(solution)/shard_map/ppermute | solution.py:70
  50.9 3.1 %partial.4 = (bf16[1,560,512]{2,1,0:T(8,128)(2,1)S(1)}, bf16[4,560,512]{2,1,0:T(8,128)(2,1)S(1)}, bf16[4,560,512]{2,1,0:T(8,128)(2,1)S(1)}) custom-call(s32[3]{0:T(128)S(1)} %pad_add_fusion.refs_0_, bf16[8,112,512]{2,1,0:T(8,128)(2,1)S(1)} %bitcast.7, bf16[8,112,512]{2,1,0:T(8,128)(2,1)S(1)} %collective-permute-done.refs_0_.refs_2_.refs_7_, ...), custom_call_target="tpu_custom_call" | custom-call | flops 1 | bytes 1 | tf_op jit(solution)/shard_map/partial/pallas_call | solution.py:49
  57.5 3.1 %partial.5 = (bf16[1,560,512]{2,1,0:T(8,128)(2,1)S(1)}, bf16[4,560,512]{2,1,0:T(8,128)(2,1)S(1)}) custom-call(s32[3]{0:T(128)S(1)} %pad_add_fusion.refs_0_, bf16[4,560,512]{2,1,0:T(8,128)(2,1)S(1)} %get-tuple-element.45.refs_1_.refs_2_, bf16[4,560,512]{2,1,0:T(8,128)(2,1)S(1)} %get-tuple-element.46.refs_2_, ...), custom_call_target="tpu_custom_call" | custom-call | flops 1 | bytes 1 | tf_op jit(solution)/shard_map/partial/pallas_call | solution.py:49
  60.8 2.2 %collective-permute-start.19 = (bf16[1,560,512]{2,1,0:T(8,128)(2,1)S(1)}, bf16[1,560,512]{2,1,0:T(8,128)(2,1)S(1)}, u32[]{:S(2)}, u32[]{:S(2)}) collective-permute-start(bf16[1,560,512]{2,1,0:T(8,128)(2,1)S(1)} %get-tuple-element.47.refs_3_.refs_0_.refs_2_), channel_id=1, source_target_pairs={{0,1},{1,0},{2,3},{3,2},{4,5},{5,4},{6,7},{7,6},{8,9},{9,8},{10,11... | collective-permute-start | bytes 1720328 | tf_op jit(solution)/shard_map/ppermute | solution.py:70
  62.9 7.0 %collective-permute-done.15.refs_4_.refs_1_.refs_3_ = bf16[1,560,512]{2,1,0:T(8,128)(2,1)S(1)} collective-permute-done((bf16[1,560,512]{2,1,0:T(8,128)(2,1)S(1)}, bf16[1,560,512]{2,1,0:T(8,128)(2,1)S(1)}, u32[]{:S(2)}, u32[]{:S(2)}) %collective-permute-start.15) | collective-permute-done | bytes 573472 | tf_op jit(solution)/shard_map/ppermute | solution.py:70
  75.2 2.6 %partial.6 = (bf16[2,224,512]{2,1,0:T(8,128)(2,1)S(1)}, bf16[4,224,512]{2,1,0:T(8,128)(2,1)S(1)}, bf16[4,224,512]{2,1,0:T(8,128)(2,1)S(1)}) custom-call(s32[3]{0:T(128)S(1)} %pad_add_fusion.refs_0_, bf16[8,112,512]{2,1,0:T(8,128)(2,1)S(1)} %collective-permute-done.2.refs_1_.refs_3_, bf16[8,112,512]{2,1,0:T(8,128)(2,1)S(1)} %collective-permute-done.5.refs_2_.refs_4_, ...), custom_call_target="tpu_custom_call" | custom-call | flops 1 | bytes 1 | tf_op jit(solution)/shard_map/partial/pallas_call | solution.py:49
  78.6 2.4 %residual.4.refs_4_ = f32[4,512,512]{2,1,0:T(8,128)S(1)} custom-call(s32[3]{0:T(128)S(1)} %pad_add_fusion.refs_0_, bf16[1,560,512]{2,1,0:T(8,128)(2,1)S(1)} %join.4.refs_1_, bf16[4,560,512]{2,1,0:T(8,128)(2,1)S(1)} %get-tuple-element.45.refs_1_.refs_2_, f32[4,512,512]{2,1,0:T(8,128)S(1)} %get-tuple-element.43.refs_6_.refs_3_), custom_call_target="tpu_custom_call" | custom-call | flops 1 | bytes 1 | tf_op jit(solution)/shard_map/residual/pallas_call | solution.py:49
  82.5 2.4 %residual.5.refs_2_.refs_3_ = f32[4,512,512]{2,1,0:T(8,128)S(1)} custom-call(s32[3]{0:T(128)S(1)} %pad_add_fusion.refs_0_, bf16[2,560,512]{2,1,0:T(8,128)(2,1)S(1)} %join.5.refs_1_, bf16[4,560,512]{2,1,0:T(8,128)(2,1)S(1)} %get-tuple-element.45.refs_1_.refs_2_, f32[4,512,512]{2,1,0:T(8,128)S(1)} %get-tuple-element.42.refs_5_.refs_3_), custom_call_target="tpu_custom_call" | custom-call | flops 1 | bytes 1 | tf_op jit(solution)/shard_map/residual/pallas_call | solution.py:49
  86.0 1.9 %partial.7 = (bf16[2,112,512]{2,1,0:T(8,128)(2,1)S(1)}, bf16[4,336,512]{2,1,0:T(8,128)(2,1)S(1)}, bf16[4,336,512]{2,1,0:T(8,128)(2,1)S(1)}) custom-call(s32[3]{0:T(128)S(1)} %pad_add_fusion.refs_0_, bf16[4,112,512]{2,1,0:T(8,128)(2,1)S(1)} %collective-permute-done.17.refs_0_.refs_1_, bf16[4,112,512]{2,1,0:T(8,128)(2,1)S(1)} %collective-permute-done.18.refs_1_.refs_2_, ...), custom_call_target="tpu_custom_call" | custom-call | flops 1 | bytes 1 | tf_op jit(solution)/shard_map/partial/pallas_call | solution.py:49
  88.4 2.7 %collective-permute-done.16.refs_1_.refs_3_ = bf16[2,224,512]{2,1,0:T(8,128)(2,1)S(1)} collective-permute-done((bf16[2,224,512]{2,1,0:T(8,128)(2,1)S(1)}, bf16[2,224,512]{2,1,0:T(8,128)(2,1)S(1)}, u32[]{:S(2)}, u32[]{:S(2)}) %collective-permute-start.16) | collective-permute-done | bytes 458784 | tf_op jit(solution)/shard_map/ppermute | solution.py:70
  91.3 4.0 %residual.6 = (f32[4,512,512]{2,1,0:T(8,128)S(1)}, f32[4,512,512]{2,1,0:T(8,128)S(1)}) custom-call(s32[3]{0:T(128)S(1)} %pad_add_fusion.refs_0_, bf16[2,560,512]{2,1,0:T(8,128)(2,1)S(1)} %collective-permute-done.21.refs_1_, bf16[4,560,512]{2,1,0:T(8,128)(2,1)S(1)} %collective-permute-done.22.refs_2_, f32[4,512,512]{2,1,0:T(8,128)S(1)} %residual.5.refs_2_.refs_3_, ...), custom_call_target="tpu_custom_call" | custom-call | flops 1 | bytes 1 | tf_op jit(solution)/shard_map/residual/pallas_call | solution.py:49
  97.1 4.9 %residual.7 = bf16[4,1024,512]{2,1,0:T(8,128)(2,1)} custom-call(s32[3]{0:T(128)S(1)} %pad_add_fusion.refs_0_, bf16[2,224,512]{2,1,0:T(8,128)(2,1)S(1)} %join.6.refs_0_.refs_1_, bf16[2,112,512]{2,1,0:T(8,128)(2,1)S(1)} %join.7.refs_2_, bf16[2,224,512]{2,1,0:T(8,128)(2,1)S(1)} %collective-permute-done.23.refs_3_, ...), custom_call_target="tpu_custom_call" | custom-call | flops 1 | bytes 1 | tf_op jit(solution)/shard_map/residual/pallas_call | solution.py:49
  (64 shorter events, 22.6 us)
Async XLA Ops:
  0.0 23.5 %collective-permute-start = (bf16[8,112,512]{2,1,0:T(8,128)(2,1)}, bf16[8,112,512]{2,1,0:T(8,128)(2,1)S(1)}, u32[]{:S(2)}, u32[]{:S(2)}) collective-permute-start(bf16[8,112,512]{2,1,0:T(8,128)(2,1)} %bitcast.5), channel_id=1, source_target_pairs={{0,8},{2,10},{8,16},{10,18},{16,24},{18,26},{24,28},{26,30},{28,20... | collective-permute-start | bytes 2752520 | tf_op jit(solution)/shard_map/ppermute | solution.py:85
  3.0 22.3 %collective-permute-start.3 = (bf16[8,112,512]{2,1,0:T(8,128)(2,1)}, bf16[8,112,512]{2,1,0:T(8,128)(2,1)S(1)}, u32[]{:S(2)}, u32[]{:S(2)}) collective-permute-start(bf16[8,112,512]{2,1,0:T(8,128)(2,1)} %bitcast.6), channel_id=1, source_target_pairs={{0,4},{2,6},{8,0},{10,2},{16,8},{18,10},{24,16},{26,18},{28,24},{3... | collective-permute-start | bytes 2752520 | tf_op jit(solution)/shard_map/ppermute | solution.py:85
  4.9 24.5 %collective-permute-start.6 = (bf16[4,240,512]{2,1,0:T(8,128)(2,1)S(1)}, bf16[4,240,512]{2,1,0:T(8,128)(2,1)S(1)}, u32[]{:S(2)}, u32[]{:S(2)}) collective-permute-start(bf16[4,240,512]{2,1,0:T(8,128)(2,1)S(1)} %cut.2.refs_2_), channel_id=1, source_target_pairs={{0,1},{1,0},{2,3},{3,2},{4,5},{5,4},{6,7},{7,6},{8,9},{9,8},{10,11... | collective-permute-start | bytes 2949128 | tf_op jit(solution)/shard_map/ppermute | solution.py:70
  11.9 13.7 %collective-permute-start.7 = (bf16[4,128,512]{2,1,0:T(8,128)(2,1)S(1)}, bf16[4,128,512]{2,1,0:T(8,128)(2,1)S(1)}, u32[]{:S(2)}, u32[]{:S(2)}) collective-permute-start(bf16[4,128,512]{2,1,0:T(8,128)(2,1)S(1)} %get-tuple-element.34.refs_5_.refs_11_.refs_3_), channel_id=1, source_target_pairs={{0,2},{2,0},{4,6},{6,4},{8,10},{10,8},{12,14},{14,12},{16,18},{18,... | collective-permute-start | bytes 1572872 | tf_op jit(solution)/shard_map/ppermute | solution.py:70
  15.1 12.2 %collective-permute-start.8 = (bf16[4,128,512]{2,1,0:T(8,128)(2,1)S(1)}, bf16[4,128,512]{2,1,0:T(8,128)(2,1)S(1)}, u32[]{:S(2)}, u32[]{:S(2)}) collective-permute-start(bf16[4,128,512]{2,1,0:T(8,128)(2,1)S(1)} %get-tuple-element.35.refs_6_.refs_12_.refs_4_), channel_id=1, source_target_pairs={{0,2},{2,0},{4,6},{6,4},{8,10},{10,8},{12,14},{14,12},{16,18},{18,... | collective-permute-start | bytes 1572872 | tf_op jit(solution)/shard_map/ppermute | solution.py:70
  23.5 22.9 %collective-permute-start.1 = (bf16[8,112,512]{2,1,0:T(8,128)(2,1)S(1)}, bf16[8,112,512]{2,1,0:T(8,128)(2,1)S(1)}, u32[]{:S(2)}, u32[]{:S(2)}) collective-permute-start(bf16[8,112,512]{2,1,0:T(8,128)(2,1)S(1)} %collective-permute-done.refs_0_.refs_2_.refs_7_), channel_id=1, source_target_pairs={{0,8},{2,10},{8,16},{10,18},{16,24},{18,26},{24,28},{26,30},{28,20... | collective-permute-start | bytes 2752520 | tf_op jit(solution)/shard_map/ppermute | solution.py:85
  25.3 21.1 %collective-permute-start.4 = (bf16[8,112,512]{2,1,0:T(8,128)(2,1)S(1)}, bf16[8,112,512]{2,1,0:T(8,128)(2,1)S(1)}, u32[]{:S(2)}, u32[]{:S(2)}) collective-permute-start(bf16[8,112,512]{2,1,0:T(8,128)(2,1)S(1)} %collective-permute-done.3.refs_1_.refs_3_.refs_8_), channel_id=1, source_target_pairs={{0,4},{2,6},{8,0},{10,2},{16,8},{18,10},{24,16},{26,18},{28,24},{3... | collective-permute-start | bytes 2752520 | tf_op jit(solution)/shard_map/ppermute | solution.py:85
  25.5 20.9 %collective-permute-start.9 = (bf16[4,208,512]{2,1,0:T(8,128)(2,1)S(1)}, bf16[4,208,512]{2,1,0:T(8,128)(2,1)S(1)}, u32[]{:S(2)}, u32[]{:S(2)}) collective-permute-start(bf16[4,208,512]{2,1,0:T(8,128)(2,1)S(1)} %get-tuple-element.32.refs_4_), channel_id=1, source_target_pairs={{0,1},{1,0},{2,3},{3,2},{4,5},{5,4},{6,7},{7,6},{8,9},{9,8},{10,11... | collective-permute-start | bytes 2555912 | tf_op jit(solution)/shard_map/ppermute | solution.py:70
  35.8 10.6 %collective-permute-start.11 = (bf16[4,128,512]{2,1,0:T(8,128)(2,1)S(1)}, bf16[4,128,512]{2,1,0:T(8,128)(2,1)S(1)}, u32[]{:S(2)}, u32[]{:S(2)}) collective-permute-start(bf16[4,128,512]{2,1,0:T(8,128)(2,1)S(1)} %get-tuple-element.37.refs_8_.refs_14_.refs_6_), channel_id=1, source_target_pairs={{0,2},{2,0},{4,6},{6,4},{8,10},{10,8},{12,14},{14,12},{16,18},{18,... | collective-permute-start | bytes 1572872 | tf_op jit(solution)/shard_map/ppermute | solution.py:70
  35.9 10.6 %collective-permute-start.10 = (bf16[4,128,512]{2,1,0:T(8,128)(2,1)S(1)}, bf16[4,128,512]{2,1,0:T(8,128)(2,1)S(1)}, u32[]{:S(2)}, u32[]{:S(2)}) collective-permute-start(bf16[4,128,512]{2,1,0:T(8,128)(2,1)S(1)} %get-tuple-element.36.refs_7_.refs_13_.refs_5_), channel_id=1, source_target_pairs={{0,2},{2,0},{4,6},{6,4},{8,10},{10,8},{12,14},{14,12},{16,18},{18,... | collective-permute-start | bytes 1572872 | tf_op jit(solution)/shard_map/ppermute | solution.py:70
  47.0 10.5 %collective-permute-start.13 = (bf16[4,448,512]{2,1,0:T(8,128)(2,1)S(1)}, bf16[4,448,512]{2,1,0:T(8,128)(2,1)S(1)}, u32[]{:S(2)}, u32[]{:S(2)}) collective-permute-start(bf16[4,448,512]{2,1,0:T(8,128)(2,1)S(1)} %mix.2.refs_19_.refs_3_.refs_9_.refs_7_), channel_id=1, source_target_pairs={{0,2},{2,0},{4,6},{6,4},{8,10},{10,8},{12,14},{14,12},{16,18},{18,... | collective-permute-start | bytes 5505032 | tf_op jit(solution)/shard_map/ppermute | solution.py:70
  47.1 8.7 %collective-permute-start.12 = (bf16[4,64,512]{2,1,0:T(8,128)(2,1)S(1)}, bf16[4,64,512]{2,1,0:T(8,128)(2,1)S(1)}, u32[]{:S(2)}, u32[]{:S(2)}) collective-permute-start(bf16[4,64,512]{2,1,0:T(8,128)(2,1)S(1)} %get-tuple-element.33.refs_5_), channel_id=1, source_target_pairs={{0,1},{1,0},{2,3},{3,2},{4,5},{5,4},{6,7},{7,6},{8,9},{9,8},{10,11... | collective-permute-start | bytes 786440 | tf_op jit(solution)/shard_map/ppermute | solution.py:70
  48.8 22.4 %collective-permute-start.2 = (bf16[8,112,512]{2,1,0:T(8,128)(2,1)S(1)}, bf16[8,112,512]{2,1,0:T(8,128)(2,1)S(1)}, u32[]{:S(2)}, u32[]{:S(2)}) collective-permute-start(bf16[8,112,512]{2,1,0:T(8,128)(2,1)S(1)} %collective-permute-done.1.refs_0_.refs_4_.refs_9_), channel_id=1, source_target_pairs={{0,8},{2,10},{8,16},{10,18},{16,24},{18,26},{24,28},{26,30},{28,20... | collective-permute-start | bytes 2752520 | tf_op jit(solution)/shard_map/ppermute | solution.py:85
  50.4 22.1 %collective-permute-start.5 = (bf16[8,112,512]{2,1,0:T(8,128)(2,1)S(1)}, bf16[8,112,512]{2,1,0:T(8,128)(2,1)S(1)}, u32[]{:S(2)}, u32[]{:S(2)}) collective-permute-start(bf16[8,112,512]{2,1,0:T(8,128)(2,1)S(1)} %collective-permute-done.4.refs_1_.refs_5_.refs_10_), channel_id=1, source_target_pairs={{0,4},{2,6},{8,0},{10,2},{16,8},{18,10},{24,16},{26,18},{28,24},{3... | collective-permute-start | bytes 2752520 | tf_op jit(solution)/shard_map/ppermute | solution.py:85
  53.9 16.0 %collective-permute-start.15 = (bf16[1,560,512]{2,1,0:T(8,128)(2,1)S(1)}, bf16[1,560,512]{2,1,0:T(8,128)(2,1)S(1)}, u32[]{:S(2)}, u32[]{:S(2)}) collective-permute-start(bf16[1,560,512]{2,1,0:T(8,128)(2,1)S(1)} %get-tuple-element.44.refs_5_.refs_0_), channel_id=1, source_target_pairs={{0,1},{1,0},{2,3},{3,2},{4,5},{5,4},{6,7},{7,6},{8,9},{9,8},{10,11... | collective-permute-start | bytes 1720328 | tf_op jit(solution)/shard_map/ppermute | solution.py:70
  60.6 30.7 %collective-permute-start.22 = (bf16[4,560,512]{2,1,0:T(8,128)(2,1)S(1)}, bf16[4,560,512]{2,1,0:T(8,128)(2,1)S(1)}, u32[]{:S(2)}, u32[]{:S(2)}) collective-permute-start(bf16[4,560,512]{2,1,0:T(8,128)(2,1)S(1)} %get-tuple-element.54), channel_id=1, source_target_pairs={{0,2},{2,0},{4,6},{6,4},{8,10},{10,8},{12,14},{14,12},{16,18},{18,... | collective-permute-start | bytes 6881288 | tf_op jit(solution)/shard_map/ppermute | solution.py:70
  60.8 21.4 %collective-permute-start.19 = (bf16[1,560,512]{2,1,0:T(8,128)(2,1)S(1)}, bf16[1,560,512]{2,1,0:T(8,128)(2,1)S(1)}, u32[]{:S(2)}, u32[]{:S(2)}) collective-permute-start(bf16[1,560,512]{2,1,0:T(8,128)(2,1)S(1)} %get-tuple-element.47.refs_3_.refs_0_.refs_2_), channel_id=1, source_target_pairs={{0,1},{1,0},{2,3},{3,2},{4,5},{5,4},{6,7},{7,6},{8,9},{9,8},{10,11... | collective-permute-start | bytes 1720328 | tf_op jit(solution)/shard_map/ppermute | solution.py:70
  73.2 11.8 %collective-permute-start.17 = (bf16[4,112,512]{2,1,0:T(8,128)(2,1)S(1)}, bf16[4,112,512]{2,1,0:T(8,128)(2,1)S(1)}, u32[]{:S(2)}, u32[]{:S(2)}) collective-permute-start(bf16[4,112,512]{2,1,0:T(8,128)(2,1)S(1)} %get-tuple-element.48.refs_0_), channel_id=1, source_target_pairs={{0,8},{2,10},{8,16},{10,18},{16,24},{18,26},{24,28},{26,30},{28,20... | collective-permute-start | bytes 1376264 | tf_op jit(solution)/shard_map/ppermute | solution.py:85
  74.8 11.2 %collective-permute-start.18 = (bf16[4,112,512]{2,1,0:T(8,128)(2,1)S(1)}, bf16[4,112,512]{2,1,0:T(8,128)(2,1)S(1)}, u32[]{:S(2)}, u32[]{:S(2)}) collective-permute-start(bf16[4,112,512]{2,1,0:T(8,128)(2,1)S(1)} %get-tuple-element.49.refs_1_), channel_id=1, source_target_pairs={{0,4},{2,6},{8,0},{10,2},{16,8},{18,10},{24,16},{26,18},{28,24},{3... | collective-permute-start | bytes 1376264 | tf_op jit(solution)/shard_map/ppermute | solution.py:85
  77.8 13.2 %collective-permute-start.16 = (bf16[2,224,512]{2,1,0:T(8,128)(2,1)S(1)}, bf16[2,224,512]{2,1,0:T(8,128)(2,1)S(1)}, u32[]{:S(2)}, u32[]{:S(2)}) collective-permute-start(bf16[2,224,512]{2,1,0:T(8,128)(2,1)S(1)} %get-tuple-element.50.refs_2_.refs_0_), channel_id=1, source_target_pairs={{0,1},{1,0},{2,3},{3,2},{4,5},{5,4},{6,7},{7,6},{8,9},{9,8},{10,11... | collective-permute-start | bytes 1376264 | tf_op jit(solution)/shard_map/ppermute | solution.py:70
  84.9 6.4 %collective-permute-start.21 = (bf16[2,560,512]{2,1,0:T(8,128)(2,1)S(1)}, bf16[2,560,512]{2,1,0:T(8,128)(2,1)S(1)}, u32[]{:S(2)}, u32[]{:S(2)}) collective-permute-start(bf16[2,560,512]{2,1,0:T(8,128)(2,1)S(1)} %join.5.refs_1_), channel_id=1, source_target_pairs={{0,2},{2,0},{4,6},{6,4},{8,10},{10,8},{12,14},{14,12},{16,18},{18,... | collective-permute-start | bytes 3440648 | tf_op jit(solution)/shard_map/ppermute | solution.py:70
  87.8 7.7 %collective-permute-start.20 = (bf16[2,112,512]{2,1,0:T(8,128)(2,1)S(1)}, bf16[2,112,512]{2,1,0:T(8,128)(2,1)S(1)}, u32[]{:S(2)}, u32[]{:S(2)}) collective-permute-start(bf16[2,112,512]{2,1,0:T(8,128)(2,1)S(1)} %get-tuple-element.53.refs_4_.refs_0_.refs_2_), channel_id=1, source_target_pairs={{0,1},{1,0},{2,3},{3,2},{4,5},{5,4},{6,7},{7,6},{8,9},{9,8},{10,11... | collective-permute-start | bytes 688136 | tf_op jit(solution)/shard_map/ppermute | solution.py:70
  88.4 7.5 %collective-permute-start.25 = (bf16[4,336,512]{2,1,0:T(8,128)(2,1)S(1)}, bf16[4,336,512]{2,1,0:T(8,128)(2,1)S(1)}, u32[]{:S(2)}, u32[]{:S(2)}) collective-permute-start(bf16[4,336,512]{2,1,0:T(8,128)(2,1)S(1)} %get-tuple-element.58), channel_id=1, source_target_pairs={{0,2},{2,0},{4,6},{6,4},{8,10},{10,8},{12,14},{14,12},{16,18},{18,... | collective-permute-start | bytes 4128776 | tf_op jit(solution)/shard_map/ppermute | solution.py:70
  91.2 4.7 %collective-permute-start.23 = (bf16[2,224,512]{2,1,0:T(8,128)(2,1)S(1)}, bf16[2,224,512]{2,1,0:T(8,128)(2,1)S(1)}, u32[]{:S(2)}, u32[]{:S(2)}) collective-permute-start(bf16[2,224,512]{2,1,0:T(8,128)(2,1)S(1)} %join.6.refs_0_.refs_1_), channel_id=1, source_target_pairs={{0,2},{2,0},{4,6},{6,4},{8,10},{10,8},{12,14},{14,12},{16,18},{18,... | collective-permute-start | bytes 1376264 | tf_op jit(solution)/shard_map/ppermute | solution.py:70
  (6 other events, 18.9 us)

commit v6 on v5

--- a/solution.py
+++ b/solution.py
@@ -337,7 +337,8 @@
     )(amplitudes, energy_virtual.reshape(2, 1, width), energy_first, energy_second)
 
 
-def residual_kernel(chunks, shards, halves, last, where, *refs):
+def residual_kernel(rows_of, depths_of, halves, last, where, *refs):
+    chunks, shards = len(rows_of), len(depths_of)
     middles, vectors, refs = refs[:chunks], refs[chunks : chunks + shards], refs[chunks + shards :]
     count, _, width = vectors[0].shape
     before, outs = refs[: len(halves)], refs[len(halves) :]
@@ -347,9 +348,11 @@
     copies = []
     for n, h in enumerate(halves):
         rows = pl.ds(pl.multiple_of(lax.rem(where[0] + h, 2) * columns, 16), columns)
-        left = joined_rows([m[h if m.shape[0] > 1 else 0] for m in middles]).T
+        parts = [m[h if m.shape[0] > 1 else 0, a:b] for m, (a, b) in zip(middles, rows_of)]
+        left = joined_rows(parts).T
         for j in range(count):
-            total = jnp.dot(left, joined_rows([v[j] for v in vectors]), preferred_element_type=F32)
+            right = joined_rows([v[j, a:b] for v, (a, b) in zip(vectors, depths_of)])
+            total = jnp.dot(left, right, preferred_element_type=F32)
             total += before[n][j]
             if last:
                 held[n, j] = total.astype(BF16)
@@ -362,6 +365,9 @@
 
 
 def residual(where, middles, vectors, halves, before, last=False, after=()):
+    whole = lambda v: v if isinstance(v, tuple) else (v, 0, v.shape[1])
+    middles, rows_of = zip(*[(v, (a, b)) for v, a, b in map(whole, middles)])
+    vectors, depths_of = zip(*[(v, (a, b)) for v, a, b in map(whole, vectors)])
     count, _, width = vectors[0].shape
     block = (count, middles[0].shape[2], width)
     args = [*middles, *vectors, *before]
@@ -370,7 +376,7 @@
         out_shapes = [((count, 2 * block[1], width), BF16)]
         scratch = [pltpu.VMEM((2,) + block, BF16), pltpu.SemaphoreType.DMA((2, count))]
     return kernel_call(
-        functools.partial(residual_kernel, len(middles), len(vectors), halves, last),
+        functools.partial(residual_kernel, rows_of, depths_of, halves, last),
         "residual",
         (1,),
         [WHOLE] * len(args),
@@ -464,18 +470,24 @@
     m_b = join(*[[((p_b, h), (p_b_sent, 1 - h))] for h in range(2)], after=[p_c])
     m_b_theirs = to_core(m_b)
     wall_5 = wall(m_b, cost=WALLS[4])
+    rows_b = m_b.shape[1]
+    taken = min(-m_a.shape[1] % 256 // 16 * 16, rows_b)
+    extra = bool(taken)
     begun = residual(
         where,
-        [m_a_theirs],
-        [handed_a],
+        [m_a_theirs] + [(m_b, 0, taken)] * extra,
+        [handed_a] + [(same_d, 0, taken)] * extra,
         [0, 1],
         [begun_own, begun_off],
         after=[wall_5],
     )
     m_c = join(*[[((p_c, h), (p_c_sent, 1 - h))] for h in range(2)], after=begun)
     m_c_theirs = to_core(m_c)
-    middles = [m_b, m_c, m_b_theirs, m_c_theirs]
-    (out,) = residual(where, middles, [same_d, handed_d], [0, 1], begun, last=True)
+    middles = [m_c, m_b_theirs, m_c_theirs]
+    vectors = [(same_d, taken, same_d.shape[1]), handed_d]
+    if taken < rows_b:
+        middles = [(m_b, taken, rows_b)] + middles
+    (out,) = residual(where, middles, vectors, [0, 1], begun, last=True)
     return out
 
 

time: 103 us -> 101 us (0.981)
  Pallas kernels: 46.1 us -> 45 us
    pallas_call x22, Pallas kernels: 46.1 us -> 44.9 us  [call(): pl.pallas_call(kernel, grid_spec=pltpu.PrefetchScalarGridSpec(num_scalar_...]
where the time goes in v6:
time: 101 us
  Pallas kernels  45 us (45%)
  waiting for transfers between devices  35.1 us (35%)
  starting transfers between devices  20.5 us (20%)
    pallas_call x22, Pallas kernels, call(): pl.pallas_call(kernel, grid_spec=pltpu.PrefetchScalarGridSpec(num_scalar_...  44.9 us
    ppermute x18, waiting for transfers between devices, swap(): lax.ppermute(x, axis, [(i, i ^ 1 << bit) for i in range(lax.axis_size(axi...  23.7 us
    ppermute x8, waiting for transfers between devices, along_ring(): return lax.ppermute(x, 'pair', pairs)  11.5 us
    ppermute x18, starting transfers between devices, swap(): lax.ppermute(x, axis, [(i, i ^ 1 << bit) for i in range(lax.axis_size(axi...  11.3 us
    ppermute x8, starting transfers between devices, along_ring(): return lax.ppermute(x, 'pair', pairs)  9.16 us
  transfers between devices with their start and end apart: 26, of which 13 were waited for; matrix products, arithmetic and copies ran while one was open for 0% of the time, Pallas kernels for 40%

profile of v6, /device:TPU:0, one launch (start us, length us, event | category | flops | bytes accessed | tf_op | source)
XLA Modules:
  0.0 101.1 jit_solution(9655989180133170338)
XLA Ops:
  0.0 3.0 %collective-permute-start = (bf16[8,112,512]{2,1,0:T(8,128)(2,1)}, bf16[8,112,512]{2,1,0:T(8,128)(2,1)S(1)}, u32[]{:S(2)}, u32[]{:S(2)}) collective-permute-start(bf16[8,112,512]{2,1,0:T(8,128)(2,1)} %bitcast.5), channel_id=1, source_target_pairs={{0,8},{2,10},{8,16},{10,18},{16,24},{18,26},{24,28},{26,30},{28,20... | collective-permute-start | bytes 2752520 | tf_op jit(solution)/shard_map/ppermute | solution.py:85
  4.9 2.0 %collective-permute-start.6 = (bf16[4,240,512]{2,1,0:T(8,128)(2,1)S(1)}, bf16[4,240,512]{2,1,0:T(8,128)(2,1)S(1)}, u32[]{:S(2)}, u32[]{:S(2)}) collective-permute-start(bf16[4,240,512]{2,1,0:T(8,128)(2,1)S(1)} %cut.2.refs_2_), channel_id=1, source_target_pairs={{0,1},{1,0},{2,3},{3,2},{4,5},{5,4},{6,7},{7,6},{8,9},{9,8},{10,11... | collective-permute-start | bytes 2949128 | tf_op jit(solution)/shard_map/ppermute | solution.py:70
  6.9 1.8 %cut.3 = (bf16[4,208,512]{2,1,0:T(8,128)(2,1)S(1)}, bf16[4,64,512]{2,1,0:T(8,128)(2,1)S(1)}) custom-call(s32[3]{0:T(128)S(1)} %pad_add_fusion.refs_0_, bf16[4,1024,512]{2,1,0:T(8,128)(2,1)} %refs_1_.13, bf16[4,240,512]{2,1,0:T(8,128)(2,1)S(1)} %cut.2.refs_2_), custom_call_target="tpu_custom_call" | custom-call | flops 1 | bytes 1 | tf_op jit(solution)/shard_map/cut/pallas_call | solution.py:49
  8.7 3.2 %turn.4 = (bf16[4,128,512]{2,1,0:T(8,128)(2,1)S(1)}, bf16[4,128,512]{2,1,0:T(8,128)(2,1)S(1)}) custom-call(s32[3]{0:T(128)S(1)} %pad_add_fusion.refs_0_, bf16[4,1024,512]{2,1,0:T(8,128)(2,1)} %refs_1_.13, bf16[4,1024,512]{2,1,0:T(8,128)(2,1)} %refs_1_.13, bf16[4,1024,512]{2,1,0:T(8,128)(2,1)} %refs_1_.13, ...), custom_call_target="tpu_custom_call" | custom-call | flops 1 | bytes 1 | tf_op jit(solution)/shard_map/turn/pallas_call | solution.py:49
  11.9 3.2 %turn.5 = (bf16[4,128,512]{2,1,0:T(8,128)(2,1)S(1)}, bf16[4,128,512]{2,1,0:T(8,128)(2,1)S(1)}) custom-call(s32[3]{0:T(128)S(1)} %pad_add_fusion.refs_0_, bf16[4,1024,512]{2,1,0:T(8,128)(2,1)} %refs_1_.13, bf16[4,1024,512]{2,1,0:T(8,128)(2,1)} %refs_1_.13, bf16[4,1024,512]{2,1,0:T(8,128)(2,1)} %refs_1_.13, ...), custom_call_target="tpu_custom_call" | custom-call | flops 1 | bytes 1 | tf_op jit(solution)/shard_map/turn/pallas_call | solution.py:49
  15.7 7.8 %collective-permute-done.refs_0_.refs_2_.refs_7_ = bf16[8,112,512]{2,1,0:T(8,128)(2,1)S(1)} collective-permute-done((bf16[8,112,512]{2,1,0:T(8,128)(2,1)}, bf16[8,112,512]{2,1,0:T(8,128)(2,1)S(1)}, u32[]{:S(2)}, u32[]{:S(2)}) %collective-permute-start) | collective-permute-done | bytes 917536 | tf_op jit(solution)/shard_map/ppermute | solution.py:85
  23.5 1.8 %collective-permute-start.1 = (bf16[8,112,512]{2,1,0:T(8,128)(2,1)S(1)}, bf16[8,112,512]{2,1,0:T(8,128)(2,1)S(1)}, u32[]{:S(2)}, u32[]{:S(2)}) collective-permute-start(bf16[8,112,512]{2,1,0:T(8,128)(2,1)S(1)} %collective-permute-done.refs_0_.refs_2_.refs_7_), channel_id=1, source_target_pairs={{0,8},{2,10},{8,16},{10,18},{16,24},{18,26},{24,28},{26,30},{28,20... | collective-permute-start | bytes 2752520 | tf_op jit(solution)/shard_map/ppermute | solution.py:85
  25.5 1.8 %collective-permute-start.9 = (bf16[4,208,512]{2,1,0:T(8,128)(2,1)S(1)}, bf16[4,208,512]{2,1,0:T(8,128)(2,1)S(1)}, u32[]{:S(2)}, u32[]{:S(2)}) collective-permute-start(bf16[4,208,512]{2,1,0:T(8,128)(2,1)S(1)} %get-tuple-element.32.refs_4_), channel_id=1, source_target_pairs={{0,1},{1,0},{2,3},{3,2},{4,5},{5,4},{6,7},{7,6},{8,9},{9,8},{10,11... | collective-permute-start | bytes 2555912 | tf_op jit(solution)/shard_map/ppermute | solution.py:70
  27.3 2.1 %collective-permute-done.6.refs_2_.refs_4_ = bf16[4,240,512]{2,1,0:T(8,128)(2,1)S(1)} collective-permute-done((bf16[4,240,512]{2,1,0:T(8,128)(2,1)S(1)}, bf16[4,240,512]{2,1,0:T(8,128)(2,1)S(1)}, u32[]{:S(2)}, u32[]{:S(2)}) %collective-permute-start.6) | collective-permute-done | bytes 983072 | tf_op jit(solution)/shard_map/ppermute | solution.py:70
  29.4 3.2 %turn.7 = (bf16[4,128,512]{2,1,0:T(8,128)(2,1)S(1)}, bf16[4,128,512]{2,1,0:T(8,128)(2,1)S(1)}) custom-call(s32[3]{0:T(128)S(1)} %pad_add_fusion.refs_0_, bf16[4,1024,512]{2,1,0:T(8,128)(2,1)} %refs_1_.13, bf16[4,1024,512]{2,1,0:T(8,128)(2,1)} %refs_1_.13, bf16[4,1024,512]{2,1,0:T(8,128)(2,1)} %refs_1_.13, f32[8,128]{1,0:T(8,128)S(1)} %wall.5.refs_4_), custom_call_target="tpu_custom_call" | custom-call | flops 1 | bytes 1 | tf_op jit(solution)/shard_map/turn/pallas_call | solution.py:49
  32.6 3.2 %turn.6 = (bf16[4,128,512]{2,1,0:T(8,128)(2,1)S(1)}, bf16[4,128,512]{2,1,0:T(8,128)(2,1)S(1)}) custom-call(s32[3]{0:T(128)S(1)} %pad_add_fusion.refs_0_, bf16[4,1024,512]{2,1,0:T(8,128)(2,1)} %refs_1_.13, bf16[4,1024,512]{2,1,0:T(8,128)(2,1)} %refs_1_.13, bf16[4,1024,512]{2,1,0:T(8,128)(2,1)} %refs_1_.13, f32[8,128]{1,0:T(8,128)S(1)} %wall.5.refs_4_), custom_call_target="tpu_custom_call" | custom-call | flops 1 | bytes 1 | tf_op jit(solution)/shard_map/turn/pallas_call | solution.py:49
  36.4 3.7 %diagonal.1 = (f32[4,512,512]{2,1,0:T(8,128)S(1)}, f32[4,512,512]{2,1,0:T(8,128)S(1)}) custom-call(s32[3]{0:T(128)S(1)} %pad_add_fusion.refs_0_, bf16[4,1024,512]{2,1,0:T(8,128)(2,1)} %refs_1_.13, f32[2,1,512]{2,1,0:T(1,128)S(1)} %bitcast.9, f32[8]{0:T(128)S(1)} %copy-done.2, f32[8]{0:T(128)S(1)} %copy-done.3, ...), custom_call_target="tpu_custom_call" | custom-call | flops 1 | bytes 1 | tf_op jit(solution)/shard_map/diagonal/pallas_call | solution.py:49
  40.1 6.4 %collective-permute-done.9.refs_2_.refs_5_ = bf16[4,208,512]{2,1,0:T(8,128)(2,1)S(1)} collective-permute-done((bf16[4,208,512]{2,1,0:T(8,128)(2,1)S(1)}, bf16[4,208,512]{2,1,0:T(8,128)(2,1)S(1)}, u32[]{:S(2)}, u32[]{:S(2)}) %collective-permute-start.9) | collective-permute-done | bytes 852000 | tf_op jit(solution)/shard_map/ppermute | solution.py:70
  50.9 3.1 %partial.4 = (bf16[1,560,512]{2,1,0:T(8,128)(2,1)S(1)}, bf16[4,560,512]{2,1,0:T(8,128)(2,1)S(1)}, bf16[4,560,512]{2,1,0:T(8,128)(2,1)S(1)}) custom-call(s32[3]{0:T(128)S(1)} %pad_add_fusion.refs_0_, bf16[8,112,512]{2,1,0:T(8,128)(2,1)S(1)} %bitcast.7, bf16[8,112,512]{2,1,0:T(8,128)(2,1)S(1)} %collective-permute-done.refs_0_.refs_2_.refs_7_, ...), custom_call_target="tpu_custom_call" | custom-call | flops 1 | bytes 1 | tf_op jit(solution)/shard_map/partial/pallas_call | solution.py:49
  57.5 3.1 %partial.5 = (bf16[1,560,512]{2,1,0:T(8,128)(2,1)S(1)}, bf16[4,560,512]{2,1,0:T(8,128)(2,1)S(1)}) custom-call(s32[3]{0:T(128)S(1)} %pad_add_fusion.refs_0_, bf16[4,560,512]{2,1,0:T(8,128)(2,1)S(1)} %get-tuple-element.45.refs_1_.refs_2_, bf16[4,560,512]{2,1,0:T(8,128)(2,1)S(1)} %get-tuple-element.46.refs_2_, ...), custom_call_target="tpu_custom_call" | custom-call | flops 1 | bytes 1 | tf_op jit(solution)/shard_map/partial/pallas_call | solution.py:49
  60.8 2.2 %collective-permute-start.19 = (bf16[1,560,512]{2,1,0:T(8,128)(2,1)S(1)}, bf16[1,560,512]{2,1,0:T(8,128)(2,1)S(1)}, u32[]{:S(2)}, u32[]{:S(2)}) collective-permute-start(bf16[1,560,512]{2,1,0:T(8,128)(2,1)S(1)} %get-tuple-element.47.refs_3_.refs_0_.refs_2_), channel_id=1, source_target_pairs={{0,1},{1,0},{2,3},{3,2},{4,5},{5,4},{6,7},{7,6},{8,9},{9,8},{10,11... | collective-permute-start | bytes 1720328 | tf_op jit(solution)/shard_map/ppermute | solution.py:70
  62.9 7.0 %collective-permute-done.15.refs_4_.refs_1_.refs_3_ = bf16[1,560,512]{2,1,0:T(8,128)(2,1)S(1)} collective-permute-done((bf16[1,560,512]{2,1,0:T(8,128)(2,1)S(1)}, bf16[1,560,512]{2,1,0:T(8,128)(2,1)S(1)}, u32[]{:S(2)}, u32[]{:S(2)}) %collective-permute-start.15) | collective-permute-done | bytes 573472 | tf_op jit(solution)/shard_map/ppermute | solution.py:70
  75.2 2.6 %partial.6 = (bf16[2,224,512]{2,1,0:T(8,128)(2,1)S(1)}, bf16[4,224,512]{2,1,0:T(8,128)(2,1)S(1)}, bf16[4,224,512]{2,1,0:T(8,128)(2,1)S(1)}) custom-call(s32[3]{0:T(128)S(1)} %pad_add_fusion.refs_0_, bf16[8,112,512]{2,1,0:T(8,128)(2,1)S(1)} %collective-permute-done.2.refs_1_.refs_3_, bf16[8,112,512]{2,1,0:T(8,128)(2,1)S(1)} %collective-permute-done.5.refs_2_.refs_4_, ...), custom_call_target="tpu_custom_call" | custom-call | flops 1 | bytes 1 | tf_op jit(solution)/shard_map/partial/pallas_call | solution.py:49
  78.6 2.4 %residual.4.refs_4_.refs_6_ = f32[4,512,512]{2,1,0:T(8,128)S(1)} custom-call(s32[3]{0:T(128)S(1)} %pad_add_fusion.refs_0_, bf16[1,560,512]{2,1,0:T(8,128)(2,1)S(1)} %join.4.refs_1_, bf16[4,560,512]{2,1,0:T(8,128)(2,1)S(1)} %get-tuple-element.45.refs_1_.refs_2_, f32[4,512,512]{2,1,0:T(8,128)S(1)} %get-tuple-element.43.refs_6_.refs_3_), custom_call_target="tpu_custom_call" | custom-call | flops 1 | bytes 1 | tf_op jit(solution)/shard_map/residual/pallas_call | solution.py:49
  82.5 2.4 %residual.5.refs_2_.refs_5_ = f32[4,512,512]{2,1,0:T(8,128)S(1)} custom-call(s32[3]{0:T(128)S(1)} %pad_add_fusion.refs_0_, bf16[2,560,512]{2,1,0:T(8,128)(2,1)S(1)} %join.5.refs_1_, bf16[4,560,512]{2,1,0:T(8,128)(2,1)S(1)} %get-tuple-element.45.refs_1_.refs_2_, f32[4,512,512]{2,1,0:T(8,128)S(1)} %get-tuple-element.42.refs_5_.refs_3_), custom_call_target="tpu_custom_call" | custom-call | flops 1 | bytes 1 | tf_op jit(solution)/shard_map/residual/pallas_call | solution.py:49
  86.0 1.9 %partial.7 = (bf16[2,112,512]{2,1,0:T(8,128)(2,1)S(1)}, bf16[4,336,512]{2,1,0:T(8,128)(2,1)S(1)}, bf16[4,336,512]{2,1,0:T(8,128)(2,1)S(1)}) custom-call(s32[3]{0:T(128)S(1)} %pad_add_fusion.refs_0_, bf16[4,112,512]{2,1,0:T(8,128)(2,1)S(1)} %collective-permute-done.17.refs_0_.refs_1_, bf16[4,112,512]{2,1,0:T(8,128)(2,1)S(1)} %collective-permute-done.18.refs_1_.refs_2_, ...), custom_call_target="tpu_custom_call" | custom-call | flops 1 | bytes 1 | tf_op jit(solution)/shard_map/partial/pallas_call | solution.py:49
  88.4 2.7 %collective-permute-done.16.refs_1_.refs_3_ = bf16[2,224,512]{2,1,0:T(8,128)(2,1)S(1)} collective-permute-done((bf16[2,224,512]{2,1,0:T(8,128)(2,1)S(1)}, bf16[2,224,512]{2,1,0:T(8,128)(2,1)S(1)}, u32[]{:S(2)}, u32[]{:S(2)}) %collective-permute-start.16) | collective-permute-done | bytes 458784 | tf_op jit(solution)/shard_map/ppermute | solution.py:70
  91.3 4.0 %residual.6 = (f32[4,512,512]{2,1,0:T(8,128)S(1)}, f32[4,512,512]{2,1,0:T(8,128)S(1)}) custom-call(s32[3]{0:T(128)S(1)} %pad_add_fusion.refs_0_, bf16[2,560,512]{2,1,0:T(8,128)(2,1)S(1)} %collective-permute-done.21.refs_1_, bf16[2,224,512]{2,1,0:T(8,128)(2,1)S(1)} %join.6.refs_0_.refs_2_.refs_1_, bf16[4,560,512]{2,1,0:T(8,128)(2,1)S(1)} %collective-permute-done.22.refs_3_, ...), custom_call_target="tpu_custom_call" | custom-call | flops 1 | bytes 1 | tf_op jit(solution)/shard_map/residual/pallas_call | solution.py:49
  97.1 3.8 %residual.7 = bf16[4,1024,512]{2,1,0:T(8,128)(2,1)} custom-call(s32[3]{0:T(128)S(1)} %pad_add_fusion.refs_0_, bf16[2,224,512]{2,1,0:T(8,128)(2,1)S(1)} %join.6.refs_0_.refs_2_.refs_1_, bf16[2,112,512]{2,1,0:T(8,128)(2,1)S(1)} %join.7.refs_2_, bf16[2,224,512]{2,1,0:T(8,128)(2,1)S(1)} %collective-permute-done.23.refs_3_, ...), custom_call_target="tpu_custom_call" | custom-call | flops 1 | bytes 1 | tf_op jit(solution)/shard_map/residual/pallas_call | solution.py:49
  (64 shorter events, 22.6 us)
Async XLA Ops:
  0.0 23.5 %collective-permute-start = (bf16[8,112,512]{2,1,0:T(8,128)(2,1)}, bf16[8,112,512]{2,1,0:T(8,128)(2,1)S(1)}, u32[]{:S(2)}, u32[]{:S(2)}) collective-permute-start(bf16[8,112,512]{2,1,0:T(8,128)(2,1)} %bitcast.5), channel_id=1, source_target_pairs={{0,8},{2,10},{8,16},{10,18},{16,24},{18,26},{24,28},{26,30},{28,20... | collective-permute-start | bytes 2752520 | tf_op jit(solution)/shard_map/ppermute | solution.py:85
  3.0 22.3 %collective-permute-start.3 = (bf16[8,112,512]{2,1,0:T(8,128)(2,1)}, bf16[8,112,512]{2,1,0:T(8,128)(2,1)S(1)}, u32[]{:S(2)}, u32[]{:S(2)}) collective-permute-start(bf16[8,112,512]{2,1,0:T(8,128)(2,1)} %bitcast.6), channel_id=1, source_target_pairs={{0,4},{2,6},{8,0},{10,2},{16,8},{18,10},{24,16},{26,18},{28,24},{3... | collective-permute-start | bytes 2752520 | tf_op jit(solution)/shard_map/ppermute | solution.py:85
  4.9 24.5 %collective-permute-start.6 = (bf16[4,240,512]{2,1,0:T(8,128)(2,1)S(1)}, bf16[4,240,512]{2,1,0:T(8,128)(2,1)S(1)}, u32[]{:S(2)}, u32[]{:S(2)}) collective-permute-start(bf16[4,240,512]{2,1,0:T(8,128)(2,1)S(1)} %cut.2.refs_2_), channel_id=1, source_target_pairs={{0,1},{1,0},{2,3},{3,2},{4,5},{5,4},{6,7},{7,6},{8,9},{9,8},{10,11... | collective-permute-start | bytes 2949128 | tf_op jit(solution)/shard_map/ppermute | solution.py:70
  11.9 13.7 %collective-permute-start.7 = (bf16[4,128,512]{2,1,0:T(8,128)(2,1)S(1)}, bf16[4,128,512]{2,1,0:T(8,128)(2,1)S(1)}, u32[]{:S(2)}, u32[]{:S(2)}) collective-permute-start(bf16[4,128,512]{2,1,0:T(8,128)(2,1)S(1)} %get-tuple-element.34.refs_5_.refs_11_.refs_3_), channel_id=1, source_target_pairs={{0,2},{2,0},{4,6},{6,4},{8,10},{10,8},{12,14},{14,12},{16,18},{18,... | collective-permute-start | bytes 1572872 | tf_op jit(solution)/shard_map/ppermute | solution.py:70
  15.1 12.2 %collective-permute-start.8 = (bf16[4,128,512]{2,1,0:T(8,128)(2,1)S(1)}, bf16[4,128,512]{2,1,0:T(8,128)(2,1)S(1)}, u32[]{:S(2)}, u32[]{:S(2)}) collective-permute-start(bf16[4,128,512]{2,1,0:T(8,128)(2,1)S(1)} %get-tuple-element.35.refs_6_.refs_12_.refs_4_), channel_id=1, source_target_pairs={{0,2},{2,0},{4,6},{6,4},{8,10},{10,8},{12,14},{14,12},{16,18},{18,... | collective-permute-start | bytes 1572872 | tf_op jit(solution)/shard_map/ppermute | solution.py:70
  23.5 22.9 %collective-permute-start.1 = (bf16[8,112,512]{2,1,0:T(8,128)(2,1)S(1)}, bf16[8,112,512]{2,1,0:T(8,128)(2,1)S(1)}, u32[]{:S(2)}, u32[]{:S(2)}) collective-permute-start(bf16[8,112,512]{2,1,0:T(8,128)(2,1)S(1)} %collective-permute-done.refs_0_.refs_2_.refs_7_), channel_id=1, source_target_pairs={{0,8},{2,10},{8,16},{10,18},{16,24},{18,26},{24,28},{26,30},{28,20... | collective-permute-start | bytes 2752520 | tf_op jit(solution)/shard_map/ppermute | solution.py:85
  25.3 21.1 %collective-permute-start.4 = (bf16[8,112,512]{2,1,0:T(8,128)(2,1)S(1)}, bf16[8,112,512]{2,1,0:T(8,128)(2,1)S(1)}, u32[]{:S(2)}, u32[]{:S(2)}) collective-permute-start(bf16[8,112,512]{2,1,0:T(8,128)(2,1)S(1)} %collective-permute-done.3.refs_1_.refs_3_.refs_8_), channel_id=1, source_target_pairs={{0,4},{2,6},{8,0},{10,2},{16,8},{18,10},{24,16},{26,18},{28,24},{3... | collective-permute-start | bytes 2752520 | tf_op jit(solution)/shard_map/ppermute | solution.py:85
  25.5 20.9 %collective-permute-start.9 = (bf16[4,208,512]{2,1,0:T(8,128)(2,1)S(1)}, bf16[4,208,512]{2,1,0:T(8,128)(2,1)S(1)}, u32[]{:S(2)}, u32[]{:S(2)}) collective-permute-start(bf16[4,208,512]{2,1,0:T(8,128)(2,1)S(1)} %get-tuple-element.32.refs_4_), channel_id=1, source_target_pairs={{0,1},{1,0},{2,3},{3,2},{4,5},{5,4},{6,7},{7,6},{8,9},{9,8},{10,11... | collective-permute-start | bytes 2555912 | tf_op jit(solution)/shard_map/ppermute | solution.py:70
  35.8 10.6 %collective-permute-start.11 = (bf16[4,128,512]{2,1,0:T(8,128)(2,1)S(1)}, bf16[4,128,512]{2,1,0:T(8,128)(2,1)S(1)}, u32[]{:S(2)}, u32[]{:S(2)}) collective-permute-start(bf16[4,128,512]{2,1,0:T(8,128)(2,1)S(1)} %get-tuple-element.37.refs_8_.refs_14_.refs_6_), channel_id=1, source_target_pairs={{0,2},{2,0},{4,6},{6,4},{8,10},{10,8},{12,14},{14,12},{16,18},{18,... | collective-permute-start | bytes 1572872 | tf_op jit(solution)/shard_map/ppermute | solution.py:70
  35.9 10.6 %collective-permute-start.10 = (bf16[4,128,512]{2,1,0:T(8,128)(2,1)S(1)}, bf16[4,128,512]{2,1,0:T(8,128)(2,1)S(1)}, u32[]{:S(2)}, u32[]{:S(2)}) collective-permute-start(bf16[4,128,512]{2,1,0:T(8,128)(2,1)S(1)} %get-tuple-element.36.refs_7_.refs_13_.refs_5_), channel_id=1, source_target_pairs={{0,2},{2,0},{4,6},{6,4},{8,10},{10,8},{12,14},{14,12},{16,18},{18,... | collective-permute-start | bytes 1572872 | tf_op jit(solution)/shard_map/ppermute | solution.py:70
  47.0 10.5 %collective-permute-start.13 = (bf16[4,448,512]{2,1,0:T(8,128)(2,1)S(1)}, bf16[4,448,512]{2,1,0:T(8,128)(2,1)S(1)}, u32[]{:S(2)}, u32[]{:S(2)}) collective-permute-start(bf16[4,448,512]{2,1,0:T(8,128)(2,1)S(1)} %mix.2.refs_19_.refs_3_.refs_9_.refs_7_), channel_id=1, source_target_pairs={{0,2},{2,0},{4,6},{6,4},{8,10},{10,8},{12,14},{14,12},{16,18},{18,... | collective-permute-start | bytes 5505032 | tf_op jit(solution)/shard_map/ppermute | solution.py:70
  47.1 8.7 %collective-permute-start.12 = (bf16[4,64,512]{2,1,0:T(8,128)(2,1)S(1)}, bf16[4,64,512]{2,1,0:T(8,128)(2,1)S(1)}, u32[]{:S(2)}, u32[]{:S(2)}) collective-permute-start(bf16[4,64,512]{2,1,0:T(8,128)(2,1)S(1)} %get-tuple-element.33.refs_5_), channel_id=1, source_target_pairs={{0,1},{1,0},{2,3},{3,2},{4,5},{5,4},{6,7},{7,6},{8,9},{9,8},{10,11... | collective-permute-start | bytes 786440 | tf_op jit(solution)/shard_map/ppermute | solution.py:70
  48.8 22.4 %collective-permute-start.2 = (bf16[8,112,512]{2,1,0:T(8,128)(2,1)S(1)}, bf16[8,112,512]{2,1,0:T(8,128)(2,1)S(1)}, u32[]{:S(2)}, u32[]{:S(2)}) collective-permute-start(bf16[8,112,512]{2,1,0:T(8,128)(2,1)S(1)} %collective-permute-done.1.refs_0_.refs_4_.refs_9_), channel_id=1, source_target_pairs={{0,8},{2,10},{8,16},{10,18},{16,24},{18,26},{24,28},{26,30},{28,20... | collective-permute-start | bytes 2752520 | tf_op jit(solution)/shard_map/ppermute | solution.py:85
  50.4 22.1 %collective-permute-start.5 = (bf16[8,112,512]{2,1,0:T(8,128)(2,1)S(1)}, bf16[8,112,512]{2,1,0:T(8,128)(2,1)S(1)}, u32[]{:S(2)}, u32[]{:S(2)}) collective-permute-start(bf16[8,112,512]{2,1,0:T(8,128)(2,1)S(1)} %collective-permute-done.4.refs_1_.refs_5_.refs_10_), channel_id=1, source_target_pairs={{0,4},{2,6},{8,0},{10,2},{16,8},{18,10},{24,16},{26,18},{28,24},{3... | collective-permute-start | bytes 2752520 | tf_op jit(solution)/shard_map/ppermute | solution.py:85
  53.9 16.0 %collective-permute-start.15 = (bf16[1,560,512]{2,1,0:T(8,128)(2,1)S(1)}, bf16[1,560,512]{2,1,0:T(8,128)(2,1)S(1)}, u32[]{:S(2)}, u32[]{:S(2)}) collective-permute-start(bf16[1,560,512]{2,1,0:T(8,128)(2,1)S(1)} %get-tuple-element.44.refs_5_.refs_0_), channel_id=1, source_target_pairs={{0,1},{1,0},{2,3},{3,2},{4,5},{5,4},{6,7},{7,6},{8,9},{9,8},{10,11... | collective-permute-start | bytes 1720328 | tf_op jit(solution)/shard_map/ppermute | solution.py:70
  60.6 30.7 %collective-permute-start.22 = (bf16[4,560,512]{2,1,0:T(8,128)(2,1)S(1)}, bf16[4,560,512]{2,1,0:T(8,128)(2,1)S(1)}, u32[]{:S(2)}, u32[]{:S(2)}) collective-permute-start(bf16[4,560,512]{2,1,0:T(8,128)(2,1)S(1)} %get-tuple-element.54), channel_id=1, source_target_pairs={{0,2},{2,0},{4,6},{6,4},{8,10},{10,8},{12,14},{14,12},{16,18},{18,... | collective-permute-start | bytes 6881288 | tf_op jit(solution)/shard_map/ppermute | solution.py:70
  60.8 21.4 %collective-permute-start.19 = (bf16[1,560,512]{2,1,0:T(8,128)(2,1)S(1)}, bf16[1,560,512]{2,1,0:T(8,128)(2,1)S(1)}, u32[]{:S(2)}, u32[]{:S(2)}) collective-permute-start(bf16[1,560,512]{2,1,0:T(8,128)(2,1)S(1)} %get-tuple-element.47.refs_3_.refs_0_.refs_2_), channel_id=1, source_target_pairs={{0,1},{1,0},{2,3},{3,2},{4,5},{5,4},{6,7},{7,6},{8,9},{9,8},{10,11... | collective-permute-start | bytes 1720328 | tf_op jit(solution)/shard_map/ppermute | solution.py:70
  73.2 11.8 %collective-permute-start.17 = (bf16[4,112,512]{2,1,0:T(8,128)(2,1)S(1)}, bf16[4,112,512]{2,1,0:T(8,128)(2,1)S(1)}, u32[]{:S(2)}, u32[]{:S(2)}) collective-permute-start(bf16[4,112,512]{2,1,0:T(8,128)(2,1)S(1)} %get-tuple-element.48.refs_0_), channel_id=1, source_target_pairs={{0,8},{2,10},{8,16},{10,18},{16,24},{18,26},{24,28},{26,30},{28,20... | collective-permute-start | bytes 1376264 | tf_op jit(solution)/shard_map/ppermute | solution.py:85
  74.8 11.2 %collective-permute-start.18 = (bf16[4,112,512]{2,1,0:T(8,128)(2,1)S(1)}, bf16[4,112,512]{2,1,0:T(8,128)(2,1)S(1)}, u32[]{:S(2)}, u32[]{:S(2)}) collective-permute-start(bf16[4,112,512]{2,1,0:T(8,128)(2,1)S(1)} %get-tuple-element.49.refs_1_), channel_id=1, source_target_pairs={{0,4},{2,6},{8,0},{10,2},{16,8},{18,10},{24,16},{26,18},{28,24},{3... | collective-permute-start | bytes 1376264 | tf_op jit(solution)/shard_map/ppermute | solution.py:85
  77.8 13.3 %collective-permute-start.16 = (bf16[2,224,512]{2,1,0:T(8,128)(2,1)S(1)}, bf16[2,224,512]{2,1,0:T(8,128)(2,1)S(1)}, u32[]{:S(2)}, u32[]{:S(2)}) collective-permute-start(bf16[2,224,512]{2,1,0:T(8,128)(2,1)S(1)} %get-tuple-element.50.refs_2_.refs_0_), channel_id=1, source_target_pairs={{0,1},{1,0},{2,3},{3,2},{4,5},{5,4},{6,7},{7,6},{8,9},{9,8},{10,11... | collective-permute-start | bytes 1376264 | tf_op jit(solution)/shard_map/ppermute | solution.py:70
  84.9 6.4 %collective-permute-start.21 = (bf16[2,560,512]{2,1,0:T(8,128)(2,1)S(1)}, bf16[2,560,512]{2,1,0:T(8,128)(2,1)S(1)}, u32[]{:S(2)}, u32[]{:S(2)}) collective-permute-start(bf16[2,560,512]{2,1,0:T(8,128)(2,1)S(1)} %join.5.refs_1_), channel_id=1, source_target_pairs={{0,2},{2,0},{4,6},{6,4},{8,10},{10,8},{12,14},{14,12},{16,18},{18,... | collective-permute-start | bytes 3440648 | tf_op jit(solution)/shard_map/ppermute | solution.py:70
  87.8 7.7 %collective-permute-start.20 = (bf16[2,112,512]{2,1,0:T(8,128)(2,1)S(1)}, bf16[2,112,512]{2,1,0:T(8,128)(2,1)S(1)}, u32[]{:S(2)}, u32[]{:S(2)}) collective-permute-start(bf16[2,112,512]{2,1,0:T(8,128)(2,1)S(1)} %get-tuple-element.53.refs_4_.refs_0_.refs_2_), channel_id=1, source_target_pairs={{0,1},{1,0},{2,3},{3,2},{4,5},{5,4},{6,7},{7,6},{8,9},{9,8},{10,11... | collective-permute-start | bytes 688136 | tf_op jit(solution)/shard_map/ppermute | solution.py:70
  88.4 7.5 %collective-permute-start.25 = (bf16[4,336,512]{2,1,0:T(8,128)(2,1)S(1)}, bf16[4,336,512]{2,1,0:T(8,128)(2,1)S(1)}, u32[]{:S(2)}, u32[]{:S(2)}) collective-permute-start(bf16[4,336,512]{2,1,0:T(8,128)(2,1)S(1)} %get-tuple-element.58), channel_id=1, source_target_pairs={{0,2},{2,0},{4,6},{6,4},{8,10},{10,8},{12,14},{14,12},{16,18},{18,... | collective-permute-start | bytes 4128776 | tf_op jit(solution)/shard_map/ppermute | solution.py:70
  91.2 4.7 %collective-permute-start.23 = (bf16[2,224,512]{2,1,0:T(8,128)(2,1)S(1)}, bf16[2,224,512]{2,1,0:T(8,128)(2,1)S(1)}, u32[]{:S(2)}, u32[]{:S(2)}) collective-permute-start(bf16[2,224,512]{2,1,0:T(8,128)(2,1)S(1)} %join.6.refs_0_.refs_2_.refs_1_), channel_id=1, source_target_pairs={{0,2},{2,0},{4,6},{6,4},{8,10},{10,8},{12,14},{14,12},{16,18},{18,... | collective-permute-start | bytes 1376264 | tf_op jit(solution)/shard_map/ppermute | solution.py:70
  (6 other events, 18.9 us)

commit v7 on v6

--- a/solution.py
+++ b/solution.py
@@ -28,17 +28,15 @@
     out_specs,
     out_shapes,
     scratch=(),
-    tile=None,
     after=(),
     far=(),
     out=pltpu.VMEM,
     cost=0,
 ):
-    scalars = 0 if tile is None else 1
     extra = len(after)
 
     def kernel(*refs):
-        keep = scalars + len(in_specs)
+        keep = len(in_specs)
         body(*refs[:keep], *refs[keep + extra :])
 
     def call(*args):
@@ -48,22 +46,25 @@
         ]
         return pl.pallas_call(
             kernel,
-            grid_spec=pltpu.PrefetchScalarGridSpec(
-                num_scalar_prefetch=scalars,
-                grid=grid,
-                in_specs=[*in_specs, *[ANYWHERE] * extra],
-                out_specs=list(out_specs),
-                scratch_shapes=list(scratch),
-            ),
+            grid=grid,
+            in_specs=[*in_specs, *[ANYWHERE] * extra],
+            out_specs=list(out_specs),
+            scratch_shapes=list(scratch),
             out_shape=[out(shape, kind) for shape, kind in out_shapes],
             compiler_params=pltpu.CompilerParams(
                 dimension_semantics=("arbitrary",) * len(grid), vmem_limit_bytes=VMEM_LIMIT
             ),
             cost_estimate=estimate(cost),
             name=name,
-        )(*([] if tile is None else [tile]), *held)
+        )(*held)
 
     return call
+
+
+def position(count):
+    groups = OCC // count
+    pair = lax.axis_index("pair")
+    return lax.axis_index("virt"), lax.rem(pair, groups), lax.div(pair, groups)
 
 
 def swap(x, axis, bit):
@@ -85,38 +86,56 @@
     return lax.ppermute(x, "pair", pairs)
 
 
-def turn_kernel(where, own, own_rows, other, near, far):
-    near[0] = (2.0 * own[0].astype(F32).T - own_rows[0].astype(F32)).astype(BF16)
-    far[0] = other[0].T
-
-
-def turn(where, amplitudes, part, parts, after=()):
+def turn_kernel(part, amplitudes, near, far, own, own_rows, other, done):
+    count, rows, width = near.shape
+    tile = lax.axis_index("virt")
+    first, second = pl.multiple_of(tile * width, 16), pl.multiple_of((1 - tile) * width, 16)
+    columns = pl.ds(part * rows, rows)
+    copies = []
+    for j in range(count):
+        sources = [
+            (amplitudes.at[j, pl.ds(first, width), columns], own),
+            (amplitudes.at[j, pl.ds(pl.multiple_of(first + part * rows, 16), rows)], own_rows),
+            (amplitudes.at[j, pl.ds(second, width), columns], other),
+        ]
+        for n, (source, held) in enumerate(sources):
+            copies.append(pltpu.make_async_copy(source, held.at[j], done.at[n, j]))
+            copies[-1].start()
+    for j in range(count):
+        for copy in copies[3 * j : 3 * j + 3]:
+            copy.wait()
+        near[j] = (2.0 * own[j].astype(F32).T - own_rows[j].astype(F32)).astype(BF16)
+        far[j] = other[j].T
+
+
+def turn(amplitudes, part, parts, after=()):
     count, _, width = amplitudes.shape
     rows = width // parts
-    block = (1, width, rows)
-    out = pl.BlockSpec((1, rows, width), lambda j, t: (j, 0, 0))
+    tall, flat = (count, width, rows), (count, rows, width)
     return kernel_call(
-        turn_kernel,
+        functools.partial(turn_kernel, part),
         "turn",
-        (count,),
+        (1,),
+        [ANYWHERE],
+        [WHOLE] * 2,
+        [(flat, BF16)] * 2,
         [
-            pl.BlockSpec(block, lambda j, t: (j, t[0], part)),
-            pl.BlockSpec((1, rows, width), lambda j, t: (j, t[0] * parts + part, 0)),
-            pl.BlockSpec(block, lambda j, t: (j, 1 - t[0], part)),
+            pltpu.VMEM(tall, BF16),
+            pltpu.VMEM(flat, BF16),
+            pltpu.VMEM(tall, BF16),
+            pltpu.SemaphoreType.DMA((3, count)),
         ],
-        [out] * 2,
-        [((count, rows, width), BF16)] * 2,
-        tile=where,
-        after=after,
-        far=(0, 1, 2),
-    )(amplitudes, amplitudes, amplitudes)
-
-
-def cut_kernel(starts, where, *refs):
+        after=after,
+        far=(0,),
+    )(amplitudes)
+
+
+def cut_kernel(starts, *refs):
     outs, done = refs[-1 - len(starts) : -1], refs[-1]
+    tile = lax.axis_index("virt")
     copies = []
     for n, (start, out) in enumerate(zip(starts, outs)):
-        at = pl.multiple_of((1 - where[0]) * out.shape[2] + start, 16)
+        at = pl.multiple_of((1 - tile) * out.shape[2] + start, 16)
         source = refs[0].at[:, pl.ds(at, out.shape[1]), :]
         copies.append(pltpu.make_async_copy(source, out, done.at[n]))
     for copy in copies:
@@ -125,7 +144,7 @@
         copy.wait()
 
 
-def cut(where, amplitudes, pieces, after=()):
+def cut(amplitudes, pieces, after=()):
     count, _, width = amplitudes.shape
     return kernel_call(
         functools.partial(cut_kernel, [start for start, _ in pieces]),
@@ -135,7 +154,6 @@
         [WHOLE] * len(pieces),
         [((count, rows, width), BF16) for _, rows in pieces],
         [pltpu.SemaphoreType.DMA((len(pieces),))],
-        tile=where,
         after=after,
         far=(0,),
     )(amplitudes)
@@ -173,13 +191,14 @@
     return out
 
 
-def partial_kernel(shards, parts, joined, extras, where, *refs):
+def partial_kernel(shards, parts, joined, extras, *refs):
     same, cross = refs[:shards], refs[shards : 2 * shards]
     refs = refs[2 * shards :]
     arrays = sum(parts)
     mine, theirs, refs = refs[:arrays], refs[arrays : 2 * arrays], refs[2 * arrays :]
     extra, outs = refs[:extras], refs[extras:]
     count = mine[0].shape[0]
+    _, group, _ = position(count)
 
     def together(arrays, j, group=0):
         pieces = [r[j + (group * count if r.shape[0] > count else 0)] for r in arrays]
@@ -187,7 +206,7 @@
 
     totals = [None] * len(parts)
     for j in range(count):
-        left, right = together(same, j, where[1]), together(cross, j, 1 - where[1])
+        left, right = together(same, j, group), together(cross, j, 1 - group)
         for n in range(joined):
             value = (left, right)[n - joined]
             outs[1 + n][j] = jnp.concatenate([extra[n][j], value], axis=0) if extras else value
@@ -202,7 +221,7 @@
         outs[0][h] = total.astype(BF16)
 
 
-def partial(where, same, cross, mine, theirs, joined=0, behind=(), after=()):
+def partial(same, cross, mine, theirs, joined=0, behind=(), after=()):
     parts = [len(m) for m in mine]
     shards, halves = len(same), len(mine)
     count, _, columns = mine[0][0].shape
@@ -220,30 +239,22 @@
         [WHOLE] * len(args),
         [WHOLE] * len(out_shapes),
         out_shapes,
-        tile=where,
         after=after,
     )(*args)
 
 
-def pick_kernel(where, forth, back, same, cross):
-    same[...] = forth[...]
-    cross[...] = back[...]
-
-
-def pick(where, forth, back, after=()):
-    block = (forth.shape[0] // 2,) + forth.shape[1:]
+def pick_kernel(forth, back, same, cross):
+    count = same.shape[0]
+    _, group, _ = position(count)
+    for j in range(count):
+        same[j] = forth[group * count + j]
+        cross[j] = back[(1 - group) * count + j]
+
+
+def pick(forth, back, after=()):
+    shape = (forth.shape[0] // 2,) + forth.shape[1:]
     return kernel_call(
-        pick_kernel,
-        "pick",
-        (1,),
-        [
-            pl.BlockSpec(block, lambda k, t: (t[1], 0, 0)),
-            pl.BlockSpec(block, lambda k, t: (1 - t[1], 0, 0)),
-        ],
-        [pl.BlockSpec(block, lambda k, t: (0, 0, 0))] * 2,
-        [(block, BF16)] * 2,
-        tile=where,
-        after=after,
+        pick_kernel, "pick", (1,), [WHOLE] * 2, [WHOLE] * 2, [(shape, BF16)] * 2, after=after
     )(forth, back)
 
 
@@ -302,25 +313,26 @@
     return jnp.concatenate(pieces, axis=0) if len(pieces) > 1 else pieces[0]
 
 
-def diagonal_kernel(where, values, energy, first_energy, second_energy, own, off, held, done):
+def diagonal_kernel(values, energy, first_energy, second_energy, own, off, held, done):
     count, columns, width = own.shape
+    here, group, place = position(count)
     copies = []
     for h in range(2):
-        tile = lax.rem(where[0] + h, 2)
+        tile = lax.rem(here + h, 2)
         rows = pl.ds(pl.multiple_of(tile * columns, 16), columns)
         for j in range(count):
             copies.append(pltpu.make_async_copy(values.at[j, rows], held.at[h, j], done.at[h, j]))
             copies[-1].start()
     for h, out in enumerate((own, off)):
-        row_energy = energy[lax.rem(where[0] + h, 2)]
+        row_energy = energy[lax.rem(here + h, 2)]
         row_energy = jnp.broadcast_to(row_energy, (128, columns)).T[:, :1]
         for j in range(count):
-            occupied = first_energy[where[2]] + second_energy[where[1] * count + j]
+            occupied = first_energy[place] + second_energy[group * count + j]
             copies[h * count + j].wait()
-            out[j] = (row_energy - occupied + energy[where[0]]) * held[h, j].astype(F32)
-
-
-def diagonal(where, amplitudes, energy_virtual, energy_first, energy_second, after=()):
+            out[j] = (row_energy - occupied + energy[here]) * held[h, j].astype(F32)
+
+
+def diagonal(amplitudes, energy_virtual, energy_first, energy_second, after=()):
     count, rows, width = amplitudes.shape
     block = (count, rows // 2, width)
     return kernel_call(
@@ -331,13 +343,12 @@
         [WHOLE] * 2,
         [(block, F32)] * 2,
         [pltpu.VMEM((2,) + block, BF16), pltpu.SemaphoreType.DMA((2, count))],
-        tile=where,
         after=after,
         far=(0,),
     )(amplitudes, energy_virtual.reshape(2, 1, width), energy_first, energy_second)
 
 
-def residual_kernel(rows_of, depths_of, halves, last, where, *refs):
+def residual_kernel(rows_of, depths_of, halves, last, *refs):
     chunks, shards = len(rows_of), len(depths_of)
     middles, vectors, refs = refs[:chunks], refs[chunks : chunks + shards], refs[chunks + shards :]
     count, _, width = vectors[0].shape
@@ -347,7 +358,7 @@
     columns = middles[0].shape[2]
     copies = []
     for n, h in enumerate(halves):
-        rows = pl.ds(pl.multiple_of(lax.rem(where[0] + h, 2) * columns, 16), columns)
+        rows = pl.ds(pl.multiple_of(lax.rem(lax.axis_index("virt") + h, 2) * columns, 16), columns)
         parts = [m[h if m.shape[0] > 1 else 0, a:b] for m, (a, b) in zip(middles, rows_of)]
         left = joined_rows(parts).T
         for j in range(count):
@@ -364,7 +375,7 @@
         copy.wait()
 
 
-def residual(where, middles, vectors, halves, before, last=False, after=()):
+def residual(middles, vectors, halves, before, last=False, after=()):
     whole = lambda v: v if isinstance(v, tuple) else (v, 0, v.shape[1])
     middles, rows_of = zip(*[(v, (a, b)) for v, a, b in map(whole, middles)])
     vectors, depths_of = zip(*[(v, (a, b)) for v, a, b in map(whole, vectors)])
@@ -383,7 +394,6 @@
         [ANYWHERE if last else WHOLE] * len(out_shapes),
         out_shapes,
         scratch,
-        tile=where,
         after=after,
         out=pltpu.HBM if last else pltpu.VMEM,
     )(*args)
@@ -393,17 +403,14 @@
     count, virtual, width = amplitudes.shape
     groups = OCC // count
     places = lax.axis_size("pair") // groups
-    place, group = lax.axis_index("pair") // groups, lax.axis_index("pair") % groups
-    y = lax.axis_index("virt")
-    where = jnp.stack([y, group, place]).astype(jnp.int32)
     ring = functools.partial(along_ring, groups=groups)
     to_core = functools.partial(swap, axis="pair", bit=0)
     to_tile = functools.partial(swap, axis="virt", bit=0)
 
     unit = width // 32
     pieces = [(0, 15 * unit), (15 * unit, 13 * unit), (28 * unit, 4 * unit)]
-    sent = cut(where, amplitudes, pieces[:1])
-    sent += cut(where, amplitudes, pieces[1:], after=sent)
+    sent = cut(amplitudes, pieces[:1])
+    sent += cut(amplitudes, pieces[1:], after=sent)
     arrived = [to_tile(v) for v in sent]
 
     own = jnp.swapaxes(cholesky, 1, 2)
@@ -417,7 +424,7 @@
     held = sent[1:]
     parts = 4
     for part in range(parts):
-        v, w = turn(where, amplitudes, part, parts, after=held)
+        v, w = turn(amplitudes, part, parts, after=held)
         near.append(v)
         far_turned.append(w)
         near_theirs.append(to_core(v))
@@ -425,38 +432,37 @@
             wall_1 = wall(*vectors[1:3], arrived[0], *near_theirs, cost=WALLS[0])
             held = [wall_1]
     begun = diagonal(
-        where, amplitudes, energy_virtual, energy_first, energy_second, after=near
+        amplitudes, energy_virtual, energy_first, energy_second, after=near
     )
     wall_2 = wall(*vectors[3:5], arrived[1], *near_theirs[parts // 2 :], *begun, cost=WALLS[1])
     far_0 = mix(far_turned, arrived[:2], 0, after=[wall_2])
     far_0_theirs = to_core(far_0)
     near, near_theirs = [near], [near_theirs]
     n_a, same_a, cross_a = partial(
-        where, vectors[:5], vectors[:5], near, near_theirs, joined=2, after=[far_0]
+        vectors[:5], vectors[:5], near, near_theirs, joined=2, after=[far_0]
     )
     n_a_sent = to_tile(n_a)
     far_1 = mix(far_turned, arrived[2:], far_0.shape[1], after=[n_a], cost=MIXED)
     far_1_theirs = to_core(far_1)
     far, far_theirs = [far_0, far_1], [far_0_theirs, far_1_theirs]
-    f_a, cross_a = partial(where, [same_a], [cross_a], [far], [far_theirs], joined=1)
+    f_a, cross_a = partial([same_a], [cross_a], [far], [far_theirs], joined=1)
     f_a_sent = to_tile(f_a)
     handed_a = to_core(cross_a)
-    picked = pick(where, *vectors[5:7], after=[f_a, n_a_sent])
+    picked = pick(*vectors[5:7], after=[f_a, n_a_sent])
     same_c, cross_c = ring(picked[0], 1), ring(picked[1], -1)
     wall_3 = wall(*picked, cost=WALLS[2])
     halves, halves_theirs = near + [far], near_theirs + [far_theirs]
     p_b, same_b, cross_b = partial(
-        where, vectors[5:7], vectors[5:7], halves, halves_theirs, joined=2, after=[wall_3]
+        vectors[5:7], vectors[5:7], halves, halves_theirs, joined=2, after=[wall_3]
     )
     p_b_sent = to_tile(p_b)
     m_off = join([((f_a, 0), (n_a_sent, 0))], after=[p_b])
-    (begun_off,) = residual(where, [m_off], [same_a], [1], begun[1:])
+    (begun_off,) = residual([m_off], [same_a], [1], begun[1:])
     m_a = join([((n_a, 0), (f_a_sent, 0))], [((f_a, 0), (n_a_sent, 0))], after=[begun_off])
     m_a_theirs = to_core(m_a)
-    (begun_own,) = residual(where, [m_a], [same_a], [0], begun[:1])
+    (begun_own,) = residual([m_a], [same_a], [0], begun[:1])
     wall_4 = wall(same_c, cross_c, begun_own, cost=WALLS[3])
     p_c, same_d, cross_d = partial(
-        where,
         [same_c],
         [cross_c],
         halves,
@@ -474,7 +480,6 @@
     taken = min(-m_a.shape[1] % 256 // 16 * 16, rows_b)
     extra = bool(taken)
     begun = residual(
-        where,
         [m_a_theirs] + [(m_b, 0, taken)] * extra,
         [handed_a] + [(same_d, 0, taken)] * extra,
         [0, 1],
@@ -487,7 +492,7 @@
     vectors = [(same_d, taken, same_d.shape[1]), handed_d]
     if taken < rows_b:
         middles = [(m_b, taken, rows_b)] + middles
-    (out,) = residual(where, middles, vectors, [0, 1], begun, last=True)
+    (out,) = residual(middles, vectors, [0, 1], begun, last=True)
     return out
 
 

time: 101 us -> 100 us (0.990)
  Pallas kernels: 45 us -> 32.9 us
  waiting for transfers between devices: 35.1 us -> 46.6 us
    pallas_call x22, Pallas kernels: 44.9 us -> 32.9 us  [call(): pl.pallas_call(kernel, grid=grid, in_specs=[*in_specs, *[ANYWHERE] * extr...]
    ppermute x18, waiting for transfers between devices: 23.7 us -> 29.6 us  [swap(): lax.ppermute(x, axis, [(i, i ^ 1 << bit) for i in range(lax.axis_size(axi...]
    ppermute x8, waiting for transfers between devices: 11.5 us -> 17 us  [along_ring(): return lax.ppermute(x, 'pair', pairs)]
  transfers between devices with their start and end apart: 26 -> 26, of which waited for: 13 -> 15; matrix products, arithmetic and copies ran while one was open for 0% -> 0% of each run, Pallas kernels for 40% -> 29%
where the time goes in v7:
time: 100 us
  waiting for transfers between devices  46.6 us (47%)
  Pallas kernels  32.9 us (33%)
  starting transfers between devices  20.1 us (20%)
    pallas_call x22, Pallas kernels, call(): pl.pallas_call(kernel, grid=grid, in_specs=[*in_specs, *[ANYWHERE] * extr...  32.9 us
    ppermute x18, waiting for transfers between devices, swap(): lax.ppermute(x, axis, [(i, i ^ 1 << bit) for i in range(lax.axis_size(axi...  29.6 us
    ppermute x8, waiting for transfers between devices, along_ring(): return lax.ppermute(x, 'pair', pairs)  17 us
    ppermute x18, starting transfers between devices, swap(): lax.ppermute(x, axis, [(i, i ^ 1 << bit) for i in range(lax.axis_size(axi...  11 us
    ppermute x8, starting transfers between devices, along_ring(): return lax.ppermute(x, 'pair', pairs)  9.16 us
  transfers between devices with their start and end apart: 26, of which 15 were waited for; matrix products, arithmetic and copies ran while one was open for 0% of the time, Pallas kernels for 29%

profile of v7, /device:TPU:0, one launch (start us, length us, event | category | flops | bytes accessed | tf_op | source)
XLA Modules:
  0.0 100.0 jit_solution(108823350854719332)
XLA Ops:
  0.0 3.0 %collective-permute-start = (bf16[8,112,512]{2,1,0:T(8,128)(2,1)}, bf16[8,112,512]{2,1,0:T(8,128)(2,1)S(1)}, u32[]{:S(2)}, u32[]{:S(2)}) collective-permute-start(bf16[8,112,512]{2,1,0:T(8,128)(2,1)} %bitcast.2), channel_id=1, source_target_pairs={{0,8},{2,10},{8,16},{10,18},{16,24},{18,26},{24,28},{26,30},{28,20... | collective-permute-start | bytes 2752520 | tf_op jit(solution)/shard_map/ppermute | solution.py:86
  4.2 2.0 %collective-permute-start.6 = (bf16[4,240,512]{2,1,0:T(8,128)(2,1)S(1)}, bf16[4,240,512]{2,1,0:T(8,128)(2,1)S(1)}, u32[]{:S(2)}, u32[]{:S(2)}) collective-permute-start(bf16[4,240,512]{2,1,0:T(8,128)(2,1)S(1)} %cut.2.refs_1_), channel_id=1, source_target_pairs={{0,1},{1,0},{2,3},{3,2},{4,5},{5,4},{6,7},{7,6},{8,9},{9,8},{10,11... | collective-permute-start | bytes 2949128 | tf_op jit(solution)/shard_map/ppermute | solution.py:71
  7.5 1.8 %turn.4 = (bf16[4,128,512]{2,1,0:T(8,128)(2,1)S(1)}, bf16[4,128,512]{2,1,0:T(8,128)(2,1)S(1)}) custom-call(bf16[4,1024,512]{2,1,0:T(8,128)(2,1)} %refs_0_.13, bf16[4,208,512]{2,1,0:T(8,128)(2,1)S(1)} %get-tuple-element.32.refs_1_, bf16[4,64,512]{2,1,0:T(8,128)(2,1)S(1)} %get-tuple-element.33.refs_2_), custom_call_target="tpu_custom_call" | custom-call | flops 1 | bytes 1 | tf_op jit(solution)/shard_map/turn/pallas_call | solution.py:47
  9.4 1.8 %turn.5 = (bf16[4,128,512]{2,1,0:T(8,128)(2,1)S(1)}, bf16[4,128,512]{2,1,0:T(8,128)(2,1)S(1)}) custom-call(bf16[4,1024,512]{2,1,0:T(8,128)(2,1)} %refs_0_.13, bf16[4,208,512]{2,1,0:T(8,128)(2,1)S(1)} %get-tuple-element.32.refs_1_, bf16[4,64,512]{2,1,0:T(8,128)(2,1)S(1)} %get-tuple-element.33.refs_2_), custom_call_target="tpu_custom_call" | custom-call | flops 1 | bytes 1 | tf_op jit(solution)/shard_map/turn/pallas_call | solution.py:47
  11.7 11.8 %collective-permute-done.refs_0_.refs_1_.refs_6_ = bf16[8,112,512]{2,1,0:T(8,128)(2,1)S(1)} collective-permute-done((bf16[8,112,512]{2,1,0:T(8,128)(2,1)}, bf16[8,112,512]{2,1,0:T(8,128)(2,1)S(1)}, u32[]{:S(2)}, u32[]{:S(2)}) %collective-permute-start) | collective-permute-done | bytes 917536 | tf_op jit(solution)/shard_map/ppermute | solution.py:86
  23.5 1.8 %collective-permute-start.1 = (bf16[8,112,512]{2,1,0:T(8,128)(2,1)S(1)}, bf16[8,112,512]{2,1,0:T(8,128)(2,1)S(1)}, u32[]{:S(2)}, u32[]{:S(2)}) collective-permute-start(bf16[8,112,512]{2,1,0:T(8,128)(2,1)S(1)} %collective-permute-done.refs_0_.refs_1_.refs_6_), channel_id=1, source_target_pairs={{0,8},{2,10},{8,16},{10,18},{16,24},{18,26},{24,28},{26,30},{28,20... | collective-permute-start | bytes 2752520 | tf_op jit(solution)/shard_map/ppermute | solution.py:86
  25.5 1.8 %collective-permute-start.9 = (bf16[4,208,512]{2,1,0:T(8,128)(2,1)S(1)}, bf16[4,208,512]{2,1,0:T(8,128)(2,1)S(1)}, u32[]{:S(2)}, u32[]{:S(2)}) collective-permute-start(bf16[4,208,512]{2,1,0:T(8,128)(2,1)S(1)} %get-tuple-element.32.refs_1_), channel_id=1, source_target_pairs={{0,1},{1,0},{2,3},{3,2},{4,5},{5,4},{6,7},{7,6},{8,9},{9,8},{10,11... | collective-permute-start | bytes 2555912 | tf_op jit(solution)/shard_map/ppermute | solution.py:71
  28.1 1.7 %turn.6 = (bf16[4,128,512]{2,1,0:T(8,128)(2,1)S(1)}, bf16[4,128,512]{2,1,0:T(8,128)(2,1)S(1)}) custom-call(bf16[4,1024,512]{2,1,0:T(8,128)(2,1)} %refs_0_.13, f32[8,128]{1,0:T(8,128)S(1)} %wall.5.refs_1_), custom_call_target="tpu_custom_call" | custom-call | flops 1 | bytes 1 | tf_op jit(solution)/shard_map/turn/pallas_call | solution.py:47
  29.9 1.8 %turn.7 = (bf16[4,128,512]{2,1,0:T(8,128)(2,1)S(1)}, bf16[4,128,512]{2,1,0:T(8,128)(2,1)S(1)}) custom-call(bf16[4,1024,512]{2,1,0:T(8,128)(2,1)} %refs_0_.13, f32[8,128]{1,0:T(8,128)S(1)} %wall.5.refs_1_), custom_call_target="tpu_custom_call" | custom-call | flops 1 | bytes 1 | tf_op jit(solution)/shard_map/turn/pallas_call | solution.py:47
  32.3 3.2 %diagonal.1 = (f32[4,512,512]{2,1,0:T(8,128)S(1)}, f32[4,512,512]{2,1,0:T(8,128)S(1)}) custom-call(bf16[4,1024,512]{2,1,0:T(8,128)(2,1)} %refs_0_.13, f32[2,1,512]{2,1,0:T(1,128)S(1)} %bitcast.6, f32[8]{0:T(128)S(1)} %copy-done.2, f32[8]{0:T(128)S(1)} %copy-done.3, bf16[4,128,512]{2,1,0:T(8,128)(2,1)S(1)} %get-tuple-element.34.refs_4_.refs_10_.refs_2_, ...), custom_call_target="tpu_custom_call" | custom-call | flops 1 | bytes 1 | tf_op jit(solution)/shard_map/diagonal/pallas_call | solution.py:47
  35.4 10.3 %collective-permute-done.9.refs_2_.refs_5_ = bf16[4,208,512]{2,1,0:T(8,128)(2,1)S(1)} collective-permute-done((bf16[4,208,512]{2,1,0:T(8,128)(2,1)S(1)}, bf16[4,208,512]{2,1,0:T(8,128)(2,1)S(1)}, u32[]{:S(2)}, u32[]{:S(2)}) %collective-permute-start.9) | collective-permute-done | bytes 852000 | tf_op jit(solution)/shard_map/ppermute | solution.py:71
  50.5 2.5 %partial.4 = (bf16[1,560,512]{2,1,0:T(8,128)(2,1)S(1)}, bf16[4,560,512]{2,1,0:T(8,128)(2,1)S(1)}, bf16[4,560,512]{2,1,0:T(8,128)(2,1)S(1)}) custom-call(bf16[8,112,512]{2,1,0:T(8,128)(2,1)S(1)} %bitcast.4, bf16[8,112,512]{2,1,0:T(8,128)(2,1)S(1)} %collective-permute-done.refs_0_.refs_1_.refs_6_, ...), custom_call_target="tpu_custom_call" | custom-call | flops 1 | bytes 1 | tf_op jit(solution)/shard_map/partial/pallas_call | solution.py:47
  53.6 2.2 %collective-permute-done.12.refs_4_ = bf16[4,64,512]{2,1,0:T(8,128)(2,1)S(1)} collective-permute-done((bf16[4,64,512]{2,1,0:T(8,128)(2,1)S(1)}, bf16[4,64,512]{2,1,0:T(8,128)(2,1)S(1)}, u32[]{:S(2)}, u32[]{:S(2)}) %collective-permute-start.12) | collective-permute-done | bytes 262176 | tf_op jit(solution)/shard_map/ppermute | solution.py:71
  57.5 2.5 %partial.5 = (bf16[1,560,512]{2,1,0:T(8,128)(2,1)S(1)}, bf16[4,560,512]{2,1,0:T(8,128)(2,1)S(1)}) custom-call(bf16[4,560,512]{2,1,0:T(8,128)(2,1)S(1)} %get-tuple-element.45.refs_0_.refs_1_, bf16[4,560,512]{2,1,0:T(8,128)(2,1)S(1)} %get-tuple-element.46.refs_1_, bf16[4,448,512]{2,1,0:T(8,128)(2,1)S(1)} %mix.2.refs_18_.refs_2_.refs_8_.refs_6_, ...), custom_call_target="tpu_custom_call" | custom-call | flops 1 | bytes 1 | tf_op jit(solution)/shard_map/partial/pallas_call | solution.py:47
  60.3 1.8 %collective-permute-start.19 = (bf16[1,560,512]{2,1,0:T(8,128)(2,1)S(1)}, bf16[1,560,512]{2,1,0:T(8,128)(2,1)S(1)}, u32[]{:S(2)}, u32[]{:S(2)}) collective-permute-start(bf16[1,560,512]{2,1,0:T(8,128)(2,1)S(1)} %get-tuple-element.47.refs_2_.refs_0_), channel_id=1, source_target_pairs={{0,1},{1,0},{2,3},{3,2},{4,5},{5,4},{6,7},{7,6},{8,9},{9,8},{10,11... | collective-permute-start | bytes 1720328 | tf_op jit(solution)/shard_map/ppermute | solution.py:71
  62.0 7.0 %collective-permute-done.15.refs_3_.refs_1_ = bf16[1,560,512]{2,1,0:T(8,128)(2,1)S(1)} collective-permute-done((bf16[1,560,512]{2,1,0:T(8,128)(2,1)S(1)}, bf16[1,560,512]{2,1,0:T(8,128)(2,1)S(1)}, u32[]{:S(2)}, u32[]{:S(2)}) %collective-permute-start.15) | collective-permute-done | bytes 573472 | tf_op jit(solution)/shard_map/ppermute | solution.py:71
  69.0 1.9 %collective-permute-done.2.refs_0_.refs_2_ = bf16[8,112,512]{2,1,0:T(8,128)(2,1)S(1)} collective-permute-done((bf16[8,112,512]{2,1,0:T(8,128)(2,1)S(1)}, bf16[8,112,512]{2,1,0:T(8,128)(2,1)S(1)}, u32[]{:S(2)}, u32[]{:S(2)}) %collective-permute-start.2) | collective-permute-done | bytes 917536 | tf_op jit(solution)/shard_map/ppermute | solution.py:86
  74.3 2.1 %partial.6 = (bf16[2,224,512]{2,1,0:T(8,128)(2,1)S(1)}, bf16[4,224,512]{2,1,0:T(8,128)(2,1)S(1)}, bf16[4,224,512]{2,1,0:T(8,128)(2,1)S(1)}) custom-call(bf16[8,112,512]{2,1,0:T(8,128)(2,1)S(1)} %collective-permute-done.2.refs_0_.refs_2_, bf16[8,112,512]{2,1,0:T(8,128)(2,1)S(1)} %collective-permute-done.5.refs_1_.refs_3_, ...), custom_call_target="tpu_custom_call" | custom-call | flops 1 | bytes 1 | tf_op jit(solution)/shard_map/partial/pallas_call | solution.py:47
  77.2 1.8 %residual.4.refs_4_.refs_5_ = f32[4,512,512]{2,1,0:T(8,128)S(1)} custom-call(bf16[1,560,512]{2,1,0:T(8,128)(2,1)S(1)} %join.4.refs_0_, bf16[4,560,512]{2,1,0:T(8,128)(2,1)S(1)} %get-tuple-element.45.refs_0_.refs_1_, f32[4,512,512]{2,1,0:T(8,128)S(1)} %get-tuple-element.43.refs_6_.refs_2_), custom_call_target="tpu_custom_call" | custom-call | flops 1 | bytes 1 | tf_op jit(solution)/shard_map/residual/pallas_call | solution.py:47
  79.0 2.3 %collective-permute-done.19.refs_1_ = bf16[1,560,512]{2,1,0:T(8,128)(2,1)S(1)} collective-permute-done((bf16[1,560,512]{2,1,0:T(8,128)(2,1)S(1)}, bf16[1,560,512]{2,1,0:T(8,128)(2,1)S(1)}, u32[]{:S(2)}, u32[]{:S(2)}) %collective-permute-start.19) | collective-permute-done | bytes 573472 | tf_op jit(solution)/shard_map/ppermute | solution.py:71
  81.6 1.9 %residual.5.refs_2_.refs_4_ = f32[4,512,512]{2,1,0:T(8,128)S(1)} custom-call(bf16[2,560,512]{2,1,0:T(8,128)(2,1)S(1)} %join.5.refs_0_, bf16[4,560,512]{2,1,0:T(8,128)(2,1)S(1)} %get-tuple-element.45.refs_0_.refs_1_, f32[4,512,512]{2,1,0:T(8,128)S(1)} %get-tuple-element.42.refs_5_.refs_2_), custom_call_target="tpu_custom_call" | custom-call | flops 1 | bytes 1 | tf_op jit(solution)/shard_map/residual/pallas_call | solution.py:47
  87.0 4.1 %collective-permute-done.16.refs_1_.refs_3_ = bf16[2,224,512]{2,1,0:T(8,128)(2,1)S(1)} collective-permute-done((bf16[2,224,512]{2,1,0:T(8,128)(2,1)S(1)}, bf16[2,224,512]{2,1,0:T(8,128)(2,1)S(1)}, u32[]{:S(2)}, u32[]{:S(2)}) %collective-permute-start.16) | collective-permute-done | bytes 458784 | tf_op jit(solution)/shard_map/ppermute | solution.py:71
  91.3 3.5 %residual.6 = (f32[4,512,512]{2,1,0:T(8,128)S(1)}, f32[4,512,512]{2,1,0:T(8,128)S(1)}) custom-call(bf16[2,560,512]{2,1,0:T(8,128)(2,1)S(1)} %collective-permute-done.21.refs_0_, bf16[2,224,512]{2,1,0:T(8,128)(2,1)S(1)} %join.6.refs_0_.refs_1_, bf16[4,560,512]{2,1,0:T(8,128)(2,1)S(1)} %collective-permute-done.22.refs_2_, ...), custom_call_target="tpu_custom_call" | custom-call | flops 1 | bytes 1 | tf_op jit(solution)/shard_map/residual/pallas_call | solution.py:47
  96.5 3.3 %residual.7 = bf16[4,1024,512]{2,1,0:T(8,128)(2,1)} custom-call(bf16[2,224,512]{2,1,0:T(8,128)(2,1)S(1)} %join.6.refs_0_.refs_1_, bf16[2,112,512]{2,1,0:T(8,128)(2,1)S(1)} %join.7.refs_1_, bf16[2,224,512]{2,1,0:T(8,128)(2,1)S(1)} %collective-permute-done.23.refs_2_, bf16[2,112,512]{2,1,0:T(8,128)(2,1)S(1)} %collective-permute-done.24.refs_3_, ...), custom_call_target="tpu_custom_call" | custom-call | flops 1 | bytes 1 | tf_op jit(solution)/shard_map/residual/pallas_call | solution.py:47
  (63 shorter events, 21.7 us)
Async XLA Ops:
  0.0 23.5 %collective-permute-start = (bf16[8,112,512]{2,1,0:T(8,128)(2,1)}, bf16[8,112,512]{2,1,0:T(8,128)(2,1)S(1)}, u32[]{:S(2)}, u32[]{:S(2)}) collective-permute-start(bf16[8,112,512]{2,1,0:T(8,128)(2,1)} %bitcast.2), channel_id=1, source_target_pairs={{0,8},{2,10},{8,16},{10,18},{16,24},{18,26},{24,28},{26,30},{28,20... | collective-permute-start | bytes 2752520 | tf_op jit(solution)/shard_map/ppermute | solution.py:86
  3.0 22.3 %collective-permute-start.3 = (bf16[8,112,512]{2,1,0:T(8,128)(2,1)}, bf16[8,112,512]{2,1,0:T(8,128)(2,1)S(1)}, u32[]{:S(2)}, u32[]{:S(2)}) collective-permute-start(bf16[8,112,512]{2,1,0:T(8,128)(2,1)} %bitcast.3), channel_id=1, source_target_pairs={{0,4},{2,6},{8,0},{10,2},{16,8},{18,10},{24,16},{26,18},{28,24},{3... | collective-permute-start | bytes 2752520 | tf_op jit(solution)/shard_map/ppermute | solution.py:86
  4.2 23.9 %collective-permute-start.6 = (bf16[4,240,512]{2,1,0:T(8,128)(2,1)S(1)}, bf16[4,240,512]{2,1,0:T(8,128)(2,1)S(1)}, u32[]{:S(2)}, u32[]{:S(2)}) collective-permute-start(bf16[4,240,512]{2,1,0:T(8,128)(2,1)S(1)} %cut.2.refs_1_), channel_id=1, source_target_pairs={{0,1},{1,0},{2,3},{3,2},{4,5},{5,4},{6,7},{7,6},{8,9},{9,8},{10,11... | collective-permute-start | bytes 2949128 | tf_op jit(solution)/shard_map/ppermute | solution.py:71
  9.3 16.3 %collective-permute-start.7 = (bf16[4,128,512]{2,1,0:T(8,128)(2,1)S(1)}, bf16[4,128,512]{2,1,0:T(8,128)(2,1)S(1)}, u32[]{:S(2)}, u32[]{:S(2)}) collective-permute-start(bf16[4,128,512]{2,1,0:T(8,128)(2,1)S(1)} %get-tuple-element.34.refs_4_.refs_10_.refs_2_), channel_id=1, source_target_pairs={{0,2},{2,0},{4,6},{6,4},{8,10},{10,8},{12,14},{14,12},{16,18},{18,... | collective-permute-start | bytes 1572872 | tf_op jit(solution)/shard_map/ppermute | solution.py:71
  11.1 16.2 %collective-permute-start.8 = (bf16[4,128,512]{2,1,0:T(8,128)(2,1)S(1)}, bf16[4,128,512]{2,1,0:T(8,128)(2,1)S(1)}, u32[]{:S(2)}, u32[]{:S(2)}) collective-permute-start(bf16[4,128,512]{2,1,0:T(8,128)(2,1)S(1)} %get-tuple-element.35.refs_5_.refs_11_.refs_3_), channel_id=1, source_target_pairs={{0,2},{2,0},{4,6},{6,4},{8,10},{10,8},{12,14},{14,12},{16,18},{18,... | collective-permute-start | bytes 1572872 | tf_op jit(solution)/shard_map/ppermute | solution.py:71
  23.5 22.3 %collective-permute-start.1 = (bf16[8,112,512]{2,1,0:T(8,128)(2,1)S(1)}, bf16[8,112,512]{2,1,0:T(8,128)(2,1)S(1)}, u32[]{:S(2)}, u32[]{:S(2)}) collective-permute-start(bf16[8,112,512]{2,1,0:T(8,128)(2,1)S(1)} %collective-permute-done.refs_0_.refs_1_.refs_6_), channel_id=1, source_target_pairs={{0,8},{2,10},{8,16},{10,18},{16,24},{18,26},{24,28},{26,30},{28,20... | collective-permute-start | bytes 2752520 | tf_op jit(solution)/shard_map/ppermute | solution.py:86
  25.3 20.9 %collective-permute-start.4 = (bf16[8,112,512]{2,1,0:T(8,128)(2,1)S(1)}, bf16[8,112,512]{2,1,0:T(8,128)(2,1)S(1)}, u32[]{:S(2)}, u32[]{:S(2)}) collective-permute-start(bf16[8,112,512]{2,1,0:T(8,128)(2,1)S(1)} %collective-permute-done.3.refs_1_.refs_2_.refs_7_), channel_id=1, source_target_pairs={{0,4},{2,6},{8,0},{10,2},{16,8},{18,10},{24,16},{26,18},{28,24},{3... | collective-permute-start | bytes 2752520 | tf_op jit(solution)/shard_map/ppermute | solution.py:86
  25.5 20.3 %collective-permute-start.9 = (bf16[4,208,512]{2,1,0:T(8,128)(2,1)S(1)}, bf16[4,208,512]{2,1,0:T(8,128)(2,1)S(1)}, u32[]{:S(2)}, u32[]{:S(2)}) collective-permute-start(bf16[4,208,512]{2,1,0:T(8,128)(2,1)S(1)} %get-tuple-element.32.refs_1_), channel_id=1, source_target_pairs={{0,1},{1,0},{2,3},{3,2},{4,5},{5,4},{6,7},{7,6},{8,9},{9,8},{10,11... | collective-permute-start | bytes 2555912 | tf_op jit(solution)/shard_map/ppermute | solution.py:71
  31.7 14.1 %collective-permute-start.10 = (bf16[4,128,512]{2,1,0:T(8,128)(2,1)S(1)}, bf16[4,128,512]{2,1,0:T(8,128)(2,1)S(1)}, u32[]{:S(2)}, u32[]{:S(2)}) collective-permute-start(bf16[4,128,512]{2,1,0:T(8,128)(2,1)S(1)} %get-tuple-element.36.refs_6_.refs_12_.refs_4_), channel_id=1, source_target_pairs={{0,2},{2,0},{4,6},{6,4},{8,10},{10,8},{12,14},{14,12},{16,18},{18,... | collective-permute-start | bytes 1572872 | tf_op jit(solution)/shard_map/ppermute | solution.py:71
  31.8 14.0 %collective-permute-start.11 = (bf16[4,128,512]{2,1,0:T(8,128)(2,1)S(1)}, bf16[4,128,512]{2,1,0:T(8,128)(2,1)S(1)}, u32[]{:S(2)}, u32[]{:S(2)}) collective-permute-start(bf16[4,128,512]{2,1,0:T(8,128)(2,1)S(1)} %get-tuple-element.37.refs_7_.refs_13_.refs_5_), channel_id=1, source_target_pairs={{0,2},{2,0},{4,6},{6,4},{8,10},{10,8},{12,14},{14,12},{16,18},{18,... | collective-permute-start | bytes 1572872 | tf_op jit(solution)/shard_map/ppermute | solution.py:71
  46.8 10.7 %collective-permute-start.13 = (bf16[4,448,512]{2,1,0:T(8,128)(2,1)S(1)}, bf16[4,448,512]{2,1,0:T(8,128)(2,1)S(1)}, u32[]{:S(2)}, u32[]{:S(2)}) collective-permute-start(bf16[4,448,512]{2,1,0:T(8,128)(2,1)S(1)} %mix.2.refs_18_.refs_2_.refs_8_.refs_6_), channel_id=1, source_target_pairs={{0,2},{2,0},{4,6},{6,4},{8,10},{10,8},{12,14},{14,12},{16,18},{18,... | collective-permute-start | bytes 5505032 | tf_op jit(solution)/shard_map/ppermute | solution.py:71
  46.9 9.0 %collective-permute-start.12 = (bf16[4,64,512]{2,1,0:T(8,128)(2,1)S(1)}, bf16[4,64,512]{2,1,0:T(8,128)(2,1)S(1)}, u32[]{:S(2)}, u32[]{:S(2)}) collective-permute-start(bf16[4,64,512]{2,1,0:T(8,128)(2,1)S(1)} %get-tuple-element.33.refs_2_), channel_id=1, source_target_pairs={{0,1},{1,0},{2,3},{3,2},{4,5},{5,4},{6,7},{7,6},{8,9},{9,8},{10,11... | collective-permute-start | bytes 786440 | tf_op jit(solution)/shard_map/ppermute | solution.py:71
  48.5 22.4 %collective-permute-start.2 = (bf16[8,112,512]{2,1,0:T(8,128)(2,1)S(1)}, bf16[8,112,512]{2,1,0:T(8,128)(2,1)S(1)}, u32[]{:S(2)}, u32[]{:S(2)}) collective-permute-start(bf16[8,112,512]{2,1,0:T(8,128)(2,1)S(1)} %collective-permute-done.1.refs_0_.refs_3_.refs_8_), channel_id=1, source_target_pairs={{0,8},{2,10},{8,16},{10,18},{16,24},{18,26},{24,28},{26,30},{28,20... | collective-permute-start | bytes 2752520 | tf_op jit(solution)/shard_map/ppermute | solution.py:86
  50.1 22.1 %collective-permute-start.5 = (bf16[8,112,512]{2,1,0:T(8,128)(2,1)S(1)}, bf16[8,112,512]{2,1,0:T(8,128)(2,1)S(1)}, u32[]{:S(2)}, u32[]{:S(2)}) collective-permute-start(bf16[8,112,512]{2,1,0:T(8,128)(2,1)S(1)} %collective-permute-done.4.refs_1_.refs_4_.refs_9_), channel_id=1, source_target_pairs={{0,4},{2,6},{8,0},{10,2},{16,8},{18,10},{24,16},{26,18},{28,24},{3... | collective-permute-start | bytes 2752520 | tf_op jit(solution)/shard_map/ppermute | solution.py:86
  53.0 16.0 %collective-permute-start.15 = (bf16[1,560,512]{2,1,0:T(8,128)(2,1)S(1)}, bf16[1,560,512]{2,1,0:T(8,128)(2,1)S(1)}, u32[]{:S(2)}, u32[]{:S(2)}) collective-permute-start(bf16[1,560,512]{2,1,0:T(8,128)(2,1)S(1)} %get-tuple-element.44.refs_5_.refs_0_), channel_id=1, source_target_pairs={{0,1},{1,0},{2,3},{3,2},{4,5},{5,4},{6,7},{7,6},{8,9},{9,8},{10,11... | collective-permute-start | bytes 1720328 | tf_op jit(solution)/shard_map/ppermute | solution.py:71
  60.1 31.3 %collective-permute-start.22 = (bf16[4,560,512]{2,1,0:T(8,128)(2,1)S(1)}, bf16[4,560,512]{2,1,0:T(8,128)(2,1)S(1)}, u32[]{:S(2)}, u32[]{:S(2)}) collective-permute-start(bf16[4,560,512]{2,1,0:T(8,128)(2,1)S(1)} %get-tuple-element.54), channel_id=1, source_target_pairs={{0,2},{2,0},{4,6},{6,4},{8,10},{10,8},{12,14},{14,12},{16,18},{18,... | collective-permute-start | bytes 6881288 | tf_op jit(solution)/shard_map/ppermute | solution.py:71
  60.3 21.0 %collective-permute-start.19 = (bf16[1,560,512]{2,1,0:T(8,128)(2,1)S(1)}, bf16[1,560,512]{2,1,0:T(8,128)(2,1)S(1)}, u32[]{:S(2)}, u32[]{:S(2)}) collective-permute-start(bf16[1,560,512]{2,1,0:T(8,128)(2,1)S(1)} %get-tuple-element.47.refs_2_.refs_0_), channel_id=1, source_target_pairs={{0,1},{1,0},{2,3},{3,2},{4,5},{5,4},{6,7},{7,6},{8,9},{9,8},{10,11... | collective-permute-start | bytes 1720328 | tf_op jit(solution)/shard_map/ppermute | solution.py:71
  72.3 11.5 %collective-permute-start.17 = (bf16[4,112,512]{2,1,0:T(8,128)(2,1)S(1)}, bf16[4,112,512]{2,1,0:T(8,128)(2,1)S(1)}, u32[]{:S(2)}, u32[]{:S(2)}) collective-permute-start(bf16[4,112,512]{2,1,0:T(8,128)(2,1)S(1)} %get-tuple-element.48.refs_0_), channel_id=1, source_target_pairs={{0,8},{2,10},{8,16},{10,18},{16,24},{18,26},{24,28},{26,30},{28,20... | collective-permute-start | bytes 1376264 | tf_op jit(solution)/shard_map/ppermute | solution.py:86
  73.9 11.2 %collective-permute-start.18 = (bf16[4,112,512]{2,1,0:T(8,128)(2,1)S(1)}, bf16[4,112,512]{2,1,0:T(8,128)(2,1)S(1)}, u32[]{:S(2)}, u32[]{:S(2)}) collective-permute-start(bf16[4,112,512]{2,1,0:T(8,128)(2,1)S(1)} %get-tuple-element.49.refs_1_), channel_id=1, source_target_pairs={{0,4},{2,6},{8,0},{10,2},{16,8},{18,10},{24,16},{26,18},{28,24},{3... | collective-permute-start | bytes 1376264 | tf_op jit(solution)/shard_map/ppermute | solution.py:86
  76.4 14.7 %collective-permute-start.16 = (bf16[2,224,512]{2,1,0:T(8,128)(2,1)S(1)}, bf16[2,224,512]{2,1,0:T(8,128)(2,1)S(1)}, u32[]{:S(2)}, u32[]{:S(2)}) collective-permute-start(bf16[2,224,512]{2,1,0:T(8,128)(2,1)S(1)} %get-tuple-element.50.refs_2_.refs_0_), channel_id=1, source_target_pairs={{0,1},{1,0},{2,3},{3,2},{4,5},{5,4},{6,7},{7,6},{8,9},{9,8},{10,11... | collective-permute-start | bytes 1376264 | tf_op jit(solution)/shard_map/ppermute | solution.py:71
  83.5 7.9 %collective-permute-start.21 = (bf16[2,560,512]{2,1,0:T(8,128)(2,1)S(1)}, bf16[2,560,512]{2,1,0:T(8,128)(2,1)S(1)}, u32[]{:S(2)}, u32[]{:S(2)}) collective-permute-start(bf16[2,560,512]{2,1,0:T(8,128)(2,1)S(1)} %join.5.refs_0_), channel_id=1, source_target_pairs={{0,2},{2,0},{4,6},{6,4},{8,10},{10,8},{12,14},{14,12},{16,18},{18,... | collective-permute-start | bytes 3440648 | tf_op jit(solution)/shard_map/ppermute | solution.py:71
  86.4 8.5 %collective-permute-start.20 = (bf16[2,112,512]{2,1,0:T(8,128)(2,1)S(1)}, bf16[2,112,512]{2,1,0:T(8,128)(2,1)S(1)}, u32[]{:S(2)}, u32[]{:S(2)}) collective-permute-start(bf16[2,112,512]{2,1,0:T(8,128)(2,1)S(1)} %get-tuple-element.53.refs_4_.refs_0_.refs_2_), channel_id=1, source_target_pairs={{0,1},{1,0},{2,3},{3,2},{4,5},{5,4},{6,7},{7,6},{8,9},{9,8},{10,11... | collective-permute-start | bytes 688136 | tf_op jit(solution)/shard_map/ppermute | solution.py:71
  87.0 8.4 %collective-permute-start.25 = (bf16[4,336,512]{2,1,0:T(8,128)(2,1)S(1)}, bf16[4,336,512]{2,1,0:T(8,128)(2,1)S(1)}, u32[]{:S(2)}, u32[]{:S(2)}) collective-permute-start(bf16[4,336,512]{2,1,0:T(8,128)(2,1)S(1)} %get-tuple-element.58), channel_id=1, source_target_pairs={{0,2},{2,0},{4,6},{6,4},{8,10},{10,8},{12,14},{14,12},{16,18},{18,... | collective-permute-start | bytes 4128776 | tf_op jit(solution)/shard_map/ppermute | solution.py:71
  91.2 4.2 %collective-permute-start.23 = (bf16[2,224,512]{2,1,0:T(8,128)(2,1)S(1)}, bf16[2,224,512]{2,1,0:T(8,128)(2,1)S(1)}, u32[]{:S(2)}, u32[]{:S(2)}) collective-permute-start(bf16[2,224,512]{2,1,0:T(8,128)(2,1)S(1)} %join.6.refs_0_.refs_1_), channel_id=1, source_target_pairs={{0,2},{2,0},{4,6},{6,4},{8,10},{10,8},{12,14},{14,12},{16,18},{18,... | collective-permute-start | bytes 1376264 | tf_op jit(solution)/shard_map/ppermute | solution.py:71
  (6 other events, 14.5 us)

commit v8 on v7

--- a/solution.py
+++ b/solution.py
@@ -488,11 +488,14 @@
     )
     m_c = join(*[[((p_c, h), (p_c_sent, 1 - h))] for h in range(2)], after=begun)
     m_c_theirs = to_core(m_c)
-    middles = [m_c, m_b_theirs, m_c_theirs]
-    vectors = [(same_d, taken, same_d.shape[1]), handed_d]
+    middles, vectors = [m_b_theirs], [(handed_d, 0, rows_b)]
     if taken < rows_b:
         middles = [(m_b, taken, rows_b)] + middles
-    (out,) = residual(middles, vectors, [0, 1], begun, last=True)
+        vectors = [(same_d, taken, rows_b)] + vectors
+    begun = residual(middles, vectors, [0, 1], begun, after=[m_c])
+    end = same_d.shape[1]
+    vectors = [(same_d, rows_b, end), (handed_d, rows_b, end)]
+    (out,) = residual([m_c, m_c_theirs], vectors, [0, 1], begun, last=True)
     return out
 
 

time: 100 us -> 99.8 us (level)
  waiting for transfers between devices: 46.6 us -> 45.4 us
    ppermute x18, waiting for transfers between devices: 29.6 us -> 28.4 us  [swap(): lax.ppermute(x, axis, [(i, i ^ 1 << bit) for i in range(lax.axis_size(axi...]
    pallas_call x22 -> x23, Pallas kernels: 32.9 us -> 33.4 us  [call(): pl.pallas_call(kernel, grid=grid, in_specs=[*in_specs, *[ANYWHERE] * extr...]
  transfers between devices with their start and end apart: 26 -> 26, of which waited for: 15 -> 13; matrix products, arithmetic and copies ran while one was open for 0% -> 0% of each run, Pallas kernels for 29% -> 31%
where the time goes in v8:
time: 99.8 us; the launch traced here: 99.5 us
  waiting for transfers between devices  45.4 us (45%)
  Pallas kernels  33.4 us (33%)
  starting transfers between devices  20.3 us (20%)
    pallas_call x23, Pallas kernels, call(): pl.pallas_call(kernel, grid=grid, in_specs=[*in_specs, *[ANYWHERE] * extr...  33.4 us
    ppermute x18, waiting for transfers between devices, swap(): lax.ppermute(x, axis, [(i, i ^ 1 << bit) for i in range(lax.axis_size(axi...  28.4 us
    ppermute x8, waiting for transfers between devices, along_ring(): return lax.ppermute(x, 'pair', pairs)  17 us
    ppermute x18, starting transfers between devices, swap(): lax.ppermute(x, axis, [(i, i ^ 1 << bit) for i in range(lax.axis_size(axi...  11.2 us
    ppermute x8, starting transfers between devices, along_ring(): return lax.ppermute(x, 'pair', pairs)  9.16 us
  transfers between devices with their start and end apart: 26, of which 13 were waited for; matrix products, arithmetic and copies ran while one was open for 0% of the time, Pallas kernels for 31%

profile of v8, /device:TPU:0, one launch (start us, length us, event | category | flops | bytes accessed | tf_op | source)
XLA Modules:
  0.0 99.5 jit_solution(964849006868738921)
XLA Ops:
  0.0 3.0 %collective-permute-start = (bf16[8,112,512]{2,1,0:T(8,128)(2,1)}, bf16[8,112,512]{2,1,0:T(8,128)(2,1)S(1)}, u32[]{:S(2)}, u32[]{:S(2)}) collective-permute-start(bf16[8,112,512]{2,1,0:T(8,128)(2,1)} %bitcast.2), channel_id=1, source_target_pairs={{0,8},{2,10},{8,16},{10,18},{16,24},{18,26},{24,28},{26,30},{28,20... | collective-permute-start | bytes 2752520 | tf_op jit(solution)/shard_map/ppermute | solution.py:86
  4.2 2.0 %collective-permute-start.6 = (bf16[4,240,512]{2,1,0:T(8,128)(2,1)S(1)}, bf16[4,240,512]{2,1,0:T(8,128)(2,1)S(1)}, u32[]{:S(2)}, u32[]{:S(2)}) collective-permute-start(bf16[4,240,512]{2,1,0:T(8,128)(2,1)S(1)} %cut.2.refs_1_), channel_id=1, source_target_pairs={{0,1},{1,0},{2,3},{3,2},{4,5},{5,4},{6,7},{7,6},{8,9},{9,8},{10,11... | collective-permute-start | bytes 2949128 | tf_op jit(solution)/shard_map/ppermute | solution.py:71
  7.5 1.8 %turn.4 = (bf16[4,128,512]{2,1,0:T(8,128)(2,1)S(1)}, bf16[4,128,512]{2,1,0:T(8,128)(2,1)S(1)}) custom-call(bf16[4,1024,512]{2,1,0:T(8,128)(2,1)} %refs_0_.13, bf16[4,208,512]{2,1,0:T(8,128)(2,1)S(1)} %get-tuple-element.34.refs_1_, bf16[4,64,512]{2,1,0:T(8,128)(2,1)S(1)} %get-tuple-element.35.refs_2_), custom_call_target="tpu_custom_call" | custom-call | flops 1 | bytes 1 | tf_op jit(solution)/shard_map/turn/pallas_call | solution.py:47
  9.4 1.8 %turn.5 = (bf16[4,128,512]{2,1,0:T(8,128)(2,1)S(1)}, bf16[4,128,512]{2,1,0:T(8,128)(2,1)S(1)}) custom-call(bf16[4,1024,512]{2,1,0:T(8,128)(2,1)} %refs_0_.13, bf16[4,208,512]{2,1,0:T(8,128)(2,1)S(1)} %get-tuple-element.34.refs_1_, bf16[4,64,512]{2,1,0:T(8,128)(2,1)S(1)} %get-tuple-element.35.refs_2_), custom_call_target="tpu_custom_call" | custom-call | flops 1 | bytes 1 | tf_op jit(solution)/shard_map/turn/pallas_call | solution.py:47
  11.7 11.8 %collective-permute-done.refs_0_.refs_1_.refs_6_ = bf16[8,112,512]{2,1,0:T(8,128)(2,1)S(1)} collective-permute-done((bf16[8,112,512]{2,1,0:T(8,128)(2,1)}, bf16[8,112,512]{2,1,0:T(8,128)(2,1)S(1)}, u32[]{:S(2)}, u32[]{:S(2)}) %collective-permute-start) | collective-permute-done | bytes 917536 | tf_op jit(solution)/shard_map/ppermute | solution.py:86
  23.5 1.8 %collective-permute-start.1 = (bf16[8,112,512]{2,1,0:T(8,128)(2,1)S(1)}, bf16[8,112,512]{2,1,0:T(8,128)(2,1)S(1)}, u32[]{:S(2)}, u32[]{:S(2)}) collective-permute-start(bf16[8,112,512]{2,1,0:T(8,128)(2,1)S(1)} %collective-permute-done.refs_0_.refs_1_.refs_6_), channel_id=1, source_target_pairs={{0,8},{2,10},{8,16},{10,18},{16,24},{18,26},{24,28},{26,30},{28,20... | collective-permute-start | bytes 2752520 | tf_op jit(solution)/shard_map/ppermute | solution.py:86
  25.5 1.8 %collective-permute-start.11 = (bf16[4,208,512]{2,1,0:T(8,128)(2,1)S(1)}, bf16[4,208,512]{2,1,0:T(8,128)(2,1)S(1)}, u32[]{:S(2)}, u32[]{:S(2)}) collective-permute-start(bf16[4,208,512]{2,1,0:T(8,128)(2,1)S(1)} %get-tuple-element.34.refs_1_), channel_id=1, source_target_pairs={{0,1},{1,0},{2,3},{3,2},{4,5},{5,4},{6,7},{7,6},{8,9},{9,8},{10,11... | collective-permute-start | bytes 2555912 | tf_op jit(solution)/shard_map/ppermute | solution.py:71
  28.1 1.7 %turn.6 = (bf16[4,128,512]{2,1,0:T(8,128)(2,1)S(1)}, bf16[4,128,512]{2,1,0:T(8,128)(2,1)S(1)}) custom-call(bf16[4,1024,512]{2,1,0:T(8,128)(2,1)} %refs_0_.13, f32[8,128]{1,0:T(8,128)S(1)} %wall.5.refs_1_), custom_call_target="tpu_custom_call" | custom-call | flops 1 | bytes 1 | tf_op jit(solution)/shard_map/turn/pallas_call | solution.py:47
  29.9 1.8 %turn.7 = (bf16[4,128,512]{2,1,0:T(8,128)(2,1)S(1)}, bf16[4,128,512]{2,1,0:T(8,128)(2,1)S(1)}) custom-call(bf16[4,1024,512]{2,1,0:T(8,128)(2,1)} %refs_0_.13, f32[8,128]{1,0:T(8,128)S(1)} %wall.5.refs_1_), custom_call_target="tpu_custom_call" | custom-call | flops 1 | bytes 1 | tf_op jit(solution)/shard_map/turn/pallas_call | solution.py:47
  32.3 3.2 %diagonal.1 = (f32[4,512,512]{2,1,0:T(8,128)S(1)}, f32[4,512,512]{2,1,0:T(8,128)S(1)}) custom-call(bf16[4,1024,512]{2,1,0:T(8,128)(2,1)} %refs_0_.13, f32[2,1,512]{2,1,0:T(1,128)S(1)} %bitcast.6, f32[8]{0:T(128)S(1)} %copy-done.2, f32[8]{0:T(128)S(1)} %copy-done.3, bf16[4,128,512]{2,1,0:T(8,128)(2,1)S(1)} %get-tuple-element.36.refs_4_.refs_10_.refs_2_, ...), custom_call_target="tpu_custom_call" | custom-call | flops 1 | bytes 1 | tf_op jit(solution)/shard_map/diagonal/pallas_call | solution.py:47
  35.4 10.3 %collective-permute-done.11.refs_2_.refs_5_ = bf16[4,208,512]{2,1,0:T(8,128)(2,1)S(1)} collective-permute-done((bf16[4,208,512]{2,1,0:T(8,128)(2,1)S(1)}, bf16[4,208,512]{2,1,0:T(8,128)(2,1)S(1)}, u32[]{:S(2)}, u32[]{:S(2)}) %collective-permute-start.11) | collective-permute-done | bytes 852000 | tf_op jit(solution)/shard_map/ppermute | solution.py:71
  50.5 2.5 %partial.4 = (bf16[1,560,512]{2,1,0:T(8,128)(2,1)S(1)}, bf16[4,560,512]{2,1,0:T(8,128)(2,1)S(1)}, bf16[4,560,512]{2,1,0:T(8,128)(2,1)S(1)}) custom-call(bf16[8,112,512]{2,1,0:T(8,128)(2,1)S(1)} %bitcast.4, bf16[8,112,512]{2,1,0:T(8,128)(2,1)S(1)} %collective-permute-done.refs_0_.refs_1_.refs_6_, ...), custom_call_target="tpu_custom_call" | custom-call | flops 1 | bytes 1 | tf_op jit(solution)/shard_map/partial/pallas_call | solution.py:47
  53.6 2.2 %collective-permute-done.12.refs_4_ = bf16[4,64,512]{2,1,0:T(8,128)(2,1)S(1)} collective-permute-done((bf16[4,64,512]{2,1,0:T(8,128)(2,1)S(1)}, bf16[4,64,512]{2,1,0:T(8,128)(2,1)S(1)}, u32[]{:S(2)}, u32[]{:S(2)}) %collective-permute-start.12) | collective-permute-done | bytes 262176 | tf_op jit(solution)/shard_map/ppermute | solution.py:71
  57.5 2.5 %partial.5 = (bf16[1,560,512]{2,1,0:T(8,128)(2,1)S(1)}, bf16[4,560,512]{2,1,0:T(8,128)(2,1)S(1)}) custom-call(bf16[4,560,512]{2,1,0:T(8,128)(2,1)S(1)} %get-tuple-element.46.refs_0_.refs_1_, bf16[4,560,512]{2,1,0:T(8,128)(2,1)S(1)} %get-tuple-element.47.refs_1_, bf16[4,448,512]{2,1,0:T(8,128)(2,1)S(1)} %mix.2.refs_18_.refs_2_.refs_8_.refs_6_, ...), custom_call_target="tpu_custom_call" | custom-call | flops 1 | bytes 1 | tf_op jit(solution)/shard_map/partial/pallas_call | solution.py:47
  60.3 1.8 %collective-permute-start.18 = (bf16[1,560,512]{2,1,0:T(8,128)(2,1)S(1)}, bf16[1,560,512]{2,1,0:T(8,128)(2,1)S(1)}, u32[]{:S(2)}, u32[]{:S(2)}) collective-permute-start(bf16[1,560,512]{2,1,0:T(8,128)(2,1)S(1)} %get-tuple-element.49.refs_2_.refs_0_), channel_id=1, source_target_pairs={{0,1},{1,0},{2,3},{3,2},{4,5},{5,4},{6,7},{7,6},{8,9},{9,8},{10,11... | collective-permute-start | bytes 1720328 | tf_op jit(solution)/shard_map/ppermute | solution.py:71
  62.0 7.0 %collective-permute-done.15.refs_3_.refs_1_ = bf16[1,560,512]{2,1,0:T(8,128)(2,1)S(1)} collective-permute-done((bf16[1,560,512]{2,1,0:T(8,128)(2,1)S(1)}, bf16[1,560,512]{2,1,0:T(8,128)(2,1)S(1)}, u32[]{:S(2)}, u32[]{:S(2)}) %collective-permute-start.15) | collective-permute-done | bytes 573472 | tf_op jit(solution)/shard_map/ppermute | solution.py:71
  69.0 1.9 %collective-permute-done.2.refs_0_.refs_2_ = bf16[8,112,512]{2,1,0:T(8,128)(2,1)S(1)} collective-permute-done((bf16[8,112,512]{2,1,0:T(8,128)(2,1)S(1)}, bf16[8,112,512]{2,1,0:T(8,128)(2,1)S(1)}, u32[]{:S(2)}, u32[]{:S(2)}) %collective-permute-start.2) | collective-permute-done | bytes 917536 | tf_op jit(solution)/shard_map/ppermute | solution.py:86
  74.3 2.1 %partial.6 = (bf16[2,224,512]{2,1,0:T(8,128)(2,1)S(1)}, bf16[4,224,512]{2,1,0:T(8,128)(2,1)S(1)}, bf16[4,224,512]{2,1,0:T(8,128)(2,1)S(1)}) custom-call(bf16[8,112,512]{2,1,0:T(8,128)(2,1)S(1)} %collective-permute-done.2.refs_0_.refs_2_, bf16[8,112,512]{2,1,0:T(8,128)(2,1)S(1)} %collective-permute-done.5.refs_1_.refs_3_, ...), custom_call_target="tpu_custom_call" | custom-call | flops 1 | bytes 1 | tf_op jit(solution)/shard_map/partial/pallas_call | solution.py:47
  77.2 1.8 %residual.5.refs_4_.refs_5_ = f32[4,512,512]{2,1,0:T(8,128)S(1)} custom-call(bf16[1,560,512]{2,1,0:T(8,128)(2,1)S(1)} %join.4.refs_0_, bf16[4,560,512]{2,1,0:T(8,128)(2,1)S(1)} %get-tuple-element.46.refs_0_.refs_1_, f32[4,512,512]{2,1,0:T(8,128)S(1)} %get-tuple-element.45.refs_6_.refs_2_), custom_call_target="tpu_custom_call" | custom-call | flops 1 | bytes 1 | tf_op jit(solution)/shard_map/residual/pallas_call | solution.py:47
  79.0 2.3 %collective-permute-done.18.refs_1_ = bf16[1,560,512]{2,1,0:T(8,128)(2,1)S(1)} collective-permute-done((bf16[1,560,512]{2,1,0:T(8,128)(2,1)S(1)}, bf16[1,560,512]{2,1,0:T(8,128)(2,1)S(1)}, u32[]{:S(2)}, u32[]{:S(2)}) %collective-permute-start.18) | collective-permute-done | bytes 573472 | tf_op jit(solution)/shard_map/ppermute | solution.py:71
  81.6 1.9 %residual.6.refs_2_.refs_4_ = f32[4,512,512]{2,1,0:T(8,128)S(1)} custom-call(bf16[2,560,512]{2,1,0:T(8,128)(2,1)S(1)} %join.5.refs_0_, bf16[4,560,512]{2,1,0:T(8,128)(2,1)S(1)} %get-tuple-element.46.refs_0_.refs_1_, f32[4,512,512]{2,1,0:T(8,128)S(1)} %get-tuple-element.44.refs_5_.refs_2_), custom_call_target="tpu_custom_call" | custom-call | flops 1 | bytes 1 | tf_op jit(solution)/shard_map/residual/pallas_call | solution.py:47
  87.0 4.1 %collective-permute-done.21.refs_1_.refs_3_ = bf16[2,224,512]{2,1,0:T(8,128)(2,1)S(1)} collective-permute-done((bf16[2,224,512]{2,1,0:T(8,128)(2,1)S(1)}, bf16[2,224,512]{2,1,0:T(8,128)(2,1)S(1)}, u32[]{:S(2)}, u32[]{:S(2)}) %collective-permute-start.21) | collective-permute-done | bytes 458784 | tf_op jit(solution)/shard_map/ppermute | solution.py:71
  91.8 3.5 %residual.7 = (f32[4,512,512]{2,1,0:T(8,128)S(1)}, f32[4,512,512]{2,1,0:T(8,128)S(1)}) custom-call(bf16[2,560,512]{2,1,0:T(8,128)(2,1)S(1)} %collective-permute-done.20.refs_0_, bf16[2,224,512]{2,1,0:T(8,128)(2,1)S(1)} %join.6.refs_0_.refs_1_, bf16[4,560,512]{2,1,0:T(8,128)(2,1)S(1)} %collective-permute-done.22.refs_2_, ...), custom_call_target="tpu_custom_call" | custom-call | flops 1 | bytes 1 | tf_op jit(solution)/shard_map/residual/pallas_call | solution.py:47
  96.9 2.4 %residual.9 = bf16[4,1024,512]{2,1,0:T(8,128)(2,1)} custom-call(bf16[2,112,512]{2,1,0:T(8,128)(2,1)S(1)} %join.7.refs_6_.refs_0_, bf16[2,112,512]{2,1,0:T(8,128)(2,1)S(1)} %collective-permute-done.23.refs_1_, bf16[4,336,512]{2,1,0:T(8,128)(2,1)S(1)} %get-tuple-element.57.refs_3_.refs_2_, bf16[4,336,512]{2,1,0:T(8,128)(2,1)S(1)} %collective-permute-done.24.refs_3_, ...), custom_call_target="tpu_custom_call" | custom-call | flops 1 | bytes 1 | tf_op jit(solution)/shard_map/residual/pallas_call | solution.py:47
  (64 shorter events, 22.1 us)
Async XLA Ops:
  0.0 23.5 %collective-permute-start = (bf16[8,112,512]{2,1,0:T(8,128)(2,1)}, bf16[8,112,512]{2,1,0:T(8,128)(2,1)S(1)}, u32[]{:S(2)}, u32[]{:S(2)}) collective-permute-start(bf16[8,112,512]{2,1,0:T(8,128)(2,1)} %bitcast.2), channel_id=1, source_target_pairs={{0,8},{2,10},{8,16},{10,18},{16,24},{18,26},{24,28},{26,30},{28,20... | collective-permute-start | bytes 2752520 | tf_op jit(solution)/shard_map/ppermute | solution.py:86
  3.0 22.3 %collective-permute-start.3 = (bf16[8,112,512]{2,1,0:T(8,128)(2,1)}, bf16[8,112,512]{2,1,0:T(8,128)(2,1)S(1)}, u32[]{:S(2)}, u32[]{:S(2)}) collective-permute-start(bf16[8,112,512]{2,1,0:T(8,128)(2,1)} %bitcast.3), channel_id=1, source_target_pairs={{0,4},{2,6},{8,0},{10,2},{16,8},{18,10},{24,16},{26,18},{28,24},{3... | collective-permute-start | bytes 2752520 | tf_op jit(solution)/shard_map/ppermute | solution.py:86
  4.2 23.9 %collective-permute-start.6 = (bf16[4,240,512]{2,1,0:T(8,128)(2,1)S(1)}, bf16[4,240,512]{2,1,0:T(8,128)(2,1)S(1)}, u32[]{:S(2)}, u32[]{:S(2)}) collective-permute-start(bf16[4,240,512]{2,1,0:T(8,128)(2,1)S(1)} %cut.2.refs_1_), channel_id=1, source_target_pairs={{0,1},{1,0},{2,3},{3,2},{4,5},{5,4},{6,7},{7,6},{8,9},{9,8},{10,11... | collective-permute-start | bytes 2949128 | tf_op jit(solution)/shard_map/ppermute | solution.py:71
  9.3 16.3 %collective-permute-start.7 = (bf16[4,128,512]{2,1,0:T(8,128)(2,1)S(1)}, bf16[4,128,512]{2,1,0:T(8,128)(2,1)S(1)}, u32[]{:S(2)}, u32[]{:S(2)}) collective-permute-start(bf16[4,128,512]{2,1,0:T(8,128)(2,1)S(1)} %get-tuple-element.36.refs_4_.refs_10_.refs_2_), channel_id=1, source_target_pairs={{0,2},{2,0},{4,6},{6,4},{8,10},{10,8},{12,14},{14,12},{16,18},{18,... | collective-permute-start | bytes 1572872 | tf_op jit(solution)/shard_map/ppermute | solution.py:71
  11.1 16.2 %collective-permute-start.8 = (bf16[4,128,512]{2,1,0:T(8,128)(2,1)S(1)}, bf16[4,128,512]{2,1,0:T(8,128)(2,1)S(1)}, u32[]{:S(2)}, u32[]{:S(2)}) collective-permute-start(bf16[4,128,512]{2,1,0:T(8,128)(2,1)S(1)} %get-tuple-element.37.refs_5_.refs_11_.refs_3_), channel_id=1, source_target_pairs={{0,2},{2,0},{4,6},{6,4},{8,10},{10,8},{12,14},{14,12},{16,18},{18,... | collective-permute-start | bytes 1572872 | tf_op jit(solution)/shard_map/ppermute | solution.py:71
  23.5 22.3 %collective-permute-start.1 = (bf16[8,112,512]{2,1,0:T(8,128)(2,1)S(1)}, bf16[8,112,512]{2,1,0:T(8,128)(2,1)S(1)}, u32[]{:S(2)}, u32[]{:S(2)}) collective-permute-start(bf16[8,112,512]{2,1,0:T(8,128)(2,1)S(1)} %collective-permute-done.refs_0_.refs_1_.refs_6_), channel_id=1, source_target_pairs={{0,8},{2,10},{8,16},{10,18},{16,24},{18,26},{24,28},{26,30},{28,20... | collective-permute-start | bytes 2752520 | tf_op jit(solution)/shard_map/ppermute | solution.py:86
  25.3 20.9 %collective-permute-start.4 = (bf16[8,112,512]{2,1,0:T(8,128)(2,1)S(1)}, bf16[8,112,512]{2,1,0:T(8,128)(2,1)S(1)}, u32[]{:S(2)}, u32[]{:S(2)}) collective-permute-start(bf16[8,112,512]{2,1,0:T(8,128)(2,1)S(1)} %collective-permute-done.3.refs_1_.refs_2_.refs_7_), channel_id=1, source_target_pairs={{0,4},{2,6},{8,0},{10,2},{16,8},{18,10},{24,16},{26,18},{28,24},{3... | collective-permute-start | bytes 2752520 | tf_op jit(solution)/shard_map/ppermute | solution.py:86
  25.5 20.3 %collective-permute-start.11 = (bf16[4,208,512]{2,1,0:T(8,128)(2,1)S(1)}, bf16[4,208,512]{2,1,0:T(8,128)(2,1)S(1)}, u32[]{:S(2)}, u32[]{:S(2)}) collective-permute-start(bf16[4,208,512]{2,1,0:T(8,128)(2,1)S(1)} %get-tuple-element.34.refs_1_), channel_id=1, source_target_pairs={{0,1},{1,0},{2,3},{3,2},{4,5},{5,4},{6,7},{7,6},{8,9},{9,8},{10,11... | collective-permute-start | bytes 2555912 | tf_op jit(solution)/shard_map/ppermute | solution.py:71
  31.7 14.1 %collective-permute-start.10 = (bf16[4,128,512]{2,1,0:T(8,128)(2,1)S(1)}, bf16[4,128,512]{2,1,0:T(8,128)(2,1)S(1)}, u32[]{:S(2)}, u32[]{:S(2)}) collective-permute-start(bf16[4,128,512]{2,1,0:T(8,128)(2,1)S(1)} %get-tuple-element.39.refs_7_.refs_13_.refs_5_), channel_id=1, source_target_pairs={{0,2},{2,0},{4,6},{6,4},{8,10},{10,8},{12,14},{14,12},{16,18},{18,... | collective-permute-start | bytes 1572872 | tf_op jit(solution)/shard_map/ppermute | solution.py:71
  31.8 14.0 %collective-permute-start.9 = (bf16[4,128,512]{2,1,0:T(8,128)(2,1)S(1)}, bf16[4,128,512]{2,1,0:T(8,128)(2,1)S(1)}, u32[]{:S(2)}, u32[]{:S(2)}) collective-permute-start(bf16[4,128,512]{2,1,0:T(8,128)(2,1)S(1)} %get-tuple-element.38.refs_6_.refs_12_.refs_4_), channel_id=1, source_target_pairs={{0,2},{2,0},{4,6},{6,4},{8,10},{10,8},{12,14},{14,12},{16,18},{18,... | collective-permute-start | bytes 1572872 | tf_op jit(solution)/shard_map/ppermute | solution.py:71
  46.8 10.7 %collective-permute-start.13 = (bf16[4,448,512]{2,1,0:T(8,128)(2,1)S(1)}, bf16[4,448,512]{2,1,0:T(8,128)(2,1)S(1)}, u32[]{:S(2)}, u32[]{:S(2)}) collective-permute-start(bf16[4,448,512]{2,1,0:T(8,128)(2,1)S(1)} %mix.2.refs_18_.refs_2_.refs_8_.refs_6_), channel_id=1, source_target_pairs={{0,2},{2,0},{4,6},{6,4},{8,10},{10,8},{12,14},{14,12},{16,18},{18,... | collective-permute-start | bytes 5505032 | tf_op jit(solution)/shard_map/ppermute | solution.py:71
  46.9 9.0 %collective-permute-start.12 = (bf16[4,64,512]{2,1,0:T(8,128)(2,1)S(1)}, bf16[4,64,512]{2,1,0:T(8,128)(2,1)S(1)}, u32[]{:S(2)}, u32[]{:S(2)}) collective-permute-start(bf16[4,64,512]{2,1,0:T(8,128)(2,1)S(1)} %get-tuple-element.35.refs_2_), channel_id=1, source_target_pairs={{0,1},{1,0},{2,3},{3,2},{4,5},{5,4},{6,7},{7,6},{8,9},{9,8},{10,11... | collective-permute-start | bytes 786440 | tf_op jit(solution)/shard_map/ppermute | solution.py:71
  48.5 22.4 %collective-permute-start.2 = (bf16[8,112,512]{2,1,0:T(8,128)(2,1)S(1)}, bf16[8,112,512]{2,1,0:T(8,128)(2,1)S(1)}, u32[]{:S(2)}, u32[]{:S(2)}) collective-permute-start(bf16[8,112,512]{2,1,0:T(8,128)(2,1)S(1)} %collective-permute-done.1.refs_0_.refs_3_.refs_8_), channel_id=1, source_target_pairs={{0,8},{2,10},{8,16},{10,18},{16,24},{18,26},{24,28},{26,30},{28,20... | collective-permute-start | bytes 2752520 | tf_op jit(solution)/shard_map/ppermute | solution.py:86
  50.1 22.1 %collective-permute-start.5 = (bf16[8,112,512]{2,1,0:T(8,128)(2,1)S(1)}, bf16[8,112,512]{2,1,0:T(8,128)(2,1)S(1)}, u32[]{:S(2)}, u32[]{:S(2)}) collective-permute-start(bf16[8,112,512]{2,1,0:T(8,128)(2,1)S(1)} %collective-permute-done.4.refs_1_.refs_4_.refs_9_), channel_id=1, source_target_pairs={{0,4},{2,6},{8,0},{10,2},{16,8},{18,10},{24,16},{26,18},{28,24},{3... | collective-permute-start | bytes 2752520 | tf_op jit(solution)/shard_map/ppermute | solution.py:86
  53.0 16.0 %collective-permute-start.15 = (bf16[1,560,512]{2,1,0:T(8,128)(2,1)S(1)}, bf16[1,560,512]{2,1,0:T(8,128)(2,1)S(1)}, u32[]{:S(2)}, u32[]{:S(2)}) collective-permute-start(bf16[1,560,512]{2,1,0:T(8,128)(2,1)S(1)} %get-tuple-element.48.refs_5_.refs_0_), channel_id=1, source_target_pairs={{0,1},{1,0},{2,3},{3,2},{4,5},{5,4},{6,7},{7,6},{8,9},{9,8},{10,11... | collective-permute-start | bytes 1720328 | tf_op jit(solution)/shard_map/ppermute | solution.py:71
  60.1 31.7 %collective-permute-start.22 = (bf16[4,560,512]{2,1,0:T(8,128)(2,1)S(1)}, bf16[4,560,512]{2,1,0:T(8,128)(2,1)S(1)}, u32[]{:S(2)}, u32[]{:S(2)}) collective-permute-start(bf16[4,560,512]{2,1,0:T(8,128)(2,1)S(1)} %get-tuple-element.56), channel_id=1, source_target_pairs={{0,2},{2,0},{4,6},{6,4},{8,10},{10,8},{12,14},{14,12},{16,18},{18,... | collective-permute-start | bytes 6881288 | tf_op jit(solution)/shard_map/ppermute | solution.py:71
  60.3 21.0 %collective-permute-start.18 = (bf16[1,560,512]{2,1,0:T(8,128)(2,1)S(1)}, bf16[1,560,512]{2,1,0:T(8,128)(2,1)S(1)}, u32[]{:S(2)}, u32[]{:S(2)}) collective-permute-start(bf16[1,560,512]{2,1,0:T(8,128)(2,1)S(1)} %get-tuple-element.49.refs_2_.refs_0_), channel_id=1, source_target_pairs={{0,1},{1,0},{2,3},{3,2},{4,5},{5,4},{6,7},{7,6},{8,9},{9,8},{10,11... | collective-permute-start | bytes 1720328 | tf_op jit(solution)/shard_map/ppermute | solution.py:71
  72.3 11.5 %collective-permute-start.16 = (bf16[4,112,512]{2,1,0:T(8,128)(2,1)S(1)}, bf16[4,112,512]{2,1,0:T(8,128)(2,1)S(1)}, u32[]{:S(2)}, u32[]{:S(2)}) collective-permute-start(bf16[4,112,512]{2,1,0:T(8,128)(2,1)S(1)} %get-tuple-element.50.refs_0_), channel_id=1, source_target_pairs={{0,8},{2,10},{8,16},{10,18},{16,24},{18,26},{24,28},{26,30},{28,20... | collective-permute-start | bytes 1376264 | tf_op jit(solution)/shard_map/ppermute | solution.py:86
  73.9 11.2 %collective-permute-start.17 = (bf16[4,112,512]{2,1,0:T(8,128)(2,1)S(1)}, bf16[4,112,512]{2,1,0:T(8,128)(2,1)S(1)}, u32[]{:S(2)}, u32[]{:S(2)}) collective-permute-start(bf16[4,112,512]{2,1,0:T(8,128)(2,1)S(1)} %get-tuple-element.51.refs_1_), channel_id=1, source_target_pairs={{0,4},{2,6},{8,0},{10,2},{16,8},{18,10},{24,16},{26,18},{28,24},{3... | collective-permute-start | bytes 1376264 | tf_op jit(solution)/shard_map/ppermute | solution.py:86
  76.4 14.7 %collective-permute-start.21 = (bf16[2,224,512]{2,1,0:T(8,128)(2,1)S(1)}, bf16[2,224,512]{2,1,0:T(8,128)(2,1)S(1)}, u32[]{:S(2)}, u32[]{:S(2)}) collective-permute-start(bf16[2,224,512]{2,1,0:T(8,128)(2,1)S(1)} %get-tuple-element.54.refs_2_.refs_0_), channel_id=1, source_target_pairs={{0,1},{1,0},{2,3},{3,2},{4,5},{5,4},{6,7},{7,6},{8,9},{9,8},{10,11... | collective-permute-start | bytes 1376264 | tf_op jit(solution)/shard_map/ppermute | solution.py:71
  83.5 8.4 %collective-permute-start.20 = (bf16[2,560,512]{2,1,0:T(8,128)(2,1)S(1)}, bf16[2,560,512]{2,1,0:T(8,128)(2,1)S(1)}, u32[]{:S(2)}, u32[]{:S(2)}) collective-permute-start(bf16[2,560,512]{2,1,0:T(8,128)(2,1)S(1)} %join.5.refs_0_), channel_id=1, source_target_pairs={{0,2},{2,0},{4,6},{6,4},{8,10},{10,8},{12,14},{14,12},{16,18},{18,... | collective-permute-start | bytes 3440648 | tf_op jit(solution)/shard_map/ppermute | solution.py:71
  86.4 8.9 %collective-permute-start.19 = (bf16[2,112,512]{2,1,0:T(8,128)(2,1)S(1)}, bf16[2,112,512]{2,1,0:T(8,128)(2,1)S(1)}, u32[]{:S(2)}, u32[]{:S(2)}) collective-permute-start(bf16[2,112,512]{2,1,0:T(8,128)(2,1)S(1)} %get-tuple-element.55.refs_4_.refs_0_.refs_2_), channel_id=1, source_target_pairs={{0,1},{1,0},{2,3},{3,2},{4,5},{5,4},{6,7},{7,6},{8,9},{9,8},{10,11... | collective-permute-start | bytes 688136 | tf_op jit(solution)/shard_map/ppermute | solution.py:71
  91.2 4.3 %collective-permute-start.25 = (bf16[2,224,512]{2,1,0:T(8,128)(2,1)S(1)}, bf16[2,224,512]{2,1,0:T(8,128)(2,1)S(1)}, u32[]{:S(2)}, u32[]{:S(2)}) collective-permute-start(bf16[2,224,512]{2,1,0:T(8,128)(2,1)S(1)} %join.6.refs_0_.refs_1_), channel_id=1, source_target_pairs={{0,2},{2,0},{4,6},{6,4},{8,10},{10,8},{12,14},{14,12},{16,18},{18,... | collective-permute-start | bytes 1376264 | tf_op jit(solution)/shard_map/ppermute | solution.py:71
  91.3 4.2 %collective-permute-start.24 = (bf16[4,336,512]{2,1,0:T(8,128)(2,1)S(1)}, bf16[4,336,512]{2,1,0:T(8,128)(2,1)S(1)}, u32[]{:S(2)}, u32[]{:S(2)}) collective-permute-start(bf16[4,336,512]{2,1,0:T(8,128)(2,1)S(1)} %get-tuple-element.60), channel_id=1, source_target_pairs={{0,2},{2,0},{4,6},{6,4},{8,10},{10,8},{12,14},{14,12},{16,18},{18,... | collective-permute-start | bytes 4128776 | tf_op jit(solution)/shard_map/ppermute | solution.py:71
  (6 other events, 14.5 us)

commit v9 on v8

--- a/solution.py
+++ b/solution.py
@@ -32,6 +32,7 @@
     far=(),
     out=pltpu.VMEM,
     cost=0,
+    aliases=None,
 ):
     extra = len(after)
 
@@ -55,6 +56,7 @@
                 dimension_semantics=("arbitrary",) * len(grid), vmem_limit_bytes=VMEM_LIMIT
             ),
             cost_estimate=estimate(cost),
+            input_output_aliases=aliases or {},
             name=name,
         )(*held)
 
@@ -159,35 +161,35 @@
     )(amplitudes)
 
 
-def mix_kernel(parts, start, *refs):
-    far, arrived, out = refs[:parts], refs[parts:-1], refs[-1]
+def mix_kernel(parts, start, at, *refs):
+    far, arrived, out = refs[:parts], refs[parts], refs[-1]
     step = far[0].shape[1]
-    first = 0
-    for r in arrived:
-        rows = r.shape[1]
-        while rows:
-            part, at = divmod(start + first, step)
-            here = min(rows, step - at)
-            came = r.shape[1] - rows
-            value = 2.0 * far[part][:, at : at + here].astype(F32)
-            value -= r[:, came : came + here].astype(F32)
-            out[:, first : first + here] = value.astype(BF16)
-            first, rows = first + here, rows - here
-
-
-def mix(far, arrived, start, after=(), cost=0):
-    count, _, width = far[0].shape
-    shape = (count, sum(r.shape[1] for r in arrived), width)
+    first, last = 0, arrived.shape[1]
+    while first < last:
+        part, row = divmod(start + first, step)
+        here = min(last - first, step - row)
+        value = 2.0 * far[part][:, row : row + here].astype(F32)
+        value -= arrived[:, first : first + here].astype(F32)
+        out[:, at + first : at + first + here] = value.astype(BF16)
+        first += here
+
+
+def mix(far, arrived, start, rows=None, into=None, after=(), cost=0):
+    count, more, width = arrived.shape
+    at = start if into is not None else 0
+    shape = (count, rows or more, width) if into is None else into.shape
+    args = [*far, arrived] + ([] if into is None else [into])
     (out,) = kernel_call(
-        functools.partial(mix_kernel, len(far), start),
+        functools.partial(mix_kernel, len(far), start, at),
         "mix",
         (1,),
-        [WHOLE] * (len(far) + len(arrived)),
+        [WHOLE] * len(args),
         [WHOLE],
         [(shape, BF16)],
         after=after,
         cost=cost,
-    )(*far, *arrived)
+        aliases=None if into is None else {len(args) - 1: 0},
+    )(*args)
     return out
 
 
@@ -431,18 +433,20 @@
         if part == parts // 2 - 1:
             wall_1 = wall(*vectors[1:3], arrived[0], *near_theirs, cost=WALLS[0])
             held = [wall_1]
-    begun = diagonal(
-        amplitudes, energy_virtual, energy_first, energy_second, after=near
-    )
-    wall_2 = wall(*vectors[3:5], arrived[1], *near_theirs[parts // 2 :], *begun, cost=WALLS[1])
-    far_0 = mix(far_turned, arrived[:2], 0, after=[wall_2])
+    begun = diagonal(amplitudes, energy_virtual, energy_first, energy_second, after=near)
+    cut_at, cut_end = (sum(v.shape[1] for v in sent[:n]) for n in (1, 2))
+    far_0 = mix(far_turned, arrived[0], 0, rows=cut_end, after=begun)
+    wall_2 = wall(
+        *vectors[3:5], arrived[1], *near_theirs[parts // 2 :], far_0, cost=WALLS[1]
+    )
+    far_0 = mix(far_turned, arrived[1], cut_at, into=far_0, after=[wall_2])
     far_0_theirs = to_core(far_0)
     near, near_theirs = [near], [near_theirs]
     n_a, same_a, cross_a = partial(
         vectors[:5], vectors[:5], near, near_theirs, joined=2, after=[far_0]
     )
     n_a_sent = to_tile(n_a)
-    far_1 = mix(far_turned, arrived[2:], far_0.shape[1], after=[n_a], cost=MIXED)
+    far_1 = mix(far_turned, arrived[2], far_0.shape[1], after=[n_a], cost=MIXED)
     far_1_theirs = to_core(far_1)
     far, far_theirs = [far_0, far_1], [far_0_theirs, far_1_theirs]
     f_a, cross_a = partial([same_a], [cross_a], [far], [far_theirs], joined=1)

time: 99.8 us -> 99.5 us (level)
    pallas_call x23 -> x24, Pallas kernels: 33.4 us -> 33.3 us  [call(): pl.pallas_call(kernel, grid=grid, in_specs=[*in_specs, *[ANYWHERE] * extr...]
  transfers between devices with their start and end apart: 26 -> 26, of which waited for: 13 -> 14; matrix products, arithmetic and copies ran while one was open for 0% -> 0% of each run, Pallas kernels for 31% -> 31%
where the time goes in v9:
time: 99.5 us; the launch traced here: 99.2 us
  waiting for transfers between devices  45.1 us (45%)
  Pallas kernels  33.3 us (33%)
  starting transfers between devices  20.3 us (20%)
    pallas_call x24, Pallas kernels, call(): pl.pallas_call(kernel, grid=grid, in_specs=[*in_specs, *[ANYWHERE] * extr...  33.3 us
    ppermute x18, waiting for transfers between devices, swap(): lax.ppermute(x, axis, [(i, i ^ 1 << bit) for i in range(lax.axis_size(axi...  28.1 us
    ppermute x8, waiting for transfers between devices, along_ring(): return lax.ppermute(x, 'pair', pairs)  17 us
    ppermute x18, starting transfers between devices, swap(): lax.ppermute(x, axis, [(i, i ^ 1 << bit) for i in range(lax.axis_size(axi...  11.2 us
    ppermute x8, starting transfers between devices, along_ring(): return lax.ppermute(x, 'pair', pairs)  9.16 us
  transfers between devices with their start and end apart: 26, of which 14 were waited for; matrix products, arithmetic and copies ran while one was open for 0% of the time, Pallas kernels for 31%

profile of v9, /device:TPU:0, one launch (start us, length us, event | category | flops | bytes accessed | tf_op | source)
XLA Modules:
  0.0 99.2 jit_solution(1295815964156359774)
XLA Ops:
  0.0 3.0 %collective-permute-start = (bf16[8,112,512]{2,1,0:T(8,128)(2,1)}, bf16[8,112,512]{2,1,0:T(8,128)(2,1)S(1)}, u32[]{:S(2)}, u32[]{:S(2)}) collective-permute-start(bf16[8,112,512]{2,1,0:T(8,128)(2,1)} %bitcast.2), channel_id=1, source_target_pairs={{0,8},{2,10},{8,16},{10,18},{16,24},{18,26},{24,28},{26,30},{28,20... | collective-permute-start | bytes 2752520 | tf_op jit(solution)/shard_map/ppermute | solution.py:88
  4.2 2.0 %collective-permute-start.6 = (bf16[4,240,512]{2,1,0:T(8,128)(2,1)S(1)}, bf16[4,240,512]{2,1,0:T(8,128)(2,1)S(1)}, u32[]{:S(2)}, u32[]{:S(2)}) collective-permute-start(bf16[4,240,512]{2,1,0:T(8,128)(2,1)S(1)} %cut.2.refs_1_), channel_id=1, source_target_pairs={{0,1},{1,0},{2,3},{3,2},{4,5},{5,4},{6,7},{7,6},{8,9},{9,8},{10,11... | collective-permute-start | bytes 2949128 | tf_op jit(solution)/shard_map/ppermute | solution.py:73
  7.5 1.8 %turn.4 = (bf16[4,128,512]{2,1,0:T(8,128)(2,1)S(1)}, bf16[4,128,512]{2,1,0:T(8,128)(2,1)S(1)}) custom-call(bf16[4,1024,512]{2,1,0:T(8,128)(2,1)} %refs_0_.13, bf16[4,208,512]{2,1,0:T(8,128)(2,1)S(1)} %get-tuple-element.34.refs_1_, bf16[4,64,512]{2,1,0:T(8,128)(2,1)S(1)} %get-tuple-element.35.refs_2_), custom_call_target="tpu_custom_call" | custom-call | flops 1 | bytes 1 | tf_op jit(solution)/shard_map/turn/pallas_call | solution.py:48
  9.4 1.8 %turn.5 = (bf16[4,128,512]{2,1,0:T(8,128)(2,1)S(1)}, bf16[4,128,512]{2,1,0:T(8,128)(2,1)S(1)}) custom-call(bf16[4,1024,512]{2,1,0:T(8,128)(2,1)} %refs_0_.13, bf16[4,208,512]{2,1,0:T(8,128)(2,1)S(1)} %get-tuple-element.34.refs_1_, bf16[4,64,512]{2,1,0:T(8,128)(2,1)S(1)} %get-tuple-element.35.refs_2_), custom_call_target="tpu_custom_call" | custom-call | flops 1 | bytes 1 | tf_op jit(solution)/shard_map/turn/pallas_call | solution.py:48
  11.7 11.8 %collective-permute-done.refs_0_.refs_1_.refs_6_ = bf16[8,112,512]{2,1,0:T(8,128)(2,1)S(1)} collective-permute-done((bf16[8,112,512]{2,1,0:T(8,128)(2,1)}, bf16[8,112,512]{2,1,0:T(8,128)(2,1)S(1)}, u32[]{:S(2)}, u32[]{:S(2)}) %collective-permute-start) | collective-permute-done | bytes 917536 | tf_op jit(solution)/shard_map/ppermute | solution.py:88
  23.5 1.8 %collective-permute-start.1 = (bf16[8,112,512]{2,1,0:T(8,128)(2,1)S(1)}, bf16[8,112,512]{2,1,0:T(8,128)(2,1)S(1)}, u32[]{:S(2)}, u32[]{:S(2)}) collective-permute-start(bf16[8,112,512]{2,1,0:T(8,128)(2,1)S(1)} %collective-permute-done.refs_0_.refs_1_.refs_6_), channel_id=1, source_target_pairs={{0,8},{2,10},{8,16},{10,18},{16,24},{18,26},{24,28},{26,30},{28,20... | collective-permute-start | bytes 2752520 | tf_op jit(solution)/shard_map/ppermute | solution.py:88
  25.5 1.8 %collective-permute-start.11 = (bf16[4,208,512]{2,1,0:T(8,128)(2,1)S(1)}, bf16[4,208,512]{2,1,0:T(8,128)(2,1)S(1)}, u32[]{:S(2)}, u32[]{:S(2)}) collective-permute-start(bf16[4,208,512]{2,1,0:T(8,128)(2,1)S(1)} %get-tuple-element.34.refs_1_), channel_id=1, source_target_pairs={{0,1},{1,0},{2,3},{3,2},{4,5},{5,4},{6,7},{7,6},{8,9},{9,8},{10,11... | collective-permute-start | bytes 2555912 | tf_op jit(solution)/shard_map/ppermute | solution.py:73
  28.1 1.7 %turn.6 = (bf16[4,128,512]{2,1,0:T(8,128)(2,1)S(1)}, bf16[4,128,512]{2,1,0:T(8,128)(2,1)S(1)}) custom-call(bf16[4,1024,512]{2,1,0:T(8,128)(2,1)} %refs_0_.13, f32[8,128]{1,0:T(8,128)S(1)} %wall.5.refs_1_), custom_call_target="tpu_custom_call" | custom-call | flops 1 | bytes 1 | tf_op jit(solution)/shard_map/turn/pallas_call | solution.py:48
  29.9 1.8 %turn.7 = (bf16[4,128,512]{2,1,0:T(8,128)(2,1)S(1)}, bf16[4,128,512]{2,1,0:T(8,128)(2,1)S(1)}) custom-call(bf16[4,1024,512]{2,1,0:T(8,128)(2,1)} %refs_0_.13, f32[8,128]{1,0:T(8,128)S(1)} %wall.5.refs_1_), custom_call_target="tpu_custom_call" | custom-call | flops 1 | bytes 1 | tf_op jit(solution)/shard_map/turn/pallas_call | solution.py:48
  32.3 3.2 %diagonal.1 = (f32[4,512,512]{2,1,0:T(8,128)S(1)}, f32[4,512,512]{2,1,0:T(8,128)S(1)}) custom-call(bf16[4,1024,512]{2,1,0:T(8,128)(2,1)} %refs_0_.13, f32[2,1,512]{2,1,0:T(1,128)S(1)} %bitcast.6, f32[8]{0:T(128)S(1)} %copy-done.2, f32[8]{0:T(128)S(1)} %copy-done.3, bf16[4,128,512]{2,1,0:T(8,128)(2,1)S(1)} %get-tuple-element.36.refs_4_.refs_10_.refs_2_, ...), custom_call_target="tpu_custom_call" | custom-call | flops 1 | bytes 1 | tf_op jit(solution)/shard_map/diagonal/pallas_call | solution.py:48
  35.7 10.0 %collective-permute-done.11.refs_2_.refs_4_ = bf16[4,208,512]{2,1,0:T(8,128)(2,1)S(1)} collective-permute-done((bf16[4,208,512]{2,1,0:T(8,128)(2,1)S(1)}, bf16[4,208,512]{2,1,0:T(8,128)(2,1)S(1)}, u32[]{:S(2)}, u32[]{:S(2)}) %collective-permute-start.11) | collective-permute-done | bytes 852000 | tf_op jit(solution)/shard_map/ppermute | solution.py:73
  50.2 2.5 %partial.4 = (bf16[1,560,512]{2,1,0:T(8,128)(2,1)S(1)}, bf16[4,560,512]{2,1,0:T(8,128)(2,1)S(1)}, bf16[4,560,512]{2,1,0:T(8,128)(2,1)S(1)}) custom-call(bf16[8,112,512]{2,1,0:T(8,128)(2,1)S(1)} %bitcast.4, bf16[8,112,512]{2,1,0:T(8,128)(2,1)S(1)} %collective-permute-done.refs_0_.refs_1_.refs_6_, ...), custom_call_target="tpu_custom_call" | custom-call | flops 1 | bytes 1 | tf_op jit(solution)/shard_map/partial/pallas_call | solution.py:48
  53.3 2.2 %collective-permute-done.12.refs_4_ = bf16[4,64,512]{2,1,0:T(8,128)(2,1)S(1)} collective-permute-done((bf16[4,64,512]{2,1,0:T(8,128)(2,1)S(1)}, bf16[4,64,512]{2,1,0:T(8,128)(2,1)S(1)}, u32[]{:S(2)}, u32[]{:S(2)}) %collective-permute-start.12) | collective-permute-done | bytes 262176 | tf_op jit(solution)/shard_map/ppermute | solution.py:73
  57.3 2.5 %partial.5 = (bf16[1,560,512]{2,1,0:T(8,128)(2,1)S(1)}, bf16[4,560,512]{2,1,0:T(8,128)(2,1)S(1)}) custom-call(bf16[4,560,512]{2,1,0:T(8,128)(2,1)S(1)} %get-tuple-element.46.refs_0_.refs_1_, bf16[4,560,512]{2,1,0:T(8,128)(2,1)S(1)} %get-tuple-element.47.refs_1_, bf16[4,448,512]{2,1,0:T(8,128)(2,1)S(1)} %mix.4.refs_18_.refs_2_.refs_8_.refs_6_, ...), custom_call_target="tpu_custom_call" | custom-call | flops 1 | bytes 1 | tf_op jit(solution)/shard_map/partial/pallas_call | solution.py:48
  60.0 1.8 %collective-permute-start.18 = (bf16[1,560,512]{2,1,0:T(8,128)(2,1)S(1)}, bf16[1,560,512]{2,1,0:T(8,128)(2,1)S(1)}, u32[]{:S(2)}, u32[]{:S(2)}) collective-permute-start(bf16[1,560,512]{2,1,0:T(8,128)(2,1)S(1)} %get-tuple-element.49.refs_2_.refs_0_), channel_id=1, source_target_pairs={{0,1},{1,0},{2,3},{3,2},{4,5},{5,4},{6,7},{7,6},{8,9},{9,8},{10,11... | collective-permute-start | bytes 1720328 | tf_op jit(solution)/shard_map/ppermute | solution.py:73
  61.7 7.0 %collective-permute-done.15.refs_3_.refs_1_ = bf16[1,560,512]{2,1,0:T(8,128)(2,1)S(1)} collective-permute-done((bf16[1,560,512]{2,1,0:T(8,128)(2,1)S(1)}, bf16[1,560,512]{2,1,0:T(8,128)(2,1)S(1)}, u32[]{:S(2)}, u32[]{:S(2)}) %collective-permute-start.15) | collective-permute-done | bytes 573472 | tf_op jit(solution)/shard_map/ppermute | solution.py:73
  68.7 1.9 %collective-permute-done.2.refs_0_.refs_2_ = bf16[8,112,512]{2,1,0:T(8,128)(2,1)S(1)} collective-permute-done((bf16[8,112,512]{2,1,0:T(8,128)(2,1)S(1)}, bf16[8,112,512]{2,1,0:T(8,128)(2,1)S(1)}, u32[]{:S(2)}, u32[]{:S(2)}) %collective-permute-start.2) | collective-permute-done | bytes 917536 | tf_op jit(solution)/shard_map/ppermute | solution.py:88
  74.1 2.1 %partial.6 = (bf16[2,224,512]{2,1,0:T(8,128)(2,1)S(1)}, bf16[4,224,512]{2,1,0:T(8,128)(2,1)S(1)}, bf16[4,224,512]{2,1,0:T(8,128)(2,1)S(1)}) custom-call(bf16[8,112,512]{2,1,0:T(8,128)(2,1)S(1)} %collective-permute-done.2.refs_0_.refs_2_, bf16[8,112,512]{2,1,0:T(8,128)(2,1)S(1)} %collective-permute-done.5.refs_1_.refs_3_, ...), custom_call_target="tpu_custom_call" | custom-call | flops 1 | bytes 1 | tf_op jit(solution)/shard_map/partial/pallas_call | solution.py:48
  76.9 1.8 %residual.5.refs_4_.refs_5_ = f32[4,512,512]{2,1,0:T(8,128)S(1)} custom-call(bf16[1,560,512]{2,1,0:T(8,128)(2,1)S(1)} %join.4.refs_0_, bf16[4,560,512]{2,1,0:T(8,128)(2,1)S(1)} %get-tuple-element.46.refs_0_.refs_1_, f32[4,512,512]{2,1,0:T(8,128)S(1)} %get-tuple-element.45.refs_6_.refs_2_), custom_call_target="tpu_custom_call" | custom-call | flops 1 | bytes 1 | tf_op jit(solution)/shard_map/residual/pallas_call | solution.py:48
  78.7 2.3 %collective-permute-done.18.refs_1_ = bf16[1,560,512]{2,1,0:T(8,128)(2,1)S(1)} collective-permute-done((bf16[1,560,512]{2,1,0:T(8,128)(2,1)S(1)}, bf16[1,560,512]{2,1,0:T(8,128)(2,1)S(1)}, u32[]{:S(2)}, u32[]{:S(2)}) %collective-permute-start.18) | collective-permute-done | bytes 573472 | tf_op jit(solution)/shard_map/ppermute | solution.py:73
  81.3 1.9 %residual.6.refs_2_.refs_4_ = f32[4,512,512]{2,1,0:T(8,128)S(1)} custom-call(bf16[2,560,512]{2,1,0:T(8,128)(2,1)S(1)} %join.5.refs_0_, bf16[4,560,512]{2,1,0:T(8,128)(2,1)S(1)} %get-tuple-element.46.refs_0_.refs_1_, f32[4,512,512]{2,1,0:T(8,128)S(1)} %get-tuple-element.44.refs_5_.refs_2_), custom_call_target="tpu_custom_call" | custom-call | flops 1 | bytes 1 | tf_op jit(solution)/shard_map/residual/pallas_call | solution.py:48
  86.7 4.1 %collective-permute-done.21.refs_1_.refs_3_ = bf16[2,224,512]{2,1,0:T(8,128)(2,1)S(1)} collective-permute-done((bf16[2,224,512]{2,1,0:T(8,128)(2,1)S(1)}, bf16[2,224,512]{2,1,0:T(8,128)(2,1)S(1)}, u32[]{:S(2)}, u32[]{:S(2)}) %collective-permute-start.21) | collective-permute-done | bytes 458784 | tf_op jit(solution)/shard_map/ppermute | solution.py:73
  91.5 3.5 %residual.7 = (f32[4,512,512]{2,1,0:T(8,128)S(1)}, f32[4,512,512]{2,1,0:T(8,128)S(1)}) custom-call(bf16[2,560,512]{2,1,0:T(8,128)(2,1)S(1)} %collective-permute-done.20.refs_0_, bf16[2,224,512]{2,1,0:T(8,128)(2,1)S(1)} %join.6.refs_0_.refs_1_, bf16[4,560,512]{2,1,0:T(8,128)(2,1)S(1)} %collective-permute-done.22.refs_2_, ...), custom_call_target="tpu_custom_call" | custom-call | flops 1 | bytes 1 | tf_op jit(solution)/shard_map/residual/pallas_call | solution.py:48
  96.6 2.4 %residual.9 = bf16[4,1024,512]{2,1,0:T(8,128)(2,1)} custom-call(bf16[2,112,512]{2,1,0:T(8,128)(2,1)S(1)} %join.7.refs_6_.refs_0_, bf16[2,112,512]{2,1,0:T(8,128)(2,1)S(1)} %collective-permute-done.23.refs_1_, bf16[4,336,512]{2,1,0:T(8,128)(2,1)S(1)} %get-tuple-element.57.refs_3_.refs_2_, bf16[4,336,512]{2,1,0:T(8,128)(2,1)S(1)} %collective-permute-done.24.refs_3_, ...), custom_call_target="tpu_custom_call" | custom-call | flops 1 | bytes 1 | tf_op jit(solution)/shard_map/residual/pallas_call | solution.py:48
  (65 shorter events, 22.1 us)
Async XLA Ops:
  0.0 23.5 %collective-permute-start = (bf16[8,112,512]{2,1,0:T(8,128)(2,1)}, bf16[8,112,512]{2,1,0:T(8,128)(2,1)S(1)}, u32[]{:S(2)}, u32[]{:S(2)}) collective-permute-start(bf16[8,112,512]{2,1,0:T(8,128)(2,1)} %bitcast.2), channel_id=1, source_target_pairs={{0,8},{2,10},{8,16},{10,18},{16,24},{18,26},{24,28},{26,30},{28,20... | collective-permute-start | bytes 2752520 | tf_op jit(solution)/shard_map/ppermute | solution.py:88
  3.0 22.3 %collective-permute-start.3 = (bf16[8,112,512]{2,1,0:T(8,128)(2,1)}, bf16[8,112,512]{2,1,0:T(8,128)(2,1)S(1)}, u32[]{:S(2)}, u32[]{:S(2)}) collective-permute-start(bf16[8,112,512]{2,1,0:T(8,128)(2,1)} %bitcast.3), channel_id=1, source_target_pairs={{0,4},{2,6},{8,0},{10,2},{16,8},{18,10},{24,16},{26,18},{28,24},{3... | collective-permute-start | bytes 2752520 | tf_op jit(solution)/shard_map/ppermute | solution.py:88
  4.2 23.9 %collective-permute-start.6 = (bf16[4,240,512]{2,1,0:T(8,128)(2,1)S(1)}, bf16[4,240,512]{2,1,0:T(8,128)(2,1)S(1)}, u32[]{:S(2)}, u32[]{:S(2)}) collective-permute-start(bf16[4,240,512]{2,1,0:T(8,128)(2,1)S(1)} %cut.2.refs_1_), channel_id=1, source_target_pairs={{0,1},{1,0},{2,3},{3,2},{4,5},{5,4},{6,7},{7,6},{8,9},{9,8},{10,11... | collective-permute-start | bytes 2949128 | tf_op jit(solution)/shard_map/ppermute | solution.py:73
  9.3 16.3 %collective-permute-start.7 = (bf16[4,128,512]{2,1,0:T(8,128)(2,1)S(1)}, bf16[4,128,512]{2,1,0:T(8,128)(2,1)S(1)}, u32[]{:S(2)}, u32[]{:S(2)}) collective-permute-start(bf16[4,128,512]{2,1,0:T(8,128)(2,1)S(1)} %get-tuple-element.36.refs_4_.refs_10_.refs_2_), channel_id=1, source_target_pairs={{0,2},{2,0},{4,6},{6,4},{8,10},{10,8},{12,14},{14,12},{16,18},{18,... | collective-permute-start | bytes 1572872 | tf_op jit(solution)/shard_map/ppermute | solution.py:73
  11.1 16.2 %collective-permute-start.8 = (bf16[4,128,512]{2,1,0:T(8,128)(2,1)S(1)}, bf16[4,128,512]{2,1,0:T(8,128)(2,1)S(1)}, u32[]{:S(2)}, u32[]{:S(2)}) collective-permute-start(bf16[4,128,512]{2,1,0:T(8,128)(2,1)S(1)} %get-tuple-element.37.refs_5_.refs_11_.refs_3_), channel_id=1, source_target_pairs={{0,2},{2,0},{4,6},{6,4},{8,10},{10,8},{12,14},{14,12},{16,18},{18,... | collective-permute-start | bytes 1572872 | tf_op jit(solution)/shard_map/ppermute | solution.py:73
  23.5 22.3 %collective-permute-start.1 = (bf16[8,112,512]{2,1,0:T(8,128)(2,1)S(1)}, bf16[8,112,512]{2,1,0:T(8,128)(2,1)S(1)}, u32[]{:S(2)}, u32[]{:S(2)}) collective-permute-start(bf16[8,112,512]{2,1,0:T(8,128)(2,1)S(1)} %collective-permute-done.refs_0_.refs_1_.refs_6_), channel_id=1, source_target_pairs={{0,8},{2,10},{8,16},{10,18},{16,24},{18,26},{24,28},{26,30},{28,20... | collective-permute-start | bytes 2752520 | tf_op jit(solution)/shard_map/ppermute | solution.py:88
  25.3 20.9 %collective-permute-start.4 = (bf16[8,112,512]{2,1,0:T(8,128)(2,1)S(1)}, bf16[8,112,512]{2,1,0:T(8,128)(2,1)S(1)}, u32[]{:S(2)}, u32[]{:S(2)}) collective-permute-start(bf16[8,112,512]{2,1,0:T(8,128)(2,1)S(1)} %collective-permute-done.3.refs_1_.refs_2_.refs_7_), channel_id=1, source_target_pairs={{0,4},{2,6},{8,0},{10,2},{16,8},{18,10},{24,16},{26,18},{28,24},{3... | collective-permute-start | bytes 2752520 | tf_op jit(solution)/shard_map/ppermute | solution.py:88
  25.5 20.3 %collective-permute-start.11 = (bf16[4,208,512]{2,1,0:T(8,128)(2,1)S(1)}, bf16[4,208,512]{2,1,0:T(8,128)(2,1)S(1)}, u32[]{:S(2)}, u32[]{:S(2)}) collective-permute-start(bf16[4,208,512]{2,1,0:T(8,128)(2,1)S(1)} %get-tuple-element.34.refs_1_), channel_id=1, source_target_pairs={{0,1},{1,0},{2,3},{3,2},{4,5},{5,4},{6,7},{7,6},{8,9},{9,8},{10,11... | collective-permute-start | bytes 2555912 | tf_op jit(solution)/shard_map/ppermute | solution.py:73
  31.7 14.1 %collective-permute-start.10 = (bf16[4,128,512]{2,1,0:T(8,128)(2,1)S(1)}, bf16[4,128,512]{2,1,0:T(8,128)(2,1)S(1)}, u32[]{:S(2)}, u32[]{:S(2)}) collective-permute-start(bf16[4,128,512]{2,1,0:T(8,128)(2,1)S(1)} %get-tuple-element.39.refs_7_.refs_13_.refs_5_), channel_id=1, source_target_pairs={{0,2},{2,0},{4,6},{6,4},{8,10},{10,8},{12,14},{14,12},{16,18},{18,... | collective-permute-start | bytes 1572872 | tf_op jit(solution)/shard_map/ppermute | solution.py:73
  31.8 14.0 %collective-permute-start.9 = (bf16[4,128,512]{2,1,0:T(8,128)(2,1)S(1)}, bf16[4,128,512]{2,1,0:T(8,128)(2,1)S(1)}, u32[]{:S(2)}, u32[]{:S(2)}) collective-permute-start(bf16[4,128,512]{2,1,0:T(8,128)(2,1)S(1)} %get-tuple-element.38.refs_6_.refs_12_.refs_4_), channel_id=1, source_target_pairs={{0,2},{2,0},{4,6},{6,4},{8,10},{10,8},{12,14},{14,12},{16,18},{18,... | collective-permute-start | bytes 1572872 | tf_op jit(solution)/shard_map/ppermute | solution.py:73
  46.5 10.7 %collective-permute-start.13 = (bf16[4,448,512]{2,1,0:T(8,128)(2,1)S(1)}, bf16[4,448,512]{2,1,0:T(8,128)(2,1)S(1)}, u32[]{:S(2)}, u32[]{:S(2)}) collective-permute-start(bf16[4,448,512]{2,1,0:T(8,128)(2,1)S(1)} %mix.4.refs_18_.refs_2_.refs_8_.refs_6_), channel_id=1, source_target_pairs={{0,2},{2,0},{4,6},{6,4},{8,10},{10,8},{12,14},{14,12},{16,18},{18,... | collective-permute-start | bytes 5505032 | tf_op jit(solution)/shard_map/ppermute | solution.py:73
  46.6 9.0 %collective-permute-start.12 = (bf16[4,64,512]{2,1,0:T(8,128)(2,1)S(1)}, bf16[4,64,512]{2,1,0:T(8,128)(2,1)S(1)}, u32[]{:S(2)}, u32[]{:S(2)}) collective-permute-start(bf16[4,64,512]{2,1,0:T(8,128)(2,1)S(1)} %get-tuple-element.35.refs_2_), channel_id=1, source_target_pairs={{0,1},{1,0},{2,3},{3,2},{4,5},{5,4},{6,7},{7,6},{8,9},{9,8},{10,11... | collective-permute-start | bytes 786440 | tf_op jit(solution)/shard_map/ppermute | solution.py:73
  48.2 22.4 %collective-permute-start.2 = (bf16[8,112,512]{2,1,0:T(8,128)(2,1)S(1)}, bf16[8,112,512]{2,1,0:T(8,128)(2,1)S(1)}, u32[]{:S(2)}, u32[]{:S(2)}) collective-permute-start(bf16[8,112,512]{2,1,0:T(8,128)(2,1)S(1)} %collective-permute-done.1.refs_0_.refs_3_.refs_8_), channel_id=1, source_target_pairs={{0,8},{2,10},{8,16},{10,18},{16,24},{18,26},{24,28},{26,30},{28,20... | collective-permute-start | bytes 2752520 | tf_op jit(solution)/shard_map/ppermute | solution.py:88
  49.8 22.1 %collective-permute-start.5 = (bf16[8,112,512]{2,1,0:T(8,128)(2,1)S(1)}, bf16[8,112,512]{2,1,0:T(8,128)(2,1)S(1)}, u32[]{:S(2)}, u32[]{:S(2)}) collective-permute-start(bf16[8,112,512]{2,1,0:T(8,128)(2,1)S(1)} %collective-permute-done.4.refs_1_.refs_4_.refs_9_), channel_id=1, source_target_pairs={{0,4},{2,6},{8,0},{10,2},{16,8},{18,10},{24,16},{26,18},{28,24},{3... | collective-permute-start | bytes 2752520 | tf_op jit(solution)/shard_map/ppermute | solution.py:88
  52.8 16.0 %collective-permute-start.15 = (bf16[1,560,512]{2,1,0:T(8,128)(2,1)S(1)}, bf16[1,560,512]{2,1,0:T(8,128)(2,1)S(1)}, u32[]{:S(2)}, u32[]{:S(2)}) collective-permute-start(bf16[1,560,512]{2,1,0:T(8,128)(2,1)S(1)} %get-tuple-element.48.refs_5_.refs_0_), channel_id=1, source_target_pairs={{0,1},{1,0},{2,3},{3,2},{4,5},{5,4},{6,7},{7,6},{8,9},{9,8},{10,11... | collective-permute-start | bytes 1720328 | tf_op jit(solution)/shard_map/ppermute | solution.py:73
  59.8 31.7 %collective-permute-start.22 = (bf16[4,560,512]{2,1,0:T(8,128)(2,1)S(1)}, bf16[4,560,512]{2,1,0:T(8,128)(2,1)S(1)}, u32[]{:S(2)}, u32[]{:S(2)}) collective-permute-start(bf16[4,560,512]{2,1,0:T(8,128)(2,1)S(1)} %get-tuple-element.56), channel_id=1, source_target_pairs={{0,2},{2,0},{4,6},{6,4},{8,10},{10,8},{12,14},{14,12},{16,18},{18,... | collective-permute-start | bytes 6881288 | tf_op jit(solution)/shard_map/ppermute | solution.py:73
  60.0 21.0 %collective-permute-start.18 = (bf16[1,560,512]{2,1,0:T(8,128)(2,1)S(1)}, bf16[1,560,512]{2,1,0:T(8,128)(2,1)S(1)}, u32[]{:S(2)}, u32[]{:S(2)}) collective-permute-start(bf16[1,560,512]{2,1,0:T(8,128)(2,1)S(1)} %get-tuple-element.49.refs_2_.refs_0_), channel_id=1, source_target_pairs={{0,1},{1,0},{2,3},{3,2},{4,5},{5,4},{6,7},{7,6},{8,9},{9,8},{10,11... | collective-permute-start | bytes 1720328 | tf_op jit(solution)/shard_map/ppermute | solution.py:73
  72.0 11.5 %collective-permute-start.16 = (bf16[4,112,512]{2,1,0:T(8,128)(2,1)S(1)}, bf16[4,112,512]{2,1,0:T(8,128)(2,1)S(1)}, u32[]{:S(2)}, u32[]{:S(2)}) collective-permute-start(bf16[4,112,512]{2,1,0:T(8,128)(2,1)S(1)} %get-tuple-element.50.refs_0_), channel_id=1, source_target_pairs={{0,8},{2,10},{8,16},{10,18},{16,24},{18,26},{24,28},{26,30},{28,20... | collective-permute-start | bytes 1376264 | tf_op jit(solution)/shard_map/ppermute | solution.py:88
  73.6 11.2 %collective-permute-start.17 = (bf16[4,112,512]{2,1,0:T(8,128)(2,1)S(1)}, bf16[4,112,512]{2,1,0:T(8,128)(2,1)S(1)}, u32[]{:S(2)}, u32[]{:S(2)}) collective-permute-start(bf16[4,112,512]{2,1,0:T(8,128)(2,1)S(1)} %get-tuple-element.51.refs_1_), channel_id=1, source_target_pairs={{0,4},{2,6},{8,0},{10,2},{16,8},{18,10},{24,16},{26,18},{28,24},{3... | collective-permute-start | bytes 1376264 | tf_op jit(solution)/shard_map/ppermute | solution.py:88
  76.1 14.7 %collective-permute-start.21 = (bf16[2,224,512]{2,1,0:T(8,128)(2,1)S(1)}, bf16[2,224,512]{2,1,0:T(8,128)(2,1)S(1)}, u32[]{:S(2)}, u32[]{:S(2)}) collective-permute-start(bf16[2,224,512]{2,1,0:T(8,128)(2,1)S(1)} %get-tuple-element.54.refs_2_.refs_0_), channel_id=1, source_target_pairs={{0,1},{1,0},{2,3},{3,2},{4,5},{5,4},{6,7},{7,6},{8,9},{9,8},{10,11... | collective-permute-start | bytes 1376264 | tf_op jit(solution)/shard_map/ppermute | solution.py:73
  83.2 8.4 %collective-permute-start.20 = (bf16[2,560,512]{2,1,0:T(8,128)(2,1)S(1)}, bf16[2,560,512]{2,1,0:T(8,128)(2,1)S(1)}, u32[]{:S(2)}, u32[]{:S(2)}) collective-permute-start(bf16[2,560,512]{2,1,0:T(8,128)(2,1)S(1)} %join.5.refs_0_), channel_id=1, source_target_pairs={{0,2},{2,0},{4,6},{6,4},{8,10},{10,8},{12,14},{14,12},{16,18},{18,... | collective-permute-start | bytes 3440648 | tf_op jit(solution)/shard_map/ppermute | solution.py:73
  86.1 8.9 %collective-permute-start.19 = (bf16[2,112,512]{2,1,0:T(8,128)(2,1)S(1)}, bf16[2,112,512]{2,1,0:T(8,128)(2,1)S(1)}, u32[]{:S(2)}, u32[]{:S(2)}) collective-permute-start(bf16[2,112,512]{2,1,0:T(8,128)(2,1)S(1)} %get-tuple-element.55.refs_4_.refs_0_.refs_2_), channel_id=1, source_target_pairs={{0,1},{1,0},{2,3},{3,2},{4,5},{5,4},{6,7},{7,6},{8,9},{9,8},{10,11... | collective-permute-start | bytes 688136 | tf_op jit(solution)/shard_map/ppermute | solution.py:73
  90.9 4.3 %collective-permute-start.25 = (bf16[2,224,512]{2,1,0:T(8,128)(2,1)S(1)}, bf16[2,224,512]{2,1,0:T(8,128)(2,1)S(1)}, u32[]{:S(2)}, u32[]{:S(2)}) collective-permute-start(bf16[2,224,512]{2,1,0:T(8,128)(2,1)S(1)} %join.6.refs_0_.refs_1_), channel_id=1, source_target_pairs={{0,2},{2,0},{4,6},{6,4},{8,10},{10,8},{12,14},{14,12},{16,18},{18,... | collective-permute-start | bytes 1376264 | tf_op jit(solution)/shard_map/ppermute | solution.py:73
  91.0 4.2 %collective-permute-start.24 = (bf16[4,336,512]{2,1,0:T(8,128)(2,1)S(1)}, bf16[4,336,512]{2,1,0:T(8,128)(2,1)S(1)}, u32[]{:S(2)}, u32[]{:S(2)}) collective-permute-start(bf16[4,336,512]{2,1,0:T(8,128)(2,1)S(1)} %get-tuple-element.60), channel_id=1, source_target_pairs={{0,2},{2,0},{4,6},{6,4},{8,10},{10,8},{12,14},{14,12},{16,18},{18,... | collective-permute-start | bytes 4128776 | tf_op jit(solution)/shard_map/ppermute | solution.py:73
  (6 other events, 14.2 us)

commit v10 on v9

--- a/solution.py
+++ b/solution.py
@@ -410,7 +410,7 @@
     to_tile = functools.partial(swap, axis="virt", bit=0)
 
     unit = width // 32
-    pieces = [(0, 15 * unit), (15 * unit, 13 * unit), (28 * unit, 4 * unit)]
+    pieces = [(0, 17 * unit), (17 * unit, 11 * unit), (28 * unit, 4 * unit)]
     sent = cut(amplitudes, pieces[:1])
     sent += cut(amplitudes, pieces[1:], after=sent)
     arrived = [to_tile(v) for v in sent]

time: 99.5 us -> 99.5 us (level)
  no operation moved by 1% of the time
where the time goes in v10:
time: 99.5 us; the launch traced here: 99.2 us
  waiting for transfers between devices  45.1 us (45%)
  Pallas kernels  33.3 us (33%)
  starting transfers between devices  20.3 us (20%)
    pallas_call x24, Pallas kernels, call(): pl.pallas_call(kernel, grid=grid, in_specs=[*in_specs, *[ANYWHERE] * extr...  33.3 us
    ppermute x18, waiting for transfers between devices, swap(): lax.ppermute(x, axis, [(i, i ^ 1 << bit) for i in range(lax.axis_size(axi...  28.2 us
    ppermute x8, waiting for transfers between devices, along_ring(): return lax.ppermute(x, 'pair', pairs)  16.9 us
    ppermute x18, starting transfers between devices, swap(): lax.ppermute(x, axis, [(i, i ^ 1 << bit) for i in range(lax.axis_size(axi...  11.2 us
    ppermute x8, starting transfers between devices, along_ring(): return lax.ppermute(x, 'pair', pairs)  9.16 us
  transfers between devices with their start and end apart: 26, of which 14 were waited for; matrix products, arithmetic and copies ran while one was open for 0% of the time, Pallas kernels for 31%

profile of v10, /device:TPU:0, one launch (start us, length us, event | category | flops | bytes accessed | tf_op | source)
XLA Modules:
  0.0 99.2 jit_solution(11295014578623225997)
XLA Ops:
  0.0 3.0 %collective-permute-start = (bf16[8,112,512]{2,1,0:T(8,128)(2,1)}, bf16[8,112,512]{2,1,0:T(8,128)(2,1)S(1)}, u32[]{:S(2)}, u32[]{:S(2)}) collective-permute-start(bf16[8,112,512]{2,1,0:T(8,128)(2,1)} %bitcast.2), channel_id=1, source_target_pairs={{0,8},{2,10},{8,16},{10,18},{16,24},{18,26},{24,28},{26,30},{28,20... | collective-permute-start | bytes 2752520 | tf_op jit(solution)/shard_map/ppermute | solution.py:88
  4.3 2.0 %collective-permute-start.6 = (bf16[4,272,512]{2,1,0:T(8,128)(2,1)S(1)}, bf16[4,272,512]{2,1,0:T(8,128)(2,1)S(1)}, u32[]{:S(2)}, u32[]{:S(2)}) collective-permute-start(bf16[4,272,512]{2,1,0:T(8,128)(2,1)S(1)} %cut.2.refs_1_), channel_id=1, source_target_pairs={{0,1},{1,0},{2,3},{3,2},{4,5},{5,4},{6,7},{7,6},{8,9},{9,8},{10,11... | collective-permute-start | bytes 3342344 | tf_op jit(solution)/shard_map/ppermute | solution.py:73
  7.5 1.8 %turn.4 = (bf16[4,128,512]{2,1,0:T(8,128)(2,1)S(1)}, bf16[4,128,512]{2,1,0:T(8,128)(2,1)S(1)}) custom-call(bf16[4,1024,512]{2,1,0:T(8,128)(2,1)} %refs_0_.13, bf16[4,176,512]{2,1,0:T(8,128)(2,1)S(1)} %get-tuple-element.34.refs_1_, bf16[4,64,512]{2,1,0:T(8,128)(2,1)S(1)} %get-tuple-element.35.refs_2_), custom_call_target="tpu_custom_call" | custom-call | flops 1 | bytes 1 | tf_op jit(solution)/shard_map/turn/pallas_call | solution.py:48
  9.4 1.8 %turn.5 = (bf16[4,128,512]{2,1,0:T(8,128)(2,1)S(1)}, bf16[4,128,512]{2,1,0:T(8,128)(2,1)S(1)}) custom-call(bf16[4,1024,512]{2,1,0:T(8,128)(2,1)} %refs_0_.13, bf16[4,176,512]{2,1,0:T(8,128)(2,1)S(1)} %get-tuple-element.34.refs_1_, bf16[4,64,512]{2,1,0:T(8,128)(2,1)S(1)} %get-tuple-element.35.refs_2_), custom_call_target="tpu_custom_call" | custom-call | flops 1 | bytes 1 | tf_op jit(solution)/shard_map/turn/pallas_call | solution.py:48
  11.7 11.8 %collective-permute-done.refs_0_.refs_1_.refs_6_ = bf16[8,112,512]{2,1,0:T(8,128)(2,1)S(1)} collective-permute-done((bf16[8,112,512]{2,1,0:T(8,128)(2,1)}, bf16[8,112,512]{2,1,0:T(8,128)(2,1)S(1)}, u32[]{:S(2)}, u32[]{:S(2)}) %collective-permute-start) | collective-permute-done | bytes 917536 | tf_op jit(solution)/shard_map/ppermute | solution.py:88
  23.5 1.8 %collective-permute-start.1 = (bf16[8,112,512]{2,1,0:T(8,128)(2,1)S(1)}, bf16[8,112,512]{2,1,0:T(8,128)(2,1)S(1)}, u32[]{:S(2)}, u32[]{:S(2)}) collective-permute-start(bf16[8,112,512]{2,1,0:T(8,128)(2,1)S(1)} %collective-permute-done.refs_0_.refs_1_.refs_6_), channel_id=1, source_target_pairs={{0,8},{2,10},{8,16},{10,18},{16,24},{18,26},{24,28},{26,30},{28,20... | collective-permute-start | bytes 2752520 | tf_op jit(solution)/shard_map/ppermute | solution.py:88
  25.5 1.8 %collective-permute-start.11 = (bf16[4,176,512]{2,1,0:T(8,128)(2,1)S(1)}, bf16[4,176,512]{2,1,0:T(8,128)(2,1)S(1)}, u32[]{:S(2)}, u32[]{:S(2)}) collective-permute-start(bf16[4,176,512]{2,1,0:T(8,128)(2,1)S(1)} %get-tuple-element.34.refs_1_), channel_id=1, source_target_pairs={{0,1},{1,0},{2,3},{3,2},{4,5},{5,4},{6,7},{7,6},{8,9},{9,8},{10,11... | collective-permute-start | bytes 2162696 | tf_op jit(solution)/shard_map/ppermute | solution.py:73
  27.3 4.5 %collective-permute-done.6.refs_2_.refs_4_ = bf16[4,272,512]{2,1,0:T(8,128)(2,1)S(1)} collective-permute-done((bf16[4,272,512]{2,1,0:T(8,128)(2,1)S(1)}, bf16[4,272,512]{2,1,0:T(8,128)(2,1)S(1)}, u32[]{:S(2)}, u32[]{:S(2)}) %collective-permute-start.6) | collective-permute-done | bytes 1114144 | tf_op jit(solution)/shard_map/ppermute | solution.py:73
  31.8 1.7 %turn.6 = (bf16[4,128,512]{2,1,0:T(8,128)(2,1)S(1)}, bf16[4,128,512]{2,1,0:T(8,128)(2,1)S(1)}) custom-call(bf16[4,1024,512]{2,1,0:T(8,128)(2,1)} %refs_0_.13, f32[8,128]{1,0:T(8,128)S(1)} %wall.5.refs_1_), custom_call_target="tpu_custom_call" | custom-call | flops 1 | bytes 1 | tf_op jit(solution)/shard_map/turn/pallas_call | solution.py:48
  33.6 1.8 %turn.7 = (bf16[4,128,512]{2,1,0:T(8,128)(2,1)S(1)}, bf16[4,128,512]{2,1,0:T(8,128)(2,1)S(1)}) custom-call(bf16[4,1024,512]{2,1,0:T(8,128)(2,1)} %refs_0_.13, f32[8,128]{1,0:T(8,128)S(1)} %wall.5.refs_1_), custom_call_target="tpu_custom_call" | custom-call | flops 1 | bytes 1 | tf_op jit(solution)/shard_map/turn/pallas_call | solution.py:48
  36.0 3.2 %diagonal.1 = (f32[4,512,512]{2,1,0:T(8,128)S(1)}, f32[4,512,512]{2,1,0:T(8,128)S(1)}) custom-call(bf16[4,1024,512]{2,1,0:T(8,128)(2,1)} %refs_0_.13, f32[2,1,512]{2,1,0:T(1,128)S(1)} %bitcast.6, f32[8]{0:T(128)S(1)} %copy-done.2, f32[8]{0:T(128)S(1)} %copy-done.3, bf16[4,128,512]{2,1,0:T(8,128)(2,1)S(1)} %get-tuple-element.36.refs_4_.refs_10_.refs_2_, ...), custom_call_target="tpu_custom_call" | custom-call | flops 1 | bytes 1 | tf_op jit(solution)/shard_map/diagonal/pallas_call | solution.py:48
  39.5 6.3 %collective-permute-done.11.refs_2_.refs_4_ = bf16[4,176,512]{2,1,0:T(8,128)(2,1)S(1)} collective-permute-done((bf16[4,176,512]{2,1,0:T(8,128)(2,1)S(1)}, bf16[4,176,512]{2,1,0:T(8,128)(2,1)S(1)}, u32[]{:S(2)}, u32[]{:S(2)}) %collective-permute-start.11) | collective-permute-done | bytes 720928 | tf_op jit(solution)/shard_map/ppermute | solution.py:73
  50.2 2.5 %partial.4 = (bf16[1,560,512]{2,1,0:T(8,128)(2,1)S(1)}, bf16[4,560,512]{2,1,0:T(8,128)(2,1)S(1)}, bf16[4,560,512]{2,1,0:T(8,128)(2,1)S(1)}) custom-call(bf16[8,112,512]{2,1,0:T(8,128)(2,1)S(1)} %bitcast.4, bf16[8,112,512]{2,1,0:T(8,128)(2,1)S(1)} %collective-permute-done.refs_0_.refs_1_.refs_6_, ...), custom_call_target="tpu_custom_call" | custom-call | flops 1 | bytes 1 | tf_op jit(solution)/shard_map/partial/pallas_call | solution.py:48
  53.3 2.2 %collective-permute-done.12.refs_4_ = bf16[4,64,512]{2,1,0:T(8,128)(2,1)S(1)} collective-permute-done((bf16[4,64,512]{2,1,0:T(8,128)(2,1)S(1)}, bf16[4,64,512]{2,1,0:T(8,128)(2,1)S(1)}, u32[]{:S(2)}, u32[]{:S(2)}) %collective-permute-start.12) | collective-permute-done | bytes 262176 | tf_op jit(solution)/shard_map/ppermute | solution.py:73
  57.2 2.5 %partial.5 = (bf16[1,560,512]{2,1,0:T(8,128)(2,1)S(1)}, bf16[4,560,512]{2,1,0:T(8,128)(2,1)S(1)}) custom-call(bf16[4,560,512]{2,1,0:T(8,128)(2,1)S(1)} %get-tuple-element.46.refs_0_.refs_1_, bf16[4,560,512]{2,1,0:T(8,128)(2,1)S(1)} %get-tuple-element.47.refs_1_, bf16[4,448,512]{2,1,0:T(8,128)(2,1)S(1)} %mix.4.refs_18_.refs_2_.refs_8_.refs_6_, ...), custom_call_target="tpu_custom_call" | custom-call | flops 1 | bytes 1 | tf_op jit(solution)/shard_map/partial/pallas_call | solution.py:48
  61.7 7.0 %collective-permute-done.15.refs_3_.refs_1_ = bf16[1,560,512]{2,1,0:T(8,128)(2,1)S(1)} collective-permute-done((bf16[1,560,512]{2,1,0:T(8,128)(2,1)S(1)}, bf16[1,560,512]{2,1,0:T(8,128)(2,1)S(1)}, u32[]{:S(2)}, u32[]{:S(2)}) %collective-permute-start.15) | collective-permute-done | bytes 573472 | tf_op jit(solution)/shard_map/ppermute | solution.py:73
  68.7 1.9 %collective-permute-done.2.refs_0_.refs_2_ = bf16[8,112,512]{2,1,0:T(8,128)(2,1)S(1)} collective-permute-done((bf16[8,112,512]{2,1,0:T(8,128)(2,1)S(1)}, bf16[8,112,512]{2,1,0:T(8,128)(2,1)S(1)}, u32[]{:S(2)}, u32[]{:S(2)}) %collective-permute-start.2) | collective-permute-done | bytes 917536 | tf_op jit(solution)/shard_map/ppermute | solution.py:88
  74.0 2.1 %partial.6 = (bf16[2,224,512]{2,1,0:T(8,128)(2,1)S(1)}, bf16[4,224,512]{2,1,0:T(8,128)(2,1)S(1)}, bf16[4,224,512]{2,1,0:T(8,128)(2,1)S(1)}) custom-call(bf16[8,112,512]{2,1,0:T(8,128)(2,1)S(1)} %collective-permute-done.2.refs_0_.refs_2_, bf16[8,112,512]{2,1,0:T(8,128)(2,1)S(1)} %collective-permute-done.5.refs_1_.refs_3_, ...), custom_call_target="tpu_custom_call" | custom-call | flops 1 | bytes 1 | tf_op jit(solution)/shard_map/partial/pallas_call | solution.py:48
  76.8 1.8 %residual.5.refs_4_.refs_5_ = f32[4,512,512]{2,1,0:T(8,128)S(1)} custom-call(bf16[1,560,512]{2,1,0:T(8,128)(2,1)S(1)} %join.4.refs_0_, bf16[4,560,512]{2,1,0:T(8,128)(2,1)S(1)} %get-tuple-element.46.refs_0_.refs_1_, f32[4,512,512]{2,1,0:T(8,128)S(1)} %get-tuple-element.45.refs_6_.refs_2_), custom_call_target="tpu_custom_call" | custom-call | flops 1 | bytes 1 | tf_op jit(solution)/shard_map/residual/pallas_call | solution.py:48
  78.7 2.3 %collective-permute-done.18.refs_1_ = bf16[1,560,512]{2,1,0:T(8,128)(2,1)S(1)} collective-permute-done((bf16[1,560,512]{2,1,0:T(8,128)(2,1)S(1)}, bf16[1,560,512]{2,1,0:T(8,128)(2,1)S(1)}, u32[]{:S(2)}, u32[]{:S(2)}) %collective-permute-start.18) | collective-permute-done | bytes 573472 | tf_op jit(solution)/shard_map/ppermute | solution.py:73
  81.3 1.9 %residual.6.refs_2_.refs_4_ = f32[4,512,512]{2,1,0:T(8,128)S(1)} custom-call(bf16[2,560,512]{2,1,0:T(8,128)(2,1)S(1)} %join.5.refs_0_, bf16[4,560,512]{2,1,0:T(8,128)(2,1)S(1)} %get-tuple-element.46.refs_0_.refs_1_, f32[4,512,512]{2,1,0:T(8,128)S(1)} %get-tuple-element.44.refs_5_.refs_2_), custom_call_target="tpu_custom_call" | custom-call | flops 1 | bytes 1 | tf_op jit(solution)/shard_map/residual/pallas_call | solution.py:48
  86.7 4.1 %collective-permute-done.21.refs_1_.refs_3_ = bf16[2,224,512]{2,1,0:T(8,128)(2,1)S(1)} collective-permute-done((bf16[2,224,512]{2,1,0:T(8,128)(2,1)S(1)}, bf16[2,224,512]{2,1,0:T(8,128)(2,1)S(1)}, u32[]{:S(2)}, u32[]{:S(2)}) %collective-permute-start.21) | collective-permute-done | bytes 458784 | tf_op jit(solution)/shard_map/ppermute | solution.py:73
  91.5 3.5 %residual.7 = (f32[4,512,512]{2,1,0:T(8,128)S(1)}, f32[4,512,512]{2,1,0:T(8,128)S(1)}) custom-call(bf16[2,560,512]{2,1,0:T(8,128)(2,1)S(1)} %collective-permute-done.20.refs_0_, bf16[2,224,512]{2,1,0:T(8,128)(2,1)S(1)} %join.6.refs_0_.refs_1_, bf16[4,560,512]{2,1,0:T(8,128)(2,1)S(1)} %collective-permute-done.22.refs_2_, ...), custom_call_target="tpu_custom_call" | custom-call | flops 1 | bytes 1 | tf_op jit(solution)/shard_map/residual/pallas_call | solution.py:48
  96.6 2.4 %residual.9 = bf16[4,1024,512]{2,1,0:T(8,128)(2,1)} custom-call(bf16[2,112,512]{2,1,0:T(8,128)(2,1)S(1)} %join.7.refs_6_.refs_0_, bf16[2,112,512]{2,1,0:T(8,128)(2,1)S(1)} %collective-permute-done.23.refs_1_, bf16[4,336,512]{2,1,0:T(8,128)(2,1)S(1)} %get-tuple-element.57.refs_3_.refs_2_, bf16[4,336,512]{2,1,0:T(8,128)(2,1)S(1)} %collective-permute-done.24.refs_3_, ...), custom_call_target="tpu_custom_call" | custom-call | flops 1 | bytes 1 | tf_op jit(solution)/shard_map/residual/pallas_call | solution.py:48
  (65 shorter events, 22.9 us)
Async XLA Ops:
  0.0 23.5 %collective-permute-start = (bf16[8,112,512]{2,1,0:T(8,128)(2,1)}, bf16[8,112,512]{2,1,0:T(8,128)(2,1)S(1)}, u32[]{:S(2)}, u32[]{:S(2)}) collective-permute-start(bf16[8,112,512]{2,1,0:T(8,128)(2,1)} %bitcast.2), channel_id=1, source_target_pairs={{0,8},{2,10},{8,16},{10,18},{16,24},{18,26},{24,28},{26,30},{28,20... | collective-permute-start | bytes 2752520 | tf_op jit(solution)/shard_map/ppermute | solution.py:88
  3.0 22.3 %collective-permute-start.3 = (bf16[8,112,512]{2,1,0:T(8,128)(2,1)}, bf16[8,112,512]{2,1,0:T(8,128)(2,1)S(1)}, u32[]{:S(2)}, u32[]{:S(2)}) collective-permute-start(bf16[8,112,512]{2,1,0:T(8,128)(2,1)} %bitcast.3), channel_id=1, source_target_pairs={{0,4},{2,6},{8,0},{10,2},{16,8},{18,10},{24,16},{26,18},{28,24},{3... | collective-permute-start | bytes 2752520 | tf_op jit(solution)/shard_map/ppermute | solution.py:88
  4.3 27.6 %collective-permute-start.6 = (bf16[4,272,512]{2,1,0:T(8,128)(2,1)S(1)}, bf16[4,272,512]{2,1,0:T(8,128)(2,1)S(1)}, u32[]{:S(2)}, u32[]{:S(2)}) collective-permute-start(bf16[4,272,512]{2,1,0:T(8,128)(2,1)S(1)} %cut.2.refs_1_), channel_id=1, source_target_pairs={{0,1},{1,0},{2,3},{3,2},{4,5},{5,4},{6,7},{7,6},{8,9},{9,8},{10,11... | collective-permute-start | bytes 3342344 | tf_op jit(solution)/shard_map/ppermute | solution.py:73
  9.3 16.2 %collective-permute-start.7 = (bf16[4,128,512]{2,1,0:T(8,128)(2,1)S(1)}, bf16[4,128,512]{2,1,0:T(8,128)(2,1)S(1)}, u32[]{:S(2)}, u32[]{:S(2)}) collective-permute-start(bf16[4,128,512]{2,1,0:T(8,128)(2,1)S(1)} %get-tuple-element.36.refs_4_.refs_10_.refs_2_), channel_id=1, source_target_pairs={{0,2},{2,0},{4,6},{6,4},{8,10},{10,8},{12,14},{14,12},{16,18},{18,... | collective-permute-start | bytes 1572872 | tf_op jit(solution)/shard_map/ppermute | solution.py:73
  11.1 16.2 %collective-permute-start.8 = (bf16[4,128,512]{2,1,0:T(8,128)(2,1)S(1)}, bf16[4,128,512]{2,1,0:T(8,128)(2,1)S(1)}, u32[]{:S(2)}, u32[]{:S(2)}) collective-permute-start(bf16[4,128,512]{2,1,0:T(8,128)(2,1)S(1)} %get-tuple-element.37.refs_5_.refs_11_.refs_3_), channel_id=1, source_target_pairs={{0,2},{2,0},{4,6},{6,4},{8,10},{10,8},{12,14},{14,12},{16,18},{18,... | collective-permute-start | bytes 1572872 | tf_op jit(solution)/shard_map/ppermute | solution.py:73
  23.5 22.3 %collective-permute-start.1 = (bf16[8,112,512]{2,1,0:T(8,128)(2,1)S(1)}, bf16[8,112,512]{2,1,0:T(8,128)(2,1)S(1)}, u32[]{:S(2)}, u32[]{:S(2)}) collective-permute-start(bf16[8,112,512]{2,1,0:T(8,128)(2,1)S(1)} %collective-permute-done.refs_0_.refs_1_.refs_6_), channel_id=1, source_target_pairs={{0,8},{2,10},{8,16},{10,18},{16,24},{18,26},{24,28},{26,30},{28,20... | collective-permute-start | bytes 2752520 | tf_op jit(solution)/shard_map/ppermute | solution.py:88
  25.3 20.9 %collective-permute-start.4 = (bf16[8,112,512]{2,1,0:T(8,128)(2,1)S(1)}, bf16[8,112,512]{2,1,0:T(8,128)(2,1)S(1)}, u32[]{:S(2)}, u32[]{:S(2)}) collective-permute-start(bf16[8,112,512]{2,1,0:T(8,128)(2,1)S(1)} %collective-permute-done.3.refs_1_.refs_2_.refs_7_), channel_id=1, source_target_pairs={{0,4},{2,6},{8,0},{10,2},{16,8},{18,10},{24,16},{26,18},{28,24},{3... | collective-permute-start | bytes 2752520 | tf_op jit(solution)/shard_map/ppermute | solution.py:88
  25.5 20.3 %collective-permute-start.11 = (bf16[4,176,512]{2,1,0:T(8,128)(2,1)S(1)}, bf16[4,176,512]{2,1,0:T(8,128)(2,1)S(1)}, u32[]{:S(2)}, u32[]{:S(2)}) collective-permute-start(bf16[4,176,512]{2,1,0:T(8,128)(2,1)S(1)} %get-tuple-element.34.refs_1_), channel_id=1, source_target_pairs={{0,1},{1,0},{2,3},{3,2},{4,5},{5,4},{6,7},{7,6},{8,9},{9,8},{10,11... | collective-permute-start | bytes 2162696 | tf_op jit(solution)/shard_map/ppermute | solution.py:73
  35.4 10.4 %collective-permute-start.10 = (bf16[4,128,512]{2,1,0:T(8,128)(2,1)S(1)}, bf16[4,128,512]{2,1,0:T(8,128)(2,1)S(1)}, u32[]{:S(2)}, u32[]{:S(2)}) collective-permute-start(bf16[4,128,512]{2,1,0:T(8,128)(2,1)S(1)} %get-tuple-element.39.refs_7_.refs_13_.refs_5_), channel_id=1, source_target_pairs={{0,2},{2,0},{4,6},{6,4},{8,10},{10,8},{12,14},{14,12},{16,18},{18,... | collective-permute-start | bytes 1572872 | tf_op jit(solution)/shard_map/ppermute | solution.py:73
  35.5 10.3 %collective-permute-start.9 = (bf16[4,128,512]{2,1,0:T(8,128)(2,1)S(1)}, bf16[4,128,512]{2,1,0:T(8,128)(2,1)S(1)}, u32[]{:S(2)}, u32[]{:S(2)}) collective-permute-start(bf16[4,128,512]{2,1,0:T(8,128)(2,1)S(1)} %get-tuple-element.38.refs_6_.refs_12_.refs_4_), channel_id=1, source_target_pairs={{0,2},{2,0},{4,6},{6,4},{8,10},{10,8},{12,14},{14,12},{16,18},{18,... | collective-permute-start | bytes 1572872 | tf_op jit(solution)/shard_map/ppermute | solution.py:73
  46.5 10.7 %collective-permute-start.13 = (bf16[4,448,512]{2,1,0:T(8,128)(2,1)S(1)}, bf16[4,448,512]{2,1,0:T(8,128)(2,1)S(1)}, u32[]{:S(2)}, u32[]{:S(2)}) collective-permute-start(bf16[4,448,512]{2,1,0:T(8,128)(2,1)S(1)} %mix.4.refs_18_.refs_2_.refs_8_.refs_6_), channel_id=1, source_target_pairs={{0,2},{2,0},{4,6},{6,4},{8,10},{10,8},{12,14},{14,12},{16,18},{18,... | collective-permute-start | bytes 5505032 | tf_op jit(solution)/shard_map/ppermute | solution.py:73
  46.6 9.0 %collective-permute-start.12 = (bf16[4,64,512]{2,1,0:T(8,128)(2,1)S(1)}, bf16[4,64,512]{2,1,0:T(8,128)(2,1)S(1)}, u32[]{:S(2)}, u32[]{:S(2)}) collective-permute-start(bf16[4,64,512]{2,1,0:T(8,128)(2,1)S(1)} %get-tuple-element.35.refs_2_), channel_id=1, source_target_pairs={{0,1},{1,0},{2,3},{3,2},{4,5},{5,4},{6,7},{7,6},{8,9},{9,8},{10,11... | collective-permute-start | bytes 786440 | tf_op jit(solution)/shard_map/ppermute | solution.py:73
  48.2 22.4 %collective-permute-start.2 = (bf16[8,112,512]{2,1,0:T(8,128)(2,1)S(1)}, bf16[8,112,512]{2,1,0:T(8,128)(2,1)S(1)}, u32[]{:S(2)}, u32[]{:S(2)}) collective-permute-start(bf16[8,112,512]{2,1,0:T(8,128)(2,1)S(1)} %collective-permute-done.1.refs_0_.refs_3_.refs_8_), channel_id=1, source_target_pairs={{0,8},{2,10},{8,16},{10,18},{16,24},{18,26},{24,28},{26,30},{28,20... | collective-permute-start | bytes 2752520 | tf_op jit(solution)/shard_map/ppermute | solution.py:88
  49.7 22.1 %collective-permute-start.5 = (bf16[8,112,512]{2,1,0:T(8,128)(2,1)S(1)}, bf16[8,112,512]{2,1,0:T(8,128)(2,1)S(1)}, u32[]{:S(2)}, u32[]{:S(2)}) collective-permute-start(bf16[8,112,512]{2,1,0:T(8,128)(2,1)S(1)} %collective-permute-done.4.refs_1_.refs_4_.refs_9_), channel_id=1, source_target_pairs={{0,4},{2,6},{8,0},{10,2},{16,8},{18,10},{24,16},{26,18},{28,24},{3... | collective-permute-start | bytes 2752520 | tf_op jit(solution)/shard_map/ppermute | solution.py:88
  52.7 16.0 %collective-permute-start.15 = (bf16[1,560,512]{2,1,0:T(8,128)(2,1)S(1)}, bf16[1,560,512]{2,1,0:T(8,128)(2,1)S(1)}, u32[]{:S(2)}, u32[]{:S(2)}) collective-permute-start(bf16[1,560,512]{2,1,0:T(8,128)(2,1)S(1)} %get-tuple-element.48.refs_5_.refs_0_), channel_id=1, source_target_pairs={{0,1},{1,0},{2,3},{3,2},{4,5},{5,4},{6,7},{7,6},{8,9},{9,8},{10,11... | collective-permute-start | bytes 1720328 | tf_op jit(solution)/shard_map/ppermute | solution.py:73
  59.8 31.7 %collective-permute-start.22 = (bf16[4,560,512]{2,1,0:T(8,128)(2,1)S(1)}, bf16[4,560,512]{2,1,0:T(8,128)(2,1)S(1)}, u32[]{:S(2)}, u32[]{:S(2)}) collective-permute-start(bf16[4,560,512]{2,1,0:T(8,128)(2,1)S(1)} %get-tuple-element.56), channel_id=1, source_target_pairs={{0,2},{2,0},{4,6},{6,4},{8,10},{10,8},{12,14},{14,12},{16,18},{18,... | collective-permute-start | bytes 6881288 | tf_op jit(solution)/shard_map/ppermute | solution.py:73
  60.0 21.0 %collective-permute-start.18 = (bf16[1,560,512]{2,1,0:T(8,128)(2,1)S(1)}, bf16[1,560,512]{2,1,0:T(8,128)(2,1)S(1)}, u32[]{:S(2)}, u32[]{:S(2)}) collective-permute-start(bf16[1,560,512]{2,1,0:T(8,128)(2,1)S(1)} %get-tuple-element.49.refs_2_.refs_0_), channel_id=1, source_target_pairs={{0,1},{1,0},{2,3},{3,2},{4,5},{5,4},{6,7},{7,6},{8,9},{9,8},{10,11... | collective-permute-start | bytes 1720328 | tf_op jit(solution)/shard_map/ppermute | solution.py:73
  71.9 11.5 %collective-permute-start.16 = (bf16[4,112,512]{2,1,0:T(8,128)(2,1)S(1)}, bf16[4,112,512]{2,1,0:T(8,128)(2,1)S(1)}, u32[]{:S(2)}, u32[]{:S(2)}) collective-permute-start(bf16[4,112,512]{2,1,0:T(8,128)(2,1)S(1)} %get-tuple-element.50.refs_0_), channel_id=1, source_target_pairs={{0,8},{2,10},{8,16},{10,18},{16,24},{18,26},{24,28},{26,30},{28,20... | collective-permute-start | bytes 1376264 | tf_op jit(solution)/shard_map/ppermute | solution.py:88
  73.6 11.2 %collective-permute-start.17 = (bf16[4,112,512]{2,1,0:T(8,128)(2,1)S(1)}, bf16[4,112,512]{2,1,0:T(8,128)(2,1)S(1)}, u32[]{:S(2)}, u32[]{:S(2)}) collective-permute-start(bf16[4,112,512]{2,1,0:T(8,128)(2,1)S(1)} %get-tuple-element.51.refs_1_), channel_id=1, source_target_pairs={{0,4},{2,6},{8,0},{10,2},{16,8},{18,10},{24,16},{26,18},{28,24},{3... | collective-permute-start | bytes 1376264 | tf_op jit(solution)/shard_map/ppermute | solution.py:88
  76.1 14.7 %collective-permute-start.21 = (bf16[2,224,512]{2,1,0:T(8,128)(2,1)S(1)}, bf16[2,224,512]{2,1,0:T(8,128)(2,1)S(1)}, u32[]{:S(2)}, u32[]{:S(2)}) collective-permute-start(bf16[2,224,512]{2,1,0:T(8,128)(2,1)S(1)} %get-tuple-element.54.refs_2_.refs_0_), channel_id=1, source_target_pairs={{0,1},{1,0},{2,3},{3,2},{4,5},{5,4},{6,7},{7,6},{8,9},{9,8},{10,11... | collective-permute-start | bytes 1376264 | tf_op jit(solution)/shard_map/ppermute | solution.py:73
  83.2 8.3 %collective-permute-start.20 = (bf16[2,560,512]{2,1,0:T(8,128)(2,1)S(1)}, bf16[2,560,512]{2,1,0:T(8,128)(2,1)S(1)}, u32[]{:S(2)}, u32[]{:S(2)}) collective-permute-start(bf16[2,560,512]{2,1,0:T(8,128)(2,1)S(1)} %join.5.refs_0_), channel_id=1, source_target_pairs={{0,2},{2,0},{4,6},{6,4},{8,10},{10,8},{12,14},{14,12},{16,18},{18,... | collective-permute-start | bytes 3440648 | tf_op jit(solution)/shard_map/ppermute | solution.py:73
  86.1 8.9 %collective-permute-start.19 = (bf16[2,112,512]{2,1,0:T(8,128)(2,1)S(1)}, bf16[2,112,512]{2,1,0:T(8,128)(2,1)S(1)}, u32[]{:S(2)}, u32[]{:S(2)}) collective-permute-start(bf16[2,112,512]{2,1,0:T(8,128)(2,1)S(1)} %get-tuple-element.55.refs_4_.refs_0_.refs_2_), channel_id=1, source_target_pairs={{0,1},{1,0},{2,3},{3,2},{4,5},{5,4},{6,7},{7,6},{8,9},{9,8},{10,11... | collective-permute-start | bytes 688136 | tf_op jit(solution)/shard_map/ppermute | solution.py:73
  90.9 4.3 %collective-permute-start.25 = (bf16[2,224,512]{2,1,0:T(8,128)(2,1)S(1)}, bf16[2,224,512]{2,1,0:T(8,128)(2,1)S(1)}, u32[]{:S(2)}, u32[]{:S(2)}) collective-permute-start(bf16[2,224,512]{2,1,0:T(8,128)(2,1)S(1)} %join.6.refs_0_.refs_1_), channel_id=1, source_target_pairs={{0,2},{2,0},{4,6},{6,4},{8,10},{10,8},{12,14},{14,12},{16,18},{18,... | collective-permute-start | bytes 1376264 | tf_op jit(solution)/shard_map/ppermute | solution.py:73
  91.0 4.2 %collective-permute-start.24 = (bf16[4,336,512]{2,1,0:T(8,128)(2,1)S(1)}, bf16[4,336,512]{2,1,0:T(8,128)(2,1)S(1)}, u32[]{:S(2)}, u32[]{:S(2)}) collective-permute-start(bf16[4,336,512]{2,1,0:T(8,128)(2,1)S(1)} %get-tuple-element.60), channel_id=1, source_target_pairs={{0,2},{2,0},{4,6},{6,4},{8,10},{10,8},{12,14},{14,12},{16,18},{18,... | collective-permute-start | bytes 4128776 | tf_op jit(solution)/shard_map/ppermute | solution.py:73
  (6 other events, 14.2 us)

commit v11 on v10

--- a/solution.py
+++ b/solution.py
@@ -410,7 +410,7 @@
     to_tile = functools.partial(swap, axis="virt", bit=0)
 
     unit = width // 32
-    pieces = [(0, 17 * unit), (17 * unit, 11 * unit), (28 * unit, 4 * unit)]
+    pieces = [(0, 16 * unit), (16 * unit, 12 * unit), (28 * unit, 4 * unit)]
     sent = cut(amplitudes, pieces[:1])
     sent += cut(amplitudes, pieces[1:], after=sent)
     arrived = [to_tile(v) for v in sent]

time: 99.5 us -> 99.5 us (level)
  transfers between devices with their start and end apart: 26 -> 26, of which waited for: 14 -> 13; matrix products, arithmetic and copies ran while one was open for 0% -> 0% of each run, Pallas kernels for 31% -> 31%
where the time goes in v11:
time: 99.5 us; the launch traced here: 99.2 us
  waiting for transfers between devices  45.1 us (45%)
  Pallas kernels  33.3 us (33%)
  starting transfers between devices  20.3 us (20%)
    pallas_call x24, Pallas kernels, call(): pl.pallas_call(kernel, grid=grid, in_specs=[*in_specs, *[ANYWHERE] * extr...  33.3 us
    ppermute x18, waiting for transfers between devices, swap(): lax.ppermute(x, axis, [(i, i ^ 1 << bit) for i in range(lax.axis_size(axi...  28.2 us
    ppermute x8, waiting for transfers between devices, along_ring(): return lax.ppermute(x, 'pair', pairs)  17 us
    ppermute x18, starting transfers between devices, swap(): lax.ppermute(x, axis, [(i, i ^ 1 << bit) for i in range(lax.axis_size(axi...  11.1 us
    ppermute x8, starting transfers between devices, along_ring(): return lax.ppermute(x, 'pair', pairs)  9.16 us
  transfers between devices with their start and end apart: 26, of which 13 were waited for; matrix products, arithmetic and copies ran while one was open for 0% of the time, Pallas kernels for 31%

profile of v11, /device:TPU:0, one launch (start us, length us, event | category | flops | bytes accessed | tf_op | source)
XLA Modules:
  0.0 99.2 jit_solution(7932950344282257415)
XLA Ops:
  0.0 3.0 %collective-permute-start = (bf16[8,112,512]{2,1,0:T(8,128)(2,1)}, bf16[8,112,512]{2,1,0:T(8,128)(2,1)S(1)}, u32[]{:S(2)}, u32[]{:S(2)}) collective-permute-start(bf16[8,112,512]{2,1,0:T(8,128)(2,1)} %bitcast.2), channel_id=1, source_target_pairs={{0,8},{2,10},{8,16},{10,18},{16,24},{18,26},{24,28},{26,30},{28,20... | collective-permute-start | bytes 2752520 | tf_op jit(solution)/shard_map/ppermute | solution.py:88
  4.3 2.0 %collective-permute-start.6 = (bf16[4,256,512]{2,1,0:T(8,128)(2,1)S(1)}, bf16[4,256,512]{2,1,0:T(8,128)(2,1)S(1)}, u32[]{:S(2)}, u32[]{:S(2)}) collective-permute-start(bf16[4,256,512]{2,1,0:T(8,128)(2,1)S(1)} %cut.2.refs_1_), channel_id=1, source_target_pairs={{0,1},{1,0},{2,3},{3,2},{4,5},{5,4},{6,7},{7,6},{8,9},{9,8},{10,11... | collective-permute-start | bytes 3145736 | tf_op jit(solution)/shard_map/ppermute | solution.py:73
  7.5 1.8 %turn.4 = (bf16[4,128,512]{2,1,0:T(8,128)(2,1)S(1)}, bf16[4,128,512]{2,1,0:T(8,128)(2,1)S(1)}) custom-call(bf16[4,1024,512]{2,1,0:T(8,128)(2,1)} %refs_0_.13, bf16[4,192,512]{2,1,0:T(8,128)(2,1)S(1)} %get-tuple-element.34.refs_1_, bf16[4,64,512]{2,1,0:T(8,128)(2,1)S(1)} %get-tuple-element.35.refs_2_), custom_call_target="tpu_custom_call" | custom-call | flops 1 | bytes 1 | tf_op jit(solution)/shard_map/turn/pallas_call | solution.py:48
  9.4 1.8 %turn.5 = (bf16[4,128,512]{2,1,0:T(8,128)(2,1)S(1)}, bf16[4,128,512]{2,1,0:T(8,128)(2,1)S(1)}) custom-call(bf16[4,1024,512]{2,1,0:T(8,128)(2,1)} %refs_0_.13, bf16[4,192,512]{2,1,0:T(8,128)(2,1)S(1)} %get-tuple-element.34.refs_1_, bf16[4,64,512]{2,1,0:T(8,128)(2,1)S(1)} %get-tuple-element.35.refs_2_), custom_call_target="tpu_custom_call" | custom-call | flops 1 | bytes 1 | tf_op jit(solution)/shard_map/turn/pallas_call | solution.py:48
  11.7 11.8 %collective-permute-done.refs_0_.refs_1_.refs_6_ = bf16[8,112,512]{2,1,0:T(8,128)(2,1)S(1)} collective-permute-done((bf16[8,112,512]{2,1,0:T(8,128)(2,1)}, bf16[8,112,512]{2,1,0:T(8,128)(2,1)S(1)}, u32[]{:S(2)}, u32[]{:S(2)}) %collective-permute-start) | collective-permute-done | bytes 917536 | tf_op jit(solution)/shard_map/ppermute | solution.py:88
  23.5 1.8 %collective-permute-start.1 = (bf16[8,112,512]{2,1,0:T(8,128)(2,1)S(1)}, bf16[8,112,512]{2,1,0:T(8,128)(2,1)S(1)}, u32[]{:S(2)}, u32[]{:S(2)}) collective-permute-start(bf16[8,112,512]{2,1,0:T(8,128)(2,1)S(1)} %collective-permute-done.refs_0_.refs_1_.refs_6_), channel_id=1, source_target_pairs={{0,8},{2,10},{8,16},{10,18},{16,24},{18,26},{24,28},{26,30},{28,20... | collective-permute-start | bytes 2752520 | tf_op jit(solution)/shard_map/ppermute | solution.py:88
  25.5 1.8 %collective-permute-start.11 = (bf16[4,192,512]{2,1,0:T(8,128)(2,1)S(1)}, bf16[4,192,512]{2,1,0:T(8,128)(2,1)S(1)}, u32[]{:S(2)}, u32[]{:S(2)}) collective-permute-start(bf16[4,192,512]{2,1,0:T(8,128)(2,1)S(1)} %get-tuple-element.34.refs_1_), channel_id=1, source_target_pairs={{0,1},{1,0},{2,3},{3,2},{4,5},{5,4},{6,7},{7,6},{8,9},{9,8},{10,11... | collective-permute-start | bytes 2359304 | tf_op jit(solution)/shard_map/ppermute | solution.py:73
  27.3 3.1 %collective-permute-done.6.refs_2_.refs_4_ = bf16[4,256,512]{2,1,0:T(8,128)(2,1)S(1)} collective-permute-done((bf16[4,256,512]{2,1,0:T(8,128)(2,1)S(1)}, bf16[4,256,512]{2,1,0:T(8,128)(2,1)S(1)}, u32[]{:S(2)}, u32[]{:S(2)}) %collective-permute-start.6) | collective-permute-done | bytes 1048608 | tf_op jit(solution)/shard_map/ppermute | solution.py:73
  30.4 1.7 %turn.6 = (bf16[4,128,512]{2,1,0:T(8,128)(2,1)S(1)}, bf16[4,128,512]{2,1,0:T(8,128)(2,1)S(1)}) custom-call(bf16[4,1024,512]{2,1,0:T(8,128)(2,1)} %refs_0_.13, f32[8,128]{1,0:T(8,128)S(1)} %wall.5.refs_1_), custom_call_target="tpu_custom_call" | custom-call | flops 1 | bytes 1 | tf_op jit(solution)/shard_map/turn/pallas_call | solution.py:48
  32.2 1.8 %turn.7 = (bf16[4,128,512]{2,1,0:T(8,128)(2,1)S(1)}, bf16[4,128,512]{2,1,0:T(8,128)(2,1)S(1)}) custom-call(bf16[4,1024,512]{2,1,0:T(8,128)(2,1)} %refs_0_.13, f32[8,128]{1,0:T(8,128)S(1)} %wall.5.refs_1_), custom_call_target="tpu_custom_call" | custom-call | flops 1 | bytes 1 | tf_op jit(solution)/shard_map/turn/pallas_call | solution.py:48
  34.6 3.2 %diagonal.1 = (f32[4,512,512]{2,1,0:T(8,128)S(1)}, f32[4,512,512]{2,1,0:T(8,128)S(1)}) custom-call(bf16[4,1024,512]{2,1,0:T(8,128)(2,1)} %refs_0_.13, f32[2,1,512]{2,1,0:T(1,128)S(1)} %bitcast.6, f32[8]{0:T(128)S(1)} %copy-done.2, f32[8]{0:T(128)S(1)} %copy-done.3, bf16[4,128,512]{2,1,0:T(8,128)(2,1)S(1)} %get-tuple-element.36.refs_4_.refs_10_.refs_2_, ...), custom_call_target="tpu_custom_call" | custom-call | flops 1 | bytes 1 | tf_op jit(solution)/shard_map/diagonal/pallas_call | solution.py:48
  38.0 7.8 %collective-permute-done.11.refs_2_.refs_4_ = bf16[4,192,512]{2,1,0:T(8,128)(2,1)S(1)} collective-permute-done((bf16[4,192,512]{2,1,0:T(8,128)(2,1)S(1)}, bf16[4,192,512]{2,1,0:T(8,128)(2,1)S(1)}, u32[]{:S(2)}, u32[]{:S(2)}) %collective-permute-start.11) | collective-permute-done | bytes 786464 | tf_op jit(solution)/shard_map/ppermute | solution.py:73
  50.2 2.5 %partial.4 = (bf16[1,560,512]{2,1,0:T(8,128)(2,1)S(1)}, bf16[4,560,512]{2,1,0:T(8,128)(2,1)S(1)}, bf16[4,560,512]{2,1,0:T(8,128)(2,1)S(1)}) custom-call(bf16[8,112,512]{2,1,0:T(8,128)(2,1)S(1)} %bitcast.4, bf16[8,112,512]{2,1,0:T(8,128)(2,1)S(1)} %collective-permute-done.refs_0_.refs_1_.refs_6_, ...), custom_call_target="tpu_custom_call" | custom-call | flops 1 | bytes 1 | tf_op jit(solution)/shard_map/partial/pallas_call | solution.py:48
  53.3 2.2 %collective-permute-done.12.refs_4_ = bf16[4,64,512]{2,1,0:T(8,128)(2,1)S(1)} collective-permute-done((bf16[4,64,512]{2,1,0:T(8,128)(2,1)S(1)}, bf16[4,64,512]{2,1,0:T(8,128)(2,1)S(1)}, u32[]{:S(2)}, u32[]{:S(2)}) %collective-permute-start.12) | collective-permute-done | bytes 262176 | tf_op jit(solution)/shard_map/ppermute | solution.py:73
  57.2 2.5 %partial.5 = (bf16[1,560,512]{2,1,0:T(8,128)(2,1)S(1)}, bf16[4,560,512]{2,1,0:T(8,128)(2,1)S(1)}) custom-call(bf16[4,560,512]{2,1,0:T(8,128)(2,1)S(1)} %get-tuple-element.46.refs_0_.refs_1_, bf16[4,560,512]{2,1,0:T(8,128)(2,1)S(1)} %get-tuple-element.47.refs_1_, bf16[4,448,512]{2,1,0:T(8,128)(2,1)S(1)} %mix.4.refs_18_.refs_2_.refs_8_.refs_6_, ...), custom_call_target="tpu_custom_call" | custom-call | flops 1 | bytes 1 | tf_op jit(solution)/shard_map/partial/pallas_call | solution.py:48
  61.7 7.0 %collective-permute-done.15.refs_3_.refs_1_ = bf16[1,560,512]{2,1,0:T(8,128)(2,1)S(1)} collective-permute-done((bf16[1,560,512]{2,1,0:T(8,128)(2,1)S(1)}, bf16[1,560,512]{2,1,0:T(8,128)(2,1)S(1)}, u32[]{:S(2)}, u32[]{:S(2)}) %collective-permute-start.15) | collective-permute-done | bytes 573472 | tf_op jit(solution)/shard_map/ppermute | solution.py:73
  68.7 1.9 %collective-permute-done.2.refs_0_.refs_2_ = bf16[8,112,512]{2,1,0:T(8,128)(2,1)S(1)} collective-permute-done((bf16[8,112,512]{2,1,0:T(8,128)(2,1)S(1)}, bf16[8,112,512]{2,1,0:T(8,128)(2,1)S(1)}, u32[]{:S(2)}, u32[]{:S(2)}) %collective-permute-start.2) | collective-permute-done | bytes 917536 | tf_op jit(solution)/shard_map/ppermute | solution.py:88
  74.0 2.1 %partial.6 = (bf16[2,224,512]{2,1,0:T(8,128)(2,1)S(1)}, bf16[4,224,512]{2,1,0:T(8,128)(2,1)S(1)}, bf16[4,224,512]{2,1,0:T(8,128)(2,1)S(1)}) custom-call(bf16[8,112,512]{2,1,0:T(8,128)(2,1)S(1)} %collective-permute-done.2.refs_0_.refs_2_, bf16[8,112,512]{2,1,0:T(8,128)(2,1)S(1)} %collective-permute-done.5.refs_1_.refs_3_, ...), custom_call_target="tpu_custom_call" | custom-call | flops 1 | bytes 1 | tf_op jit(solution)/shard_map/partial/pallas_call | solution.py:48
  76.8 1.8 %residual.5.refs_4_.refs_5_ = f32[4,512,512]{2,1,0:T(8,128)S(1)} custom-call(bf16[1,560,512]{2,1,0:T(8,128)(2,1)S(1)} %join.4.refs_0_, bf16[4,560,512]{2,1,0:T(8,128)(2,1)S(1)} %get-tuple-element.46.refs_0_.refs_1_, f32[4,512,512]{2,1,0:T(8,128)S(1)} %get-tuple-element.45.refs_6_.refs_2_), custom_call_target="tpu_custom_call" | custom-call | flops 1 | bytes 1 | tf_op jit(solution)/shard_map/residual/pallas_call | solution.py:48
  78.7 2.3 %collective-permute-done.18.refs_1_ = bf16[1,560,512]{2,1,0:T(8,128)(2,1)S(1)} collective-permute-done((bf16[1,560,512]{2,1,0:T(8,128)(2,1)S(1)}, bf16[1,560,512]{2,1,0:T(8,128)(2,1)S(1)}, u32[]{:S(2)}, u32[]{:S(2)}) %collective-permute-start.18) | collective-permute-done | bytes 573472 | tf_op jit(solution)/shard_map/ppermute | solution.py:73
  81.3 1.9 %residual.6.refs_2_.refs_4_ = f32[4,512,512]{2,1,0:T(8,128)S(1)} custom-call(bf16[2,560,512]{2,1,0:T(8,128)(2,1)S(1)} %join.5.refs_0_, bf16[4,560,512]{2,1,0:T(8,128)(2,1)S(1)} %get-tuple-element.46.refs_0_.refs_1_, f32[4,512,512]{2,1,0:T(8,128)S(1)} %get-tuple-element.44.refs_5_.refs_2_), custom_call_target="tpu_custom_call" | custom-call | flops 1 | bytes 1 | tf_op jit(solution)/shard_map/residual/pallas_call | solution.py:48
  86.7 4.2 %collective-permute-done.21.refs_1_.refs_3_ = bf16[2,224,512]{2,1,0:T(8,128)(2,1)S(1)} collective-permute-done((bf16[2,224,512]{2,1,0:T(8,128)(2,1)S(1)}, bf16[2,224,512]{2,1,0:T(8,128)(2,1)S(1)}, u32[]{:S(2)}, u32[]{:S(2)}) %collective-permute-start.21) | collective-permute-done | bytes 458784 | tf_op jit(solution)/shard_map/ppermute | solution.py:73
  91.5 3.5 %residual.7 = (f32[4,512,512]{2,1,0:T(8,128)S(1)}, f32[4,512,512]{2,1,0:T(8,128)S(1)}) custom-call(bf16[2,560,512]{2,1,0:T(8,128)(2,1)S(1)} %collective-permute-done.20.refs_0_, bf16[2,224,512]{2,1,0:T(8,128)(2,1)S(1)} %join.6.refs_0_.refs_1_, bf16[4,560,512]{2,1,0:T(8,128)(2,1)S(1)} %collective-permute-done.22.refs_2_, ...), custom_call_target="tpu_custom_call" | custom-call | flops 1 | bytes 1 | tf_op jit(solution)/shard_map/residual/pallas_call | solution.py:48
  96.6 2.4 %residual.9 = bf16[4,1024,512]{2,1,0:T(8,128)(2,1)} custom-call(bf16[2,112,512]{2,1,0:T(8,128)(2,1)S(1)} %join.7.refs_6_.refs_0_, bf16[2,112,512]{2,1,0:T(8,128)(2,1)S(1)} %collective-permute-done.23.refs_1_, bf16[4,336,512]{2,1,0:T(8,128)(2,1)S(1)} %get-tuple-element.57.refs_3_.refs_2_, bf16[4,336,512]{2,1,0:T(8,128)(2,1)S(1)} %collective-permute-done.24.refs_3_, ...), custom_call_target="tpu_custom_call" | custom-call | flops 1 | bytes 1 | tf_op jit(solution)/shard_map/residual/pallas_call | solution.py:48
  (65 shorter events, 22.9 us)
Async XLA Ops:
  0.0 23.5 %collective-permute-start = (bf16[8,112,512]{2,1,0:T(8,128)(2,1)}, bf16[8,112,512]{2,1,0:T(8,128)(2,1)S(1)}, u32[]{:S(2)}, u32[]{:S(2)}) collective-permute-start(bf16[8,112,512]{2,1,0:T(8,128)(2,1)} %bitcast.2), channel_id=1, source_target_pairs={{0,8},{2,10},{8,16},{10,18},{16,24},{18,26},{24,28},{26,30},{28,20... | collective-permute-start | bytes 2752520 | tf_op jit(solution)/shard_map/ppermute | solution.py:88
  3.0 22.3 %collective-permute-start.3 = (bf16[8,112,512]{2,1,0:T(8,128)(2,1)}, bf16[8,112,512]{2,1,0:T(8,128)(2,1)S(1)}, u32[]{:S(2)}, u32[]{:S(2)}) collective-permute-start(bf16[8,112,512]{2,1,0:T(8,128)(2,1)} %bitcast.3), channel_id=1, source_target_pairs={{0,4},{2,6},{8,0},{10,2},{16,8},{18,10},{24,16},{26,18},{28,24},{3... | collective-permute-start | bytes 2752520 | tf_op jit(solution)/shard_map/ppermute | solution.py:88
  4.3 26.1 %collective-permute-start.6 = (bf16[4,256,512]{2,1,0:T(8,128)(2,1)S(1)}, bf16[4,256,512]{2,1,0:T(8,128)(2,1)S(1)}, u32[]{:S(2)}, u32[]{:S(2)}) collective-permute-start(bf16[4,256,512]{2,1,0:T(8,128)(2,1)S(1)} %cut.2.refs_1_), channel_id=1, source_target_pairs={{0,1},{1,0},{2,3},{3,2},{4,5},{5,4},{6,7},{7,6},{8,9},{9,8},{10,11... | collective-permute-start | bytes 3145736 | tf_op jit(solution)/shard_map/ppermute | solution.py:73
  9.3 16.3 %collective-permute-start.7 = (bf16[4,128,512]{2,1,0:T(8,128)(2,1)S(1)}, bf16[4,128,512]{2,1,0:T(8,128)(2,1)S(1)}, u32[]{:S(2)}, u32[]{:S(2)}) collective-permute-start(bf16[4,128,512]{2,1,0:T(8,128)(2,1)S(1)} %get-tuple-element.36.refs_4_.refs_10_.refs_2_), channel_id=1, source_target_pairs={{0,2},{2,0},{4,6},{6,4},{8,10},{10,8},{12,14},{14,12},{16,18},{18,... | collective-permute-start | bytes 1572872 | tf_op jit(solution)/shard_map/ppermute | solution.py:73
  11.1 16.2 %collective-permute-start.8 = (bf16[4,128,512]{2,1,0:T(8,128)(2,1)S(1)}, bf16[4,128,512]{2,1,0:T(8,128)(2,1)S(1)}, u32[]{:S(2)}, u32[]{:S(2)}) collective-permute-start(bf16[4,128,512]{2,1,0:T(8,128)(2,1)S(1)} %get-tuple-element.37.refs_5_.refs_11_.refs_3_), channel_id=1, source_target_pairs={{0,2},{2,0},{4,6},{6,4},{8,10},{10,8},{12,14},{14,12},{16,18},{18,... | collective-permute-start | bytes 1572872 | tf_op jit(solution)/shard_map/ppermute | solution.py:73
  23.5 22.3 %collective-permute-start.1 = (bf16[8,112,512]{2,1,0:T(8,128)(2,1)S(1)}, bf16[8,112,512]{2,1,0:T(8,128)(2,1)S(1)}, u32[]{:S(2)}, u32[]{:S(2)}) collective-permute-start(bf16[8,112,512]{2,1,0:T(8,128)(2,1)S(1)} %collective-permute-done.refs_0_.refs_1_.refs_6_), channel_id=1, source_target_pairs={{0,8},{2,10},{8,16},{10,18},{16,24},{18,26},{24,28},{26,30},{28,20... | collective-permute-start | bytes 2752520 | tf_op jit(solution)/shard_map/ppermute | solution.py:88
  25.3 20.9 %collective-permute-start.4 = (bf16[8,112,512]{2,1,0:T(8,128)(2,1)S(1)}, bf16[8,112,512]{2,1,0:T(8,128)(2,1)S(1)}, u32[]{:S(2)}, u32[]{:S(2)}) collective-permute-start(bf16[8,112,512]{2,1,0:T(8,128)(2,1)S(1)} %collective-permute-done.3.refs_1_.refs_2_.refs_7_), channel_id=1, source_target_pairs={{0,4},{2,6},{8,0},{10,2},{16,8},{18,10},{24,16},{26,18},{28,24},{3... | collective-permute-start | bytes 2752520 | tf_op jit(solution)/shard_map/ppermute | solution.py:88
  25.5 20.3 %collective-permute-start.11 = (bf16[4,192,512]{2,1,0:T(8,128)(2,1)S(1)}, bf16[4,192,512]{2,1,0:T(8,128)(2,1)S(1)}, u32[]{:S(2)}, u32[]{:S(2)}) collective-permute-start(bf16[4,192,512]{2,1,0:T(8,128)(2,1)S(1)} %get-tuple-element.34.refs_1_), channel_id=1, source_target_pairs={{0,1},{1,0},{2,3},{3,2},{4,5},{5,4},{6,7},{7,6},{8,9},{9,8},{10,11... | collective-permute-start | bytes 2359304 | tf_op jit(solution)/shard_map/ppermute | solution.py:73
  34.0 11.8 %collective-permute-start.10 = (bf16[4,128,512]{2,1,0:T(8,128)(2,1)S(1)}, bf16[4,128,512]{2,1,0:T(8,128)(2,1)S(1)}, u32[]{:S(2)}, u32[]{:S(2)}) collective-permute-start(bf16[4,128,512]{2,1,0:T(8,128)(2,1)S(1)} %get-tuple-element.39.refs_7_.refs_13_.refs_5_), channel_id=1, source_target_pairs={{0,2},{2,0},{4,6},{6,4},{8,10},{10,8},{12,14},{14,12},{16,18},{18,... | collective-permute-start | bytes 1572872 | tf_op jit(solution)/shard_map/ppermute | solution.py:73
  34.1 11.8 %collective-permute-start.9 = (bf16[4,128,512]{2,1,0:T(8,128)(2,1)S(1)}, bf16[4,128,512]{2,1,0:T(8,128)(2,1)S(1)}, u32[]{:S(2)}, u32[]{:S(2)}) collective-permute-start(bf16[4,128,512]{2,1,0:T(8,128)(2,1)S(1)} %get-tuple-element.38.refs_6_.refs_12_.refs_4_), channel_id=1, source_target_pairs={{0,2},{2,0},{4,6},{6,4},{8,10},{10,8},{12,14},{14,12},{16,18},{18,... | collective-permute-start | bytes 1572872 | tf_op jit(solution)/shard_map/ppermute | solution.py:73
  46.5 10.7 %collective-permute-start.13 = (bf16[4,448,512]{2,1,0:T(8,128)(2,1)S(1)}, bf16[4,448,512]{2,1,0:T(8,128)(2,1)S(1)}, u32[]{:S(2)}, u32[]{:S(2)}) collective-permute-start(bf16[4,448,512]{2,1,0:T(8,128)(2,1)S(1)} %mix.4.refs_18_.refs_2_.refs_8_.refs_6_), channel_id=1, source_target_pairs={{0,2},{2,0},{4,6},{6,4},{8,10},{10,8},{12,14},{14,12},{16,18},{18,... | collective-permute-start | bytes 5505032 | tf_op jit(solution)/shard_map/ppermute | solution.py:73
  46.6 9.0 %collective-permute-start.12 = (bf16[4,64,512]{2,1,0:T(8,128)(2,1)S(1)}, bf16[4,64,512]{2,1,0:T(8,128)(2,1)S(1)}, u32[]{:S(2)}, u32[]{:S(2)}) collective-permute-start(bf16[4,64,512]{2,1,0:T(8,128)(2,1)S(1)} %get-tuple-element.35.refs_2_), channel_id=1, source_target_pairs={{0,1},{1,0},{2,3},{3,2},{4,5},{5,4},{6,7},{7,6},{8,9},{9,8},{10,11... | collective-permute-start | bytes 786440 | tf_op jit(solution)/shard_map/ppermute | solution.py:73
  48.2 22.4 %collective-permute-start.2 = (bf16[8,112,512]{2,1,0:T(8,128)(2,1)S(1)}, bf16[8,112,512]{2,1,0:T(8,128)(2,1)S(1)}, u32[]{:S(2)}, u32[]{:S(2)}) collective-permute-start(bf16[8,112,512]{2,1,0:T(8,128)(2,1)S(1)} %collective-permute-done.1.refs_0_.refs_3_.refs_8_), channel_id=1, source_target_pairs={{0,8},{2,10},{8,16},{10,18},{16,24},{18,26},{24,28},{26,30},{28,20... | collective-permute-start | bytes 2752520 | tf_op jit(solution)/shard_map/ppermute | solution.py:88
  49.7 22.1 %collective-permute-start.5 = (bf16[8,112,512]{2,1,0:T(8,128)(2,1)S(1)}, bf16[8,112,512]{2,1,0:T(8,128)(2,1)S(1)}, u32[]{:S(2)}, u32[]{:S(2)}) collective-permute-start(bf16[8,112,512]{2,1,0:T(8,128)(2,1)S(1)} %collective-permute-done.4.refs_1_.refs_4_.refs_9_), channel_id=1, source_target_pairs={{0,4},{2,6},{8,0},{10,2},{16,8},{18,10},{24,16},{26,18},{28,24},{3... | collective-permute-start | bytes 2752520 | tf_op jit(solution)/shard_map/ppermute | solution.py:88
  52.7 16.0 %collective-permute-start.15 = (bf16[1,560,512]{2,1,0:T(8,128)(2,1)S(1)}, bf16[1,560,512]{2,1,0:T(8,128)(2,1)S(1)}, u32[]{:S(2)}, u32[]{:S(2)}) collective-permute-start(bf16[1,560,512]{2,1,0:T(8,128)(2,1)S(1)} %get-tuple-element.48.refs_5_.refs_0_), channel_id=1, source_target_pairs={{0,1},{1,0},{2,3},{3,2},{4,5},{5,4},{6,7},{7,6},{8,9},{9,8},{10,11... | collective-permute-start | bytes 1720328 | tf_op jit(solution)/shard_map/ppermute | solution.py:73
  59.8 31.7 %collective-permute-start.22 = (bf16[4,560,512]{2,1,0:T(8,128)(2,1)S(1)}, bf16[4,560,512]{2,1,0:T(8,128)(2,1)S(1)}, u32[]{:S(2)}, u32[]{:S(2)}) collective-permute-start(bf16[4,560,512]{2,1,0:T(8,128)(2,1)S(1)} %get-tuple-element.56), channel_id=1, source_target_pairs={{0,2},{2,0},{4,6},{6,4},{8,10},{10,8},{12,14},{14,12},{16,18},{18,... | collective-permute-start | bytes 6881288 | tf_op jit(solution)/shard_map/ppermute | solution.py:73
  60.0 21.0 %collective-permute-start.18 = (bf16[1,560,512]{2,1,0:T(8,128)(2,1)S(1)}, bf16[1,560,512]{2,1,0:T(8,128)(2,1)S(1)}, u32[]{:S(2)}, u32[]{:S(2)}) collective-permute-start(bf16[1,560,512]{2,1,0:T(8,128)(2,1)S(1)} %get-tuple-element.49.refs_2_.refs_0_), channel_id=1, source_target_pairs={{0,1},{1,0},{2,3},{3,2},{4,5},{5,4},{6,7},{7,6},{8,9},{9,8},{10,11... | collective-permute-start | bytes 1720328 | tf_op jit(solution)/shard_map/ppermute | solution.py:73
  72.0 11.5 %collective-permute-start.16 = (bf16[4,112,512]{2,1,0:T(8,128)(2,1)S(1)}, bf16[4,112,512]{2,1,0:T(8,128)(2,1)S(1)}, u32[]{:S(2)}, u32[]{:S(2)}) collective-permute-start(bf16[4,112,512]{2,1,0:T(8,128)(2,1)S(1)} %get-tuple-element.50.refs_0_), channel_id=1, source_target_pairs={{0,8},{2,10},{8,16},{10,18},{16,24},{18,26},{24,28},{26,30},{28,20... | collective-permute-start | bytes 1376264 | tf_op jit(solution)/shard_map/ppermute | solution.py:88
  73.6 11.2 %collective-permute-start.17 = (bf16[4,112,512]{2,1,0:T(8,128)(2,1)S(1)}, bf16[4,112,512]{2,1,0:T(8,128)(2,1)S(1)}, u32[]{:S(2)}, u32[]{:S(2)}) collective-permute-start(bf16[4,112,512]{2,1,0:T(8,128)(2,1)S(1)} %get-tuple-element.51.refs_1_), channel_id=1, source_target_pairs={{0,4},{2,6},{8,0},{10,2},{16,8},{18,10},{24,16},{26,18},{28,24},{3... | collective-permute-start | bytes 1376264 | tf_op jit(solution)/shard_map/ppermute | solution.py:88
  76.1 14.7 %collective-permute-start.21 = (bf16[2,224,512]{2,1,0:T(8,128)(2,1)S(1)}, bf16[2,224,512]{2,1,0:T(8,128)(2,1)S(1)}, u32[]{:S(2)}, u32[]{:S(2)}) collective-permute-start(bf16[2,224,512]{2,1,0:T(8,128)(2,1)S(1)} %get-tuple-element.54.refs_2_.refs_0_), channel_id=1, source_target_pairs={{0,1},{1,0},{2,3},{3,2},{4,5},{5,4},{6,7},{7,6},{8,9},{9,8},{10,11... | collective-permute-start | bytes 1376264 | tf_op jit(solution)/shard_map/ppermute | solution.py:73
  83.2 8.4 %collective-permute-start.20 = (bf16[2,560,512]{2,1,0:T(8,128)(2,1)S(1)}, bf16[2,560,512]{2,1,0:T(8,128)(2,1)S(1)}, u32[]{:S(2)}, u32[]{:S(2)}) collective-permute-start(bf16[2,560,512]{2,1,0:T(8,128)(2,1)S(1)} %join.5.refs_0_), channel_id=1, source_target_pairs={{0,2},{2,0},{4,6},{6,4},{8,10},{10,8},{12,14},{14,12},{16,18},{18,... | collective-permute-start | bytes 3440648 | tf_op jit(solution)/shard_map/ppermute | solution.py:73
  86.1 8.9 %collective-permute-start.19 = (bf16[2,112,512]{2,1,0:T(8,128)(2,1)S(1)}, bf16[2,112,512]{2,1,0:T(8,128)(2,1)S(1)}, u32[]{:S(2)}, u32[]{:S(2)}) collective-permute-start(bf16[2,112,512]{2,1,0:T(8,128)(2,1)S(1)} %get-tuple-element.55.refs_4_.refs_0_.refs_2_), channel_id=1, source_target_pairs={{0,1},{1,0},{2,3},{3,2},{4,5},{5,4},{6,7},{7,6},{8,9},{9,8},{10,11... | collective-permute-start | bytes 688136 | tf_op jit(solution)/shard_map/ppermute | solution.py:73
  90.9 4.3 %collective-permute-start.25 = (bf16[2,224,512]{2,1,0:T(8,128)(2,1)S(1)}, bf16[2,224,512]{2,1,0:T(8,128)(2,1)S(1)}, u32[]{:S(2)}, u32[]{:S(2)}) collective-permute-start(bf16[2,224,512]{2,1,0:T(8,128)(2,1)S(1)} %join.6.refs_0_.refs_1_), channel_id=1, source_target_pairs={{0,2},{2,0},{4,6},{6,4},{8,10},{10,8},{12,14},{14,12},{16,18},{18,... | collective-permute-start | bytes 1376264 | tf_op jit(solution)/shard_map/ppermute | solution.py:73
  91.0 4.2 %collective-permute-start.24 = (bf16[4,336,512]{2,1,0:T(8,128)(2,1)S(1)}, bf16[4,336,512]{2,1,0:T(8,128)(2,1)S(1)}, u32[]{:S(2)}, u32[]{:S(2)}) collective-permute-start(bf16[4,336,512]{2,1,0:T(8,128)(2,1)S(1)} %get-tuple-element.60), channel_id=1, source_target_pairs={{0,2},{2,0},{4,6},{6,4},{8,10},{10,8},{12,14},{14,12},{16,18},{18,... | collective-permute-start | bytes 4128776 | tf_op jit(solution)/shard_map/ppermute | solution.py:73
  (6 other events, 14.2 us)
